TPU v7x, 32 devices: a whole 2x2x4 slice. The times are simulated.
32 devices in a mesh: dp: 2 (over x), ctx: 16 (over z, y, core).
Axes of the slice: x: 2, y: 2, z: 4, core: 2. Of those that a mesh axis runs over, the one named last changes fastest.
Arguments:
- queries: bfloat16 [4096, 2048], P(('dp', 'ctx')), parts along dimension 0, may hold values from -6 to 6
- keys: bfloat16 [4096, 2048], P(('dp', 'ctx')), parts along dimension 0, may hold values from -6 to 6
- values: bfloat16 [4096, 2048], P(('dp', 'ctx')), parts along dimension 0, may hold values from -6 to 6
- cotangent: bfloat16 [4096, 2048], P(('dp', 'ctx')), parts along dimension 0, may hold values from -6 to 6
- partner: int32 [16], P('dp'), parts along dimension 0, may hold values from 0 to 7, each once
Outputs:
- attended: bfloat16 [4096, 2048], P(('dp', 'ctx')), parts along dimension 0
- grad_queries: bfloat16 [4096, 2048], P(('dp', 'ctx')), parts along dimension 0
- grad_keys: bfloat16 [4096, 2048], P(('dp', 'ctx')), parts along dimension 0
- grad_values: bfloat16 [4096, 2048], P(('dp', 'ctx')), parts along dimension 0
There are 2 independent parts, one for each index of `dp`. A program takes and returns all parts, laid end to end along the dimension named above; each array names one. Nothing has to cross between parts.
Inputs may be any that keep to these rules, and one draw needn't show every extreme that they name: `partner`: a permutation of the 8 block numbers.
All inputs are finite; a program needn't handle non-finite values.
Results may differ from a plain program's by a relative error of at most 0.012.
The roundings to bfloat16 on the way count: a program that leaves them out, or rounds other values in their place, can miss the bound.
Values may be sent and summed in bfloat16 or wider, within the bound.
No kernel may reach another device: no remote copies, remote signals or barrier semaphores. Data moves between devices by JAX's collectives and lax.ppermute only.
A program may use at most 128 MiB of HBM per device.

v0:
```python
import jax
import jax.numpy as jnp
from jax import lax
from jax.sharding import PartitionSpec as P

HEAD = 128


def swapped(array, axis, distance):
    return lax.ppermute(array, axis, [(i, i ^ 1 << distance) for i in range(lax.axis_size(axis))])


def attend(query_heads, key_heads, value_heads, grad_heads):
    scale_factor = HEAD ** (-0.5)
    scores = (
        jnp.einsum("qhd,khd->hqk", query_heads, key_heads, preferred_element_type=jnp.float32)
        * scale_factor
    )
    row_peak = jnp.max(scores, axis=2, keepdims=True)
    exponent = jnp.exp(scores - row_peak)
    row_total = jnp.sum(exponent, axis=2, keepdims=True)
    weights = exponent / row_total
    coarse = weights.astype(jnp.bfloat16)
    attended_part = jnp.einsum(
        "hqk,khd->qhd", coarse, value_heads, preferred_element_type=jnp.float32
    ).astype(jnp.bfloat16)
    stored = lax.optimization_barrier(attended_part)
    row_delta = jnp.sum(grad_heads.astype(jnp.float32) * stored.astype(jnp.float32), axis=2)
    grad_weights = jnp.einsum(
        "qhd,khd->hqk", grad_heads, value_heads, preferred_element_type=jnp.float32
    )
    grad_scores = (weights * (grad_weights - row_delta.T[:, :, None])).astype(jnp.bfloat16)
    grad_query_part = (
        scale_factor
        * jnp.einsum("hqk,khd->qhd", grad_scores, key_heads, preferred_element_type=jnp.float32)
    ).astype(jnp.bfloat16)
    key_terms = scale_factor * jnp.einsum(
        "hqk,qhd->khd", grad_scores, query_heads, preferred_element_type=jnp.float32
    )
    value_terms = jnp.einsum("hqk,qhd->khd", coarse, grad_heads, preferred_element_type=jnp.float32)
    statistics = jnp.stack([row_peak[:, :, 0].T, row_total[:, :, 0].T, row_delta])
    return (attended_part, grad_query_part, key_terms, value_terms, statistics)


def owner_terms(query_heads, grad_heads, key_heads, value_heads, statistics):
    scale_factor = HEAD ** (-0.5)
    row_peak = statistics[0].T[:, :, None]
    row_total = statistics[1].T[:, :, None]
    row_delta = statistics[2].T[:, :, None]
    scores = (
        jnp.einsum("qhd,khd->hqk", query_heads, key_heads, preferred_element_type=jnp.float32)
        * scale_factor
    )
    weights = jnp.exp(scores - row_peak) / row_total
    coarse = weights.astype(jnp.bfloat16)
    grad_weights = jnp.einsum(
        "qhd,khd->hqk", grad_heads, value_heads, preferred_element_type=jnp.float32
    )
    grad_scores = (weights * (grad_weights - row_delta)).astype(jnp.bfloat16)
    key_terms = scale_factor * jnp.einsum(
        "hqk,qhd->khd", grad_scores, query_heads, preferred_element_type=jnp.float32
    )
    value_terms = jnp.einsum("hqk,qhd->khd", coarse, grad_heads, preferred_element_type=jnp.float32)
    return (key_terms, value_terms)


def arrange_pair(own_piece, other_piece, half_index):
    both = jnp.stack([own_piece, other_piece])
    first = lax.dynamic_index_in_dim(both, half_index, 0, keepdims=False)
    second = lax.dynamic_index_in_dim(both, 1 - half_index, 0, keepdims=False)
    return jnp.concatenate([first, second], axis=1)


def body(queries, keys, values, cotangent, partner):
    row_count = queries.shape[0]
    feature_width = queries.shape[1]
    devices = lax.axis_size("ctx")
    slice_rows = row_count // devices
    piece_width = slice_rows * feature_width
    half_index = lax.axis_index("ctx") % 2
    block_count = partner.shape[0]
    block_ids = jnp.arange(block_count, dtype=jnp.int32)
    inverse = jnp.sum(
        jnp.where(partner[:, None] == block_ids[None, :], block_ids[:, None], 0), axis=0
    )
    partner_by_device = jnp.repeat(partner, 2)
    inverse_by_device = jnp.repeat(inverse, 2)
    stacked = jnp.stack([keys, values])
    spread_parts = lax.all_to_all(
        stacked.reshape(2, devices, piece_width), "ctx", split_axis=1, concat_axis=1, tiled=True
    )
    source = jnp.concatenate([2 * partner_by_device, 2 * partner_by_device + 1])
    outgoing = jnp.take(spread_parts, source, axis=1).reshape(2, 2, devices, piece_width)
    arrived = lax.all_to_all(outgoing, "ctx", split_axis=2, concat_axis=2, tiled=True)
    partner_rows = arrived.reshape(2, 2 * row_count, feature_width)
    other_half = swapped(stacked, "ctx", 0)
    own_rows = arrange_pair(stacked, other_half, half_index)
    context = jnp.concatenate([own_rows, partner_rows], axis=1)
    head_count = feature_width // HEAD
    group_heads = 4
    column_span = group_heads * HEAD
    group_count = head_count // group_heads
    key_count = 4 * row_count

    def one_group(group_index, buffers):
        attended_buf, grad_query_buf, grad_buf, stats_buf = buffers
        column_start = group_index * column_span

        def columns(source_array, column_axis):
            return lax.dynamic_slice_in_dim(source_array, column_start, column_span, column_axis)

        query_heads = columns(queries, 1).reshape(row_count, group_heads, HEAD)
        grad_heads = columns(cotangent, 1).reshape(row_count, group_heads, HEAD)
        key_heads = columns(context[0], 1).reshape(key_count, group_heads, HEAD)
        value_heads = columns(context[1], 1).reshape(key_count, group_heads, HEAD)
        attended_part, grad_query_part, key_terms, value_terms, statistics = attend(
            query_heads, key_heads, value_heads, grad_heads
        )
        attended_buf = lax.dynamic_update_slice_in_dim(
            attended_buf, attended_part.reshape(row_count, column_span), column_start, 1
        )
        grad_query_buf = lax.dynamic_update_slice_in_dim(
            grad_query_buf, grad_query_part.reshape(row_count, column_span), column_start, 1
        )
        term_pair = jnp.stack(
            [key_terms.reshape(key_count, column_span), value_terms.reshape(key_count, column_span)]
        )
        grad_buf = lax.dynamic_update_slice_in_dim(grad_buf, term_pair, column_start, 2)
        stats_buf = lax.dynamic_update_slice_in_dim(
            stats_buf, statistics, group_index * group_heads, 2
        )
        return (attended_buf, grad_query_buf, grad_buf, stats_buf)

    buffers = (
        jnp.zeros((row_count, feature_width), jnp.bfloat16),
        jnp.zeros((row_count, feature_width), jnp.bfloat16),
        jnp.zeros((2, key_count, feature_width), jnp.float32),
        jnp.zeros((3, row_count, head_count), jnp.float32),
    )
    attended, grad_queries, grad_buf, stats_buf = lax.fori_loop(0, group_count, one_group, buffers)
    own_terms = lax.dynamic_slice_in_dim(grad_buf, half_index * row_count, row_count, 1)
    their_terms = lax.dynamic_slice_in_dim(grad_buf, (1 - half_index) * row_count, row_count, 1)
    returned = swapped(their_terms.astype(jnp.bfloat16), "ctx", 0).astype(their_terms.dtype)
    stats_width = slice_rows * head_count
    query_stack = jnp.stack([queries, cotangent]).reshape(2, devices, piece_width)
    query_parts = lax.all_to_all(query_stack, "ctx", split_axis=1, concat_axis=1, tiled=True)
    stats_parts = lax.all_to_all(
        stats_buf.reshape(3, devices, stats_width), "ctx", split_axis=1, concat_axis=1, tiled=True
    )
    anchor = jnp.concatenate([2 * inverse_by_device, 2 * inverse_by_device + 1])
    query_out = jnp.take(query_parts, anchor, axis=1).reshape(2, 2, devices, piece_width)
    stats_out = jnp.take(stats_parts, anchor, axis=1).reshape(3, 2, devices, stats_width)
    query_block = lax.all_to_all(query_out, "ctx", split_axis=2, concat_axis=2, tiled=True).reshape(
        2, 2 * row_count, feature_width
    )
    stats_block = lax.all_to_all(stats_out, "ctx", split_axis=2, concat_axis=2, tiled=True).reshape(
        3, 2 * row_count, head_count
    )

    def owner_group(group_index, moved_buf):
        column_start = group_index * column_span
        query_heads = lax.dynamic_slice_in_dim(
            query_block[0], column_start, column_span, 1
        ).reshape(2 * row_count, group_heads, HEAD)
        grad_heads = lax.dynamic_slice_in_dim(query_block[1], column_start, column_span, 1).reshape(
            2 * row_count, group_heads, HEAD
        )
        key_heads = lax.dynamic_slice_in_dim(keys, column_start, column_span, 1).reshape(
            row_count, group_heads, HEAD
        )
        value_heads = lax.dynamic_slice_in_dim(values, column_start, column_span, 1).reshape(
            row_count, group_heads, HEAD
        )
        statistics = lax.dynamic_slice_in_dim(
            stats_block, group_index * group_heads, group_heads, 2
        )
        key_terms, value_terms = owner_terms(
            query_heads, grad_heads, key_heads, value_heads, statistics
        )
        term_pair = jnp.stack(
            [key_terms.reshape(row_count, column_span), value_terms.reshape(row_count, column_span)]
        )
        return lax.dynamic_update_slice_in_dim(moved_buf, term_pair, column_start, 2)

    partner_sum = lax.fori_loop(
        0, group_count, owner_group, jnp.zeros((2, row_count, feature_width), jnp.float32)
    )
    gradients = (own_terms + returned + partner_sum).astype(jnp.bfloat16)
    return (attended, grad_queries, gradients[0], gradients[1])


def solution(mesh):
    return jax.shard_map(
        body,
        mesh=mesh,
        in_specs=(
            P(("dp", "ctx"), None),
            P(("dp", "ctx"), None),
            P(("dp", "ctx"), None),
            P(("dp", "ctx"), None),
            P("dp"),
        ),
        out_specs=(
            P(("dp", "ctx"), None),
            P(("dp", "ctx"), None),
            P(("dp", "ctx"), None),
            P(("dp", "ctx"), None),
        ),
        check_vma=False,
    )
```

profile of v0, /device:TPU:9, one launch (start us, length us, event | category | flops | bytes accessed | tf_op | source)
XLA Modules:
  0.0 342.1 jit_solution(14928584802931060726)
XLA Ops:
  0.6 2.5 stack.88
  3.1 2.5 stack.87
  5.6 3.2 pad_maximum_fusion.4
  8.8 6.6 %all-to-all-start = ((bf16[2,16,16384]{2,0,1:T(2,128)(2,1)}), bf16[2,16,16384]{2,0,1:T(2,128)(2,1)S(1)}, u32[]{:S(2)}, u32[]{:S(2)}) async-start(bf16[2,16,16384]{2,0,1:T(2,128)(2,1)} %pad_maximum_fusion.4), calls=%async_computation | async-start | bytes 2097152 | tf_op jit(solution)/shard_map/all_to_all | solution.py:89
  16.6 2.5 stack.89
  19.1 3.2 pad_maximum_fusion.5
  22.3 18.0 %all-to-all-done = bf16[2,16,16384]{2,0,1:T(2,128)(2,1)S(1)} async-done(((bf16[2,16,16384]{2,0,1:T(2,128)(2,1)}), bf16[2,16,16384]{2,0,1:T(2,128)(2,1)S(1)}, u32[]{:S(2)}, u32[]{:S(2)}) %all-to-all-start) | async-done | bytes 1048608 | tf_op jit(solution)/shard_map/all_to_all | solution.py:89
  40.3 5.0 %all-to-all-start.2 = ((bf16[2,16,16384]{2,0,1:T(2,128)(2,1)}), bf16[2,16,16384]{2,0,1:T(2,128)(2,1)S(1)}, u32[]{:S(2)}, u32[]{:S(2)}) async-start(bf16[2,16,16384]{2,0,1:T(2,128)(2,1)} %pad_maximum_fusion.5), calls=%async_computation.2 | async-start | bytes 2097152 | tf_op jit(solution)/shard_map/all_to_all | solution.py:146
  45.3 6.2 %gather_fusion.1 = bf16[32,2,16384]{2,1,0:T(2,128)(2,1)} fusion(bf16[2,16,16384]{2,0,1:T(2,128)(2,1)S(1)} %all-to-all-done, s32[1024]{0:T(1024)S(1)} %pad_clamp_fusion.2), kind=kCustom, calls=%fused_computation.clone | custom fusion | bytes 4194432 | tf_op jit(solution)/shard_map/jit(_take)/gather | solution.py:93
  51.4 3.5 %broadcast_select_fusion.1 = bf16[32,2,16384]{2,1,0:T(2,128)(2,1)S(1)} fusion(bf16[32,2,16384]{2,1,0:T(2,128)(2,1)} %gather_fusion.1, pred[32]{0:T(512)(128)(4,1)S(1)} %get-tuple-element.393), kind=kLoop, calls=%fused_computation.48 | loop fusion | flops 1048576 | bytes 4194336 | tf_op jit(solution)/shard_map/jit(_take)/select_n | solution.py:93
  54.9 3.6 %copy.143 = bf16[2,2,16,16384]{3,1,0,2:T(2,128)(2,1)} copy(bf16[2,2,16,16384]{3,0,2,1:T(2,128)(2,1)S(1)} %bitcast.195) | data formatting | bytes 4194304 | tf_op jit(solution)/shard_map/reshape | solution.py:93
  58.5 11.6 %all-to-all-done.2 = bf16[2,16,16384]{2,0,1:T(2,128)(2,1)S(1)} async-done(((bf16[2,16,16384]{2,0,1:T(2,128)(2,1)}), bf16[2,16,16384]{2,0,1:T(2,128)(2,1)S(1)}, u32[]{:S(2)}, u32[]{:S(2)}) %all-to-all-start.2) | async-done | bytes 1048608 | tf_op jit(solution)/shard_map/all_to_all | solution.py:146
  70.1 5.0 %all-to-all-start.1 = ((bf16[2,2,16,16384]{3,1,0,2:T(2,128)(2,1)}), bf16[2,2,16,16384]{3,1,0,2:T(2,128)(2,1)S(1)}, u32[]{:S(2)}, u32[]{:S(2)}) async-start(bf16[2,2,16,16384]{3,1,0,2:T(2,128)(2,1)} %copy.143), calls=%async_computation.1 | async-start | bytes 4194304 | tf_op jit(solution)/shard_map/all_to_all | solution.py:94
  75.1 2.6 pad_maximum_fusion.3
  78.4 2.3 collective-permute-done
  80.7 3.6 %fusion.19 = (bf16[2,128,2048]{2,1,0:T(8,128)(2,1)}, bf16[2,128,2048]{2,1,0:T(8,128)(2,1)}) fusion(s32[]{:T(128)S(6)} %select_n.91, bf16[1,2,128,2048]{3,2,1,0:T(8,128)(2,1)} %get-tuple-element.415, bf16[1,2,128,2048]{3,2,1,0:T(8,128)(2,1)} %bitcast.35, s32[]{:T(128)S(6)} %select_n.92), kind=kLoop, calls=%fused_computation.58 | loop fusion | flops 1048576 | bytes 4194312 | tf_op jit(solution)/shard_map/jit(dynamic_index_in_dim)/squeeze | solution.py:69
  84.3 6.2 %gather_fusion.2 = bf16[32,2,16384]{2,1,0:T(2,128)(2,1)} fusion(bf16[2,16,16384]{2,0,1:T(2,128)(2,1)S(1)} %all-to-all-done.2, s32[1024]{0:T(1024)S(1)} %pad_clamp_fusion.1), kind=kCustom, calls=%fused_computation.1.clone | custom fusion | bytes 4194432 | tf_op jit(solution)/shard_map/jit(_take)/gather | solution.py:151
  90.5 30.5 %all-to-all-done.1 = bf16[2,2,16,16384]{3,1,0,2:T(2,128)(2,1)S(1)} async-done(((bf16[2,2,16,16384]{3,1,0,2:T(2,128)(2,1)}), bf16[2,2,16,16384]{3,1,0,2:T(2,128)(2,1)S(1)}, u32[]{:S(2)}, u32[]{:S(2)}) %all-to-all-start.1) | async-done | bytes 2097184 | tf_op jit(solution)/shard_map/all_to_all | solution.py:94
  121.0 2.5 copy.144
  123.5 3.0 reshape.247
  126.5 3.2 pad_maximum_fusion.2
  129.7 6.3 %copy.145 = bf16[2,512,2048]{1,2,0:T(8,128)(2,1)} copy(bf16[2,512,2048]{2,1,0:T(8,128)(2,1)} %pad_maximum_fusion.2) | data formatting | bytes 8388608 | tf_op jit(solution)/shard_map/while | solution.py:140
  137.7 4.3 %broadcast_in_dim.67.clone = f32[2,512,2048]{2,1,0:T(8,128)} broadcast(f32[]{:T(128)} %constant.173.clone.1), dimensions={} | broadcast | bytes 8388612 | tf_op jit(solution)/shard_map/broadcast_in_dim | solution.py:137
  142.0 62.9 %while.32 = (s32[]{:T(128)}, bf16[128,2048]{1,0:T(8,128)(2,1)}, bf16[128,2048]{1,0:T(8,128)(2,1)}, f32[2,512,2048]{2,1,0:T(8,128)}, f32[3,128,16]{1,2,0:T(8,128)...) while((s32[]{:T(128)}, bf16[128,2048]{1,0:T(8,128)(2,1)}, ...), condition=%wide.region_4.6_spmd, body=%wide.region_0.5_spmd.sunk | while | flops 407045632 | bytes 37779716 | solution.py:140
  142.0 3.8 %fusion.87 = (bf16[1,512,2048]{1,2,0:T(8,128)(2,1)}, bf16[1,512,2048]{1,2,0:T(8,128)(2,1)S(1)}) fusion(bf16[2,512,2048]{1,2,0:T(8,128)(2,1)} %get-tuple-element.567), kind=kLoop, calls=%fused_computation.85.clone.1 | loop fusion | bytes 8388608 | tf_op jit(solution)/shard_map/while/body/eval_jaxpr/slice | solution.py:114
  152.7 1.5 pad_maximum_fusion.8
  154.2 1.9 copy.199
  156.1 1.5 constant_dynamic-update-slice_fusion.8
  157.7 3.8 %fusion.87 = (bf16[1,512,2048]{1,2,0:T(8,128)(2,1)}, bf16[1,512,2048]{1,2,0:T(8,128)(2,1)S(1)}) fusion(bf16[2,512,2048]{1,2,0:T(8,128)(2,1)} %get-tuple-element.567), kind=kLoop, calls=%fused_computation.85.clone.1 | loop fusion | bytes 8388608 | tf_op jit(solution)/shard_map/while/body/eval_jaxpr/slice | solution.py:114
  168.4 1.5 pad_maximum_fusion.8
  169.9 1.9 copy.199
  171.8 1.6 constant_dynamic-update-slice_fusion.8
  173.4 3.8 %fusion.87 = (bf16[1,512,2048]{1,2,0:T(8,128)(2,1)}, bf16[1,512,2048]{1,2,0:T(8,128)(2,1)S(1)}) fusion(bf16[2,512,2048]{1,2,0:T(8,128)(2,1)} %get-tuple-element.567), kind=kLoop, calls=%fused_computation.85.clone.1 | loop fusion | bytes 8388608 | tf_op jit(solution)/shard_map/while/body/eval_jaxpr/slice | solution.py:114
  184.1 1.5 pad_maximum_fusion.8
  185.6 1.9 copy.199
  187.5 1.6 constant_dynamic-update-slice_fusion.8
  189.1 3.8 %fusion.87 = (bf16[1,512,2048]{1,2,0:T(8,128)(2,1)}, bf16[1,512,2048]{1,2,0:T(8,128)(2,1)S(1)}) fusion(bf16[2,512,2048]{1,2,0:T(8,128)(2,1)} %get-tuple-element.567), kind=kLoop, calls=%fused_computation.85.clone.1 | loop fusion | bytes 8388608 | tf_op jit(solution)/shard_map/while/body/eval_jaxpr/slice | solution.py:114
  199.8 1.5 pad_maximum_fusion.8
  201.3 1.9 copy.199
  203.3 1.6 constant_dynamic-update-slice_fusion.8
  205.7 6.3 %all-to-all-start.4 = ((f32[3,16,128]{2,0,1:T(4,128)}), f32[3,16,128]{2,0,1:T(4,128)S(1)}, u32[]{:S(2)}, u32[]{:S(2)}) async-start(f32[3,16,128]{2,0,1:T(4,128)} %copy.156), calls=%async_computation.4 | async-start | bytes 65536 | tf_op jit(solution)/shard_map/all_to_all | solution.py:147
  212.1 3.5 %broadcast_select_fusion = bf16[32,2,16384]{2,1,0:T(2,128)(2,1)S(1)} fusion(bf16[32,2,16384]{2,1,0:T(2,128)(2,1)} %gather_fusion.2, pred[32]{0:T(512)(128)(4,1)S(1)} %get-tuple-element.391), kind=kLoop, calls=%fused_computation.47 | loop fusion | flops 1048576 | bytes 4194336 | tf_op jit(solution)/shard_map/jit(_take)/select_n | solution.py:151
  215.6 3.6 %copy.152 = bf16[2,2,16,16384]{3,1,0,2:T(2,128)(2,1)} copy(bf16[2,2,16,16384]{3,0,2,1:T(2,128)(2,1)S(1)} %bitcast.196) | data formatting | bytes 4194304 | tf_op jit(solution)/shard_map/reshape | solution.py:151
  219.2 6.0 %all-to-all-start.3 = ((bf16[2,2,16,16384]{3,1,0,2:T(2,128)(2,1)}), bf16[2,2,16,16384]{3,1,0,2:T(2,128)(2,1)S(1)}, u32[]{:S(2)}, u32[]{:S(2)}) async-start(bf16[2,2,16,16384]{3,1,0,2:T(2,128)(2,1)} %copy.152), calls=%async_computation.3 | async-start | bytes 4194304 | tf_op jit(solution)/shard_map/all_to_all | solution.py:153
  226.9 44.3 %all-to-all-done.3 = bf16[2,2,16,16384]{3,1,0,2:T(2,128)(2,1)S(1)} async-done(((bf16[2,2,16,16384]{3,1,0,2:T(2,128)(2,1)}), bf16[2,2,16,16384]{3,1,0,2:T(2,128)(2,1)S(1)}, u32[]{:S(2)}, u32[]{:S(2)}) %all-to-all-start.3) | async-done | bytes 2097184 | tf_op jit(solution)/shard_map/all_to_all | solution.py:153
  271.2 6.3 %all-to-all-start.5 = ((f32[3,2,16,128]{3,1,0,2:T(2,128)}), f32[3,2,16,128]{3,1,0,2:T(2,128)S(1)}, u32[]{:S(2)}, u32[]{:S(2)}) async-start(f32[3,2,16,128]{3,1,0,2:T(2,128)} %copy_select_fusion), calls=%async_computation.5 | async-start | bytes 98304 | tf_op jit(solution)/shard_map/all_to_all | solution.py:156
  277.6 2.8 dynamic-slice_convert_fusion
  280.3 2.5 copy.153
  282.9 4.2 %reshape.249 = bf16[2,256,2048]{2,1,0:T(8,128)(2,1)} reshape(bf16[2,2,16,16384]{3,2,1,0:T(8,128)(2,1)} %copy.153) | data formatting | bytes 4194304 | tf_op jit(solution)/shard_map/reshape | solution.py:153
  287.1 2.8 copy.159
  291.3 1.6 broadcast_in_dim.70.clone
  293.0 45.0 %while.33 = (s32[]{:T(128)}, f32[2,128,2048]{2,1,0:T(8,128)}, bf16[2,256,2048]{1,2,0:T(8,128)(2,1)S(1)}, bf16[128,2048]{1,0:T(8,128)(2,1)}, f32[3,256,16]{1,2,0:...) while((s32[]{:T(128)}, f32[2,128,2048]{2,1,0:T(8,128)}, ...), condition=%wide.region_7.9_spmd, body=%wide.region_6.8_spmd.sunk | while | flops 135331856 | bytes 13930805 | solution.py:185
  294.1 1.7 constant_dynamic-slice_fusion.18
  297.7 1.4 fusion.102
  300.1 2.1 fusion.104
  305.3 1.7 constant_dynamic-slice_fusion.18
  308.9 1.4 fusion.102
  311.3 2.1 fusion.104
  316.6 1.7 constant_dynamic-slice_fusion.18
  322.5 2.1 fusion.104
  327.8 1.7 constant_dynamic-slice_fusion.18
  331.4 1.4 fusion.102
  333.8 2.1 fusion.104
  337.9 3.0 add_convert_fusion
  (165 shorter events, 61.3 us)
Async XLA Ops:
  5.6 9.8 %copy-start.3 = (s32[8]{0:T(128)S(1)}, s32[8]{0:T(128)}, u32[]{:S(2)}) copy-start(s32[8]{0:T(128)} %param.15) | copy-start | bytes 100
  5.6 10.1 %copy-start.2 = (bf16[128,2048]{1,0:T(8,128)(2,1)S(1)}, bf16[128,2048]{1,0:T(8,128)(2,1)}, u32[]{:S(2)}) copy-start(bf16[128,2048]{1,0:T(8,128)(2,1)} %param.14) | copy-start | bytes 1572868
  8.8 31.5 %all-to-all-start = ((bf16[2,16,16384]{2,0,1:T(2,128)(2,1)}), bf16[2,16,16384]{2,0,1:T(2,128)(2,1)S(1)}, u32[]{:S(2)}, u32[]{:S(2)}) async-start(bf16[2,16,16384]{2,0,1:T(2,128)(2,1)} %pad_maximum_fusion.4), calls=%async_computation | async-start | bytes 2097152 | tf_op jit(solution)/shard_map/all_to_all | solution.py:89
  40.3 29.8 %all-to-all-start.2 = ((bf16[2,16,16384]{2,0,1:T(2,128)(2,1)}), bf16[2,16,16384]{2,0,1:T(2,128)(2,1)S(1)}, u32[]{:S(2)}, u32[]{:S(2)}) async-start(bf16[2,16,16384]{2,0,1:T(2,128)(2,1)} %pad_maximum_fusion.5), calls=%async_computation.2 | async-start | bytes 2097152 | tf_op jit(solution)/shard_map/all_to_all | solution.py:146
  70.1 51.0 %all-to-all-start.1 = ((bf16[2,2,16,16384]{3,1,0,2:T(2,128)(2,1)}), bf16[2,2,16,16384]{3,1,0,2:T(2,128)(2,1)S(1)}, u32[]{:S(2)}, u32[]{:S(2)}) async-start(bf16[2,2,16,16384]{3,1,0,2:T(2,128)(2,1)} %copy.143), calls=%async_computation.1 | async-start | bytes 4194304 | tf_op jit(solution)/shard_map/all_to_all | solution.py:94
  77.7 3.0 collective-permute-start
  123.5 3.0 copy-start.1
  205.7 13.5 %all-to-all-start.4 = ((f32[3,16,128]{2,0,1:T(4,128)}), f32[3,16,128]{2,0,1:T(4,128)S(1)}, u32[]{:S(2)}, u32[]{:S(2)}) async-start(f32[3,16,128]{2,0,1:T(4,128)} %copy.156), calls=%async_computation.4 | async-start | bytes 65536 | tf_op jit(solution)/shard_map/all_to_all | solution.py:147
  219.2 52.0 %all-to-all-start.3 = ((bf16[2,2,16,16384]{3,1,0,2:T(2,128)(2,1)}), bf16[2,2,16,16384]{3,1,0,2:T(2,128)(2,1)S(1)}, u32[]{:S(2)}, u32[]{:S(2)}) async-start(bf16[2,2,16,16384]{3,1,0,2:T(2,128)(2,1)} %copy.152), calls=%async_computation.3 | async-start | bytes 4194304 | tf_op jit(solution)/shard_map/all_to_all | solution.py:153
  271.2 19.2 %all-to-all-start.5 = ((f32[3,2,16,128]{3,1,0,2:T(2,128)}), f32[3,2,16,128]{3,1,0,2:T(2,128)S(1)}, u32[]{:S(2)}, u32[]{:S(2)}) async-start(f32[3,2,16,128]{3,1,0,2:T(2,128)} %copy_select_fusion), calls=%async_computation.5 | async-start | bytes 98304 | tf_op jit(solution)/shard_map/all_to_all | solution.py:156
  290.0 48.0 %collective-permute-start.1 = (bf16[2,128,2048]{2,1,0:T(8,128)(2,1)}, bf16[2,128,2048]{2,1,0:T(8,128)(2,1)}, u32[]{:S(2)}, u32[]{:S(2)}) collective-permute-start(bf16[2,128,2048]{2,1,0:T(8,128)(2,1)} %dynamic-slice_convert_fusion), channel_id=1, source_target_pairs={{0,1},{1,0},{2,3},{3,2},{4,5},{5,4},{6,7},{7,6},{8,9},{9,8},{10,11... | collective-permute-start | bytes 3145736 | tf_op jit(solution)/shard_map/ppermute | solution.py:10
  296.8 3.3 copy-start
  308.0 3.3 copy-start
  319.2 3.3 copy-start
  330.5 3.3 copy-start
where the time goes:
time: 345 us; the launch traced here: 342 us
  local copies, waits for them, and re-layouts  135 us (39%)
  waiting for transfers between devices  107 us (31%)
  other arithmetic  39.5 us (11%)
  starting transfers between devices  36 us (10%)
  matrix products  22.9 us (7%)
    all_to_all x1, waiting for transfers between devices, body(): lax.all_to_all(query_out, 'ctx', split_axis=2, concat_axis=2, tiled=True)  44.3 us
    all_to_all x1, waiting for transfers between devices, body(): lax.all_to_all(outgoing, 'ctx', split_axis=2, concat_axis=2, tiled=True)  30.5 us
    all_to_all x1, waiting for transfers between devices, body(): lax.all_to_all(stacked.reshape(2, devices, piece_width), 'ctx', split_axi...  18 us
    slice x4, local copies, waits for them, and re-layouts, one_group(): key_heads = columns(context[0], 1).reshape(key_count, group_heads, HEAD)  15.2 us
    dynamic_update_slice x8, local copies, waits for them, and re-layouts, one_group(): lax.dynamic_update_slice_in_dim(grad_buf, term_pair, column_start, 2)  14 us
    dynamic_slice x24, local copies, waits for them, and re-layouts, columns(): lax.dynamic_slice_in_dim(source_array, column_start, column_span, column_...  12.8 us
    all_to_all x1, waiting for transfers between devices, body(): lax.all_to_all(query_stack, 'ctx', split_axis=1, concat_axis=1, tiled=True)  11.6 us
    dot_general x4, matrix products, owner_terms(): jnp.einsum('hqk,qhd->khd', grad_scores, query_heads, preferred_element_ty...  8.37 us
  transfers between devices with their start and end apart: 8, of which 5 were waited for; matrix products, arithmetic and copies ran while one was open for 30% of the time, Pallas kernels for 0%

commit v1 on v0

v1 whole, which is shorter than its diff:
```python
import functools

import jax
import jax.numpy as jnp
from jax import lax
from jax.experimental import pallas as pl
from jax.experimental.pallas import tpu as pltpu
from jax.sharding import PartitionSpec as P

HEAD = 128
SCALE = HEAD ** (-0.5)

NN = (((1,), (0,)), ((), ()))
NT = (((1,), (1,)), ((), ()))
TN = (((0,), (0,)), ((), ()))


def mm(a, b, dims):
    return lax.dot_general(a, b, dims, preferred_element_type=jnp.float32)


def attention_kernel(pieces, blocks, first, partner, local, far, out, grad_k, grad_v, acc_k, acc_v):
    per_block = pieces // blocks
    block_rows = per_block * local.shape[2]
    total_blocks = acc_k.shape[0]

    def rows(ref, piece, which):
        return ref[pl.ds(piece * per_block, per_block), which].reshape(block_rows, HEAD)

    acc_k[...] = jnp.zeros_like(acc_k)
    acc_v[...] = jnp.zeros_like(acc_v)

    def one(b, carry):
        own = first[0] + b
        p = partner[own]
        q = rows(local, b, 0)
        do = rows(local, b, 3)
        ks, vs = [rows(local, b, 1)], [rows(local, b, 2)]
        if far is None:
            ks.append(rows(local, p, 1))
            vs.append(rows(local, p, 2))
        else:
            ks.append(rows(far, p, 0))
            vs.append(rows(far, p, 1))
        scores = [mm(q, k, NT) * SCALE for k in ks]
        peak = jnp.max(jnp.maximum(scores[0], scores[1]), axis=1, keepdims=True)
        exps = [jnp.exp(s - peak) for s in scores]
        total = jnp.sum(exps[0] + exps[1], axis=1, keepdims=True)
        inverse = 1.0 / total
        weights = [e * inverse for e in exps]
        coarse = [w.astype(jnp.bfloat16) for w in weights]
        attended = (mm(coarse[0], vs[0], NN) + mm(coarse[1], vs[1], NN)).astype(jnp.bfloat16)
        delta = jnp.sum(
            do.astype(jnp.float32) * attended.astype(jnp.float32), axis=1, keepdims=True
        )
        gs = [
            (w * (mm(do, v, NT) - delta)).astype(jnp.bfloat16) for w, v in zip(weights, vs)
        ]
        grad_q = (SCALE * (mm(gs[0], ks[0], NN) + mm(gs[1], ks[1], NN))).astype(jnp.bfloat16)
        here = pl.ds(b * per_block, per_block)
        out[here, 0] = attended.reshape(per_block, -1, HEAD)
        out[here, 1] = grad_q.reshape(per_block, -1, HEAD)
        for target, g, c in zip((own, p), gs, coarse):
            acc_k[target] += SCALE * mm(g, q, TN)
            acc_v[target] += mm(c, do, TN)
        return carry

    lax.fori_loop(0, blocks, one, 0)
    if grad_k is None:
        for which, acc in ((2, acc_k), (3, acc_v)):
            out[:, which] = acc[...].reshape(pieces, -1, HEAD).astype(jnp.bfloat16)
    else:
        grad_k[...] = acc_k[...]
        grad_v[...] = acc_v[...]


def attention(partner, first, local, far, blocks):
    pieces, _, rows, _ = local.shape
    total_blocks = partner.shape[0]
    block_rows = pieces // blocks * rows
    whole = far is None
    smem = pl.BlockSpec(memory_space=pltpu.SMEM)
    vmem = pl.BlockSpec(memory_space=pltpu.VMEM)
    grads = jax.ShapeDtypeStruct((total_blocks, block_rows, HEAD), jnp.float32)
    out_shape = [jax.ShapeDtypeStruct((pieces, 4 if whole else 2, rows, HEAD), jnp.bfloat16)]
    operands = [first, partner, local]
    if not whole:
        out_shape += [grads, grads]
        operands.append(far)

    def kernel(*refs):
        n = len(operands)
        m = n + len(out_shape)
        ins, outs, scratch = refs[:n], refs[n:m], refs[m:]
        attention_kernel(
            pieces,
            blocks,
            ins[0],
            ins[1],
            ins[2],
            None if whole else ins[3],
            outs[0],
            None if whole else outs[1],
            None if whole else outs[2],
            *scratch,
        )

    flops = 12 * blocks * block_rows * 2 * block_rows * HEAD
    return pl.pallas_call(
        kernel,
        out_shape=out_shape,
        in_specs=[smem, smem] + [vmem] * (len(operands) - 2),
        out_specs=[vmem] * len(out_shape),
        scratch_shapes=[pltpu.VMEM((total_blocks, block_rows, HEAD), jnp.float32)] * 2,
        compiler_params=pltpu.CompilerParams(vmem_limit_bytes=48 * 1024 * 1024),
        cost_estimate=pl.CostEstimate(
            flops=flops,
            bytes_accessed=2 * local.size * 2,
            transcendentals=blocks * block_rows * 2 * block_rows,
        ),
    )(*operands)


def body(queries, keys, values, cotangent, partner):
    rows, width = queries.shape
    devices = lax.axis_size("ctx")
    heads = width // HEAD
    blocks = partner.shape[0]
    spread = min(heads, devices)
    groups = devices // spread
    heads_here = heads // spread
    near = [[g * spread + i for i in range(spread)] for g in range(groups)]
    across = [[g * spread + i for g in range(groups)] for i in range(spread)]
    group = lax.axis_index("ctx") // spread
    exchange = functools.partial(
        lax.all_to_all,
        axis_name="ctx",
        split_axis=0,
        concat_axis=0,
        tiled=True,
        axis_index_groups=near if groups > 1 else None,
    )

    def pack(arrays):
        stacked = jnp.stack(arrays).reshape(len(arrays), rows, spread, heads_here, HEAD)
        return stacked.transpose(2, 3, 0, 1, 4)

    def unpack(packed):
        kinds = packed.shape[2]
        full = packed.transpose(2, 3, 0, 1, 4).reshape(kinds, rows, width)
        return [full[i] for i in range(kinds)]

    local_blocks = blocks // groups
    first = (group * local_blocks).astype(jnp.int32).reshape(1)
    local = exchange(pack([queries, keys, values, cotangent]))
    outs = []
    for h in range(heads_here):
        mine = local[:, h]
        if groups == 1:
            outs.append(attention(partner, first, mine, None, local_blocks)[0])
        else:
            far = lax.all_gather(
                mine[:, 1:3], "ctx", axis=0, tiled=True, axis_index_groups=across
            )
            out, grad_k, grad_v = attention(partner, first, mine, far, local_blocks)
            grads = lax.psum_scatter(
                jnp.stack([grad_k, grad_v], axis=1),
                "ctx",
                scatter_dimension=0,
                tiled=True,
                axis_index_groups=across,
            ).astype(jnp.bfloat16)
            grads = grads.transpose(0, 2, 1, 3).reshape(spread, rows, 2, HEAD).transpose(0, 2, 1, 3)
            outs.append(jnp.concatenate([out, grads], axis=1))
    return tuple(unpack(exchange(jnp.stack(outs, axis=1))))


def solution(mesh):
    split = P(("dp", "ctx"), None)
    return jax.shard_map(
        body,
        mesh=mesh,
        in_specs=(split, split, split, split, P("dp")),
        out_specs=(split, split, split, split),
        check_vma=False,
    )
```

time: 345 us -> 137 us (0.40)
  local copies, waits for them, and re-layouts: 135 us -> 17.6 us
  waiting for transfers between devices: 107 us -> 46 us
  blocking collectives: 0 us -> 54.1 us
  other arithmetic: 39.5 us -> 1.46 us
  starting transfers between devices: 36 us -> 6.74 us
  matrix products: 22.9 us -> 0 us
  Pallas kernels: 0 us -> 9.02 us
    all_to_all x6 -> x1, waiting for transfers between devices: 104 us -> 46 us  [body(): local = exchange(pack([queries, keys, values, cotangent]))]
    all_to_all x0 -> x1, blocking collectives: none -> 54.1 us  [body(): return tuple(unpack(exchange(jnp.stack(outs, axis=1))))]
    all_to_all x6 -> x1, starting transfers between devices: 35.3 us -> 6.74 us  [body(): local = exchange(pack([queries, keys, values, cotangent]))]
    dynamic_slice x40 -> x0, local copies, waits for them, and re-layouts: 27 us -> none  [the longest x24 12.8 us: columns(): lax.dynamic_slice_in_dim(source_array, column_start, column_span, column_...]
    dot_general x36 -> x0, matrix products: 22.9 us -> none  [the longest x4 8.37 us: owner_terms(): jnp.einsum('hqk,qhd->khd', grad_scores, query_heads, preferred_element_ty...]
    dynamic_update_slice x28 -> x0, local copies, waits for them, and re-layouts: 22 us -> none  [the longest x8 14 us: one_group(): lax.dynamic_update_slice_in_dim(grad_buf, term_pair, column_start, 2)]
    another operation x11 -> x0, other arithmetic: 19 us -> none  [the longest x4 5.95 us: one_group(): jnp.stack([key_terms.reshape(key_count, column_span), value_terms.reshape...]
    slice x8 -> x1, local copies, waits for them, and re-layouts: 19.8 us -> 1.16 us  [unpack(): return [full[i] for i in range(kinds)]]
  transfers between devices with their start and end apart: 8 -> 1, of which waited for: 5 -> 1; matrix products, arithmetic and copies ran while one was open for 30% -> 0% of each run, Pallas kernels for 0% -> 0%
where the time goes in v1:
time: 137 us; the launch traced here: 136 us
  blocking collectives  54.1 us (39%)
  waiting for transfers between devices  46 us (34%)
  local copies, waits for them, and re-layouts  17.6 us (13%)
  Pallas kernels  9.02 us (7%)
  starting transfers between devices  6.74 us (5%)
  other arithmetic  1.46 us (1%)
    all_to_all x1, blocking collectives, body(): return tuple(unpack(exchange(jnp.stack(outs, axis=1))))  54.1 us
    all_to_all x1, waiting for transfers between devices, body(): local = exchange(pack([queries, keys, values, cotangent]))  46 us
    unnamed x14, local copies, waits for them, and re-layouts  10.8 us
    pallas_call x1, Pallas kernels, attention(): pl.pallas_call(kernel, out_shape=out_shape, in_specs=[smem, smem] + [vmem...  9.02 us
    all_to_all x1, starting transfers between devices, body(): local = exchange(pack([queries, keys, values, cotangent]))  6.74 us
    all_to_all x1, local copies, waits for them, and re-layouts, body(): return tuple(unpack(exchange(jnp.stack(outs, axis=1))))  3.04 us
  transfers between devices with their start and end apart: 1, of which 1 were waited for; matrix products, arithmetic and copies ran while one was open for 0% of the time, Pallas kernels for 0%

profile of v1, /device:TPU:9, one launch (start us, length us, event | category | flops | bytes accessed | tf_op | source)
XLA Modules:
  0.0 135.6 jit_solution(6638245300330791220)
XLA Ops:
  0.6 0.0 copy-start.1
  0.6 0.0 copy-start.2
  0.7 1.4 %copy.25 = bf16[128,2048]{0,1:T(8,128)(2,1)S(1)} copy(bf16[128,2048]{1,0:T(8,128)(2,1)} %param.5) | data formatting | bytes 1048576 | tf_op args[0]
  2.1 1.3 copy.26
  3.4 0.0 copy-done.1
  3.4 1.0 copy.27
  4.4 0.0 copy-done.2
  4.4 1.0 copy.28
  5.4 1.5 %maximum_bitcast_fusion = bf16[16,1,4,128,128]{3,4,0,1,2:T(8,128)(2,1)S(1)} fusion(bf16[1,128,16,1,128]{1,4,2,3,0:T(8,128)(2,1)} %bitcast.26, bf16[1,128,16,1,128]{1,4,2,3,0:T(8,128)(2,1)} %bitcast.25, bf16[1,128,16,1,128]{1,4,2,3,0:T(8,128)(2,1)S(1)} %bitcast.24, bf16[1,128,16,1,128]{1,4,2,3,0:T(8,128)(2,1)S(1)} %bitcast.23), kind=kLoop, calls=%fused_computation | loop fusion | flops 3145728 | bytes 4194304 | tf_op jit(solution)/shard_map/transpose | solution.py:146
  6.8 2.6 %copy.29 = bf16[16,1,4,128,128]{4,3,2,1,0:T(8,128)(2,1)} copy(bf16[16,1,4,128,128]{3,4,0,1,2:T(8,128)(2,1)S(1)} %maximum_bitcast_fusion) | data formatting | bytes 4194304 | tf_op jit(solution)/shard_map/transpose | solution.py:146
  9.5 0.0 copy-start
  9.5 6.7 %all-to-all-start = ((bf16[16,1,4,128,128]{4,3,2,1,0:T(8,128)(2,1)}), bf16[16,1,4,128,128]{4,3,2,1,0:T(8,128)(2,1)S(1)}, u32[]{:S(2)}, u32[]{:S(2)}) async-start(bf16[16,1,4,128,128]{4,3,2,1,0:T(8,128)(2,1)} %copy.29), calls=%async_computation | async-start | bytes 4194304 | tf_op jit(solution)/shard_map/all_to_all | solution.py:155
  16.2 46.0 %all-to-all-done = bf16[16,1,4,128,128]{4,3,2,1,0:T(8,128)(2,1)S(1)} async-done(((bf16[16,1,4,128,128]{4,3,2,1,0:T(8,128)(2,1)}), bf16[16,1,4,128,128]{4,3,2,1,0:T(8,128)(2,1)S(1)}, u32[]{:S(2)}, u32[]{:S(2)}) %all-to-all-start) | async-done | bytes 2097184 | tf_op jit(solution)/shard_map/all_to_all | solution.py:155
  62.2 0.0 copy-done
  62.2 9.0 %shard_map.84 = bf16[16,4,128,128]{3,2,1,0:T(8,128)(2,1)S(1)} custom-call(s32[1]{0:T(128)} %bitcast.refs_0_, s32[8]{0:T(128)S(1)} %copy-done, bf16[16,4,128,128]{3,2,1,0:T(8,128)(2,1)S(1)} %bitcast.16), custom_call_target="tpu_custom_call" | custom-call | flops 1610612736 | bytes 4194304 | tf_op jit(solution)/shard_map/pallas_call | solution.py:109
  71.2 54.1 %all_to_all.10 = bf16[16,1,4,128,128]{4,3,2,1,0:T(8,128)(2,1)} all-to-all(bf16[16,1,4,128,128]{4,3,2,1,0:T(8,128)(2,1)S(1)} %bitcast.17), channel_id=1, replica_groups=mesh['dp'=2,'ctx'=16] {'ctx'}, dimensions={0} | all-to-all | bytes 4194304 | tf_op jit(solution)/shard_map/all_to_all | solution.py:175
  125.3 3.0 %copy.31 = bf16[16,1,4,128,128]{3,4,0,1,2:T(8,128)(2,1)S(1)} copy(bf16[16,1,4,128,128]{4,3,2,1,0:T(8,128)(2,1)} %all_to_all.10) | data formatting | bytes 4194304 | tf_op jit(solution)/shard_map/all_to_all | solution.py:175
  128.4 1.2 fusion
  129.5 2.0 %copy.35 = bf16[128,2048]{1,0:T(8,128)(2,1)} copy(bf16[128,2048]{0,1:T(8,128)(2,1)} %bitcast.22) | data formatting | bytes 1048576
  131.6 2.0 %copy.34 = bf16[128,2048]{1,0:T(8,128)(2,1)} copy(bf16[128,2048]{0,1:T(8,128)(2,1)} %bitcast.21) | data formatting | bytes 1048576
  133.6 1.0 copy.33
  134.6 1.0 copy.32
Async XLA Ops:
  0.6 2.7 %copy-start.1 = (bf16[128,2048]{1,0:T(8,128)(2,1)S(1)}, bf16[128,2048]{1,0:T(8,128)(2,1)}, u32[]{:S(2)}) copy-start(bf16[128,2048]{1,0:T(8,128)(2,1)} %param.7) | copy-start | bytes 1572868
  0.6 3.7 %copy-start.2 = (bf16[128,2048]{1,0:T(8,128)(2,1)S(1)}, bf16[128,2048]{1,0:T(8,128)(2,1)}, u32[]{:S(2)}) copy-start(bf16[128,2048]{1,0:T(8,128)(2,1)} %param.8) | copy-start | bytes 1572868
  9.5 52.7 %copy-start = (s32[8]{0:T(128)S(1)}, s32[8]{0:T(128)}, u32[]{:S(2)}) copy-start(s32[8]{0:T(128)} %refs_1_.1) | copy-start | bytes 100
  9.5 52.7 %all-to-all-start = ((bf16[16,1,4,128,128]{4,3,2,1,0:T(8,128)(2,1)}), bf16[16,1,4,128,128]{4,3,2,1,0:T(8,128)(2,1)S(1)}, u32[]{:S(2)}, u32[]{:S(2)}) async-start(bf16[16,1,4,128,128]{4,3,2,1,0:T(8,128)(2,1)} %copy.29), calls=%async_computation | async-start | bytes 4194304 | tf_op jit(solution)/shard_map/all_to_all | solution.py:155

commit v2 on v1

--- a/solution.py
+++ b/solution.py
@@ -121,7 +121,7 @@
     )(*operands)
 
 
-def body(queries, keys, values, cotangent, partner):
+def by_all_to_all(queries, keys, values, cotangent, partner):
     rows, width = queries.shape
     devices = lax.axis_size("ctx")
     heads = width // HEAD
@@ -175,6 +175,189 @@
     return tuple(unpack(exchange(jnp.stack(outs, axis=1))))
 
 
+def call(kernel, place, arrays, out_shape, scratch=(), flops=0, exps=0):
+    smem = pl.BlockSpec(memory_space=pltpu.SMEM)
+    vmem = pl.BlockSpec(memory_space=pltpu.VMEM)
+    moved = sum(a.size * a.dtype.itemsize for a in arrays)
+    moved += sum(a.size * a.dtype.itemsize for a in out_shape)
+    return pl.pallas_call(
+        kernel,
+        out_shape=out_shape,
+        in_specs=[smem] * len(place) + [vmem] * len(arrays),
+        out_specs=[vmem] * len(out_shape),
+        scratch_shapes=list(scratch),
+        compiler_params=pltpu.CompilerParams(vmem_limit_bytes=40 * 1024 * 1024),
+        cost_estimate=pl.CostEstimate(flops=flops, bytes_accessed=moved, transcendentals=exps),
+    )(*place, *arrays)
+
+
+def pack(place, arrays, chips):
+    count = len(arrays)
+    rows, width = arrays[0].shape
+    span = width // chips
+
+    def kernel(where, *refs):
+        for k in range(chips):
+            start = pl.multiple_of((where[0] ^ k) * span, span)
+            for i in range(count):
+                refs[count + k][i] = refs[i][:, pl.ds(start, span)]
+
+    piece = jax.ShapeDtypeStruct((count, rows, span), jnp.bfloat16)
+    return call(kernel, [place], arrays, [piece] * chips)
+
+
+def unpack(place, mine, theirs):
+    chips = len(mine)
+    count, both, head = mine[0].shape
+    rows = both // 2
+
+    def kernel(where, *refs):
+        core = where[1]
+        half = pl.ds(pl.multiple_of(core * rows, rows), rows)
+        for k in range(chips):
+            start = (where[0] ^ k) * 2
+            here = pl.multiple_of((start + core) * head, head)
+            there = pl.multiple_of((start + 1 - core) * head, head)
+            for i in range(count):
+                out = refs[2 * chips + i]
+                out[:, pl.ds(here, head)] = refs[k][i, half]
+                out[:, pl.ds(there, head)] = refs[chips + k][i, half]
+
+    out = jax.ShapeDtypeStruct((rows, chips * 2 * head), jnp.bfloat16)
+    return call(kernel, [place], [*mine, *theirs], [out] * count)
+
+
+def merge(where, mine, theirs, target):
+    core = where[1]
+    rows = mine[0].shape[1]
+    column = pl.ds(pl.multiple_of(core * HEAD, HEAD), HEAD)
+    here = pl.ds(pl.multiple_of(core * rows, rows), rows)
+    there = pl.ds(pl.multiple_of((1 - core) * rows, rows), rows)
+    for k in range(len(mine)):
+        block = where[0] ^ k
+        for i in range(mine[0].shape[0]):
+            target[block, i, here] = mine[k][i, :, column]
+            target[block, i, there] = theirs[k][i, :, column]
+
+
+def forward(place, partner, mine, theirs):
+    chips = len(mine)
+    size = 2 * mine[0].shape[1]
+
+    def kernel(where, partner, *refs):
+        ins, outs = refs[: 2 * chips], refs[2 * chips :]
+        held, weights = outs[chips], outs[chips + 1]
+        merge(where, ins[:chips], ins[chips:], held)
+        for k in range(chips):
+            b = where[0] ^ k
+            p = partner[b]
+            q = held[b, 0]
+            s = mm(q, held[b, 1], NT) * SCALE
+            t = mm(q, held[p, 1], NT) * SCALE
+            peak = jnp.max(jnp.maximum(s, t), axis=1, keepdims=True)
+            s, t = jnp.exp(s - peak), jnp.exp(t - peak)
+            inverse = 1.0 / jnp.sum(s + t, axis=1, keepdims=True)
+            s, t = s * inverse, t * inverse
+            weights[b, 0] = s
+            weights[b, 1] = t
+            attended = mm(s.astype(jnp.bfloat16), held[b, 2], NN)
+            attended += mm(t.astype(jnp.bfloat16), held[p, 2], NN)
+            attended = attended.astype(jnp.bfloat16)
+            outs[k][0] = attended
+            held[b, 3] = attended
+
+    out_shape = [jax.ShapeDtypeStruct((1, size, HEAD), jnp.bfloat16)] * chips
+    out_shape += [
+        jax.ShapeDtypeStruct((chips, 4, size, HEAD), jnp.bfloat16),
+        jax.ShapeDtypeStruct((chips, 2, size, size), jnp.float32),
+    ]
+    flops = chips * 8 * size * size * HEAD
+    outs = call(
+        kernel, [place, partner], [*mine, *theirs], out_shape, (), flops, chips * 2 * size * size
+    )
+    return outs[:chips], outs[chips], outs[chips + 1]
+
+
+def backward(place, partner, mine, theirs, held, weights):
+    chips = len(mine)
+    size = held.shape[2]
+
+    def kernel(where, partner, *refs):
+        ins, outs = refs[: 2 * chips + 2], refs[2 * chips + 2 : 3 * chips + 2]
+        held, weights = ins[2 * chips :]
+        grads, acc_k, acc_v = refs[3 * chips + 2 :]
+        merge(where, ins[:chips], ins[chips : 2 * chips], grads)
+        acc_k[...] = jnp.zeros_like(acc_k)
+        acc_v[...] = jnp.zeros_like(acc_v)
+        for k in range(chips):
+            b = where[0] ^ k
+            q, do = held[b, 0], grads[b, 0]
+            delta = jnp.sum(
+                do.astype(jnp.float32) * held[b, 3].astype(jnp.float32), axis=1, keepdims=True
+            )
+            grad_q = None
+            for side, c in enumerate((b, partner[b])):
+                w = weights[b, side]
+                g = (w * (mm(do, held[c, 2], NT) - delta)).astype(jnp.bfloat16)
+                term = mm(g, held[c, 1], NN)
+                grad_q = term if side == 0 else grad_q + term
+                acc_k[c] += mm(g, q, TN)
+                acc_v[c] += mm(w.astype(jnp.bfloat16), do, TN)
+            outs[k][0] = (SCALE * grad_q).astype(jnp.bfloat16)
+        for k in range(chips):
+            b = where[0] ^ k
+            outs[k][1] = (SCALE * acc_k[b]).astype(jnp.bfloat16)
+            outs[k][2] = acc_v[b].astype(jnp.bfloat16)
+
+    out_shape = [jax.ShapeDtypeStruct((3, size, HEAD), jnp.bfloat16)] * chips
+    scratch = [
+        pltpu.VMEM((chips, 1, size, HEAD), jnp.bfloat16),
+        pltpu.VMEM((chips, size, HEAD), jnp.float32),
+        pltpu.VMEM((chips, size, HEAD), jnp.float32),
+    ]
+    flops = chips * 16 * size * size * HEAD
+    return call(
+        kernel, [place, partner], [*mine, *theirs, held, weights], out_shape, scratch, flops
+    )
+
+
+def between_chips(pieces):
+    devices = 2 * len(pieces)
+    return [
+        lax.ppermute(p, "ctx", [(i, i ^ (2 * k)) for i in range(devices)]) if k else p
+        for k, p in enumerate(pieces)
+    ]
+
+
+def between_cores(pieces):
+    devices = 2 * len(pieces)
+    return [lax.ppermute(p, "ctx", [(i, i ^ 1) for i in range(devices)]) for p in pieces]
+
+
+def by_permutes(queries, keys, values, cotangent, partner):
+    chips = lax.axis_size("ctx") // 2
+    me = lax.axis_index("ctx")
+    place = jnp.stack([me // 2, me % 2]).astype(jnp.int32)
+    first = between_chips(pack(place, [queries, keys, values], chips))
+    second = between_chips(pack(place, [cotangent], chips))
+    attended, held, weights = forward(place, partner, first, between_cores(first))
+    grads = backward(place, partner, second, between_cores(second), held, weights)
+    attended = between_chips(attended)
+    outs = unpack(place, attended, between_cores(attended))
+    grads = between_chips(grads)
+    return tuple(outs) + tuple(unpack(place, grads, between_cores(grads)))
+
+
+def body(queries, keys, values, cotangent, partner):
+    rows, width = queries.shape
+    devices = lax.axis_size("ctx")
+    blocks = partner.shape[0]
+    in_pairs = devices == 2 * blocks and devices * HEAD == width
+    if in_pairs and blocks & (blocks - 1) == 0:
+        return by_permutes(queries, keys, values, cotangent, partner)
+    return by_all_to_all(queries, keys, values, cotangent, partner)
+
+
 def solution(mesh):
     split = P(("dp", "ctx"), None)
     return jax.shard_map(

time: 137 us -> 140 us (1.022)
  starting transfers between devices: 6.74 us -> 68 us
  blocking collectives: 54.1 us -> 0 us
  local copies, waits for them, and re-layouts: 17.6 us -> 4.82 us
  Pallas kernels: 9.02 us -> 16.3 us
  waiting for transfers between devices: 46 us -> 49.2 us
    ppermute x0 -> x60, starting transfers between devices: none -> 68 us  [the longest x32 36.9 us: between_cores(): lax.ppermute(p, 'ctx', [(i, i ^ 1) for i in range(devices)])]
    all_to_all x1 -> x0, blocking collectives: 54.1 us -> none  [body(): return tuple(unpack(exchange(jnp.stack(outs, axis=1))))]
    ppermute x0 -> x60, waiting for transfers between devices: none -> 49.2 us  [the longest x28 49.1 us: between_chips(): lax.ppermute(p, 'ctx', [(i, i ^ 2 * k) for i in range(devices)])]
    all_to_all x1 -> x0, waiting for transfers between devices: 46 us -> none  [body(): local = exchange(pack([queries, keys, values, cotangent]))]
    pallas_call x1 -> x6, Pallas kernels: 9.02 us -> 16.3 us  [call(): pl.pallas_call(kernel, out_shape=out_shape, in_specs=[smem] * len(place)...]
    all_to_all x1 -> x0, starting transfers between devices: 6.74 us -> none  [body(): local = exchange(pack([queries, keys, values, cotangent]))]
    unnamed x14 -> x10, local copies, waits for them, and re-layouts: 10.8 us -> 4.82 us
    all_to_all x1 -> x0, local copies, waits for them, and re-layouts: 3.04 us -> none  [body(): return tuple(unpack(exchange(jnp.stack(outs, axis=1))))]
  transfers between devices with their start and end apart: 1 -> 60, of which waited for: 1 -> 14; matrix products, arithmetic and copies ran while one was open for 0% -> 0% of each run, Pallas kernels for 0% -> 10%
where the time goes in v2:
time: 140 us; the launch traced here: 139 us
  starting transfers between devices  68 us (49%)
  waiting for transfers between devices  49.2 us (35%)
  Pallas kernels  16.3 us (12%)
  local copies, waits for them, and re-layouts  4.82 us (3%)
    ppermute x28, waiting for transfers between devices, between_chips(): lax.ppermute(p, 'ctx', [(i, i ^ 2 * k) for i in range(devices)])  49.1 us
    ppermute x32, starting transfers between devices, between_cores(): lax.ppermute(p, 'ctx', [(i, i ^ 1) for i in range(devices)])  36.9 us
    ppermute x28, starting transfers between devices, between_chips(): lax.ppermute(p, 'ctx', [(i, i ^ 2 * k) for i in range(devices)])  31.1 us
    pallas_call x6, Pallas kernels, call(): pl.pallas_call(kernel, out_shape=out_shape, in_specs=[smem] * len(place)...  16.3 us
    unnamed x10, local copies, waits for them, and re-layouts  4.82 us
  transfers between devices with their start and end apart: 60, of which 14 were waited for; matrix products, arithmetic and copies ran while one was open for 0% of the time, Pallas kernels for 10%

profile of v2, /device:TPU:9, one launch (start us, length us, event | category | flops | bytes accessed | tf_op | source)
XLA Modules:
  0.0 139.2 jit_solution(14858096839182465296)
XLA Ops:
  0.7 1.0 copy-done
  1.8 0.6 shard_map.87
  2.4 1.3 collective-permute-start.30
  3.9 1.2 collective-permute-start.32
  5.1 2.3 %collective-permute-start.33 = (bf16[1,128,256]{2,1,0:T(8,128)(2,1)S(1)}, bf16[1,128,256]{2,1,0:T(8,128)(2,1)S(1)}, u32[]{:S(2)}, u32[]{:S(2)}) collective-permute-start(bf16[1,128,256]{2,1,0:T(8,128)(2,1)S(1)} %get-tuple-element.61), channel_id=1, source_target_pairs={{0,8},{1,9},{2,10},{3,11},{4,12},{5,13},{6,14},{7,15},{8,0},{9,1},... | collective-permute-start | bytes 196616 | tf_op jit(solution)/shard_map/ppermute | solution.py:327
  7.4 1.0 collective-permute-start.34
  8.4 1.3 collective-permute-start.35
  9.8 2.6 %collective-permute-start.37 = (bf16[1,128,256]{2,1,0:T(8,128)(2,1)S(1)}, bf16[1,128,256]{2,1,0:T(8,128)(2,1)S(1)}, u32[]{:S(2)}, u32[]{:S(2)}) collective-permute-start(bf16[1,128,256]{2,1,0:T(8,128)(2,1)S(1)} %get-tuple-element.57.refs_0_), channel_id=1, source_target_pairs={{0,1},{1,0},{2,3},{3,2},{4,5},{5,4},{6,7},{7,6},{8,9},{9,8},{10,11... | collective-permute-start | bytes 196616 | tf_op jit(solution)/shard_map/ppermute | solution.py:334
  12.5 1.8 %collective-permute-start.38 = (bf16[1,128,256]{2,1,0:T(8,128)(2,1)S(1)}, bf16[1,128,256]{2,1,0:T(8,128)(2,1)S(1)}, u32[]{:S(2)}, u32[]{:S(2)}) collective-permute-start(bf16[1,128,256]{2,1,0:T(8,128)(2,1)S(1)} %collective-permute-done.30.refs_1_), channel_id=1, source_target_pairs={{0,1},{1,0},{2,3},{3,2},{4,5},{5,4},{6,7},{7,6},{8,9},{9,8},{10,11... | collective-permute-start | bytes 196616 | tf_op jit(solution)/shard_map/ppermute | solution.py:334
  14.3 2.8 %collective-permute-start.39 = (bf16[1,128,256]{2,1,0:T(8,128)(2,1)S(1)}, bf16[1,128,256]{2,1,0:T(8,128)(2,1)S(1)}, u32[]{:S(2)}, u32[]{:S(2)}) collective-permute-start(bf16[1,128,256]{2,1,0:T(8,128)(2,1)S(1)} %collective-permute-done.31.refs_2_), channel_id=1, source_target_pairs={{0,1},{1,0},{2,3},{3,2},{4,5},{5,4},{6,7},{7,6},{8,9},{9,8},{10,11... | collective-permute-start | bytes 196616 | tf_op jit(solution)/shard_map/ppermute | solution.py:334
  17.1 1.0 copy-done.1
  18.2 1.0 copy-done.2
  19.2 1.0 copy-done.3
  20.2 0.8 shard_map.84
  21.0 2.7 %collective-permute-start.2 = (bf16[3,128,256]{2,1,0:T(8,128)(2,1)S(1)}, bf16[3,128,256]{2,1,0:T(8,128)(2,1)S(1)}, u32[]{:S(2)}, u32[]{:S(2)}) collective-permute-start(bf16[3,128,256]{2,1,0:T(8,128)(2,1)S(1)} %get-tuple-element.44), channel_id=1, source_target_pairs={{0,6},{1,7},{2,4},{3,5},{4,2},{5,3},{6,0},{7,1},{8,14},{9,15},{10,... | collective-permute-start | bytes 589832 | tf_op jit(solution)/shard_map/ppermute | solution.py:327
  23.7 1.7 %collective-permute-start.3 = (bf16[3,128,256]{2,1,0:T(8,128)(2,1)S(1)}, bf16[3,128,256]{2,1,0:T(8,128)(2,1)S(1)}, u32[]{:S(2)}, u32[]{:S(2)}) collective-permute-start(bf16[3,128,256]{2,1,0:T(8,128)(2,1)S(1)} %get-tuple-element.45), channel_id=1, source_target_pairs={{0,8},{1,9},{2,10},{3,11},{4,12},{5,13},{6,14},{7,15},{8,0},{9,1},... | collective-permute-start | bytes 589832 | tf_op jit(solution)/shard_map/ppermute | solution.py:327
  25.4 1.4 %collective-permute-start.4 = (bf16[3,128,256]{2,1,0:T(8,128)(2,1)S(1)}, bf16[3,128,256]{2,1,0:T(8,128)(2,1)S(1)}, u32[]{:S(2)}, u32[]{:S(2)}) collective-permute-start(bf16[3,128,256]{2,1,0:T(8,128)(2,1)S(1)} %get-tuple-element.46), channel_id=1, source_target_pairs={{0,10},{1,11},{2,8},{3,9},{4,14},{5,15},{6,12},{7,13},{8,2},{9,3},... | collective-permute-start | bytes 589832 | tf_op jit(solution)/shard_map/ppermute | solution.py:327
  26.8 2.0 %collective-permute-start.5 = (bf16[3,128,256]{2,1,0:T(8,128)(2,1)S(1)}, bf16[3,128,256]{2,1,0:T(8,128)(2,1)S(1)}, u32[]{:S(2)}, u32[]{:S(2)}) collective-permute-start(bf16[3,128,256]{2,1,0:T(8,128)(2,1)S(1)} %get-tuple-element.47), channel_id=1, source_target_pairs={{0,12},{1,13},{2,14},{3,15},{4,8},{5,9},{6,10},{7,11},{8,4},{9,5},... | collective-permute-start | bytes 589832 | tf_op jit(solution)/shard_map/ppermute | solution.py:327
  28.9 3.2 %collective-permute-done.2.refs_3_ = bf16[3,128,256]{2,1,0:T(8,128)(2,1)S(1)} collective-permute-done((bf16[3,128,256]{2,1,0:T(8,128)(2,1)S(1)}, bf16[3,128,256]{2,1,0:T(8,128)(2,1)S(1)}, u32[]{:S(2)}, u32[]{:S(2)}) %collective-permute-start.2) | collective-permute-done | bytes 196640 | tf_op jit(solution)/shard_map/ppermute | solution.py:327
  32.1 14.5 %collective-permute-done.3.refs_4_ = bf16[3,128,256]{2,1,0:T(8,128)(2,1)S(1)} collective-permute-done((bf16[3,128,256]{2,1,0:T(8,128)(2,1)S(1)}, bf16[3,128,256]{2,1,0:T(8,128)(2,1)S(1)}, u32[]{:S(2)}, u32[]{:S(2)}) %collective-permute-start.3) | collective-permute-done | bytes 196640 | tf_op jit(solution)/shard_map/ppermute | solution.py:327
  46.6 4.2 %collective-permute-done.4.refs_5_ = bf16[3,128,256]{2,1,0:T(8,128)(2,1)S(1)} collective-permute-done((bf16[3,128,256]{2,1,0:T(8,128)(2,1)S(1)}, bf16[3,128,256]{2,1,0:T(8,128)(2,1)S(1)}, u32[]{:S(2)}, u32[]{:S(2)}) %collective-permute-start.4) | collective-permute-done | bytes 196640 | tf_op jit(solution)/shard_map/ppermute | solution.py:327
  50.8 1.2 collective-permute-start.7
  52.0 4.0 %collective-permute-done.5.refs_6_ = bf16[3,128,256]{2,1,0:T(8,128)(2,1)S(1)} collective-permute-done((bf16[3,128,256]{2,1,0:T(8,128)(2,1)S(1)}, bf16[3,128,256]{2,1,0:T(8,128)(2,1)S(1)}, u32[]{:S(2)}, u32[]{:S(2)}) %collective-permute-start.5) | collective-permute-done | bytes 196640 | tf_op jit(solution)/shard_map/ppermute | solution.py:327
  55.9 1.2 collective-permute-start.10
  57.1 4.0 %collective-permute-done.6.refs_7_ = bf16[3,128,256]{2,1,0:T(8,128)(2,1)S(1)} collective-permute-done((bf16[3,128,256]{2,1,0:T(8,128)(2,1)S(1)}, bf16[3,128,256]{2,1,0:T(8,128)(2,1)S(1)}, u32[]{:S(2)}, u32[]{:S(2)}) %collective-permute-start.6) | collective-permute-done | bytes 196640 | tf_op jit(solution)/shard_map/ppermute | solution.py:327
  61.1 0.8 collective-permute-start.11
  61.9 0.5 collective-permute-start.13
  62.5 0.4 collective-permute-start.8
  62.9 0.4 collective-permute-start.9
  64.8 0.7 copy-done.4
  65.4 5.5 %shard_map.85 = (bf16[1,256,128]{2,1,0:T(8,128)(2,1)S(1)}, bf16[1,256,128]{2,1,0:T(8,128)(2,1)S(1)}, bf16[1,256,128]{2,1,0:T(8,128)(2,1)S(1)}, bf16[1,256,128]{2...) custom-call(s32[2]{0:T(128)S(1)} %pad_add_fusion.where, ...), custom_call_target="tpu_custom_call" | custom-call | flops 536870912 | bytes 9961472 | tf_op jit(solution)/shard_map/pallas_call | solution.py:183
  70.9 0.3 collective-permute-start.15
  71.2 2.4 %collective-permute-start.17 = (bf16[1,256,128]{2,1,0:T(8,128)(2,1)S(1)}, bf16[1,256,128]{2,1,0:T(8,128)(2,1)S(1)}, u32[]{:S(2)}, u32[]{:S(2)}) collective-permute-start(bf16[1,256,128]{2,1,0:T(8,128)(2,1)S(1)} %get-tuple-element.52), channel_id=1, source_target_pairs={{0,6},{1,7},{2,4},{3,5},{4,2},{5,3},{6,0},{7,1},{8,14},{9,15},{10,... | collective-permute-start | bytes 196616 | tf_op jit(solution)/shard_map/ppermute | solution.py:327
  73.8 2.2 %collective-permute-start.19 = (bf16[1,256,128]{2,1,0:T(8,128)(2,1)S(1)}, bf16[1,256,128]{2,1,0:T(8,128)(2,1)S(1)}, u32[]{:S(2)}, u32[]{:S(2)}) collective-permute-start(bf16[1,256,128]{2,1,0:T(8,128)(2,1)S(1)} %get-tuple-element.54), channel_id=1, source_target_pairs={{0,10},{1,11},{2,8},{3,9},{4,14},{5,15},{6,12},{7,13},{8,2},{9,3},... | collective-permute-start | bytes 196616 | tf_op jit(solution)/shard_map/ppermute | solution.py:327
  76.0 1.3 collective-permute-start.20
  77.3 1.1 collective-permute-start.21
  78.4 2.2 %collective-permute-start.22 = (bf16[1,256,128]{2,1,0:T(8,128)(2,1)S(1)}, bf16[1,256,128]{2,1,0:T(8,128)(2,1)S(1)}, u32[]{:S(2)}, u32[]{:S(2)}) collective-permute-start(bf16[1,256,128]{2,1,0:T(8,128)(2,1)S(1)} %get-tuple-element.49.refs_0_), channel_id=1, source_target_pairs={{0,1},{1,0},{2,3},{3,2},{4,5},{5,4},{6,7},{7,6},{8,9},{9,8},{10,11... | collective-permute-start | bytes 196616 | tf_op jit(solution)/shard_map/ppermute | solution.py:334
  80.7 1.4 %collective-permute-done.19.refs_5_ = bf16[1,256,128]{2,1,0:T(8,128)(2,1)S(1)} collective-permute-done((bf16[1,256,128]{2,1,0:T(8,128)(2,1)S(1)}, bf16[1,256,128]{2,1,0:T(8,128)(2,1)S(1)}, u32[]{:S(2)}, u32[]{:S(2)}) %collective-permute-start.19) | collective-permute-done | bytes 65568 | tf_op jit(solution)/shard_map/ppermute | solution.py:327
  82.1 1.0 collective-permute-start.24
  83.1 3.2 %collective-permute-done.20.refs_6_ = bf16[1,256,128]{2,1,0:T(8,128)(2,1)S(1)} collective-permute-done((bf16[1,256,128]{2,1,0:T(8,128)(2,1)S(1)}, bf16[1,256,128]{2,1,0:T(8,128)(2,1)S(1)}, u32[]{:S(2)}, u32[]{:S(2)}) %collective-permute-start.20) | collective-permute-done | bytes 65568 | tf_op jit(solution)/shard_map/ppermute | solution.py:327
  86.3 0.7 collective-permute-start.25
  87.0 0.8 collective-permute-done.21.refs_7_
  87.7 0.5 collective-permute-start.26
  88.3 0.5 collective-permute-start.28
  88.9 5.9 %shard_map.88 = (bf16[3,256,128]{2,1,0:T(8,128)(2,1)S(1)}, bf16[3,256,128]{2,1,0:T(8,128)(2,1)S(1)}, bf16[3,256,128]{2,1,0:T(8,128)(2,1)S(1)}, bf16[3,256,128]{2...) custom-call(s32[2]{0:T(128)S(1)} %pad_add_fusion.where, ...), custom_call_target="tpu_custom_call" | custom-call | flops 1073741824 | bytes 8912896 | tf_op jit(solution)/shard_map/pallas_call | solution.py:183
  94.7 1.2 collective-permute-start.45
  96.0 1.5 %collective-permute-start.47 = (bf16[3,256,128]{2,1,0:T(8,128)(2,1)S(1)}, bf16[3,256,128]{2,1,0:T(8,128)(2,1)S(1)}, u32[]{:S(2)}, u32[]{:S(2)}) collective-permute-start(bf16[3,256,128]{2,1,0:T(8,128)(2,1)S(1)} %get-tuple-element.70), channel_id=1, source_target_pairs={{0,6},{1,7},{2,4},{3,5},{4,2},{5,3},{6,0},{7,1},{8,14},{9,15},{10,... | collective-permute-start | bytes 589832 | tf_op jit(solution)/shard_map/ppermute | solution.py:327
  97.5 1.0 collective-permute-start.48
  98.5 2.2 %collective-permute-start.49 = (bf16[3,256,128]{2,1,0:T(8,128)(2,1)S(1)}, bf16[3,256,128]{2,1,0:T(8,128)(2,1)S(1)}, u32[]{:S(2)}, u32[]{:S(2)}) collective-permute-start(bf16[3,256,128]{2,1,0:T(8,128)(2,1)S(1)} %get-tuple-element.72), channel_id=1, source_target_pairs={{0,10},{1,11},{2,8},{3,9},{4,14},{5,15},{6,12},{7,13},{8,2},{9,3},... | collective-permute-start | bytes 589832 | tf_op jit(solution)/shard_map/ppermute | solution.py:327
  100.8 1.2 collective-permute-start.50
  102.1 4.0 %collective-permute-done.46.refs_2_ = bf16[3,256,128]{2,1,0:T(8,128)(2,1)S(1)} collective-permute-done((bf16[3,256,128]{2,1,0:T(8,128)(2,1)S(1)}, bf16[3,256,128]{2,1,0:T(8,128)(2,1)S(1)}, u32[]{:S(2)}, u32[]{:S(2)}) %collective-permute-start.46) | collective-permute-done | bytes 196640 | tf_op jit(solution)/shard_map/ppermute | solution.py:327
  106.1 1.2 collective-permute-start.51
  107.3 3.8 %collective-permute-done.47.refs_3_ = bf16[3,256,128]{2,1,0:T(8,128)(2,1)S(1)} collective-permute-done((bf16[3,256,128]{2,1,0:T(8,128)(2,1)S(1)}, bf16[3,256,128]{2,1,0:T(8,128)(2,1)S(1)}, u32[]{:S(2)}, u32[]{:S(2)}) %collective-permute-start.47) | collective-permute-done | bytes 196640 | tf_op jit(solution)/shard_map/ppermute | solution.py:327
  111.1 1.3 collective-permute-start.52
  112.4 0.7 collective-permute-start.53
  113.1 2.3 %collective-permute-done.49.refs_5_ = bf16[3,256,128]{2,1,0:T(8,128)(2,1)S(1)} collective-permute-done((bf16[3,256,128]{2,1,0:T(8,128)(2,1)S(1)}, bf16[3,256,128]{2,1,0:T(8,128)(2,1)S(1)}, u32[]{:S(2)}, u32[]{:S(2)}) %collective-permute-start.49) | collective-permute-done | bytes 196640 | tf_op jit(solution)/shard_map/ppermute | solution.py:327
  115.4 10.8 %collective-permute-start.54 = (bf16[3,256,128]{2,1,0:T(8,128)(2,1)S(1)}, bf16[3,256,128]{2,1,0:T(8,128)(2,1)S(1)}, u32[]{:S(2)}, u32[]{:S(2)}) collective-permute-start(bf16[3,256,128]{2,1,0:T(8,128)(2,1)S(1)} %collective-permute-done.46.refs_2_), channel_id=1, source_target_pairs={{0,1},{1,0},{2,3},{3,2},{4,5},{5,4},{6,7},{7,6},{8,9},{9,8},{10,11... | collective-permute-start | bytes 589832 | tf_op jit(solution)/shard_map/ppermute | solution.py:334
  126.2 1.8 %collective-permute-done.50.refs_6_ = bf16[3,256,128]{2,1,0:T(8,128)(2,1)S(1)} collective-permute-done((bf16[3,256,128]{2,1,0:T(8,128)(2,1)S(1)}, bf16[3,256,128]{2,1,0:T(8,128)(2,1)S(1)}, u32[]{:S(2)}, u32[]{:S(2)}) %collective-permute-start.50) | collective-permute-done | bytes 196640 | tf_op jit(solution)/shard_map/ppermute | solution.py:327
  128.0 3.3 %collective-permute-start.55 = (bf16[3,256,128]{2,1,0:T(8,128)(2,1)S(1)}, bf16[3,256,128]{2,1,0:T(8,128)(2,1)S(1)}, u32[]{:S(2)}, u32[]{:S(2)}) collective-permute-start(bf16[3,256,128]{2,1,0:T(8,128)(2,1)S(1)} %collective-permute-done.47.refs_3_), channel_id=1, source_target_pairs={{0,1},{1,0},{2,3},{3,2},{4,5},{5,4},{6,7},{7,6},{8,9},{9,8},{10,11... | collective-permute-start | bytes 589832 | tf_op jit(solution)/shard_map/ppermute | solution.py:334
  131.4 1.7 %collective-permute-done.51.refs_7_ = bf16[3,256,128]{2,1,0:T(8,128)(2,1)S(1)} collective-permute-done((bf16[3,256,128]{2,1,0:T(8,128)(2,1)S(1)}, bf16[3,256,128]{2,1,0:T(8,128)(2,1)S(1)}, u32[]{:S(2)}, u32[]{:S(2)}) %collective-permute-start.51) | collective-permute-done | bytes 196640 | tf_op jit(solution)/shard_map/ppermute | solution.py:327
  133.1 1.9 %collective-permute-start.56 = (bf16[3,256,128]{2,1,0:T(8,128)(2,1)S(1)}, bf16[3,256,128]{2,1,0:T(8,128)(2,1)S(1)}, u32[]{:S(2)}, u32[]{:S(2)}) collective-permute-start(bf16[3,256,128]{2,1,0:T(8,128)(2,1)S(1)} %collective-permute-done.48.refs_4_), channel_id=1, source_target_pairs={{0,1},{1,0},{2,3},{3,2},{4,5},{5,4},{6,7},{7,6},{8,9},{9,8},{10,11... | collective-permute-start | bytes 589832 | tf_op jit(solution)/shard_map/ppermute | solution.py:334
  135.0 0.5 collective-permute-start.58
  135.6 1.5 %shard_map.86 = bf16[128,2048]{1,0:T(8,128)(2,1)} custom-call(s32[2]{0:T(128)S(1)} %pad_add_fusion.where, bf16[1,256,128]{2,1,0:T(8,128)(2,1)S(1)} %get-tuple-element.49.refs_0_, bf16[1,256,128]{2,1,0:T(8,128)(2,1)S(1)} %collective-permute-done.15.refs_1_, bf16[1,256,128]{2,1,0:T(8,128)(2,1)S(1)} %collective-permute-done.16.refs_2_, ...), custom_call_target="tpu_custom_call" | custom-call | bytes 1572864 | tf_op jit(solution)/shard_map/pallas_call | solution.py:183
  137.1 2.1 %shard_map.89 = (bf16[128,2048]{1,0:T(8,128)(2,1)}, bf16[128,2048]{1,0:T(8,128)(2,1)}, bf16[128,2048]{1,0:T(8,128)(2,1)}) custom-call(s32[2]{0:T(128)S(1)} %pad_add_fusion.where, bf16[3,256,128]{2,1,0:T(8,128)(2,1)S(1)} %get-tuple-element.67.refs_0_, bf16[3,256,128]{2,1,0:T(8,128)(2,1)S(1)} %collective-permute-done.45.refs_1_, ...), custom_call_target="tpu_custom_call" | custom-call | bytes 4718592 | tf_op jit(solution)/shard_map/pallas_call | solution.py:183
  (73 shorter events, 2.7 us)
Async XLA Ops:
  0.7 1.0 copy-start
  2.4 6.0 %collective-permute-start.30 = (bf16[1,128,256]{2,1,0:T(8,128)(2,1)S(1)}, bf16[1,128,256]{2,1,0:T(8,128)(2,1)S(1)}, u32[]{:S(2)}, u32[]{:S(2)}) collective-permute-start(bf16[1,128,256]{2,1,0:T(8,128)(2,1)S(1)} %get-tuple-element.58), channel_id=1, source_target_pairs={{0,2},{1,3},{2,0},{3,1},{4,6},{5,7},{6,4},{7,5},{8,10},{9,11},{10,... | collective-permute-start | bytes 196616 | tf_op jit(solution)/shard_map/ppermute | solution.py:327
  3.7 6.0 %collective-permute-start.31 = (bf16[1,128,256]{2,1,0:T(8,128)(2,1)S(1)}, bf16[1,128,256]{2,1,0:T(8,128)(2,1)S(1)}, u32[]{:S(2)}, u32[]{:S(2)}) collective-permute-start(bf16[1,128,256]{2,1,0:T(8,128)(2,1)S(1)} %get-tuple-element.59), channel_id=1, source_target_pairs={{0,4},{1,5},{2,6},{3,7},{4,0},{5,1},{6,2},{7,3},{8,12},{9,13},{10,... | collective-permute-start | bytes 196616 | tf_op jit(solution)/shard_map/ppermute | solution.py:327
  3.9 6.0 %collective-permute-start.32 = (bf16[1,128,256]{2,1,0:T(8,128)(2,1)S(1)}, bf16[1,128,256]{2,1,0:T(8,128)(2,1)S(1)}, u32[]{:S(2)}, u32[]{:S(2)}) collective-permute-start(bf16[1,128,256]{2,1,0:T(8,128)(2,1)S(1)} %get-tuple-element.60), channel_id=1, source_target_pairs={{0,6},{1,7},{2,4},{3,5},{4,2},{5,3},{6,0},{7,1},{8,14},{9,15},{10,... | collective-permute-start | bytes 196616 | tf_op jit(solution)/shard_map/ppermute | solution.py:327
  5.1 7.4 %collective-permute-start.33 = (bf16[1,128,256]{2,1,0:T(8,128)(2,1)S(1)}, bf16[1,128,256]{2,1,0:T(8,128)(2,1)S(1)}, u32[]{:S(2)}, u32[]{:S(2)}) collective-permute-start(bf16[1,128,256]{2,1,0:T(8,128)(2,1)S(1)} %get-tuple-element.61), channel_id=1, source_target_pairs={{0,8},{1,9},{2,10},{3,11},{4,12},{5,13},{6,14},{7,15},{8,0},{9,1},... | collective-permute-start | bytes 196616 | tf_op jit(solution)/shard_map/ppermute | solution.py:327
  7.4 6.9 %collective-permute-start.34 = (bf16[1,128,256]{2,1,0:T(8,128)(2,1)S(1)}, bf16[1,128,256]{2,1,0:T(8,128)(2,1)S(1)}, u32[]{:S(2)}, u32[]{:S(2)}) collective-permute-start(bf16[1,128,256]{2,1,0:T(8,128)(2,1)S(1)} %get-tuple-element.62), channel_id=1, source_target_pairs={{0,10},{1,11},{2,8},{3,9},{4,14},{5,15},{6,12},{7,13},{8,2},{9,3},... | collective-permute-start | bytes 196616 | tf_op jit(solution)/shard_map/ppermute | solution.py:327
  8.4 12.6 %collective-permute-start.35 = (bf16[1,128,256]{2,1,0:T(8,128)(2,1)S(1)}, bf16[1,128,256]{2,1,0:T(8,128)(2,1)S(1)}, u32[]{:S(2)}, u32[]{:S(2)}) collective-permute-start(bf16[1,128,256]{2,1,0:T(8,128)(2,1)S(1)} %get-tuple-element.63), channel_id=1, source_target_pairs={{0,12},{1,13},{2,14},{3,15},{4,8},{5,9},{6,10},{7,11},{8,4},{9,5},... | collective-permute-start | bytes 196616 | tf_op jit(solution)/shard_map/ppermute | solution.py:327
  9.7 14.0 %collective-permute-start.36 = (bf16[1,128,256]{2,1,0:T(8,128)(2,1)S(1)}, bf16[1,128,256]{2,1,0:T(8,128)(2,1)S(1)}, u32[]{:S(2)}, u32[]{:S(2)}) collective-permute-start(bf16[1,128,256]{2,1,0:T(8,128)(2,1)S(1)} %get-tuple-element.64), channel_id=1, source_target_pairs={{0,14},{1,15},{2,12},{3,13},{4,10},{5,11},{6,8},{7,9},{8,6},{9,7},... | collective-permute-start | bytes 196616 | tf_op jit(solution)/shard_map/ppermute | solution.py:327
  9.8 15.5 %collective-permute-start.37 = (bf16[1,128,256]{2,1,0:T(8,128)(2,1)S(1)}, bf16[1,128,256]{2,1,0:T(8,128)(2,1)S(1)}, u32[]{:S(2)}, u32[]{:S(2)}) collective-permute-start(bf16[1,128,256]{2,1,0:T(8,128)(2,1)S(1)} %get-tuple-element.57.refs_0_), channel_id=1, source_target_pairs={{0,1},{1,0},{2,3},{3,2},{4,5},{5,4},{6,7},{7,6},{8,9},{9,8},{10,11... | collective-permute-start | bytes 196616 | tf_op jit(solution)/shard_map/ppermute | solution.py:334
  12.5 14.3 %collective-permute-start.38 = (bf16[1,128,256]{2,1,0:T(8,128)(2,1)S(1)}, bf16[1,128,256]{2,1,0:T(8,128)(2,1)S(1)}, u32[]{:S(2)}, u32[]{:S(2)}) collective-permute-start(bf16[1,128,256]{2,1,0:T(8,128)(2,1)S(1)} %collective-permute-done.30.refs_1_), channel_id=1, source_target_pairs={{0,1},{1,0},{2,3},{3,2},{4,5},{5,4},{6,7},{7,6},{8,9},{9,8},{10,11... | collective-permute-start | bytes 196616 | tf_op jit(solution)/shard_map/ppermute | solution.py:334
  14.3 14.5 %collective-permute-start.39 = (bf16[1,128,256]{2,1,0:T(8,128)(2,1)S(1)}, bf16[1,128,256]{2,1,0:T(8,128)(2,1)S(1)}, u32[]{:S(2)}, u32[]{:S(2)}) collective-permute-start(bf16[1,128,256]{2,1,0:T(8,128)(2,1)S(1)} %collective-permute-done.31.refs_2_), channel_id=1, source_target_pairs={{0,1},{1,0},{2,3},{3,2},{4,5},{5,4},{6,7},{7,6},{8,9},{9,8},{10,11... | collective-permute-start | bytes 196616 | tf_op jit(solution)/shard_map/ppermute | solution.py:334
  17.1 1.0 copy-start.1
  18.2 1.0 copy-start.2
  19.2 1.0 copy-start.3
  21.0 11.0 %collective-permute-start.2 = (bf16[3,128,256]{2,1,0:T(8,128)(2,1)S(1)}, bf16[3,128,256]{2,1,0:T(8,128)(2,1)S(1)}, u32[]{:S(2)}, u32[]{:S(2)}) collective-permute-start(bf16[3,128,256]{2,1,0:T(8,128)(2,1)S(1)} %get-tuple-element.44), channel_id=1, source_target_pairs={{0,6},{1,7},{2,4},{3,5},{4,2},{5,3},{6,0},{7,1},{8,14},{9,15},{10,... | collective-permute-start | bytes 589832 | tf_op jit(solution)/shard_map/ppermute | solution.py:327
  23.7 22.9 %collective-permute-start.3 = (bf16[3,128,256]{2,1,0:T(8,128)(2,1)S(1)}, bf16[3,128,256]{2,1,0:T(8,128)(2,1)S(1)}, u32[]{:S(2)}, u32[]{:S(2)}) collective-permute-start(bf16[3,128,256]{2,1,0:T(8,128)(2,1)S(1)} %get-tuple-element.45), channel_id=1, source_target_pairs={{0,8},{1,9},{2,10},{3,11},{4,12},{5,13},{6,14},{7,15},{8,0},{9,1},... | collective-permute-start | bytes 589832 | tf_op jit(solution)/shard_map/ppermute | solution.py:327
  25.4 25.4 %collective-permute-start.4 = (bf16[3,128,256]{2,1,0:T(8,128)(2,1)S(1)}, bf16[3,128,256]{2,1,0:T(8,128)(2,1)S(1)}, u32[]{:S(2)}, u32[]{:S(2)}) collective-permute-start(bf16[3,128,256]{2,1,0:T(8,128)(2,1)S(1)} %get-tuple-element.46), channel_id=1, source_target_pairs={{0,10},{1,11},{2,8},{3,9},{4,14},{5,15},{6,12},{7,13},{8,2},{9,3},... | collective-permute-start | bytes 589832 | tf_op jit(solution)/shard_map/ppermute | solution.py:327
  26.8 29.1 %collective-permute-start.5 = (bf16[3,128,256]{2,1,0:T(8,128)(2,1)S(1)}, bf16[3,128,256]{2,1,0:T(8,128)(2,1)S(1)}, u32[]{:S(2)}, u32[]{:S(2)}) collective-permute-start(bf16[3,128,256]{2,1,0:T(8,128)(2,1)S(1)} %get-tuple-element.47), channel_id=1, source_target_pairs={{0,12},{1,13},{2,14},{3,15},{4,8},{5,9},{6,10},{7,11},{8,4},{9,5},... | collective-permute-start | bytes 589832 | tf_op jit(solution)/shard_map/ppermute | solution.py:327
  28.8 32.2 %collective-permute-start.6 = (bf16[3,128,256]{2,1,0:T(8,128)(2,1)S(1)}, bf16[3,128,256]{2,1,0:T(8,128)(2,1)S(1)}, u32[]{:S(2)}, u32[]{:S(2)}) collective-permute-start(bf16[3,128,256]{2,1,0:T(8,128)(2,1)S(1)} %get-tuple-element.48), channel_id=1, source_target_pairs={{0,14},{1,15},{2,12},{3,13},{4,10},{5,11},{6,8},{7,9},{8,6},{9,7},... | collective-permute-start | bytes 589832 | tf_op jit(solution)/shard_map/ppermute | solution.py:327
  32.1 29.8 %collective-permute-start = (bf16[3,128,256]{2,1,0:T(8,128)(2,1)S(1)}, bf16[3,128,256]{2,1,0:T(8,128)(2,1)S(1)}, u32[]{:S(2)}, u32[]{:S(2)}) collective-permute-start(bf16[3,128,256]{2,1,0:T(8,128)(2,1)S(1)} %get-tuple-element.42), channel_id=1, source_target_pairs={{0,2},{1,3},{2,0},{3,1},{4,6},{5,7},{6,4},{7,5},{8,10},{9,11},{10,... | collective-permute-start | bytes 589832 | tf_op jit(solution)/shard_map/ppermute | solution.py:327
  46.6 15.3 %collective-permute-start.1 = (bf16[3,128,256]{2,1,0:T(8,128)(2,1)S(1)}, bf16[3,128,256]{2,1,0:T(8,128)(2,1)S(1)}, u32[]{:S(2)}, u32[]{:S(2)}) collective-permute-start(bf16[3,128,256]{2,1,0:T(8,128)(2,1)S(1)} %get-tuple-element.43), channel_id=1, source_target_pairs={{0,4},{1,5},{2,6},{3,7},{4,0},{5,1},{6,2},{7,3},{8,12},{9,13},{10,... | collective-permute-start | bytes 589832 | tf_op jit(solution)/shard_map/ppermute | solution.py:327
  50.8 11.6 %collective-permute-start.7 = (bf16[3,128,256]{2,1,0:T(8,128)(2,1)S(1)}, bf16[3,128,256]{2,1,0:T(8,128)(2,1)S(1)}, u32[]{:S(2)}, u32[]{:S(2)}) collective-permute-start(bf16[3,128,256]{2,1,0:T(8,128)(2,1)S(1)} %get-tuple-element.41.refs_0_), channel_id=1, source_target_pairs={{0,1},{1,0},{2,3},{3,2},{4,5},{5,4},{6,7},{7,6},{8,9},{9,8},{10,11... | collective-permute-start | bytes 589832 | tf_op jit(solution)/shard_map/ppermute | solution.py:334
  55.9 6.5 %collective-permute-start.10 = (bf16[3,128,256]{2,1,0:T(8,128)(2,1)S(1)}, bf16[3,128,256]{2,1,0:T(8,128)(2,1)S(1)}, u32[]{:S(2)}, u32[]{:S(2)}) collective-permute-start(bf16[3,128,256]{2,1,0:T(8,128)(2,1)S(1)} %collective-permute-done.2.refs_3_), channel_id=1, source_target_pairs={{0,1},{1,0},{2,3},{3,2},{4,5},{5,4},{6,7},{7,6},{8,9},{9,8},{10,11... | collective-permute-start | bytes 589832 | tf_op jit(solution)/shard_map/ppermute | solution.py:334
  61.1 1.9 %collective-permute-start.11 = (bf16[3,128,256]{2,1,0:T(8,128)(2,1)S(1)}, bf16[3,128,256]{2,1,0:T(8,128)(2,1)S(1)}, u32[]{:S(2)}, u32[]{:S(2)}) collective-permute-start(bf16[3,128,256]{2,1,0:T(8,128)(2,1)S(1)} %collective-permute-done.3.refs_4_), channel_id=1, source_target_pairs={{0,1},{1,0},{2,3},{3,2},{4,5},{5,4},{6,7},{7,6},{8,9},{9,8},{10,11... | collective-permute-start | bytes 589832 | tf_op jit(solution)/shard_map/ppermute | solution.py:334
  61.9 1.4 %collective-permute-start.12 = (bf16[3,128,256]{2,1,0:T(8,128)(2,1)S(1)}, bf16[3,128,256]{2,1,0:T(8,128)(2,1)S(1)}, u32[]{:S(2)}, u32[]{:S(2)}) collective-permute-start(bf16[3,128,256]{2,1,0:T(8,128)(2,1)S(1)} %collective-permute-done.4.refs_5_), channel_id=1, source_target_pairs={{0,1},{1,0},{2,3},{3,2},{4,5},{5,4},{6,7},{7,6},{8,9},{9,8},{10,11... | collective-permute-start | bytes 589832 | tf_op jit(solution)/shard_map/ppermute | solution.py:334
  61.9 1.7 %collective-permute-start.13 = (bf16[3,128,256]{2,1,0:T(8,128)(2,1)S(1)}, bf16[3,128,256]{2,1,0:T(8,128)(2,1)S(1)}, u32[]{:S(2)}, u32[]{:S(2)}) collective-permute-start(bf16[3,128,256]{2,1,0:T(8,128)(2,1)S(1)} %collective-permute-done.5.refs_6_), channel_id=1, source_target_pairs={{0,1},{1,0},{2,3},{3,2},{4,5},{5,4},{6,7},{7,6},{8,9},{9,8},{10,11... | collective-permute-start | bytes 589832 | tf_op jit(solution)/shard_map/ppermute | solution.py:334
  62.4 1.5 %collective-permute-start.14 = (bf16[3,128,256]{2,1,0:T(8,128)(2,1)S(1)}, bf16[3,128,256]{2,1,0:T(8,128)(2,1)S(1)}, u32[]{:S(2)}, u32[]{:S(2)}) collective-permute-start(bf16[3,128,256]{2,1,0:T(8,128)(2,1)S(1)} %collective-permute-done.6.refs_7_), channel_id=1, source_target_pairs={{0,1},{1,0},{2,3},{3,2},{4,5},{5,4},{6,7},{7,6},{8,9},{9,8},{10,11... | collective-permute-start | bytes 589832 | tf_op jit(solution)/shard_map/ppermute | solution.py:334
  62.5 1.7 %collective-permute-start.8 = (bf16[3,128,256]{2,1,0:T(8,128)(2,1)S(1)}, bf16[3,128,256]{2,1,0:T(8,128)(2,1)S(1)}, u32[]{:S(2)}, u32[]{:S(2)}) collective-permute-start(bf16[3,128,256]{2,1,0:T(8,128)(2,1)S(1)} %collective-permute-done.refs_1_), channel_id=1, source_target_pairs={{0,1},{1,0},{2,3},{3,2},{4,5},{5,4},{6,7},{7,6},{8,9},{9,8},{10,11... | collective-permute-start | bytes 589832 | tf_op jit(solution)/shard_map/ppermute | solution.py:334
  62.9 1.5 %collective-permute-start.9 = (bf16[3,128,256]{2,1,0:T(8,128)(2,1)S(1)}, bf16[3,128,256]{2,1,0:T(8,128)(2,1)S(1)}, u32[]{:S(2)}, u32[]{:S(2)}) collective-permute-start(bf16[3,128,256]{2,1,0:T(8,128)(2,1)S(1)} %collective-permute-done.1.refs_2_), channel_id=1, source_target_pairs={{0,1},{1,0},{2,3},{3,2},{4,5},{5,4},{6,7},{7,6},{8,9},{9,8},{10,11... | collective-permute-start | bytes 589832 | tf_op jit(solution)/shard_map/ppermute | solution.py:334
  63.3 7.6 %collective-permute-start.40 = (bf16[1,128,256]{2,1,0:T(8,128)(2,1)S(1)}, bf16[1,128,256]{2,1,0:T(8,128)(2,1)S(1)}, u32[]{:S(2)}, u32[]{:S(2)}) collective-permute-start(bf16[1,128,256]{2,1,0:T(8,128)(2,1)S(1)} %collective-permute-done.32.refs_3_), channel_id=1, source_target_pairs={{0,1},{1,0},{2,3},{3,2},{4,5},{5,4},{6,7},{7,6},{8,9},{9,8},{10,11... | collective-permute-start | bytes 196616 | tf_op jit(solution)/shard_map/ppermute | solution.py:334
  63.6 7.6 %collective-permute-start.41 = (bf16[1,128,256]{2,1,0:T(8,128)(2,1)S(1)}, bf16[1,128,256]{2,1,0:T(8,128)(2,1)S(1)}, u32[]{:S(2)}, u32[]{:S(2)}) collective-permute-start(bf16[1,128,256]{2,1,0:T(8,128)(2,1)S(1)} %collective-permute-done.33.refs_4_), channel_id=1, source_target_pairs={{0,1},{1,0},{2,3},{3,2},{4,5},{5,4},{6,7},{7,6},{8,9},{9,8},{10,11... | collective-permute-start | bytes 196616 | tf_op jit(solution)/shard_map/ppermute | solution.py:334
  63.9 7.4 %collective-permute-start.42 = (bf16[1,128,256]{2,1,0:T(8,128)(2,1)S(1)}, bf16[1,128,256]{2,1,0:T(8,128)(2,1)S(1)}, u32[]{:S(2)}, u32[]{:S(2)}) collective-permute-start(bf16[1,128,256]{2,1,0:T(8,128)(2,1)S(1)} %collective-permute-done.34.refs_5_), channel_id=1, source_target_pairs={{0,1},{1,0},{2,3},{3,2},{4,5},{5,4},{6,7},{7,6},{8,9},{9,8},{10,11... | collective-permute-start | bytes 196616 | tf_op jit(solution)/shard_map/ppermute | solution.py:334
  64.2 9.5 %collective-permute-start.43 = (bf16[1,128,256]{2,1,0:T(8,128)(2,1)S(1)}, bf16[1,128,256]{2,1,0:T(8,128)(2,1)S(1)}, u32[]{:S(2)}, u32[]{:S(2)}) collective-permute-start(bf16[1,128,256]{2,1,0:T(8,128)(2,1)S(1)} %collective-permute-done.35.refs_6_), channel_id=1, source_target_pairs={{0,1},{1,0},{2,3},{3,2},{4,5},{5,4},{6,7},{7,6},{8,9},{9,8},{10,11... | collective-permute-start | bytes 196616 | tf_op jit(solution)/shard_map/ppermute | solution.py:334
  64.4 9.3 %collective-permute-start.44 = (bf16[1,128,256]{2,1,0:T(8,128)(2,1)S(1)}, bf16[1,128,256]{2,1,0:T(8,128)(2,1)S(1)}, u32[]{:S(2)}, u32[]{:S(2)}) collective-permute-start(bf16[1,128,256]{2,1,0:T(8,128)(2,1)S(1)} %collective-permute-done.36.refs_7_), channel_id=1, source_target_pairs={{0,1},{1,0},{2,3},{3,2},{4,5},{5,4},{6,7},{7,6},{8,9},{9,8},{10,11... | collective-permute-start | bytes 196616 | tf_op jit(solution)/shard_map/ppermute | solution.py:334
  70.9 5.1 %collective-permute-start.15 = (bf16[1,256,128]{2,1,0:T(8,128)(2,1)S(1)}, bf16[1,256,128]{2,1,0:T(8,128)(2,1)S(1)}, u32[]{:S(2)}, u32[]{:S(2)}) collective-permute-start(bf16[1,256,128]{2,1,0:T(8,128)(2,1)S(1)} %get-tuple-element.50), channel_id=1, source_target_pairs={{0,2},{1,3},{2,0},{3,1},{4,6},{5,7},{6,4},{7,5},{8,10},{9,11},{10,... | collective-permute-start | bytes 196616 | tf_op jit(solution)/shard_map/ppermute | solution.py:327
  71.2 6.0 %collective-permute-start.16 = (bf16[1,256,128]{2,1,0:T(8,128)(2,1)S(1)}, bf16[1,256,128]{2,1,0:T(8,128)(2,1)S(1)}, u32[]{:S(2)}, u32[]{:S(2)}) collective-permute-start(bf16[1,256,128]{2,1,0:T(8,128)(2,1)S(1)} %get-tuple-element.51), channel_id=1, source_target_pairs={{0,4},{1,5},{2,6},{3,7},{4,0},{5,1},{6,2},{7,3},{8,12},{9,13},{10,... | collective-permute-start | bytes 196616 | tf_op jit(solution)/shard_map/ppermute | solution.py:327
  71.2 7.1 %collective-permute-start.17 = (bf16[1,256,128]{2,1,0:T(8,128)(2,1)S(1)}, bf16[1,256,128]{2,1,0:T(8,128)(2,1)S(1)}, u32[]{:S(2)}, u32[]{:S(2)}) collective-permute-start(bf16[1,256,128]{2,1,0:T(8,128)(2,1)S(1)} %get-tuple-element.52), channel_id=1, source_target_pairs={{0,6},{1,7},{2,4},{3,5},{4,2},{5,3},{6,0},{7,1},{8,14},{9,15},{10,... | collective-permute-start | bytes 196616 | tf_op jit(solution)/shard_map/ppermute | solution.py:327
  73.6 6.9 %collective-permute-start.18 = (bf16[1,256,128]{2,1,0:T(8,128)(2,1)S(1)}, bf16[1,256,128]{2,1,0:T(8,128)(2,1)S(1)}, u32[]{:S(2)}, u32[]{:S(2)}) collective-permute-start(bf16[1,256,128]{2,1,0:T(8,128)(2,1)S(1)} %get-tuple-element.53), channel_id=1, source_target_pairs={{0,8},{1,9},{2,10},{3,11},{4,12},{5,13},{6,14},{7,15},{8,0},{9,1},... | collective-permute-start | bytes 196616 | tf_op jit(solution)/shard_map/ppermute | solution.py:327
  73.8 8.3 %collective-permute-start.19 = (bf16[1,256,128]{2,1,0:T(8,128)(2,1)S(1)}, bf16[1,256,128]{2,1,0:T(8,128)(2,1)S(1)}, u32[]{:S(2)}, u32[]{:S(2)}) collective-permute-start(bf16[1,256,128]{2,1,0:T(8,128)(2,1)S(1)} %get-tuple-element.54), channel_id=1, source_target_pairs={{0,10},{1,11},{2,8},{3,9},{4,14},{5,15},{6,12},{7,13},{8,2},{9,3},... | collective-permute-start | bytes 196616 | tf_op jit(solution)/shard_map/ppermute | solution.py:327
  76.0 10.3 %collective-permute-start.20 = (bf16[1,256,128]{2,1,0:T(8,128)(2,1)S(1)}, bf16[1,256,128]{2,1,0:T(8,128)(2,1)S(1)}, u32[]{:S(2)}, u32[]{:S(2)}) collective-permute-start(bf16[1,256,128]{2,1,0:T(8,128)(2,1)S(1)} %get-tuple-element.55), channel_id=1, source_target_pairs={{0,12},{1,13},{2,14},{3,15},{4,8},{5,9},{6,10},{7,11},{8,4},{9,5},... | collective-permute-start | bytes 196616 | tf_op jit(solution)/shard_map/ppermute | solution.py:327
  77.3 10.5 %collective-permute-start.21 = (bf16[1,256,128]{2,1,0:T(8,128)(2,1)S(1)}, bf16[1,256,128]{2,1,0:T(8,128)(2,1)S(1)}, u32[]{:S(2)}, u32[]{:S(2)}) collective-permute-start(bf16[1,256,128]{2,1,0:T(8,128)(2,1)S(1)} %get-tuple-element.56), channel_id=1, source_target_pairs={{0,14},{1,15},{2,12},{3,13},{4,10},{5,11},{6,8},{7,9},{8,6},{9,7},... | collective-permute-start | bytes 196616 | tf_op jit(solution)/shard_map/ppermute | solution.py:327
  78.4 9.9 %collective-permute-start.22 = (bf16[1,256,128]{2,1,0:T(8,128)(2,1)S(1)}, bf16[1,256,128]{2,1,0:T(8,128)(2,1)S(1)}, u32[]{:S(2)}, u32[]{:S(2)}) collective-permute-start(bf16[1,256,128]{2,1,0:T(8,128)(2,1)S(1)} %get-tuple-element.49.refs_0_), channel_id=1, source_target_pairs={{0,1},{1,0},{2,3},{3,2},{4,5},{5,4},{6,7},{7,6},{8,9},{9,8},{10,11... | collective-permute-start | bytes 196616 | tf_op jit(solution)/shard_map/ppermute | solution.py:334
  80.5 7.7 %collective-permute-start.23 = (bf16[1,256,128]{2,1,0:T(8,128)(2,1)S(1)}, bf16[1,256,128]{2,1,0:T(8,128)(2,1)S(1)}, u32[]{:S(2)}, u32[]{:S(2)}) collective-permute-start(bf16[1,256,128]{2,1,0:T(8,128)(2,1)S(1)} %collective-permute-done.15.refs_1_), channel_id=1, source_target_pairs={{0,1},{1,0},{2,3},{3,2},{4,5},{5,4},{6,7},{7,6},{8,9},{9,8},{10,11... | collective-permute-start | bytes 196616 | tf_op jit(solution)/shard_map/ppermute | solution.py:334
  82.1 6.7 %collective-permute-start.24 = (bf16[1,256,128]{2,1,0:T(8,128)(2,1)S(1)}, bf16[1,256,128]{2,1,0:T(8,128)(2,1)S(1)}, u32[]{:S(2)}, u32[]{:S(2)}) collective-permute-start(bf16[1,256,128]{2,1,0:T(8,128)(2,1)S(1)} %collective-permute-done.16.refs_2_), channel_id=1, source_target_pairs={{0,1},{1,0},{2,3},{3,2},{4,5},{5,4},{6,7},{7,6},{8,9},{9,8},{10,11... | collective-permute-start | bytes 196616 | tf_op jit(solution)/shard_map/ppermute | solution.py:334
  86.3 8.4 %collective-permute-start.25 = (bf16[1,256,128]{2,1,0:T(8,128)(2,1)S(1)}, bf16[1,256,128]{2,1,0:T(8,128)(2,1)S(1)}, u32[]{:S(2)}, u32[]{:S(2)}) collective-permute-start(bf16[1,256,128]{2,1,0:T(8,128)(2,1)S(1)} %collective-permute-done.17.refs_3_), channel_id=1, source_target_pairs={{0,1},{1,0},{2,3},{3,2},{4,5},{5,4},{6,7},{7,6},{8,9},{9,8},{10,11... | collective-permute-start | bytes 196616 | tf_op jit(solution)/shard_map/ppermute | solution.py:334
  87.7 8.2 %collective-permute-start.26 = (bf16[1,256,128]{2,1,0:T(8,128)(2,1)S(1)}, bf16[1,256,128]{2,1,0:T(8,128)(2,1)S(1)}, u32[]{:S(2)}, u32[]{:S(2)}) collective-permute-start(bf16[1,256,128]{2,1,0:T(8,128)(2,1)S(1)} %collective-permute-done.18.refs_4_), channel_id=1, source_target_pairs={{0,1},{1,0},{2,3},{3,2},{4,5},{5,4},{6,7},{7,6},{8,9},{9,8},{10,11... | collective-permute-start | bytes 196616 | tf_op jit(solution)/shard_map/ppermute | solution.py:334
  88.3 7.7 %collective-permute-start.27 = (bf16[1,256,128]{2,1,0:T(8,128)(2,1)S(1)}, bf16[1,256,128]{2,1,0:T(8,128)(2,1)S(1)}, u32[]{:S(2)}, u32[]{:S(2)}) collective-permute-start(bf16[1,256,128]{2,1,0:T(8,128)(2,1)S(1)} %collective-permute-done.19.refs_5_), channel_id=1, source_target_pairs={{0,1},{1,0},{2,3},{3,2},{4,5},{5,4},{6,7},{7,6},{8,9},{9,8},{10,11... | collective-permute-start | bytes 196616 | tf_op jit(solution)/shard_map/ppermute | solution.py:334
  88.3 9.2 %collective-permute-start.28 = (bf16[1,256,128]{2,1,0:T(8,128)(2,1)S(1)}, bf16[1,256,128]{2,1,0:T(8,128)(2,1)S(1)}, u32[]{:S(2)}, u32[]{:S(2)}) collective-permute-start(bf16[1,256,128]{2,1,0:T(8,128)(2,1)S(1)} %collective-permute-done.20.refs_6_), channel_id=1, source_target_pairs={{0,1},{1,0},{2,3},{3,2},{4,5},{5,4},{6,7},{7,6},{8,9},{9,8},{10,11... | collective-permute-start | bytes 196616 | tf_op jit(solution)/shard_map/ppermute | solution.py:334
  88.8 9.7 %collective-permute-start.29 = (bf16[1,256,128]{2,1,0:T(8,128)(2,1)S(1)}, bf16[1,256,128]{2,1,0:T(8,128)(2,1)S(1)}, u32[]{:S(2)}, u32[]{:S(2)}) collective-permute-start(bf16[1,256,128]{2,1,0:T(8,128)(2,1)S(1)} %collective-permute-done.21.refs_7_), channel_id=1, source_target_pairs={{0,1},{1,0},{2,3},{3,2},{4,5},{5,4},{6,7},{7,6},{8,9},{9,8},{10,11... | collective-permute-start | bytes 196616 | tf_op jit(solution)/shard_map/ppermute | solution.py:334
  94.7 6.1 %collective-permute-start.45 = (bf16[3,256,128]{2,1,0:T(8,128)(2,1)S(1)}, bf16[3,256,128]{2,1,0:T(8,128)(2,1)S(1)}, u32[]{:S(2)}, u32[]{:S(2)}) collective-permute-start(bf16[3,256,128]{2,1,0:T(8,128)(2,1)S(1)} %get-tuple-element.68), channel_id=1, source_target_pairs={{0,2},{1,3},{2,0},{3,1},{4,6},{5,7},{6,4},{7,5},{8,10},{9,11},{10,... | collective-permute-start | bytes 589832 | tf_op jit(solution)/shard_map/ppermute | solution.py:327
  96.0 10.1 %collective-permute-start.46 = (bf16[3,256,128]{2,1,0:T(8,128)(2,1)S(1)}, bf16[3,256,128]{2,1,0:T(8,128)(2,1)S(1)}, u32[]{:S(2)}, u32[]{:S(2)}) collective-permute-start(bf16[3,256,128]{2,1,0:T(8,128)(2,1)S(1)} %get-tuple-element.69), channel_id=1, source_target_pairs={{0,4},{1,5},{2,6},{3,7},{4,0},{5,1},{6,2},{7,3},{8,12},{9,13},{10,... | collective-permute-start | bytes 589832 | tf_op jit(solution)/shard_map/ppermute | solution.py:327
  96.0 15.2 %collective-permute-start.47 = (bf16[3,256,128]{2,1,0:T(8,128)(2,1)S(1)}, bf16[3,256,128]{2,1,0:T(8,128)(2,1)S(1)}, u32[]{:S(2)}, u32[]{:S(2)}) collective-permute-start(bf16[3,256,128]{2,1,0:T(8,128)(2,1)S(1)} %get-tuple-element.70), channel_id=1, source_target_pairs={{0,6},{1,7},{2,4},{3,5},{4,2},{5,3},{6,0},{7,1},{8,14},{9,15},{10,... | collective-permute-start | bytes 589832 | tf_op jit(solution)/shard_map/ppermute | solution.py:327
  97.5 14.9 %collective-permute-start.48 = (bf16[3,256,128]{2,1,0:T(8,128)(2,1)S(1)}, bf16[3,256,128]{2,1,0:T(8,128)(2,1)S(1)}, u32[]{:S(2)}, u32[]{:S(2)}) collective-permute-start(bf16[3,256,128]{2,1,0:T(8,128)(2,1)S(1)} %get-tuple-element.71), channel_id=1, source_target_pairs={{0,8},{1,9},{2,10},{3,11},{4,12},{5,13},{6,14},{7,15},{8,0},{9,1},... | collective-permute-start | bytes 589832 | tf_op jit(solution)/shard_map/ppermute | solution.py:327
  98.5 16.9 %collective-permute-start.49 = (bf16[3,256,128]{2,1,0:T(8,128)(2,1)S(1)}, bf16[3,256,128]{2,1,0:T(8,128)(2,1)S(1)}, u32[]{:S(2)}, u32[]{:S(2)}) collective-permute-start(bf16[3,256,128]{2,1,0:T(8,128)(2,1)S(1)} %get-tuple-element.72), channel_id=1, source_target_pairs={{0,10},{1,11},{2,8},{3,9},{4,14},{5,15},{6,12},{7,13},{8,2},{9,3},... | collective-permute-start | bytes 589832 | tf_op jit(solution)/shard_map/ppermute | solution.py:327
  100.8 27.2 %collective-permute-start.50 = (bf16[3,256,128]{2,1,0:T(8,128)(2,1)S(1)}, bf16[3,256,128]{2,1,0:T(8,128)(2,1)S(1)}, u32[]{:S(2)}, u32[]{:S(2)}) collective-permute-start(bf16[3,256,128]{2,1,0:T(8,128)(2,1)S(1)} %get-tuple-element.73), channel_id=1, source_target_pairs={{0,12},{1,13},{2,14},{3,15},{4,8},{5,9},{6,10},{7,11},{8,4},{9,5},... | collective-permute-start | bytes 589832 | tf_op jit(solution)/shard_map/ppermute | solution.py:327
  106.1 27.0 %collective-permute-start.51 = (bf16[3,256,128]{2,1,0:T(8,128)(2,1)S(1)}, bf16[3,256,128]{2,1,0:T(8,128)(2,1)S(1)}, u32[]{:S(2)}, u32[]{:S(2)}) collective-permute-start(bf16[3,256,128]{2,1,0:T(8,128)(2,1)S(1)} %get-tuple-element.74), channel_id=1, source_target_pairs={{0,14},{1,15},{2,12},{3,13},{4,10},{5,11},{6,8},{7,9},{8,6},{9,7},... | collective-permute-start | bytes 589832 | tf_op jit(solution)/shard_map/ppermute | solution.py:327
  111.1 23.9 %collective-permute-start.52 = (bf16[3,256,128]{2,1,0:T(8,128)(2,1)S(1)}, bf16[3,256,128]{2,1,0:T(8,128)(2,1)S(1)}, u32[]{:S(2)}, u32[]{:S(2)}) collective-permute-start(bf16[3,256,128]{2,1,0:T(8,128)(2,1)S(1)} %get-tuple-element.67.refs_0_), channel_id=1, source_target_pairs={{0,1},{1,0},{2,3},{3,2},{4,5},{5,4},{6,7},{7,6},{8,9},{9,8},{10,11... | collective-permute-start | bytes 589832 | tf_op jit(solution)/shard_map/ppermute | solution.py:334
  112.4 22.6 %collective-permute-start.53 = (bf16[3,256,128]{2,1,0:T(8,128)(2,1)S(1)}, bf16[3,256,128]{2,1,0:T(8,128)(2,1)S(1)}, u32[]{:S(2)}, u32[]{:S(2)}) collective-permute-start(bf16[3,256,128]{2,1,0:T(8,128)(2,1)S(1)} %collective-permute-done.45.refs_1_), channel_id=1, source_target_pairs={{0,1},{1,0},{2,3},{3,2},{4,5},{5,4},{6,7},{7,6},{8,9},{9,8},{10,11... | collective-permute-start | bytes 589832 | tf_op jit(solution)/shard_map/ppermute | solution.py:334
  115.4 20.1 %collective-permute-start.54 = (bf16[3,256,128]{2,1,0:T(8,128)(2,1)S(1)}, bf16[3,256,128]{2,1,0:T(8,128)(2,1)S(1)}, u32[]{:S(2)}, u32[]{:S(2)}) collective-permute-start(bf16[3,256,128]{2,1,0:T(8,128)(2,1)S(1)} %collective-permute-done.46.refs_2_), channel_id=1, source_target_pairs={{0,1},{1,0},{2,3},{3,2},{4,5},{5,4},{6,7},{7,6},{8,9},{9,8},{10,11... | collective-permute-start | bytes 589832 | tf_op jit(solution)/shard_map/ppermute | solution.py:334
  128.0 9.0 %collective-permute-start.55 = (bf16[3,256,128]{2,1,0:T(8,128)(2,1)S(1)}, bf16[3,256,128]{2,1,0:T(8,128)(2,1)S(1)}, u32[]{:S(2)}, u32[]{:S(2)}) collective-permute-start(bf16[3,256,128]{2,1,0:T(8,128)(2,1)S(1)} %collective-permute-done.47.refs_3_), channel_id=1, source_target_pairs={{0,1},{1,0},{2,3},{3,2},{4,5},{5,4},{6,7},{7,6},{8,9},{9,8},{10,11... | collective-permute-start | bytes 589832 | tf_op jit(solution)/shard_map/ppermute | solution.py:334
  133.1 4.0 %collective-permute-start.56 = (bf16[3,256,128]{2,1,0:T(8,128)(2,1)S(1)}, bf16[3,256,128]{2,1,0:T(8,128)(2,1)S(1)}, u32[]{:S(2)}, u32[]{:S(2)}) collective-permute-start(bf16[3,256,128]{2,1,0:T(8,128)(2,1)S(1)} %collective-permute-done.48.refs_4_), channel_id=1, source_target_pairs={{0,1},{1,0},{2,3},{3,2},{4,5},{5,4},{6,7},{7,6},{8,9},{9,8},{10,11... | collective-permute-start | bytes 589832 | tf_op jit(solution)/shard_map/ppermute | solution.py:334
  135.0 2.1 %collective-permute-start.57 = (bf16[3,256,128]{2,1,0:T(8,128)(2,1)S(1)}, bf16[3,256,128]{2,1,0:T(8,128)(2,1)S(1)}, u32[]{:S(2)}, u32[]{:S(2)}) collective-permute-start(bf16[3,256,128]{2,1,0:T(8,128)(2,1)S(1)} %collective-permute-done.49.refs_5_), channel_id=1, source_target_pairs={{0,1},{1,0},{2,3},{3,2},{4,5},{5,4},{6,7},{7,6},{8,9},{9,8},{10,11... | collective-permute-start | bytes 589832 | tf_op jit(solution)/shard_map/ppermute | solution.py:334
  135.0 2.1 %collective-permute-start.58 = (bf16[3,256,128]{2,1,0:T(8,128)(2,1)S(1)}, bf16[3,256,128]{2,1,0:T(8,128)(2,1)S(1)}, u32[]{:S(2)}, u32[]{:S(2)}) collective-permute-start(bf16[3,256,128]{2,1,0:T(8,128)(2,1)S(1)} %collective-permute-done.50.refs_6_), channel_id=1, source_target_pairs={{0,1},{1,0},{2,3},{3,2},{4,5},{5,4},{6,7},{7,6},{8,9},{9,8},{10,11... | collective-permute-start | bytes 589832 | tf_op jit(solution)/shard_map/ppermute | solution.py:334
  135.5 1.6 %collective-permute-start.59 = (bf16[3,256,128]{2,1,0:T(8,128)(2,1)S(1)}, bf16[3,256,128]{2,1,0:T(8,128)(2,1)S(1)}, u32[]{:S(2)}, u32[]{:S(2)}) collective-permute-start(bf16[3,256,128]{2,1,0:T(8,128)(2,1)S(1)} %collective-permute-done.51.refs_7_), channel_id=1, source_target_pairs={{0,1},{1,0},{2,3},{3,2},{4,5},{5,4},{6,7},{7,6},{8,9},{9,8},{10,11... | collective-permute-start | bytes 589832 | tf_op jit(solution)/shard_map/ppermute | solution.py:334
  (1 other events, 0.7 us)

commit v3 on v1

--- a/solution.py
+++ b/solution.py
@@ -121,7 +121,7 @@
     )(*operands)
 
 
-def body(queries, keys, values, cotangent, partner):
+def by_all_to_all(queries, keys, values, cotangent, partner):
     rows, width = queries.shape
     devices = lax.axis_size("ctx")
     heads = width // HEAD
@@ -175,6 +175,233 @@
     return tuple(unpack(exchange(jnp.stack(outs, axis=1))))
 
 
+def call(kernel, place, arrays, out_shape, scratch=(), flops=0, exps=0, in_place=0):
+    smem = pl.BlockSpec(memory_space=pltpu.SMEM)
+    vmem = pl.BlockSpec(memory_space=pltpu.VMEM)
+    moved = sum(a.size * a.dtype.itemsize for a in arrays)
+    moved += sum(a.size * a.dtype.itemsize for a in out_shape)
+    return pl.pallas_call(
+        kernel,
+        out_shape=out_shape,
+        in_specs=[smem] * len(place)
+        + [pl.BlockSpec(memory_space=pltpu.HBM)] * in_place
+        + [vmem] * (len(arrays) - in_place),
+        out_specs=[vmem] * len(out_shape),
+        scratch_shapes=list(scratch),
+        compiler_params=pltpu.CompilerParams(vmem_limit_bytes=40 * 1024 * 1024),
+        cost_estimate=pl.CostEstimate(flops=flops, bytes_accessed=moved, transcendentals=exps),
+    )(*place, *arrays)
+
+
+def pack(place, mine, theirs, chips):
+    count = len(mine)
+    rows, width = mine[0].shape
+
+    def kernel(where, *refs):
+        mine, theirs = refs[:count], refs[count : 2 * count]
+        outs, sems = refs[2 * count : -1], refs[-1]
+        here, there = halves(where, rows)
+        column = [
+            pl.ds(pl.multiple_of(((where[0] ^ k) * 2 + where[1]) * HEAD, HEAD), HEAD)
+            for k in range(chips)
+        ]
+        copies = [
+            pltpu.make_async_copy(mine[i].at[:, column[k]], outs[k].at[i, here], sems.at[k, i])
+            for k in range(chips)
+            for i in range(count)
+        ]
+        for copy in copies:
+            copy.start()
+        for k in range(chips):
+            for i in range(count):
+                outs[k][i, there] = theirs[i][:, column[k]]
+        for copy in copies:
+            copy.wait()
+
+    piece = jax.ShapeDtypeStruct((count, 2 * rows, HEAD), jnp.bfloat16)
+    return call(
+        kernel,
+        [place],
+        [*mine, *theirs],
+        [piece] * chips,
+        [pltpu.SemaphoreType.DMA((chips, count))],
+        in_place=count,
+    )
+
+
+def pair(place, keep, got):
+    chips, count, rows, _ = keep.shape
+
+    def kernel(where, keep, got, *outs):
+        core = where[1]
+        here = pl.ds(pl.multiple_of(core * HEAD, HEAD), HEAD)
+        there = pl.ds(pl.multiple_of((1 - core) * HEAD, HEAD), HEAD)
+        for k in range(chips):
+            for i in range(count):
+                outs[k][i, :, here] = keep[k, i]
+                outs[k][i, :, there] = got[k, i]
+
+    piece = jax.ShapeDtypeStruct((count, rows, 2 * HEAD), jnp.bfloat16)
+    return call(kernel, [place], [keep, got], [piece] * chips)
+
+
+def unpack(place, ks, pieces):
+    chips = len(pieces)
+    count, rows, span = pieces[0].shape
+
+    def kernel(where, *refs):
+        for n, k in enumerate(ks):
+            column = pl.ds(pl.multiple_of((where[0] ^ k) * span, span), span)
+            for i in range(count):
+                refs[chips + i][:, column] = refs[n][i]
+
+    out = jax.ShapeDtypeStruct((rows, chips * span), jnp.bfloat16)
+    return call(kernel, [place], pieces, [out] * count)
+
+
+def halves(where, rows):
+    core = where[1]
+    here = pl.ds(pl.multiple_of(core * rows, rows), rows)
+    there = pl.ds(pl.multiple_of((1 - core) * rows, rows), rows)
+    return here, there
+
+
+def forward(place, partner, ks, pieces):
+    chips = len(pieces)
+    size = pieces[0].shape[1]
+
+    def kernel(where, partner, *refs):
+        keep, give, held, weights = refs[chips:]
+        here, there = halves(where, size // 2)
+        for n, k in enumerate(ks):
+            held[where[0] ^ k, :3] = refs[n][...]
+        for k in range(chips):
+            b = where[0] ^ k
+            p = partner[b]
+            q = held[b, 0]
+            s = mm(q, held[b, 1], NT) * SCALE
+            t = mm(q, held[p, 1], NT) * SCALE
+            peak = jnp.max(jnp.maximum(s, t), axis=1, keepdims=True)
+            s, t = jnp.exp(s - peak), jnp.exp(t - peak)
+            inverse = 1.0 / jnp.sum(s + t, axis=1, keepdims=True)
+            s, t = s * inverse, t * inverse
+            weights[b, 0] = s
+            weights[b, 1] = t
+            attended = mm(s.astype(jnp.bfloat16), held[b, 2], NN)
+            attended += mm(t.astype(jnp.bfloat16), held[p, 2], NN)
+            held[b, 3] = attended.astype(jnp.bfloat16)
+            keep[k, 0] = held[b, 3, here]
+            give[k, 0] = held[b, 3, there]
+
+    half = jax.ShapeDtypeStruct((chips, 1, size // 2, HEAD), jnp.bfloat16)
+    out_shape = [
+        half,
+        half,
+        jax.ShapeDtypeStruct((chips, 4, size, HEAD), jnp.bfloat16),
+        jax.ShapeDtypeStruct((chips, 2, size, size), jnp.float32),
+    ]
+    flops = chips * 8 * size * size * HEAD
+    return call(kernel, [place, partner], pieces, out_shape, (), flops, chips * 2 * size * size)
+
+
+def backward(place, partner, ks, pieces, held, weights):
+    chips = len(pieces)
+    size = held.shape[2]
+
+    def kernel(where, partner, *refs):
+        held, weights, keep, give, grads, acc_k, acc_v, grad_q = refs[chips:]
+        here, there = halves(where, size // 2)
+        for n, k in enumerate(ks):
+            grads[where[0] ^ k] = refs[n][0]
+        acc_k[...] = jnp.zeros_like(acc_k)
+        acc_v[...] = jnp.zeros_like(acc_v)
+        for k in range(chips):
+            b = where[0] ^ k
+            q, do = held[b, 0], grads[b]
+            delta = jnp.sum(
+                do.astype(jnp.float32) * held[b, 3].astype(jnp.float32), axis=1, keepdims=True
+            )
+            total = None
+            for side, c in enumerate((b, partner[b])):
+                w = weights[b, side]
+                g = (w * (mm(do, held[c, 2], NT) - delta)).astype(jnp.bfloat16)
+                term = mm(g, held[c, 1], NN)
+                total = term if side == 0 else total + term
+                acc_k[c] += mm(g, q, TN)
+                acc_v[c] += mm(w.astype(jnp.bfloat16), do, TN)
+            grad_q[k] = (SCALE * total).astype(jnp.bfloat16)
+            keep[k, 0] = grad_q[k, here]
+            give[k, 0] = grad_q[k, there]
+        for k in range(chips):
+            b = where[0] ^ k
+            keep[k, 1] = (SCALE * acc_k[b, here]).astype(jnp.bfloat16)
+            give[k, 1] = (SCALE * acc_k[b, there]).astype(jnp.bfloat16)
+            keep[k, 2] = acc_v[b, here].astype(jnp.bfloat16)
+            give[k, 2] = acc_v[b, there].astype(jnp.bfloat16)
+
+    half = jax.ShapeDtypeStruct((chips, 3, size // 2, HEAD), jnp.bfloat16)
+    scratch = [
+        pltpu.VMEM((chips, size, HEAD), jnp.bfloat16),
+        pltpu.VMEM((chips, size, HEAD), jnp.float32),
+        pltpu.VMEM((chips, size, HEAD), jnp.float32),
+        pltpu.VMEM((chips, size, HEAD), jnp.bfloat16),
+    ]
+    flops = chips * 16 * size * size * HEAD
+    return call(
+        kernel, [place, partner], [*pieces, held, weights], [half, half], scratch, flops
+    )
+
+
+def after(array, *earlier):
+    return lax.optimization_barrier((array, *earlier))[0]
+
+
+def by_permutes(queries, keys, values, cotangent, partner):
+    devices = lax.axis_size("ctx")
+    chips = devices // 2
+    me = lax.axis_index("ctx")
+    place = jnp.stack([me // 2, me % 2]).astype(jnp.int32)
+
+    def hop(piece, distance):
+        return lax.ppermute(piece, "ctx", [(i, i ^ distance) for i in range(devices)])
+
+    far = list(range(chips // 2, chips))
+    near = list(range(1, chips // 2))
+    ks = [0, 1, *far[:-1], *near[1:-1], far[-1], near[-1]]
+
+    def to_chips(pieces, ks):
+        return {k: hop(pieces[k], 2 * k) for k in ks}
+
+    def in_order(arrived):
+        return [arrived[k] for k in ks]
+
+    ins = [queries, keys, values]
+    one = pack(place, ins, [hop(a, 1) for a in ins], chips)
+    two = pack(place, [cotangent], [hop(cotangent, 1)], chips)
+    first = {0: one[0]} | to_chips(one, far + near)
+    second = {0: two[0]} | to_chips(two, far + near)
+    keep, give, held, weights = forward(place, partner, ks, in_order(first))
+    three = pair(place, keep, hop(after(give, *(second[k] for k in far[:-1])), 1))
+    third = {0: three[0]} | to_chips(three, far)
+    second[0] = after(two[0], three[0])
+    keep, give = backward(place, partner, ks, in_order(second), held, weights)
+    third |= to_chips([after(p, keep) for p in three], near)
+    four = pair(place, keep, hop(after(give, *(third[k] for k in far[:-1])), 1))
+    fourth = {0: four[0]} | to_chips(four, far + near)
+    outs = unpack(place, ks, in_order(third)) + unpack(place, ks, in_order(fourth))
+    return tuple(outs)
+
+
+def body(queries, keys, values, cotangent, partner):
+    rows, width = queries.shape
+    devices = lax.axis_size("ctx")
+    blocks = partner.shape[0]
+    in_pairs = devices == 2 * blocks and devices * HEAD == width
+    if in_pairs and blocks & (blocks - 1) == 0:
+        return by_permutes(queries, keys, values, cotangent, partner)
+    return by_all_to_all(queries, keys, values, cotangent, partner)
+
+
 def solution(mesh):
     split = P(("dp", "ctx"), None)
     return jax.shard_map(

time: 137 us -> 124 us (0.905)
  blocking collectives: 54.1 us -> 0 us
  starting transfers between devices: 6.74 us -> 39.2 us
  waiting for transfers between devices: 46 us -> 61.1 us
  local copies, waits for them, and re-layouts: 17.6 us -> 4.17 us
  Pallas kernels: 9.02 us -> 17.9 us
  other arithmetic: 1.46 us -> 0.07 us
    ppermute x0 -> x34, waiting for transfers between devices: none -> 61.1 us  [hop(): lax.ppermute(piece, 'ctx', [(i, i ^ distance) for i in range(devices)])]
    all_to_all x1 -> x0, blocking collectives: 54.1 us -> none  [body(): return tuple(unpack(exchange(jnp.stack(outs, axis=1))))]
    all_to_all x1 -> x0, waiting for transfers between devices: 46 us -> none  [body(): local = exchange(pack([queries, keys, values, cotangent]))]
    ppermute x0 -> x34, starting transfers between devices: none -> 39.2 us  [hop(): lax.ppermute(piece, 'ctx', [(i, i ^ distance) for i in range(devices)])]
    pallas_call x1 -> x8, Pallas kernels: 9.02 us -> 17.9 us  [call(): pl.pallas_call(kernel, out_shape=out_shape, in_specs=[smem] * len(place)...]
    all_to_all x1 -> x0, starting transfers between devices: 6.74 us -> none  [body(): local = exchange(pack([queries, keys, values, cotangent]))]
    unnamed x14 -> x10, local copies, waits for them, and re-layouts: 10.8 us -> 4.17 us
    all_to_all x1 -> x0, local copies, waits for them, and re-layouts: 3.04 us -> none  [body(): return tuple(unpack(exchange(jnp.stack(outs, axis=1))))]
  transfers between devices with their start and end apart: 1 -> 34, of which waited for: 1 -> 13; matrix products, arithmetic and copies ran while one was open for 0% -> 0% of each run, Pallas kernels for 0% -> 12%
where the time goes in v3:
time: 124 us; the launch traced here: 123 us
  waiting for transfers between devices  61.1 us (49%)
  starting transfers between devices  39.2 us (32%)
  Pallas kernels  17.9 us (14%)
  local copies, waits for them, and re-layouts  4.17 us (3%)
    ppermute x34, waiting for transfers between devices, hop(): lax.ppermute(piece, 'ctx', [(i, i ^ distance) for i in range(devices)])  61.1 us
    ppermute x34, starting transfers between devices, hop(): lax.ppermute(piece, 'ctx', [(i, i ^ distance) for i in range(devices)])  39.2 us
    pallas_call x8, Pallas kernels, call(): pl.pallas_call(kernel, out_shape=out_shape, in_specs=[smem] * len(place)...  17.9 us
    unnamed x10, local copies, waits for them, and re-layouts  4.17 us
  transfers between devices with their start and end apart: 34, of which 13 were waited for; matrix products, arithmetic and copies ran while one was open for 0% of the time, Pallas kernels for 12%

profile of v3, /device:TPU:9, one launch (start us, length us, event | category | flops | bytes accessed | tf_op | source)
XLA Modules:
  0.0 123.2 jit_solution(11139528855368012486)
XLA Ops:
  0.6 0.7 collective-permute-start
  1.4 0.1 collective-permute-start.1
  1.5 0.4 collective-permute-start.2
  1.9 0.1 collective-permute-start.10
  2.0 0.1 pad_add_fusion.where
  2.0 1.1 collective-permute-done.refs_3_
  3.1 0.7 collective-permute-done.1.refs_4_
  3.9 0.7 collective-permute-done.2.refs_5_
  4.6 1.0 copy-done.1
  5.7 1.0 copy-done.2
  6.7 1.0 copy-done.3
  7.8 1.2 %shard_map.84 = (bf16[3,256,128]{2,1,0:T(8,128)(2,1)S(1)}, bf16[3,256,128]{2,1,0:T(8,128)(2,1)S(1)}, bf16[3,256,128]{2,1,0:T(8,128)(2,1)S(1)}, bf16[3,256,128]{2...) custom-call(s32[2]{0:T(128)S(1)} %pad_add_fusion.where, ...), custom_call_target="tpu_custom_call" | custom-call | bytes 4718592 | tf_op jit(solution)/shard_map/pallas_call | solution.py:183
  9.0 1.3 %collective-permute-start.3 = (bf16[3,256,128]{2,1,0:T(8,128)(2,1)S(1)}, bf16[3,256,128]{2,1,0:T(8,128)(2,1)S(1)}, u32[]{:S(2)}, u32[]{:S(2)}) collective-permute-start(bf16[3,256,128]{2,1,0:T(8,128)(2,1)S(1)} %get-tuple-element.52), channel_id=1, source_target_pairs={{0,2},{1,3},{2,0},{3,1},{4,6},{5,7},{6,4},{7,5},{8,10},{9,11},{10,... | collective-permute-start | bytes 589832 | tf_op jit(solution)/shard_map/ppermute | solution.py:366
  10.3 2.3 %collective-permute-start.4 = (bf16[3,256,128]{2,1,0:T(8,128)(2,1)S(1)}, bf16[3,256,128]{2,1,0:T(8,128)(2,1)S(1)}, u32[]{:S(2)}, u32[]{:S(2)}) collective-permute-start(bf16[3,256,128]{2,1,0:T(8,128)(2,1)S(1)} %get-tuple-element.53), channel_id=1, source_target_pairs={{0,8},{1,9},{2,10},{3,11},{4,12},{5,13},{6,14},{7,15},{8,0},{9,1},... | collective-permute-start | bytes 589832 | tf_op jit(solution)/shard_map/ppermute | solution.py:366
  12.6 1.3 %collective-permute-start.6 = (bf16[3,256,128]{2,1,0:T(8,128)(2,1)S(1)}, bf16[3,256,128]{2,1,0:T(8,128)(2,1)S(1)}, u32[]{:S(2)}, u32[]{:S(2)}) collective-permute-start(bf16[3,256,128]{2,1,0:T(8,128)(2,1)S(1)} %get-tuple-element.55), channel_id=1, source_target_pairs={{0,12},{1,13},{2,14},{3,15},{4,8},{5,9},{6,10},{7,11},{8,4},{9,5},... | collective-permute-start | bytes 589832 | tf_op jit(solution)/shard_map/ppermute | solution.py:366
  13.9 0.0 collective-permute-done.10.refs_1_
  13.9 2.2 %collective-permute-start.7 = (bf16[3,256,128]{2,1,0:T(8,128)(2,1)S(1)}, bf16[3,256,128]{2,1,0:T(8,128)(2,1)S(1)}, u32[]{:S(2)}, u32[]{:S(2)}) collective-permute-start(bf16[3,256,128]{2,1,0:T(8,128)(2,1)S(1)} %get-tuple-element.56), channel_id=1, source_target_pairs={{0,4},{1,5},{2,6},{3,7},{4,0},{5,1},{6,2},{7,3},{8,12},{9,13},{10,... | collective-permute-start | bytes 589832 | tf_op jit(solution)/shard_map/ppermute | solution.py:366
  16.1 1.3 %collective-permute-start.8 = (bf16[3,256,128]{2,1,0:T(8,128)(2,1)S(1)}, bf16[3,256,128]{2,1,0:T(8,128)(2,1)S(1)}, u32[]{:S(2)}, u32[]{:S(2)}) collective-permute-start(bf16[3,256,128]{2,1,0:T(8,128)(2,1)S(1)} %get-tuple-element.57), channel_id=1, source_target_pairs={{0,14},{1,15},{2,12},{3,13},{4,10},{5,11},{6,8},{7,9},{8,6},{9,7},... | collective-permute-start | bytes 589832 | tf_op jit(solution)/shard_map/ppermute | solution.py:366
  17.4 12.8 %collective-permute-done.4.refs_2_ = bf16[3,256,128]{2,1,0:T(8,128)(2,1)S(1)} collective-permute-done((bf16[3,256,128]{2,1,0:T(8,128)(2,1)S(1)}, bf16[3,256,128]{2,1,0:T(8,128)(2,1)S(1)}, u32[]{:S(2)}, u32[]{:S(2)}) %collective-permute-start.4) | collective-permute-done | bytes 196640 | tf_op jit(solution)/shard_map/ppermute | solution.py:366
  30.3 0.0 collective-permute-start.9
  30.3 1.0 copy-done
  31.3 0.8 shard_map.86
  32.1 6.1 %collective-permute-done.5.refs_3_ = bf16[3,256,128]{2,1,0:T(8,128)(2,1)S(1)} collective-permute-done((bf16[3,256,128]{2,1,0:T(8,128)(2,1)S(1)}, bf16[3,256,128]{2,1,0:T(8,128)(2,1)S(1)}, u32[]{:S(2)}, u32[]{:S(2)}) %collective-permute-start.5) | collective-permute-done | bytes 196640 | tf_op jit(solution)/shard_map/ppermute | solution.py:366
  38.2 3.0 %collective-permute-start.11 = (bf16[1,256,128]{2,1,0:T(8,128)(2,1)S(1)}, bf16[1,256,128]{2,1,0:T(8,128)(2,1)S(1)}, u32[]{:S(2)}, u32[]{:S(2)}) collective-permute-start(bf16[1,256,128]{2,1,0:T(8,128)(2,1)S(1)} %get-tuple-element.61), channel_id=1, source_target_pairs={{0,8},{1,9},{2,10},{3,11},{4,12},{5,13},{6,14},{7,15},{8,0},{9,1},... | collective-permute-start | bytes 196616 | tf_op jit(solution)/shard_map/ppermute | solution.py:366
  41.3 2.6 %collective-permute-done.6.refs_4_ = bf16[3,256,128]{2,1,0:T(8,128)(2,1)S(1)} collective-permute-done((bf16[3,256,128]{2,1,0:T(8,128)(2,1)S(1)}, bf16[3,256,128]{2,1,0:T(8,128)(2,1)S(1)}, u32[]{:S(2)}, u32[]{:S(2)}) %collective-permute-start.6) | collective-permute-done | bytes 196640 | tf_op jit(solution)/shard_map/ppermute | solution.py:366
  43.9 0.0 collective-permute-start.12
  43.9 2.2 %collective-permute-start.13 = (bf16[1,256,128]{2,1,0:T(8,128)(2,1)S(1)}, bf16[1,256,128]{2,1,0:T(8,128)(2,1)S(1)}, u32[]{:S(2)}, u32[]{:S(2)}) collective-permute-start(bf16[1,256,128]{2,1,0:T(8,128)(2,1)S(1)} %get-tuple-element.63), channel_id=1, source_target_pairs={{0,12},{1,13},{2,14},{3,15},{4,8},{5,9},{6,10},{7,11},{8,4},{9,5},... | collective-permute-start | bytes 196616 | tf_op jit(solution)/shard_map/ppermute | solution.py:366
  46.1 4.7 %collective-permute-done.8.refs_6_ = bf16[3,256,128]{2,1,0:T(8,128)(2,1)S(1)} collective-permute-done((bf16[3,256,128]{2,1,0:T(8,128)(2,1)S(1)}, bf16[3,256,128]{2,1,0:T(8,128)(2,1)S(1)}, u32[]{:S(2)}, u32[]{:S(2)}) %collective-permute-start.8) | collective-permute-done | bytes 196640 | tf_op jit(solution)/shard_map/ppermute | solution.py:366
  50.7 5.4 %shard_map.85 = (bf16[8,1,128,128]{3,2,1,0:T(8,128)(2,1)S(1)}, bf16[8,1,128,128]{3,2,1,0:T(8,128)(2,1)S(1)}, bf16[8,4,256,128]{3,2,1,0:T(8,128)(2,1)S(1)}, f32[8,2,256,256]{3,2,1,0:T(8,128)S(1)}) custom-call(s32[2]{0:T(128)S(1)} %pad_add_fusion.where, s32[8]{0:T(128)S(1)} %copy-done.4, bf16[3,256,128]{2,1,0:T(8,128)(2,1)S(1)} %get-tuple-element.51.refs_0_, ...), custom_call_target="tpu_custom_call" | custom-call | flops 536870912 | bytes 8388608 | tf_op jit(solution)/shard_map/pallas_call | solution.py:183
  56.1 0.0 collective-permute-done.11.refs_2_
  56.2 0.0 collective-permute-done.13.refs_4_
  56.2 0.8 collective-permute-start.14
  57.0 0.7 collective-permute-start.15
  57.7 0.0 collective-permute-start.16
  57.7 2.4 %collective-permute-start.17 = (bf16[1,256,128]{2,1,0:T(8,128)(2,1)S(1)}, bf16[1,256,128]{2,1,0:T(8,128)(2,1)S(1)}, u32[]{:S(2)}, u32[]{:S(2)}) collective-permute-start(bf16[1,256,128]{2,1,0:T(8,128)(2,1)S(1)} %get-tuple-element.71), channel_id=1, source_target_pairs={{0,14},{1,15},{2,12},{3,13},{4,10},{5,11},{6,8},{7,9},{8,6},{9,7},... | collective-permute-start | bytes 196616 | tf_op jit(solution)/shard_map/ppermute | solution.py:366
  60.1 3.6 %collective-permute-start.18 = (bf16[1,256,128]{2,1,0:T(8,128)(2,1)S(1)}, bf16[1,256,128]{2,1,0:T(8,128)(2,1)S(1)}, u32[]{:S(2)}, u32[]{:S(2)}) collective-permute-start(bf16[1,256,128]{2,1,0:T(8,128)(2,1)S(1)} %get-tuple-element.72), channel_id=1, source_target_pairs={{0,6},{1,7},{2,4},{3,5},{4,2},{5,3},{6,0},{7,1},{8,14},{9,15},{10,... | collective-permute-start | bytes 196616 | tf_op jit(solution)/shard_map/ppermute | solution.py:366
  63.6 0.0 collective-permute-done.14.got
  63.6 0.6 shard_map.87
  64.3 0.1 collective-permute-start.20
  64.3 0.0 collective-permute-done.15.refs_1_
  64.4 2.0 %collective-permute-start.21 = (bf16[1,128,256]{2,1,0:T(8,128)(2,1)S(1)}, bf16[1,128,256]{2,1,0:T(8,128)(2,1)S(1)}, u32[]{:S(2)}, u32[]{:S(2)}) collective-permute-start(bf16[1,128,256]{2,1,0:T(8,128)(2,1)S(1)} %get-tuple-element.78), channel_id=1, source_target_pairs={{0,10},{1,11},{2,8},{3,9},{4,14},{5,15},{6,12},{7,13},{8,2},{9,3},... | collective-permute-start | bytes 196616 | tf_op jit(solution)/shard_map/ppermute | solution.py:366
  66.4 0.0 collective-permute-done.16.refs_5_
  66.4 0.0 collective-permute-start.22
  66.4 5.8 %shard_map.88 = (bf16[8,3,128,128]{3,2,1,0:T(8,128)(2,1)S(1)}, bf16[8,3,128,128]{3,2,1,0:T(8,128)(2,1)S(1)}) custom-call(s32[2]{0:T(128)S(1)} %pad_add_fusion.where, s32[8]{0:T(128)S(1)} %copy-done.4, bf16[1,256,128]{2,1,0:T(8,128)(2,1)S(1)} %get-tuple-element.68.refs_0_, bf16[1,256,128]{2,1,0:T(8,128)(2,1)S(1)} %collective-permute-done.15.refs_1_, ...), custom_call_target="tpu_custom_call" | custom-call | flops 1073741824 | bytes 8388608 | tf_op jit(solution)/shard_map/pallas_call | solution.py:183
  72.2 1.7 %collective-permute-done.22.refs_4_ = bf16[1,128,256]{2,1,0:T(8,128)(2,1)S(1)} collective-permute-done((bf16[1,128,256]{2,1,0:T(8,128)(2,1)S(1)}, bf16[1,128,256]{2,1,0:T(8,128)(2,1)S(1)}, u32[]{:S(2)}, u32[]{:S(2)}) %collective-permute-start.22) | collective-permute-done | bytes 65568 | tf_op jit(solution)/shard_map/ppermute | solution.py:366
  73.9 1.4 %collective-permute-start.26 = (bf16[8,3,128,128]{3,2,1,0:T(8,128)(2,1)S(1)}, bf16[8,3,128,128]{3,2,1,0:T(8,128)(2,1)S(1)}, u32[]{:S(2)}, u32[]{:S(2)}) collective-permute-start(bf16[8,3,128,128]{3,2,1,0:T(8,128)(2,1)S(1)} %get-tuple-element.86), channel_id=1, source_target_pairs={{0,1},{1,0},{2,3},{3,2},{4,5},{5,4},{6,7},{7,6},{8,9},{9,8},{10,11... | collective-permute-start | bytes 2359304 | tf_op jit(solution)/shard_map/ppermute | solution.py:366
  75.3 1.9 %collective-permute-done.26.got = bf16[8,3,128,128]{3,2,1,0:T(8,128)(2,1)S(1)} collective-permute-done((bf16[8,3,128,128]{3,2,1,0:T(8,128)(2,1)S(1)}, bf16[8,3,128,128]{3,2,1,0:T(8,128)(2,1)S(1)}, u32[]{:S(2)}, u32[]{:S(2)}) %collective-permute-start.26) | collective-permute-done | bytes 786464 | tf_op jit(solution)/shard_map/ppermute | solution.py:366
  77.2 0.8 shard_map.90
  78.1 0.8 collective-permute-start.27
  78.8 1.1 collective-permute-start.28
  79.9 0.8 collective-permute-start.19
  80.7 0.6 collective-permute-start.23
  81.3 1.2 %collective-permute-start.25 = (bf16[1,128,256]{2,1,0:T(8,128)(2,1)S(1)}, bf16[1,128,256]{2,1,0:T(8,128)(2,1)S(1)}, u32[]{:S(2)}, u32[]{:S(2)}) collective-permute-start(bf16[1,128,256]{2,1,0:T(8,128)(2,1)S(1)} %get-tuple-element.84), channel_id=1, source_target_pairs={{0,6},{1,7},{2,4},{3,5},{4,2},{5,3},{6,0},{7,1},{8,14},{9,15},{10,... | collective-permute-start | bytes 196616 | tf_op jit(solution)/shard_map/ppermute | solution.py:366
  82.6 3.1 %collective-permute-done.19.refs_1_ = bf16[1,128,256]{2,1,0:T(8,128)(2,1)S(1)} collective-permute-done((bf16[1,128,256]{2,1,0:T(8,128)(2,1)S(1)}, bf16[1,128,256]{2,1,0:T(8,128)(2,1)S(1)}, u32[]{:S(2)}, u32[]{:S(2)}) %collective-permute-start.19) | collective-permute-done | bytes 65568 | tf_op jit(solution)/shard_map/ppermute | solution.py:366
  85.6 1.7 %collective-permute-start.24 = (bf16[1,128,256]{2,1,0:T(8,128)(2,1)S(1)}, bf16[1,128,256]{2,1,0:T(8,128)(2,1)S(1)}, u32[]{:S(2)}, u32[]{:S(2)}) collective-permute-start(bf16[1,128,256]{2,1,0:T(8,128)(2,1)S(1)} %get-tuple-element.82), channel_id=1, source_target_pairs={{0,14},{1,15},{2,12},{3,13},{4,10},{5,11},{6,8},{7,9},{8,6},{9,7},... | collective-permute-start | bytes 196616 | tf_op jit(solution)/shard_map/ppermute | solution.py:366
  87.3 2.9 %collective-permute-start.29 = (bf16[3,128,256]{2,1,0:T(8,128)(2,1)S(1)}, bf16[3,128,256]{2,1,0:T(8,128)(2,1)S(1)}, u32[]{:S(2)}, u32[]{:S(2)}) collective-permute-start(bf16[3,128,256]{2,1,0:T(8,128)(2,1)S(1)} %get-tuple-element.90), channel_id=1, source_target_pairs={{0,10},{1,11},{2,8},{3,9},{4,14},{5,15},{6,12},{7,13},{8,2},{9,3},... | collective-permute-start | bytes 589832 | tf_op jit(solution)/shard_map/ppermute | solution.py:366
  90.2 0.3 collective-permute-start.30
  90.6 11.3 %collective-permute-done.24.refs_6_ = bf16[1,128,256]{2,1,0:T(8,128)(2,1)S(1)} collective-permute-done((bf16[1,128,256]{2,1,0:T(8,128)(2,1)S(1)}, bf16[1,128,256]{2,1,0:T(8,128)(2,1)S(1)}, u32[]{:S(2)}, u32[]{:S(2)}) %collective-permute-start.24) | collective-permute-done | bytes 65568 | tf_op jit(solution)/shard_map/ppermute | solution.py:366
  101.9 0.0 collective-permute-start.32
  101.9 3.7 %collective-permute-start.33 = (bf16[3,128,256]{2,1,0:T(8,128)(2,1)S(1)}, bf16[3,128,256]{2,1,0:T(8,128)(2,1)S(1)}, u32[]{:S(2)}, u32[]{:S(2)}) collective-permute-start(bf16[3,128,256]{2,1,0:T(8,128)(2,1)S(1)} %get-tuple-element.94), channel_id=1, source_target_pairs={{0,6},{1,7},{2,4},{3,5},{4,2},{5,3},{6,0},{7,1},{8,14},{9,15},{10,... | collective-permute-start | bytes 589832 | tf_op jit(solution)/shard_map/ppermute | solution.py:366
  105.6 1.4 %shard_map.89 = bf16[128,2048]{1,0:T(8,128)(2,1)} custom-call(s32[2]{0:T(128)S(1)} %pad_add_fusion.where, bf16[1,128,256]{2,1,0:T(8,128)(2,1)S(1)} %get-tuple-element.65.refs_0_, bf16[1,128,256]{2,1,0:T(8,128)(2,1)S(1)} %collective-permute-done.19.refs_1_, bf16[1,128,256]{2,1,0:T(8,128)(2,1)S(1)} %collective-permute-done.20.refs_2_, ...), custom_call_target="tpu_custom_call" | custom-call | bytes 1048576 | tf_op jit(solution)/shard_map/pallas_call | solution.py:183
  107.0 7.6 %collective-permute-done.30.refs_4_ = bf16[3,128,256]{2,1,0:T(8,128)(2,1)S(1)} collective-permute-done((bf16[3,128,256]{2,1,0:T(8,128)(2,1)S(1)}, bf16[3,128,256]{2,1,0:T(8,128)(2,1)S(1)}, u32[]{:S(2)}, u32[]{:S(2)}) %collective-permute-start.30) | collective-permute-done | bytes 196640 | tf_op jit(solution)/shard_map/ppermute | solution.py:366
  114.7 6.7 %collective-permute-done.32.refs_6_ = bf16[3,128,256]{2,1,0:T(8,128)(2,1)S(1)} collective-permute-done((bf16[3,128,256]{2,1,0:T(8,128)(2,1)S(1)}, bf16[3,128,256]{2,1,0:T(8,128)(2,1)S(1)}, u32[]{:S(2)}, u32[]{:S(2)}) %collective-permute-start.32) | collective-permute-done | bytes 196640 | tf_op jit(solution)/shard_map/ppermute | solution.py:366
  121.4 1.9 %shard_map.91 = (bf16[128,2048]{1,0:T(8,128)(2,1)}, bf16[128,2048]{1,0:T(8,128)(2,1)}, bf16[128,2048]{1,0:T(8,128)(2,1)}) custom-call(s32[2]{0:T(128)S(1)} %pad_add_fusion.where, bf16[3,128,256]{2,1,0:T(8,128)(2,1)S(1)} %get-tuple-element.87.refs_0_, bf16[3,128,256]{2,1,0:T(8,128)(2,1)S(1)} %collective-permute-done.27.refs_1_, ...), custom_call_target="tpu_custom_call" | custom-call | bytes 3145728 | tf_op jit(solution)/shard_map/pallas_call | solution.py:183
  (23 shorter events, 0.1 us)
Async XLA Ops:
  0.6 50.1 %copy-start.4 = (s32[8]{0:T(128)S(1)}, s32[8]{0:T(128)}, u32[]{:S(2)}) copy-start(s32[8]{0:T(128)} %partner.3) | copy-start | bytes 100
  0.6 2.5 %collective-permute-start = (bf16[128,2048]{1,0:T(8,128)(2,1)}, bf16[128,2048]{1,0:T(8,128)(2,1)S(1)}, u32[]{:S(2)}, u32[]{:S(2)}) collective-permute-start(bf16[128,2048]{1,0:T(8,128)(2,1)} %refs_0_.2), channel_id=1, source_target_pairs={{0,1},{1,0},{2,3},{3,2},{4,5},{5,4},{6,7},{7,6},{8,9},{9,8},{10,11... | collective-permute-start | bytes 1572872 | tf_op jit(solution)/shard_map/ppermute | solution.py:366
  1.4 2.5 %collective-permute-start.1 = (bf16[128,2048]{1,0:T(8,128)(2,1)}, bf16[128,2048]{1,0:T(8,128)(2,1)S(1)}, u32[]{:S(2)}, u32[]{:S(2)}) collective-permute-start(bf16[128,2048]{1,0:T(8,128)(2,1)} %refs_1_.1), channel_id=1, source_target_pairs={{0,1},{1,0},{2,3},{3,2},{4,5},{5,4},{6,7},{7,6},{8,9},{9,8},{10,11... | collective-permute-start | bytes 1572872 | tf_op jit(solution)/shard_map/ppermute | solution.py:366
  1.5 3.2 %collective-permute-start.2 = (bf16[128,2048]{1,0:T(8,128)(2,1)}, bf16[128,2048]{1,0:T(8,128)(2,1)S(1)}, u32[]{:S(2)}, u32[]{:S(2)}) collective-permute-start(bf16[128,2048]{1,0:T(8,128)(2,1)} %refs_2_.1), channel_id=1, source_target_pairs={{0,1},{1,0},{2,3},{3,2},{4,5},{5,4},{6,7},{7,6},{8,9},{9,8},{10,11... | collective-permute-start | bytes 1572872 | tf_op jit(solution)/shard_map/ppermute | solution.py:366
  1.9 12.0 %collective-permute-start.10 = (bf16[128,2048]{1,0:T(8,128)(2,1)}, bf16[128,2048]{1,0:T(8,128)(2,1)S(1)}, u32[]{:S(2)}, u32[]{:S(2)}) collective-permute-start(bf16[128,2048]{1,0:T(8,128)(2,1)} %refs_0_.3), channel_id=1, source_target_pairs={{0,1},{1,0},{2,3},{3,2},{4,5},{5,4},{6,7},{7,6},{8,9},{9,8},{10,11... | collective-permute-start | bytes 1572872 | tf_op jit(solution)/shard_map/ppermute | solution.py:366
  4.6 1.0 copy-start.1
  5.7 1.0 copy-start.2
  6.7 1.0 copy-start.3
  9.0 7.1 %collective-permute-start.3 = (bf16[3,256,128]{2,1,0:T(8,128)(2,1)S(1)}, bf16[3,256,128]{2,1,0:T(8,128)(2,1)S(1)}, u32[]{:S(2)}, u32[]{:S(2)}) collective-permute-start(bf16[3,256,128]{2,1,0:T(8,128)(2,1)S(1)} %get-tuple-element.52), channel_id=1, source_target_pairs={{0,2},{1,3},{2,0},{3,1},{4,6},{5,7},{6,4},{7,5},{8,10},{9,11},{10,... | collective-permute-start | bytes 589832 | tf_op jit(solution)/shard_map/ppermute | solution.py:366
  10.3 19.9 %collective-permute-start.4 = (bf16[3,256,128]{2,1,0:T(8,128)(2,1)S(1)}, bf16[3,256,128]{2,1,0:T(8,128)(2,1)S(1)}, u32[]{:S(2)}, u32[]{:S(2)}) collective-permute-start(bf16[3,256,128]{2,1,0:T(8,128)(2,1)S(1)} %get-tuple-element.53), channel_id=1, source_target_pairs={{0,8},{1,9},{2,10},{3,11},{4,12},{5,13},{6,14},{7,15},{8,0},{9,1},... | collective-permute-start | bytes 589832 | tf_op jit(solution)/shard_map/ppermute | solution.py:366
  12.6 25.6 %collective-permute-start.5 = (bf16[3,256,128]{2,1,0:T(8,128)(2,1)S(1)}, bf16[3,256,128]{2,1,0:T(8,128)(2,1)S(1)}, u32[]{:S(2)}, u32[]{:S(2)}) collective-permute-start(bf16[3,256,128]{2,1,0:T(8,128)(2,1)S(1)} %get-tuple-element.54), channel_id=1, source_target_pairs={{0,10},{1,11},{2,8},{3,9},{4,14},{5,15},{6,12},{7,13},{8,2},{9,3},... | collective-permute-start | bytes 589832 | tf_op jit(solution)/shard_map/ppermute | solution.py:366
  12.6 31.2 %collective-permute-start.6 = (bf16[3,256,128]{2,1,0:T(8,128)(2,1)S(1)}, bf16[3,256,128]{2,1,0:T(8,128)(2,1)S(1)}, u32[]{:S(2)}, u32[]{:S(2)}) collective-permute-start(bf16[3,256,128]{2,1,0:T(8,128)(2,1)S(1)} %get-tuple-element.55), channel_id=1, source_target_pairs={{0,12},{1,13},{2,14},{3,15},{4,8},{5,9},{6,10},{7,11},{8,4},{9,5},... | collective-permute-start | bytes 589832 | tf_op jit(solution)/shard_map/ppermute | solution.py:366
  13.9 29.9 %collective-permute-start.7 = (bf16[3,256,128]{2,1,0:T(8,128)(2,1)S(1)}, bf16[3,256,128]{2,1,0:T(8,128)(2,1)S(1)}, u32[]{:S(2)}, u32[]{:S(2)}) collective-permute-start(bf16[3,256,128]{2,1,0:T(8,128)(2,1)S(1)} %get-tuple-element.56), channel_id=1, source_target_pairs={{0,4},{1,5},{2,6},{3,7},{4,0},{5,1},{6,2},{7,3},{8,12},{9,13},{10,... | collective-permute-start | bytes 589832 | tf_op jit(solution)/shard_map/ppermute | solution.py:366
  16.1 34.6 %collective-permute-start.8 = (bf16[3,256,128]{2,1,0:T(8,128)(2,1)S(1)}, bf16[3,256,128]{2,1,0:T(8,128)(2,1)S(1)}, u32[]{:S(2)}, u32[]{:S(2)}) collective-permute-start(bf16[3,256,128]{2,1,0:T(8,128)(2,1)S(1)} %get-tuple-element.57), channel_id=1, source_target_pairs={{0,14},{1,15},{2,12},{3,13},{4,10},{5,11},{6,8},{7,9},{8,6},{9,7},... | collective-permute-start | bytes 589832 | tf_op jit(solution)/shard_map/ppermute | solution.py:366
  30.3 20.5 %collective-permute-start.9 = (bf16[3,256,128]{2,1,0:T(8,128)(2,1)S(1)}, bf16[3,256,128]{2,1,0:T(8,128)(2,1)S(1)}, u32[]{:S(2)}, u32[]{:S(2)}) collective-permute-start(bf16[3,256,128]{2,1,0:T(8,128)(2,1)S(1)} %get-tuple-element.58), channel_id=1, source_target_pairs={{0,6},{1,7},{2,4},{3,5},{4,2},{5,3},{6,0},{7,1},{8,14},{9,15},{10,... | collective-permute-start | bytes 589832 | tf_op jit(solution)/shard_map/ppermute | solution.py:366
  30.3 1.0 copy-start
  38.2 17.9 %collective-permute-start.11 = (bf16[1,256,128]{2,1,0:T(8,128)(2,1)S(1)}, bf16[1,256,128]{2,1,0:T(8,128)(2,1)S(1)}, u32[]{:S(2)}, u32[]{:S(2)}) collective-permute-start(bf16[1,256,128]{2,1,0:T(8,128)(2,1)S(1)} %get-tuple-element.61), channel_id=1, source_target_pairs={{0,8},{1,9},{2,10},{3,11},{4,12},{5,13},{6,14},{7,15},{8,0},{9,1},... | collective-permute-start | bytes 196616 | tf_op jit(solution)/shard_map/ppermute | solution.py:366
  43.9 12.3 %collective-permute-start.12 = (bf16[1,256,128]{2,1,0:T(8,128)(2,1)S(1)}, bf16[1,256,128]{2,1,0:T(8,128)(2,1)S(1)}, u32[]{:S(2)}, u32[]{:S(2)}) collective-permute-start(bf16[1,256,128]{2,1,0:T(8,128)(2,1)S(1)} %get-tuple-element.62), channel_id=1, source_target_pairs={{0,10},{1,11},{2,8},{3,9},{4,14},{5,15},{6,12},{7,13},{8,2},{9,3},... | collective-permute-start | bytes 196616 | tf_op jit(solution)/shard_map/ppermute | solution.py:366
  43.9 12.3 %collective-permute-start.13 = (bf16[1,256,128]{2,1,0:T(8,128)(2,1)S(1)}, bf16[1,256,128]{2,1,0:T(8,128)(2,1)S(1)}, u32[]{:S(2)}, u32[]{:S(2)}) collective-permute-start(bf16[1,256,128]{2,1,0:T(8,128)(2,1)S(1)} %get-tuple-element.63), channel_id=1, source_target_pairs={{0,12},{1,13},{2,14},{3,15},{4,8},{5,9},{6,10},{7,11},{8,4},{9,5},... | collective-permute-start | bytes 196616 | tf_op jit(solution)/shard_map/ppermute | solution.py:366
  56.2 7.5 %collective-permute-start.14 = (bf16[8,1,128,128]{3,2,1,0:T(8,128)(2,1)S(1)}, bf16[8,1,128,128]{3,2,1,0:T(8,128)(2,1)S(1)}, u32[]{:S(2)}, u32[]{:S(2)}) collective-permute-start(bf16[8,1,128,128]{3,2,1,0:T(8,128)(2,1)S(1)} %get-tuple-element.64), channel_id=1, source_target_pairs={{0,1},{1,0},{2,3},{3,2},{4,5},{5,4},{6,7},{7,6},{8,9},{9,8},{10,11... | collective-permute-start | bytes 786440 | tf_op jit(solution)/shard_map/ppermute | solution.py:366
  57.0 7.4 %collective-permute-start.15 = (bf16[1,256,128]{2,1,0:T(8,128)(2,1)S(1)}, bf16[1,256,128]{2,1,0:T(8,128)(2,1)S(1)}, u32[]{:S(2)}, u32[]{:S(2)}) collective-permute-start(bf16[1,256,128]{2,1,0:T(8,128)(2,1)S(1)} %get-tuple-element.69), channel_id=1, source_target_pairs={{0,2},{1,3},{2,0},{3,1},{4,6},{5,7},{6,4},{7,5},{8,10},{9,11},{10,... | collective-permute-start | bytes 196616 | tf_op jit(solution)/shard_map/ppermute | solution.py:366
  57.7 8.7 %collective-permute-start.16 = (bf16[1,256,128]{2,1,0:T(8,128)(2,1)S(1)}, bf16[1,256,128]{2,1,0:T(8,128)(2,1)S(1)}, u32[]{:S(2)}, u32[]{:S(2)}) collective-permute-start(bf16[1,256,128]{2,1,0:T(8,128)(2,1)S(1)} %get-tuple-element.70), channel_id=1, source_target_pairs={{0,4},{1,5},{2,6},{3,7},{4,0},{5,1},{6,2},{7,3},{8,12},{9,13},{10,... | collective-permute-start | bytes 196616 | tf_op jit(solution)/shard_map/ppermute | solution.py:366
  57.7 8.7 %collective-permute-start.17 = (bf16[1,256,128]{2,1,0:T(8,128)(2,1)S(1)}, bf16[1,256,128]{2,1,0:T(8,128)(2,1)S(1)}, u32[]{:S(2)}, u32[]{:S(2)}) collective-permute-start(bf16[1,256,128]{2,1,0:T(8,128)(2,1)S(1)} %get-tuple-element.71), channel_id=1, source_target_pairs={{0,14},{1,15},{2,12},{3,13},{4,10},{5,11},{6,8},{7,9},{8,6},{9,7},... | collective-permute-start | bytes 196616 | tf_op jit(solution)/shard_map/ppermute | solution.py:366
  60.1 6.4 %collective-permute-start.18 = (bf16[1,256,128]{2,1,0:T(8,128)(2,1)S(1)}, bf16[1,256,128]{2,1,0:T(8,128)(2,1)S(1)}, u32[]{:S(2)}, u32[]{:S(2)}) collective-permute-start(bf16[1,256,128]{2,1,0:T(8,128)(2,1)S(1)} %get-tuple-element.72), channel_id=1, source_target_pairs={{0,6},{1,7},{2,4},{3,5},{4,2},{5,3},{6,0},{7,1},{8,14},{9,15},{10,... | collective-permute-start | bytes 196616 | tf_op jit(solution)/shard_map/ppermute | solution.py:366
  64.3 8.0 %collective-permute-start.20 = (bf16[1,128,256]{2,1,0:T(8,128)(2,1)S(1)}, bf16[1,128,256]{2,1,0:T(8,128)(2,1)S(1)}, u32[]{:S(2)}, u32[]{:S(2)}) collective-permute-start(bf16[1,128,256]{2,1,0:T(8,128)(2,1)S(1)} %get-tuple-element.77), channel_id=1, source_target_pairs={{0,8},{1,9},{2,10},{3,11},{4,12},{5,13},{6,14},{7,15},{8,0},{9,1},... | collective-permute-start | bytes 196616 | tf_op jit(solution)/shard_map/ppermute | solution.py:366
  64.4 7.9 %collective-permute-start.21 = (bf16[1,128,256]{2,1,0:T(8,128)(2,1)S(1)}, bf16[1,128,256]{2,1,0:T(8,128)(2,1)S(1)}, u32[]{:S(2)}, u32[]{:S(2)}) collective-permute-start(bf16[1,128,256]{2,1,0:T(8,128)(2,1)S(1)} %get-tuple-element.78), channel_id=1, source_target_pairs={{0,10},{1,11},{2,8},{3,9},{4,14},{5,15},{6,12},{7,13},{8,2},{9,3},... | collective-permute-start | bytes 196616 | tf_op jit(solution)/shard_map/ppermute | solution.py:366
  66.4 7.5 %collective-permute-start.22 = (bf16[1,128,256]{2,1,0:T(8,128)(2,1)S(1)}, bf16[1,128,256]{2,1,0:T(8,128)(2,1)S(1)}, u32[]{:S(2)}, u32[]{:S(2)}) collective-permute-start(bf16[1,128,256]{2,1,0:T(8,128)(2,1)S(1)} %get-tuple-element.79), channel_id=1, source_target_pairs={{0,12},{1,13},{2,14},{3,15},{4,8},{5,9},{6,10},{7,11},{8,4},{9,5},... | collective-permute-start | bytes 196616 | tf_op jit(solution)/shard_map/ppermute | solution.py:366
  73.9 3.3 %collective-permute-start.26 = (bf16[8,3,128,128]{3,2,1,0:T(8,128)(2,1)S(1)}, bf16[8,3,128,128]{3,2,1,0:T(8,128)(2,1)S(1)}, u32[]{:S(2)}, u32[]{:S(2)}) collective-permute-start(bf16[8,3,128,128]{3,2,1,0:T(8,128)(2,1)S(1)} %get-tuple-element.86), channel_id=1, source_target_pairs={{0,1},{1,0},{2,3},{3,2},{4,5},{5,4},{6,7},{7,6},{8,9},{9,8},{10,11... | collective-permute-start | bytes 2359304 | tf_op jit(solution)/shard_map/ppermute | solution.py:366
  78.1 23.8 %collective-permute-start.27 = (bf16[3,128,256]{2,1,0:T(8,128)(2,1)S(1)}, bf16[3,128,256]{2,1,0:T(8,128)(2,1)S(1)}, u32[]{:S(2)}, u32[]{:S(2)}) collective-permute-start(bf16[3,128,256]{2,1,0:T(8,128)(2,1)S(1)} %get-tuple-element.88), channel_id=1, source_target_pairs={{0,2},{1,3},{2,0},{3,1},{4,6},{5,7},{6,4},{7,5},{8,10},{9,11},{10,... | collective-permute-start | bytes 589832 | tf_op jit(solution)/shard_map/ppermute | solution.py:366
  78.8 23.1 %collective-permute-start.28 = (bf16[3,128,256]{2,1,0:T(8,128)(2,1)S(1)}, bf16[3,128,256]{2,1,0:T(8,128)(2,1)S(1)}, u32[]{:S(2)}, u32[]{:S(2)}) collective-permute-start(bf16[3,128,256]{2,1,0:T(8,128)(2,1)S(1)} %get-tuple-element.89), channel_id=1, source_target_pairs={{0,8},{1,9},{2,10},{3,11},{4,12},{5,13},{6,14},{7,15},{8,0},{9,1},... | collective-permute-start | bytes 589832 | tf_op jit(solution)/shard_map/ppermute | solution.py:366
  79.9 5.7 %collective-permute-start.19 = (bf16[1,128,256]{2,1,0:T(8,128)(2,1)S(1)}, bf16[1,128,256]{2,1,0:T(8,128)(2,1)S(1)}, u32[]{:S(2)}, u32[]{:S(2)}) collective-permute-start(bf16[1,128,256]{2,1,0:T(8,128)(2,1)S(1)} %get-tuple-element.76), channel_id=1, source_target_pairs={{0,2},{1,3},{2,0},{3,1},{4,6},{5,7},{6,4},{7,5},{8,10},{9,11},{10,... | collective-permute-start | bytes 196616 | tf_op jit(solution)/shard_map/ppermute | solution.py:366
  80.7 6.6 %collective-permute-start.23 = (bf16[1,128,256]{2,1,0:T(8,128)(2,1)S(1)}, bf16[1,128,256]{2,1,0:T(8,128)(2,1)S(1)}, u32[]{:S(2)}, u32[]{:S(2)}) collective-permute-start(bf16[1,128,256]{2,1,0:T(8,128)(2,1)S(1)} %get-tuple-element.81), channel_id=1, source_target_pairs={{0,4},{1,5},{2,6},{3,7},{4,0},{5,1},{6,2},{7,3},{8,12},{9,13},{10,... | collective-permute-start | bytes 196616 | tf_op jit(solution)/shard_map/ppermute | solution.py:366
  81.3 8.9 %collective-permute-start.25 = (bf16[1,128,256]{2,1,0:T(8,128)(2,1)S(1)}, bf16[1,128,256]{2,1,0:T(8,128)(2,1)S(1)}, u32[]{:S(2)}, u32[]{:S(2)}) collective-permute-start(bf16[1,128,256]{2,1,0:T(8,128)(2,1)S(1)} %get-tuple-element.84), channel_id=1, source_target_pairs={{0,6},{1,7},{2,4},{3,5},{4,2},{5,3},{6,0},{7,1},{8,14},{9,15},{10,... | collective-permute-start | bytes 196616 | tf_op jit(solution)/shard_map/ppermute | solution.py:366
  85.6 16.3 %collective-permute-start.24 = (bf16[1,128,256]{2,1,0:T(8,128)(2,1)S(1)}, bf16[1,128,256]{2,1,0:T(8,128)(2,1)S(1)}, u32[]{:S(2)}, u32[]{:S(2)}) collective-permute-start(bf16[1,128,256]{2,1,0:T(8,128)(2,1)S(1)} %get-tuple-element.82), channel_id=1, source_target_pairs={{0,14},{1,15},{2,12},{3,13},{4,10},{5,11},{6,8},{7,9},{8,6},{9,7},... | collective-permute-start | bytes 196616 | tf_op jit(solution)/shard_map/ppermute | solution.py:366
  87.3 19.7 %collective-permute-start.29 = (bf16[3,128,256]{2,1,0:T(8,128)(2,1)S(1)}, bf16[3,128,256]{2,1,0:T(8,128)(2,1)S(1)}, u32[]{:S(2)}, u32[]{:S(2)}) collective-permute-start(bf16[3,128,256]{2,1,0:T(8,128)(2,1)S(1)} %get-tuple-element.90), channel_id=1, source_target_pairs={{0,10},{1,11},{2,8},{3,9},{4,14},{5,15},{6,12},{7,13},{8,2},{9,3},... | collective-permute-start | bytes 589832 | tf_op jit(solution)/shard_map/ppermute | solution.py:366
  90.2 24.4 %collective-permute-start.30 = (bf16[3,128,256]{2,1,0:T(8,128)(2,1)S(1)}, bf16[3,128,256]{2,1,0:T(8,128)(2,1)S(1)}, u32[]{:S(2)}, u32[]{:S(2)}) collective-permute-start(bf16[3,128,256]{2,1,0:T(8,128)(2,1)S(1)} %get-tuple-element.91), channel_id=1, source_target_pairs={{0,12},{1,13},{2,14},{3,15},{4,8},{5,9},{6,10},{7,11},{8,4},{9,5},... | collective-permute-start | bytes 589832 | tf_op jit(solution)/shard_map/ppermute | solution.py:366
  101.9 12.8 %collective-permute-start.31 = (bf16[3,128,256]{2,1,0:T(8,128)(2,1)S(1)}, bf16[3,128,256]{2,1,0:T(8,128)(2,1)S(1)}, u32[]{:S(2)}, u32[]{:S(2)}) collective-permute-start(bf16[3,128,256]{2,1,0:T(8,128)(2,1)S(1)} %get-tuple-element.92), channel_id=1, source_target_pairs={{0,4},{1,5},{2,6},{3,7},{4,0},{5,1},{6,2},{7,3},{8,12},{9,13},{10,... | collective-permute-start | bytes 589832 | tf_op jit(solution)/shard_map/ppermute | solution.py:366
  101.9 19.4 %collective-permute-start.32 = (bf16[3,128,256]{2,1,0:T(8,128)(2,1)S(1)}, bf16[3,128,256]{2,1,0:T(8,128)(2,1)S(1)}, u32[]{:S(2)}, u32[]{:S(2)}) collective-permute-start(bf16[3,128,256]{2,1,0:T(8,128)(2,1)S(1)} %get-tuple-element.93), channel_id=1, source_target_pairs={{0,14},{1,15},{2,12},{3,13},{4,10},{5,11},{6,8},{7,9},{8,6},{9,7},... | collective-permute-start | bytes 589832 | tf_op jit(solution)/shard_map/ppermute | solution.py:366
  101.9 19.4 %collective-permute-start.33 = (bf16[3,128,256]{2,1,0:T(8,128)(2,1)S(1)}, bf16[3,128,256]{2,1,0:T(8,128)(2,1)S(1)}, u32[]{:S(2)}, u32[]{:S(2)}) collective-permute-start(bf16[3,128,256]{2,1,0:T(8,128)(2,1)S(1)} %get-tuple-element.94), channel_id=1, source_target_pairs={{0,6},{1,7},{2,4},{3,5},{4,2},{5,3},{6,0},{7,1},{8,14},{9,15},{10,... | collective-permute-start | bytes 589832 | tf_op jit(solution)/shard_map/ppermute | solution.py:366

commit v4 on v2

--- a/solution.py
+++ b/solution.py
@@ -184,6 +184,7 @@
         kernel,
         out_shape=out_shape,
         in_specs=[smem] * len(place) + [vmem] * len(arrays),
+
         out_specs=[vmem] * len(out_shape),
         scratch_shapes=list(scratch),
         compiler_params=pltpu.CompilerParams(vmem_limit_bytes=40 * 1024 * 1024),
@@ -191,63 +192,93 @@
     )(*place, *arrays)
 
 
-def pack(place, arrays, chips):
+def own_columns(place, arrays, chips):
     count = len(arrays)
-    rows, width = arrays[0].shape
-    span = width // chips
+    rows = arrays[0].shape[0]
 
     def kernel(where, *refs):
         for k in range(chips):
-            start = pl.multiple_of((where[0] ^ k) * span, span)
+            column = pl.ds(pl.multiple_of(((where[0] ^ k) * 2 + where[1]) * HEAD, HEAD), HEAD)
             for i in range(count):
-                refs[count + k][i] = refs[i][:, pl.ds(start, span)]
-
-    piece = jax.ShapeDtypeStruct((count, rows, span), jnp.bfloat16)
-    return call(kernel, [place], arrays, [piece] * chips)
-
-
-def unpack(place, mine, theirs):
-    chips = len(mine)
-    count, both, head = mine[0].shape
-    rows = both // 2
+                refs[count][k, i] = refs[i][:, column]
+
+    out = jax.ShapeDtypeStruct((chips, count, rows, HEAD), jnp.bfloat16)
+    return call(kernel, [place], arrays, [out])[0]
+
+
+def pack(place, ks, keeps, theirs):
+    rows = keeps[0].shape[2]
+    count = len(theirs)
+
+    def kernel(where, *refs):
+        here, there = halves(where, rows)
+        keep = [(ref, i) for ref in refs[: len(keeps)] for i in range(ref.shape[1])]
+        theirs = refs[len(keeps) : len(keeps) + count]
+        for n, k in enumerate(ks):
+            column = pl.ds(pl.multiple_of(((where[0] ^ k) * 2 + where[1]) * HEAD, HEAD), HEAD)
+            out = refs[len(keeps) + count + n]
+            for i, (ref, j) in enumerate(keep):
+                out[i, here] = ref[k, j]
+                out[i, there] = theirs[i][:, column]
+
+    piece = jax.ShapeDtypeStruct((count, 2 * rows, HEAD), jnp.bfloat16)
+    pieces = call(kernel, [place], [*keeps, *theirs], [piece] * len(ks))
+    return dict(zip(ks, pieces))
+
+
+def cut(place, pieces, bases, count):
+    number = len(pieces)
+    size = pieces[0].shape[1]
+
+    def kernel(where, *refs):
+        there = halves(where, size // 2)[1]
+        for n in range(number):
+            refs[number][n] = refs[n][bases[n] : bases[n] + count, there]
+
+    out = jax.ShapeDtypeStruct((number, count, size // 2, HEAD), jnp.bfloat16)
+    return call(kernel, [place], pieces, [out])[0]
+
+
+def unpack(place, ks, pieces, bases, count, batches):
+    chips = len(pieces)
+    size = pieces[0].shape[1]
 
     def kernel(where, *refs):
         core = where[1]
-        half = pl.ds(pl.multiple_of(core * rows, rows), rows)
-        for k in range(chips):
+        half = halves(where, size // 2)[0]
+        outs = refs[chips + len(batches) :]
+        got = [ref.at[n] for ref in refs[chips : chips + len(batches)] for n in range(ref.shape[0])]
+        for n, k in enumerate(ks):
             start = (where[0] ^ k) * 2
-            here = pl.multiple_of((start + core) * head, head)
-            there = pl.multiple_of((start + 1 - core) * head, head)
+            here = pl.ds(pl.multiple_of((start + core) * HEAD, HEAD), HEAD)
+            there = pl.ds(pl.multiple_of((start + 1 - core) * HEAD, HEAD), HEAD)
             for i in range(count):
-                out = refs[2 * chips + i]
-                out[:, pl.ds(here, head)] = refs[k][i, half]
-                out[:, pl.ds(there, head)] = refs[chips + k][i, half]
-
-    out = jax.ShapeDtypeStruct((rows, chips * 2 * head), jnp.bfloat16)
-    return call(kernel, [place], [*mine, *theirs], [out] * count)
-
-
-def merge(where, mine, theirs, target):
+                outs[i][:, here] = refs[n][bases[n] + i, half]
+                outs[i][:, there] = got[n][i]
+
+    out = jax.ShapeDtypeStruct((size // 2, chips * 2 * HEAD), jnp.bfloat16)
+    return call(kernel, [place], [*pieces, *batches], [out] * count)
+
+
+def halves(where, rows):
     core = where[1]
-    rows = mine[0].shape[1]
-    column = pl.ds(pl.multiple_of(core * HEAD, HEAD), HEAD)
     here = pl.ds(pl.multiple_of(core * rows, rows), rows)
     there = pl.ds(pl.multiple_of((1 - core) * rows, rows), rows)
-    for k in range(len(mine)):
-        block = where[0] ^ k
-        for i in range(mine[0].shape[0]):
-            target[block, i, here] = mine[k][i, :, column]
-            target[block, i, there] = theirs[k][i, :, column]
-
-
-def forward(place, partner, mine, theirs):
-    chips = len(mine)
-    size = 2 * mine[0].shape[1]
+    return here, there
+
+
+def forward(place, partner, ks, far, pieces):
+    chips = len(pieces)
+    size = pieces[0].shape[1]
 
     def kernel(where, partner, *refs):
-        ins, outs = refs[: 2 * chips], refs[2 * chips :]
-        held, weights = outs[chips], outs[chips + 1]
-        merge(where, ins[:chips], ins[chips:], held)
+        outs = refs[chips:-2]
+        held, weights = refs[-2:]
+        for n, k in enumerate(ks):
+            b = where[0] ^ k
+            held[b, :3] = refs[n][:3]
+            if k not in far:
+                held[b, 4] = refs[n][3]
         for k in range(chips):
             b = where[0] ^ k
             p = partner[b]
@@ -263,89 +294,111 @@
             attended = mm(s.astype(jnp.bfloat16), held[b, 2], NN)
             attended += mm(t.astype(jnp.bfloat16), held[p, 2], NN)
             attended = attended.astype(jnp.bfloat16)
-            outs[k][0] = attended
             held[b, 3] = attended
-
-    out_shape = [jax.ShapeDtypeStruct((1, size, HEAD), jnp.bfloat16)] * chips
-    out_shape += [
-        jax.ShapeDtypeStruct((chips, 4, size, HEAD), jnp.bfloat16),
+            if k in far:
+                outs[far.index(k)][0] = attended
+
+    out_shape = [
+        *[jax.ShapeDtypeStruct((1, size, HEAD), jnp.bfloat16)] * len(far),
+        jax.ShapeDtypeStruct((chips, 5, size, HEAD), jnp.bfloat16),
         jax.ShapeDtypeStruct((chips, 2, size, size), jnp.float32),
     ]
     flops = chips * 8 * size * size * HEAD
-    outs = call(
-        kernel, [place, partner], [*mine, *theirs], out_shape, (), flops, chips * 2 * size * size
-    )
-    return outs[:chips], outs[chips], outs[chips + 1]
-
-
-def backward(place, partner, mine, theirs, held, weights):
-    chips = len(mine)
-    size = held.shape[2]
+    outs = call(kernel, [place, partner], pieces, out_shape, (), flops, chips * 2 * size * size)
+    return dict(zip(far, outs)), outs[-2], outs[-1]
+
+
+def backward(place, partner, far, pieces, held, weights):
+    chips, _, size, _ = held.shape
 
     def kernel(where, partner, *refs):
-        ins, outs = refs[: 2 * chips + 2], refs[2 * chips + 2 : 3 * chips + 2]
-        held, weights = ins[2 * chips :]
-        grads, acc_k, acc_v = refs[3 * chips + 2 :]
-        merge(where, ins[:chips], ins[chips : 2 * chips], grads)
+        ins = refs[: len(far)]
+        held, weights = refs[len(far) : len(far) + 2]
+        outs = refs[len(far) + 2 : len(far) + 2 + chips]
+        acc_k, acc_v = refs[len(far) + 2 + chips :]
         acc_k[...] = jnp.zeros_like(acc_k)
         acc_v[...] = jnp.zeros_like(acc_v)
         for k in range(chips):
             b = where[0] ^ k
-            q, do = held[b, 0], grads[b, 0]
+            q = held[b, 0]
+            do = ins[far.index(k)][0] if k in far else held[b, 4]
             delta = jnp.sum(
                 do.astype(jnp.float32) * held[b, 3].astype(jnp.float32), axis=1, keepdims=True
             )
-            grad_q = None
+            total = None
             for side, c in enumerate((b, partner[b])):
                 w = weights[b, side]
                 g = (w * (mm(do, held[c, 2], NT) - delta)).astype(jnp.bfloat16)
                 term = mm(g, held[c, 1], NN)
-                grad_q = term if side == 0 else grad_q + term
+                total = term if side == 0 else total + term
                 acc_k[c] += mm(g, q, TN)
                 acc_v[c] += mm(w.astype(jnp.bfloat16), do, TN)
-            outs[k][0] = (SCALE * grad_q).astype(jnp.bfloat16)
+            outs[k][0] = (SCALE * total).astype(jnp.bfloat16)
         for k in range(chips):
             b = where[0] ^ k
             outs[k][1] = (SCALE * acc_k[b]).astype(jnp.bfloat16)
             outs[k][2] = acc_v[b].astype(jnp.bfloat16)
-
-    out_shape = [jax.ShapeDtypeStruct((3, size, HEAD), jnp.bfloat16)] * chips
-    scratch = [
-        pltpu.VMEM((chips, 1, size, HEAD), jnp.bfloat16),
-        pltpu.VMEM((chips, size, HEAD), jnp.float32),
-        pltpu.VMEM((chips, size, HEAD), jnp.float32),
+            if k not in far:
+                outs[k][3] = held[b, 3]
+
+    out_shape = [
+        jax.ShapeDtypeStruct((3 if k in far else 4, size, HEAD), jnp.bfloat16) for k in range(chips)
     ]
+    scratch = [pltpu.VMEM((chips, size, HEAD), jnp.float32)] * 2
     flops = chips * 16 * size * size * HEAD
-    return call(
-        kernel, [place, partner], [*mine, *theirs, held, weights], out_shape, scratch, flops
+    outs = call(
+        kernel, [place, partner], [*pieces, held, weights], out_shape, scratch, flops
     )
-
-
-def between_chips(pieces):
-    devices = 2 * len(pieces)
-    return [
-        lax.ppermute(p, "ctx", [(i, i ^ (2 * k)) for i in range(devices)]) if k else p
-        for k, p in enumerate(pieces)
-    ]
-
-
-def between_cores(pieces):
-    devices = 2 * len(pieces)
-    return [lax.ppermute(p, "ctx", [(i, i ^ 1) for i in range(devices)]) for p in pieces]
+    return dict(enumerate(outs))
+
+
+def after(array, *earlier):
+    return lax.optimization_barrier((array, *earlier))[0]
 
 
 def by_permutes(queries, keys, values, cotangent, partner):
-    chips = lax.axis_size("ctx") // 2
+    devices = lax.axis_size("ctx")
+    chips = devices // 2
     me = lax.axis_index("ctx")
     place = jnp.stack([me // 2, me % 2]).astype(jnp.int32)
-    first = between_chips(pack(place, [queries, keys, values], chips))
-    second = between_chips(pack(place, [cotangent], chips))
-    attended, held, weights = forward(place, partner, first, between_cores(first))
-    grads = backward(place, partner, second, between_cores(second), held, weights)
-    attended = between_chips(attended)
-    outs = unpack(place, attended, between_cores(attended))
-    grads = between_chips(grads)
-    return tuple(outs) + tuple(unpack(place, grads, between_cores(grads)))
+
+    def hop(piece, distance):
+        return lax.ppermute(piece, "ctx", [(i, i ^ distance) for i in range(devices)])
+
+    far = list(range(chips // 2, chips))
+    near = list(range(1, chips // 2))
+    ks = [0, *near[:1], *far[:2], *near[1:2], *far[2:3], *near[2:], *far[3:]]
+
+    def to_chips(pieces, ks):
+        return {k: hop(pieces[k], 2 * k) for k in ks}
+
+    def in_order(arrived):
+        return [arrived[k] for k in ks]
+
+    ins = [queries, keys, values]
+    theirs = [hop(a, 1) for a in ins]
+    keep = own_columns(place, ins, chips)
+    one = pack(place, far, [keep], theirs)
+    their_do = hop(cotangent, 1)
+    keep_do = own_columns(place, [cotangent], chips)
+    one |= pack(place, [0, *near], [keep, keep_do], [*theirs, their_do])
+    two = pack(place, far, [keep_do], [their_do])
+    first = {0: one[0]} | to_chips(one, far + near)
+    second = to_chips(two, far)
+    three, held, weights = forward(place, partner, ks, far, in_order(first))
+    third = {k: hop(after(three[k], second[k]), 2 * k) for k in far}
+    four = backward(place, partner, far, [second[k] for k in far], held, weights)
+    done = [third[k] for k in far]
+    fourth = {0: four[0]} | {k: hop(after(four[k], *done), 2 * k) for k in far + near}
+    third |= {k: fourth[k] for k in [0, *near]}
+    bases = [0 if k in far else 3 for k in ks]
+    third = in_order(third)
+    third[0] = after(third[0], *(fourth[k] for k in far[:3]))
+    outs = unpack(place, ks, third, bases, 1, [hop(cut(place, third, bases, 1), 1)])
+    fourth = in_order(fourth)
+    bases = [0] * chips
+    batches = [hop(cut(place, fourth, bases, 3), 1)]
+    return tuple(outs) + tuple(unpack(place, ks, fourth, bases, 3, batches))
 
 
 def body(queries, keys, values, cotangent, partner):

time: 140 us -> 115 us (0.82)
  starting transfers between devices: 68 us -> 24.8 us
  waiting for transfers between devices: 49.2 us -> 65.6 us
  Pallas kernels: 16.3 us -> 19.2 us
  local copies, waits for them, and re-layouts: 4.82 us -> 3.13 us
    ppermute x60 -> x28, starting transfers between devices: 68 us -> 24.8 us  [hop(): lax.ppermute(piece, 'ctx', [(i, i ^ distance) for i in range(devices)])]
    ppermute x60 -> x28, waiting for transfers between devices: 49.2 us -> 65.6 us  [hop(): lax.ppermute(piece, 'ctx', [(i, i ^ distance) for i in range(devices)])]
    pallas_call x6 -> x11, Pallas kernels: 16.3 us -> 19.2 us  [call(): pl.pallas_call(kernel, out_shape=out_shape, in_specs=[smem] * len(place)...]
    unnamed x10, local copies, waits for them, and re-layouts: 4.82 us -> 3.13 us
  transfers between devices with their start and end apart: 60 -> 28, of which waited for: 14 -> 11; matrix products, arithmetic and copies ran while one was open for 0% -> 0% of each run, Pallas kernels for 10% -> 15%
where the time goes in v4:
time: 115 us; the launch traced here: 114 us
  waiting for transfers between devices  65.6 us (57%)
  starting transfers between devices  24.8 us (22%)
  Pallas kernels  19.2 us (17%)
  local copies, waits for them, and re-layouts  3.13 us (3%)
    ppermute x28, waiting for transfers between devices, hop(): lax.ppermute(piece, 'ctx', [(i, i ^ distance) for i in range(devices)])  65.6 us
    ppermute x28, starting transfers between devices, hop(): lax.ppermute(piece, 'ctx', [(i, i ^ distance) for i in range(devices)])  24.8 us
    pallas_call x11, Pallas kernels, call(): pl.pallas_call(kernel, out_shape=out_shape, in_specs=[smem] * len(place)...  19.2 us
    unnamed x10, local copies, waits for them, and re-layouts  3.13 us
  transfers between devices with their start and end apart: 28, of which 11 were waited for; matrix products, arithmetic and copies ran while one was open for 0% of the time, Pallas kernels for 15%

profile of v4, /device:TPU:9, one launch (start us, length us, event | category | flops | bytes accessed | tf_op | source)
XLA Modules:
  0.0 113.6 jit_solution(1858747454664941032)
XLA Ops:
  0.6 0.7 collective-permute-start.5
  1.4 0.1 collective-permute-start.6
  1.5 0.4 collective-permute-start.7
  1.9 0.1 collective-permute-start
  2.0 0.1 pad_add_fusion.where
  2.0 1.0 copy-done
  3.1 1.0 copy-done.1
  4.1 1.0 copy-done.2
  5.2 0.8 shard_map.86.refs_0_
  5.9 0.0 collective-permute-done.5.refs_2_.refs_1_
  5.9 0.0 collective-permute-done.6.refs_3_.refs_2_
  5.9 0.0 collective-permute-done.7.refs_4_.refs_3_
  6.0 0.7 shard_map.88
  6.6 2.4 %collective-permute-start.9 = (bf16[3,256,128]{2,1,0:T(8,128)(2,1)S(1)}, bf16[3,256,128]{2,1,0:T(8,128)(2,1)S(1)}, u32[]{:S(2)}, u32[]{:S(2)}) collective-permute-start(bf16[3,256,128]{2,1,0:T(8,128)(2,1)S(1)} %get-tuple-element.51), channel_id=1, source_target_pairs={{0,8},{1,9},{2,10},{3,11},{4,12},{5,13},{6,14},{7,15},{8,0},{9,1},... | collective-permute-start | bytes 589832 | tf_op jit(solution)/shard_map/ppermute | solution.py:366
  9.0 1.0 collective-permute-start.10
  10.1 0.6 shard_map.84.refs_0_.refs_1_
  10.7 0.0 collective-permute-done.refs_1_.refs_5_
  10.7 0.7 shard_map.87
  11.4 0.3 collective-permute-start.8
  11.7 0.2 collective-permute-start.11
  11.9 2.3 %collective-permute-start.13 = (bf16[4,256,128]{2,1,0:T(8,128)(2,1)S(1)}, bf16[4,256,128]{2,1,0:T(8,128)(2,1)S(1)}, u32[]{:S(2)}, u32[]{:S(2)}) collective-permute-start(bf16[4,256,128]{2,1,0:T(8,128)(2,1)S(1)} %get-tuple-element.55), channel_id=1, source_target_pairs={{0,6},{1,7},{2,4},{3,5},{4,2},{5,3},{6,0},{7,1},{8,14},{9,15},{10,... | collective-permute-start | bytes 786440 | tf_op jit(solution)/shard_map/ppermute | solution.py:366
  14.1 7.9 %collective-permute-done.9.refs_2_ = bf16[3,256,128]{2,1,0:T(8,128)(2,1)S(1)} collective-permute-done((bf16[3,256,128]{2,1,0:T(8,128)(2,1)S(1)}, bf16[3,256,128]{2,1,0:T(8,128)(2,1)S(1)}, u32[]{:S(2)}, u32[]{:S(2)}) %collective-permute-start.9) | collective-permute-done | bytes 196640 | tf_op jit(solution)/shard_map/ppermute | solution.py:366
  22.0 0.0 collective-permute-start.12
  22.0 4.2 %collective-permute-done.10.refs_3_ = bf16[3,256,128]{2,1,0:T(8,128)(2,1)S(1)} collective-permute-done((bf16[3,256,128]{2,1,0:T(8,128)(2,1)S(1)}, bf16[3,256,128]{2,1,0:T(8,128)(2,1)S(1)}, u32[]{:S(2)}, u32[]{:S(2)}) %collective-permute-start.10) | collective-permute-done | bytes 196640 | tf_op jit(solution)/shard_map/ppermute | solution.py:366
  26.2 0.0 collective-permute-start.14
  26.2 0.6 shard_map.85
  26.8 12.0 %collective-permute-done.12.refs_5_ = bf16[3,256,128]{2,1,0:T(8,128)(2,1)S(1)} collective-permute-done((bf16[3,256,128]{2,1,0:T(8,128)(2,1)S(1)}, bf16[3,256,128]{2,1,0:T(8,128)(2,1)S(1)}, u32[]{:S(2)}, u32[]{:S(2)}) %collective-permute-start.12) | collective-permute-done | bytes 196640 | tf_op jit(solution)/shard_map/ppermute | solution.py:366
  38.9 0.0 collective-permute-start.1
  38.9 4.8 %collective-permute-done.14.refs_7_ = bf16[3,256,128]{2,1,0:T(8,128)(2,1)S(1)} collective-permute-done((bf16[3,256,128]{2,1,0:T(8,128)(2,1)S(1)}, bf16[3,256,128]{2,1,0:T(8,128)(2,1)S(1)}, u32[]{:S(2)}, u32[]{:S(2)}) %collective-permute-start.14) | collective-permute-done | bytes 196640 | tf_op jit(solution)/shard_map/ppermute | solution.py:366
  43.6 4.0 %collective-permute-start.3 = (bf16[1,256,128]{2,1,0:T(8,128)(2,1)S(1)}, bf16[1,256,128]{2,1,0:T(8,128)(2,1)S(1)}, u32[]{:S(2)}, u32[]{:S(2)}) collective-permute-start(bf16[1,256,128]{2,1,0:T(8,128)(2,1)S(1)} %get-tuple-element.47), channel_id=1, source_target_pairs={{0,12},{1,13},{2,14},{3,15},{4,8},{5,9},{6,10},{7,11},{8,4},{9,5},... | collective-permute-start | bytes 196616 | tf_op jit(solution)/shard_map/ppermute | solution.py:366
  47.6 0.0 collective-permute-start.4
  47.7 5.3 %shard_map.89 = (bf16[1,256,128]{2,1,0:T(8,128)(2,1)S(1)}, bf16[1,256,128]{2,1,0:T(8,128)(2,1)S(1)}, bf16[1,256,128]{2,1,0:T(8,128)(2,1)S(1)}, bf16[1,256,128]{2...) custom-call(s32[2]{0:T(128)S(1)} %pad_add_fusion.where, s32[8]{0:T(128)S(1)} %copy-done.4, ...), custom_call_target="tpu_custom_call" | custom-call | flops 536870912 | bytes 8912896 | tf_op jit(solution)/shard_map/pallas_call | solution.py:183
  53.0 0.0 collective-permute-done.1.refs_0_
  53.0 0.0 collective-permute-done.2.refs_1_
  53.0 3.2 %collective-permute-done.4.refs_3_ = bf16[1,256,128]{2,1,0:T(8,128)(2,1)S(1)} collective-permute-done((bf16[1,256,128]{2,1,0:T(8,128)(2,1)S(1)}, bf16[1,256,128]{2,1,0:T(8,128)(2,1)S(1)}, u32[]{:S(2)}, u32[]{:S(2)}) %collective-permute-start.4) | collective-permute-done | bytes 65568 | tf_op jit(solution)/shard_map/ppermute | solution.py:366
  56.2 1.4 %collective-permute-start.17 = (bf16[1,256,128]{2,1,0:T(8,128)(2,1)S(1)}, bf16[1,256,128]{2,1,0:T(8,128)(2,1)S(1)}, u32[]{:S(2)}, u32[]{:S(2)}) collective-permute-start(bf16[1,256,128]{2,1,0:T(8,128)(2,1)S(1)} %get-tuple-element.66), channel_id=1, source_target_pairs={{0,12},{1,13},{2,14},{3,15},{4,8},{5,9},{6,10},{7,11},{8,4},{9,5},... | collective-permute-start | bytes 196616 | tf_op jit(solution)/shard_map/ppermute | solution.py:366
  57.6 3.9 %collective-permute-start.16 = (bf16[1,256,128]{2,1,0:T(8,128)(2,1)S(1)}, bf16[1,256,128]{2,1,0:T(8,128)(2,1)S(1)}, u32[]{:S(2)}, u32[]{:S(2)}) collective-permute-start(bf16[1,256,128]{2,1,0:T(8,128)(2,1)S(1)} %get-tuple-element.64), channel_id=1, source_target_pairs={{0,10},{1,11},{2,8},{3,9},{4,14},{5,15},{6,12},{7,13},{8,2},{9,3},... | collective-permute-start | bytes 196616 | tf_op jit(solution)/shard_map/ppermute | solution.py:366
  61.5 0.0 collective-permute-start.15
  61.5 5.8 %shard_map.90 = (bf16[4,256,128]{2,1,0:T(8,128)(2,1)S(1)}, bf16[4,256,128]{2,1,0:T(8,128)(2,1)S(1)}, bf16[4,256,128]{2,1,0:T(8,128)(2,1)S(1)}, bf16[4,256,128]{2...) custom-call(s32[2]{0:T(128)S(1)} %pad_add_fusion.where, ...), custom_call_target="tpu_custom_call" | custom-call | flops 1073741824 | bytes 8912896 | tf_op jit(solution)/shard_map/pallas_call | solution.py:183
  67.3 0.0 collective-permute-done.17.refs_5_
  67.3 0.0 collective-permute-done.16.refs_3_
  67.3 1.9 %collective-permute-done.15.refs_2_ = bf16[1,256,128]{2,1,0:T(8,128)(2,1)S(1)} collective-permute-done((bf16[1,256,128]{2,1,0:T(8,128)(2,1)S(1)}, bf16[1,256,128]{2,1,0:T(8,128)(2,1)S(1)}, u32[]{:S(2)}, u32[]{:S(2)}) %collective-permute-start.15) | collective-permute-done | bytes 65568 | tf_op jit(solution)/shard_map/ppermute | solution.py:366
  69.2 3.2 %collective-permute-start.19 = (bf16[3,256,128]{2,1,0:T(8,128)(2,1)S(1)}, bf16[3,256,128]{2,1,0:T(8,128)(2,1)S(1)}, u32[]{:S(2)}, u32[]{:S(2)}) collective-permute-start(bf16[3,256,128]{2,1,0:T(8,128)(2,1)S(1)} %get-tuple-element.69), channel_id=1, source_target_pairs={{0,8},{1,9},{2,10},{3,11},{4,12},{5,13},{6,14},{7,15},{8,0},{9,1},... | collective-permute-start | bytes 589832 | tf_op jit(solution)/shard_map/ppermute | solution.py:366
  72.4 0.0 collective-permute-start.20
  72.4 1.2 %collective-permute-start.22 = (bf16[4,256,128]{2,1,0:T(8,128)(2,1)S(1)}, bf16[4,256,128]{2,1,0:T(8,128)(2,1)S(1)}, u32[]{:S(2)}, u32[]{:S(2)}) collective-permute-start(bf16[4,256,128]{2,1,0:T(8,128)(2,1)S(1)} %get-tuple-element.76), channel_id=1, source_target_pairs={{0,2},{1,3},{2,0},{3,1},{4,6},{5,7},{6,4},{7,5},{8,10},{9,11},{10,... | collective-permute-start | bytes 786440 | tf_op jit(solution)/shard_map/ppermute | solution.py:366
  73.6 1.8 %collective-permute-start.23 = (bf16[4,256,128]{2,1,0:T(8,128)(2,1)S(1)}, bf16[4,256,128]{2,1,0:T(8,128)(2,1)S(1)}, u32[]{:S(2)}, u32[]{:S(2)}) collective-permute-start(bf16[4,256,128]{2,1,0:T(8,128)(2,1)S(1)} %get-tuple-element.78), channel_id=1, source_target_pairs={{0,4},{1,5},{2,6},{3,7},{4,0},{5,1},{6,2},{7,3},{8,12},{9,13},{10,... | collective-permute-start | bytes 786440 | tf_op jit(solution)/shard_map/ppermute | solution.py:366
  75.4 0.3 collective-permute-start.24
  75.7 9.0 %collective-permute-done.19.refs_2_ = bf16[3,256,128]{2,1,0:T(8,128)(2,1)S(1)} collective-permute-done((bf16[3,256,128]{2,1,0:T(8,128)(2,1)S(1)}, bf16[3,256,128]{2,1,0:T(8,128)(2,1)S(1)}, u32[]{:S(2)}, u32[]{:S(2)}) %collective-permute-start.19) | collective-permute-done | bytes 196640 | tf_op jit(solution)/shard_map/ppermute | solution.py:366
  84.7 0.8 collective-permute-start.21
  85.5 3.4 %collective-permute-done.20.refs_3_ = bf16[3,256,128]{2,1,0:T(8,128)(2,1)S(1)} collective-permute-done((bf16[3,256,128]{2,1,0:T(8,128)(2,1)S(1)}, bf16[3,256,128]{2,1,0:T(8,128)(2,1)S(1)}, u32[]{:S(2)}, u32[]{:S(2)}) %collective-permute-start.20) | collective-permute-done | bytes 196640 | tf_op jit(solution)/shard_map/ppermute | solution.py:366
  88.9 0.0 collective-permute-start.26
  88.9 14.2 %collective-permute-done.21.refs_5_ = bf16[3,256,128]{2,1,0:T(8,128)(2,1)S(1)} collective-permute-done((bf16[3,256,128]{2,1,0:T(8,128)(2,1)S(1)}, bf16[3,256,128]{2,1,0:T(8,128)(2,1)S(1)}, u32[]{:S(2)}, u32[]{:S(2)}) %collective-permute-start.21) | collective-permute-done | bytes 196640 | tf_op jit(solution)/shard_map/ppermute | solution.py:366
  103.1 3.4 %collective-permute-done.26.refs_7_ = bf16[3,256,128]{2,1,0:T(8,128)(2,1)S(1)} collective-permute-done((bf16[3,256,128]{2,1,0:T(8,128)(2,1)S(1)}, bf16[3,256,128]{2,1,0:T(8,128)(2,1)S(1)}, u32[]{:S(2)}, u32[]{:S(2)}) %collective-permute-start.26) | collective-permute-done | bytes 196640 | tf_op jit(solution)/shard_map/ppermute | solution.py:366
  106.5 0.0 collective-permute-done.22.refs_1_
  106.5 0.0 collective-permute-done.23.refs_4_
  106.5 0.0 collective-permute-done.24.refs_6_
  106.5 0.6 shard_map.93
  107.2 0.6 collective-permute-start.27
  107.7 0.6 shard_map.91
  108.3 0.1 collective-permute-start.25
  108.4 1.6 %collective-permute-done.25.refs_8_ = bf16[8,1,128,128]{3,2,1,0:T(8,128)(2,1)S(1)} collective-permute-done((bf16[8,1,128,128]{3,2,1,0:T(8,128)(2,1)S(1)}, bf16[8,1,128,128]{3,2,1,0:T(8,128)(2,1)S(1)}, u32[]{:S(2)}, u32[]{:S(2)}) %collective-permute-start.25) | collective-permute-done | bytes 262176 | tf_op jit(solution)/shard_map/ppermute | solution.py:366
  110.0 1.5 %shard_map.92 = bf16[128,2048]{1,0:T(8,128)(2,1)} custom-call(s32[2]{0:T(128)S(1)} %pad_add_fusion.where, bf16[4,256,128]{2,1,0:T(8,128)(2,1)S(1)} %get-tuple-element.74.refs_0_, bf16[4,256,128]{2,1,0:T(8,128)(2,1)S(1)} %collective-permute-done.22.refs_1_, bf16[1,256,128]{2,1,0:T(8,128)(2,1)S(1)} %collective-permute-done.15.refs_2_, ...), custom_call_target="tpu_custom_call" | custom-call | bytes 2097152 | tf_op jit(solution)/shard_map/pallas_call | solution.py:183
  111.5 0.0 collective-permute-done.27.refs_8_
  111.5 2.1 %shard_map.94 = (bf16[128,2048]{1,0:T(8,128)(2,1)}, bf16[128,2048]{1,0:T(8,128)(2,1)}, bf16[128,2048]{1,0:T(8,128)(2,1)}) custom-call(s32[2]{0:T(128)S(1)} %pad_add_fusion.where, bf16[4,256,128]{2,1,0:T(8,128)(2,1)S(1)} %get-tuple-element.74.refs_0_, bf16[4,256,128]{2,1,0:T(8,128)(2,1)S(1)} %collective-permute-done.22.refs_1_, ...), custom_call_target="tpu_custom_call" | custom-call | bytes 4194304 | tf_op jit(solution)/shard_map/pallas_call | solution.py:183
  (14 shorter events, 0.0 us)
Async XLA Ops:
  0.6 5.3 %collective-permute-start.5 = (bf16[128,2048]{1,0:T(8,128)(2,1)}, bf16[128,2048]{1,0:T(8,128)(2,1)S(1)}, u32[]{:S(2)}, u32[]{:S(2)}) collective-permute-start(bf16[128,2048]{1,0:T(8,128)(2,1)} %refs_0_.3), channel_id=1, source_target_pairs={{0,1},{1,0},{2,3},{3,2},{4,5},{5,4},{6,7},{7,6},{8,9},{9,8},{10,11... | collective-permute-start | bytes 1572872 | tf_op jit(solution)/shard_map/ppermute | solution.py:366
  1.4 4.6 %collective-permute-start.6 = (bf16[128,2048]{1,0:T(8,128)(2,1)}, bf16[128,2048]{1,0:T(8,128)(2,1)S(1)}, u32[]{:S(2)}, u32[]{:S(2)}) collective-permute-start(bf16[128,2048]{1,0:T(8,128)(2,1)} %refs_1_.1), channel_id=1, source_target_pairs={{0,1},{1,0},{2,3},{3,2},{4,5},{5,4},{6,7},{7,6},{8,9},{9,8},{10,11... | collective-permute-start | bytes 1572872 | tf_op jit(solution)/shard_map/ppermute | solution.py:366
  1.5 4.5 %collective-permute-start.7 = (bf16[128,2048]{1,0:T(8,128)(2,1)}, bf16[128,2048]{1,0:T(8,128)(2,1)S(1)}, u32[]{:S(2)}, u32[]{:S(2)}) collective-permute-start(bf16[128,2048]{1,0:T(8,128)(2,1)} %refs_2_.1), channel_id=1, source_target_pairs={{0,1},{1,0},{2,3},{3,2},{4,5},{5,4},{6,7},{7,6},{8,9},{9,8},{10,11... | collective-permute-start | bytes 1572872 | tf_op jit(solution)/shard_map/ppermute | solution.py:366
  1.9 8.8 %collective-permute-start = (bf16[128,2048]{1,0:T(8,128)(2,1)}, bf16[128,2048]{1,0:T(8,128)(2,1)S(1)}, u32[]{:S(2)}, u32[]{:S(2)}) collective-permute-start(bf16[128,2048]{1,0:T(8,128)(2,1)} %refs_0_.2), channel_id=1, source_target_pairs={{0,1},{1,0},{2,3},{3,2},{4,5},{5,4},{6,7},{7,6},{8,9},{9,8},{10,11... | collective-permute-start | bytes 1572872 | tf_op jit(solution)/shard_map/ppermute | solution.py:366
  2.0 1.0 copy-start
  3.1 1.0 copy-start.1
  4.1 1.0 copy-start.2
  5.2 4.9 %copy-start.3 = (bf16[128,2048]{1,0:T(8,128)(2,1)S(1)}, bf16[128,2048]{1,0:T(8,128)(2,1)}, u32[]{:S(2)}) copy-start(bf16[128,2048]{1,0:T(8,128)(2,1)} %refs_0_.2) | copy-start | bytes 1572868
  5.2 42.5 %copy-start.4 = (s32[8]{0:T(128)S(1)}, s32[8]{0:T(128)}, u32[]{:S(2)}) copy-start(s32[8]{0:T(128)} %partner.3) | copy-start | bytes 100
  6.6 15.4 %collective-permute-start.9 = (bf16[3,256,128]{2,1,0:T(8,128)(2,1)S(1)}, bf16[3,256,128]{2,1,0:T(8,128)(2,1)S(1)}, u32[]{:S(2)}, u32[]{:S(2)}) collective-permute-start(bf16[3,256,128]{2,1,0:T(8,128)(2,1)S(1)} %get-tuple-element.51), channel_id=1, source_target_pairs={{0,8},{1,9},{2,10},{3,11},{4,12},{5,13},{6,14},{7,15},{8,0},{9,1},... | collective-permute-start | bytes 589832 | tf_op jit(solution)/shard_map/ppermute | solution.py:366
  9.0 17.2 %collective-permute-start.10 = (bf16[3,256,128]{2,1,0:T(8,128)(2,1)S(1)}, bf16[3,256,128]{2,1,0:T(8,128)(2,1)S(1)}, u32[]{:S(2)}, u32[]{:S(2)}) collective-permute-start(bf16[3,256,128]{2,1,0:T(8,128)(2,1)S(1)} %get-tuple-element.52), channel_id=1, source_target_pairs={{0,10},{1,11},{2,8},{3,9},{4,14},{5,15},{6,12},{7,13},{8,2},{9,3},... | collective-permute-start | bytes 589832 | tf_op jit(solution)/shard_map/ppermute | solution.py:366
  11.4 32.2 %collective-permute-start.8 = (bf16[4,256,128]{2,1,0:T(8,128)(2,1)S(1)}, bf16[4,256,128]{2,1,0:T(8,128)(2,1)S(1)}, u32[]{:S(2)}, u32[]{:S(2)}) collective-permute-start(bf16[4,256,128]{2,1,0:T(8,128)(2,1)S(1)} %get-tuple-element.50), channel_id=1, source_target_pairs={{0,2},{1,3},{2,0},{3,1},{4,6},{5,7},{6,4},{7,5},{8,10},{9,11},{10,... | collective-permute-start | bytes 786440 | tf_op jit(solution)/shard_map/ppermute | solution.py:366
  11.7 35.9 %collective-permute-start.11 = (bf16[4,256,128]{2,1,0:T(8,128)(2,1)S(1)}, bf16[4,256,128]{2,1,0:T(8,128)(2,1)S(1)}, u32[]{:S(2)}, u32[]{:S(2)}) collective-permute-start(bf16[4,256,128]{2,1,0:T(8,128)(2,1)S(1)} %get-tuple-element.53), channel_id=1, source_target_pairs={{0,4},{1,5},{2,6},{3,7},{4,0},{5,1},{6,2},{7,3},{8,12},{9,13},{10,... | collective-permute-start | bytes 786440 | tf_op jit(solution)/shard_map/ppermute | solution.py:366
  11.9 35.8 %collective-permute-start.13 = (bf16[4,256,128]{2,1,0:T(8,128)(2,1)S(1)}, bf16[4,256,128]{2,1,0:T(8,128)(2,1)S(1)}, u32[]{:S(2)}, u32[]{:S(2)}) collective-permute-start(bf16[4,256,128]{2,1,0:T(8,128)(2,1)S(1)} %get-tuple-element.55), channel_id=1, source_target_pairs={{0,6},{1,7},{2,4},{3,5},{4,2},{5,3},{6,0},{7,1},{8,14},{9,15},{10,... | collective-permute-start | bytes 786440 | tf_op jit(solution)/shard_map/ppermute | solution.py:366
  22.0 16.9 %collective-permute-start.12 = (bf16[3,256,128]{2,1,0:T(8,128)(2,1)S(1)}, bf16[3,256,128]{2,1,0:T(8,128)(2,1)S(1)}, u32[]{:S(2)}, u32[]{:S(2)}) collective-permute-start(bf16[3,256,128]{2,1,0:T(8,128)(2,1)S(1)} %get-tuple-element.54), channel_id=1, source_target_pairs={{0,12},{1,13},{2,14},{3,15},{4,8},{5,9},{6,10},{7,11},{8,4},{9,5},... | collective-permute-start | bytes 589832 | tf_op jit(solution)/shard_map/ppermute | solution.py:366
  26.2 17.4 %collective-permute-start.14 = (bf16[3,256,128]{2,1,0:T(8,128)(2,1)S(1)}, bf16[3,256,128]{2,1,0:T(8,128)(2,1)S(1)}, u32[]{:S(2)}, u32[]{:S(2)}) collective-permute-start(bf16[3,256,128]{2,1,0:T(8,128)(2,1)S(1)} %get-tuple-element.56), channel_id=1, source_target_pairs={{0,14},{1,15},{2,12},{3,13},{4,10},{5,11},{6,8},{7,9},{8,6},{9,7},... | collective-permute-start | bytes 589832 | tf_op jit(solution)/shard_map/ppermute | solution.py:366
  38.9 14.1 %collective-permute-start.1 = (bf16[1,256,128]{2,1,0:T(8,128)(2,1)S(1)}, bf16[1,256,128]{2,1,0:T(8,128)(2,1)S(1)}, u32[]{:S(2)}, u32[]{:S(2)}) collective-permute-start(bf16[1,256,128]{2,1,0:T(8,128)(2,1)S(1)} %get-tuple-element.45), channel_id=1, source_target_pairs={{0,8},{1,9},{2,10},{3,11},{4,12},{5,13},{6,14},{7,15},{8,0},{9,1},... | collective-permute-start | bytes 196616 | tf_op jit(solution)/shard_map/ppermute | solution.py:366
  43.6 9.4 %collective-permute-start.2 = (bf16[1,256,128]{2,1,0:T(8,128)(2,1)S(1)}, bf16[1,256,128]{2,1,0:T(8,128)(2,1)S(1)}, u32[]{:S(2)}, u32[]{:S(2)}) collective-permute-start(bf16[1,256,128]{2,1,0:T(8,128)(2,1)S(1)} %get-tuple-element.46), channel_id=1, source_target_pairs={{0,10},{1,11},{2,8},{3,9},{4,14},{5,15},{6,12},{7,13},{8,2},{9,3},... | collective-permute-start | bytes 196616 | tf_op jit(solution)/shard_map/ppermute | solution.py:366
  43.6 9.4 %collective-permute-start.3 = (bf16[1,256,128]{2,1,0:T(8,128)(2,1)S(1)}, bf16[1,256,128]{2,1,0:T(8,128)(2,1)S(1)}, u32[]{:S(2)}, u32[]{:S(2)}) collective-permute-start(bf16[1,256,128]{2,1,0:T(8,128)(2,1)S(1)} %get-tuple-element.47), channel_id=1, source_target_pairs={{0,12},{1,13},{2,14},{3,15},{4,8},{5,9},{6,10},{7,11},{8,4},{9,5},... | collective-permute-start | bytes 196616 | tf_op jit(solution)/shard_map/ppermute | solution.py:366
  47.6 8.6 %collective-permute-start.4 = (bf16[1,256,128]{2,1,0:T(8,128)(2,1)S(1)}, bf16[1,256,128]{2,1,0:T(8,128)(2,1)S(1)}, u32[]{:S(2)}, u32[]{:S(2)}) collective-permute-start(bf16[1,256,128]{2,1,0:T(8,128)(2,1)S(1)} %get-tuple-element.48), channel_id=1, source_target_pairs={{0,14},{1,15},{2,12},{3,13},{4,10},{5,11},{6,8},{7,9},{8,6},{9,7},... | collective-permute-start | bytes 196616 | tf_op jit(solution)/shard_map/ppermute | solution.py:366
  56.2 11.0 %collective-permute-start.18 = (bf16[1,256,128]{2,1,0:T(8,128)(2,1)S(1)}, bf16[1,256,128]{2,1,0:T(8,128)(2,1)S(1)}, u32[]{:S(2)}, u32[]{:S(2)}) collective-permute-start(bf16[1,256,128]{2,1,0:T(8,128)(2,1)S(1)} %get-tuple-element.68), channel_id=1, source_target_pairs={{0,14},{1,15},{2,12},{3,13},{4,10},{5,11},{6,8},{7,9},{8,6},{9,7},... | collective-permute-start | bytes 196616 | tf_op jit(solution)/shard_map/ppermute | solution.py:366
  56.2 11.1 %collective-permute-start.17 = (bf16[1,256,128]{2,1,0:T(8,128)(2,1)S(1)}, bf16[1,256,128]{2,1,0:T(8,128)(2,1)S(1)}, u32[]{:S(2)}, u32[]{:S(2)}) collective-permute-start(bf16[1,256,128]{2,1,0:T(8,128)(2,1)S(1)} %get-tuple-element.66), channel_id=1, source_target_pairs={{0,12},{1,13},{2,14},{3,15},{4,8},{5,9},{6,10},{7,11},{8,4},{9,5},... | collective-permute-start | bytes 196616 | tf_op jit(solution)/shard_map/ppermute | solution.py:366
  57.6 9.7 %collective-permute-start.16 = (bf16[1,256,128]{2,1,0:T(8,128)(2,1)S(1)}, bf16[1,256,128]{2,1,0:T(8,128)(2,1)S(1)}, u32[]{:S(2)}, u32[]{:S(2)}) collective-permute-start(bf16[1,256,128]{2,1,0:T(8,128)(2,1)S(1)} %get-tuple-element.64), channel_id=1, source_target_pairs={{0,10},{1,11},{2,8},{3,9},{4,14},{5,15},{6,12},{7,13},{8,2},{9,3},... | collective-permute-start | bytes 196616 | tf_op jit(solution)/shard_map/ppermute | solution.py:366
  61.5 7.7 %collective-permute-start.15 = (bf16[1,256,128]{2,1,0:T(8,128)(2,1)S(1)}, bf16[1,256,128]{2,1,0:T(8,128)(2,1)S(1)}, u32[]{:S(2)}, u32[]{:S(2)}) collective-permute-start(bf16[1,256,128]{2,1,0:T(8,128)(2,1)S(1)} %get-tuple-element.62), channel_id=1, source_target_pairs={{0,8},{1,9},{2,10},{3,11},{4,12},{5,13},{6,14},{7,15},{8,0},{9,1},... | collective-permute-start | bytes 196616 | tf_op jit(solution)/shard_map/ppermute | solution.py:366
  69.2 15.5 %collective-permute-start.19 = (bf16[3,256,128]{2,1,0:T(8,128)(2,1)S(1)}, bf16[3,256,128]{2,1,0:T(8,128)(2,1)S(1)}, u32[]{:S(2)}, u32[]{:S(2)}) collective-permute-start(bf16[3,256,128]{2,1,0:T(8,128)(2,1)S(1)} %get-tuple-element.69), channel_id=1, source_target_pairs={{0,8},{1,9},{2,10},{3,11},{4,12},{5,13},{6,14},{7,15},{8,0},{9,1},... | collective-permute-start | bytes 589832 | tf_op jit(solution)/shard_map/ppermute | solution.py:366
  72.4 16.5 %collective-permute-start.20 = (bf16[3,256,128]{2,1,0:T(8,128)(2,1)S(1)}, bf16[3,256,128]{2,1,0:T(8,128)(2,1)S(1)}, u32[]{:S(2)}, u32[]{:S(2)}) collective-permute-start(bf16[3,256,128]{2,1,0:T(8,128)(2,1)S(1)} %get-tuple-element.71), channel_id=1, source_target_pairs={{0,10},{1,11},{2,8},{3,9},{4,14},{5,15},{6,12},{7,13},{8,2},{9,3},... | collective-permute-start | bytes 589832 | tf_op jit(solution)/shard_map/ppermute | solution.py:366
  72.4 34.1 %collective-permute-start.22 = (bf16[4,256,128]{2,1,0:T(8,128)(2,1)S(1)}, bf16[4,256,128]{2,1,0:T(8,128)(2,1)S(1)}, u32[]{:S(2)}, u32[]{:S(2)}) collective-permute-start(bf16[4,256,128]{2,1,0:T(8,128)(2,1)S(1)} %get-tuple-element.76), channel_id=1, source_target_pairs={{0,2},{1,3},{2,0},{3,1},{4,6},{5,7},{6,4},{7,5},{8,10},{9,11},{10,... | collective-permute-start | bytes 786440 | tf_op jit(solution)/shard_map/ppermute | solution.py:366
  73.6 32.9 %collective-permute-start.23 = (bf16[4,256,128]{2,1,0:T(8,128)(2,1)S(1)}, bf16[4,256,128]{2,1,0:T(8,128)(2,1)S(1)}, u32[]{:S(2)}, u32[]{:S(2)}) collective-permute-start(bf16[4,256,128]{2,1,0:T(8,128)(2,1)S(1)} %get-tuple-element.78), channel_id=1, source_target_pairs={{0,4},{1,5},{2,6},{3,7},{4,0},{5,1},{6,2},{7,3},{8,12},{9,13},{10,... | collective-permute-start | bytes 786440 | tf_op jit(solution)/shard_map/ppermute | solution.py:366
  75.4 31.1 %collective-permute-start.24 = (bf16[4,256,128]{2,1,0:T(8,128)(2,1)S(1)}, bf16[4,256,128]{2,1,0:T(8,128)(2,1)S(1)}, u32[]{:S(2)}, u32[]{:S(2)}) collective-permute-start(bf16[4,256,128]{2,1,0:T(8,128)(2,1)S(1)} %get-tuple-element.80), channel_id=1, source_target_pairs={{0,6},{1,7},{2,4},{3,5},{4,2},{5,3},{6,0},{7,1},{8,14},{9,15},{10,... | collective-permute-start | bytes 786440 | tf_op jit(solution)/shard_map/ppermute | solution.py:366
  84.7 18.4 %collective-permute-start.21 = (bf16[3,256,128]{2,1,0:T(8,128)(2,1)S(1)}, bf16[3,256,128]{2,1,0:T(8,128)(2,1)S(1)}, u32[]{:S(2)}, u32[]{:S(2)}) collective-permute-start(bf16[3,256,128]{2,1,0:T(8,128)(2,1)S(1)} %get-tuple-element.73), channel_id=1, source_target_pairs={{0,12},{1,13},{2,14},{3,15},{4,8},{5,9},{6,10},{7,11},{8,4},{9,5},... | collective-permute-start | bytes 589832 | tf_op jit(solution)/shard_map/ppermute | solution.py:366
  88.9 17.6 %collective-permute-start.26 = (bf16[3,256,128]{2,1,0:T(8,128)(2,1)S(1)}, bf16[3,256,128]{2,1,0:T(8,128)(2,1)S(1)}, u32[]{:S(2)}, u32[]{:S(2)}) collective-permute-start(bf16[3,256,128]{2,1,0:T(8,128)(2,1)S(1)} %get-tuple-element.82), channel_id=1, source_target_pairs={{0,14},{1,15},{2,12},{3,13},{4,10},{5,11},{6,8},{7,9},{8,6},{9,7},... | collective-permute-start | bytes 589832 | tf_op jit(solution)/shard_map/ppermute | solution.py:366
  107.2 4.3 %collective-permute-start.27 = (bf16[8,3,128,128]{3,2,1,0:T(8,128)(2,1)S(1)}, bf16[8,3,128,128]{3,2,1,0:T(8,128)(2,1)S(1)}, u32[]{:S(2)}, u32[]{:S(2)}) collective-permute-start(bf16[8,3,128,128]{3,2,1,0:T(8,128)(2,1)S(1)} %shard_map.93), channel_id=1, source_target_pairs={{0,1},{1,0},{2,3},{3,2},{4,5},{5,4},{6,7},{7,6},{8,9},{9,8},{10,11... | collective-permute-start | bytes 2359304 | tf_op jit(solution)/shard_map/ppermute | solution.py:366
  108.3 1.7 %collective-permute-start.25 = (bf16[8,1,128,128]{3,2,1,0:T(8,128)(2,1)S(1)}, bf16[8,1,128,128]{3,2,1,0:T(8,128)(2,1)S(1)}, u32[]{:S(2)}, u32[]{:S(2)}) collective-permute-start(bf16[8,1,128,128]{3,2,1,0:T(8,128)(2,1)S(1)} %shard_map.91), channel_id=1, source_target_pairs={{0,1},{1,0},{2,3},{3,2},{4,5},{5,4},{6,7},{7,6},{8,9},{9,8},{10,11... | collective-permute-start | bytes 786440 | tf_op jit(solution)/shard_map/ppermute | solution.py:366

commit v5 on v4

--- a/solution.py
+++ b/solution.py
@@ -197,13 +197,27 @@
     rows = arrays[0].shape[0]
 
     def kernel(where, *refs):
+        out, sems = refs[count:]
+        copies = []
         for k in range(chips):
             column = pl.ds(pl.multiple_of(((where[0] ^ k) * 2 + where[1]) * HEAD, HEAD), HEAD)
             for i in range(count):
-                refs[count][k, i] = refs[i][:, column]
-
-    out = jax.ShapeDtypeStruct((chips, count, rows, HEAD), jnp.bfloat16)
-    return call(kernel, [place], arrays, [out])[0]
+                copies.append(
+                    pltpu.make_async_copy(refs[i].at[:, column], out.at[k, i], sems.at[k, i])
+                )
+        for copy in copies:
+            copy.start()
+        for copy in copies:
+            copy.wait()
+
+    return pl.pallas_call(
+        kernel,
+        out_shape=jax.ShapeDtypeStruct((chips, count, rows, HEAD), jnp.bfloat16),
+        in_specs=[pl.BlockSpec(memory_space=pltpu.SMEM)] + [pl.BlockSpec(memory_space=pltpu.HBM)] * count,
+        out_specs=pl.BlockSpec(memory_space=pltpu.VMEM),
+        scratch_shapes=[pltpu.SemaphoreType.DMA((chips, count))],
+        compiler_params=pltpu.CompilerParams(vmem_limit_bytes=40 * 1024 * 1024),
+    )(place, *[pltpu.with_memory_space_constraint(a, pltpu.HBM) for a in arrays])
 
 
 def pack(place, ks, keeps, theirs):

time: 115 us -> 113 us (0.983)
  local copies, waits for them, and re-layouts: 3.13 us -> 0.01 us
  Pallas kernels: 19.2 us -> 21.2 us
    pallas_call x0 -> x2, Pallas kernels: none -> 3.35 us  [own_columns(): pl.pallas_call(kernel, out_shape=jax.ShapeDtypeStruct((chips, count, rows...]
    unnamed x10 -> x2, local copies, waits for them, and re-layouts: 3.13 us -> 0.01 us
    pallas_call x11 -> x9, Pallas kernels: 19.2 us -> 17.8 us  [call(): pl.pallas_call(kernel, out_shape=out_shape, in_specs=[smem] * len(place)...]
  transfers between devices with their start and end apart: 28 -> 28, of which waited for: 11 -> 12; matrix products, arithmetic and copies ran while one was open for 0% -> 0% of each run, Pallas kernels for 15% -> 16%
where the time goes in v5:
time: 113 us; the launch traced here: 112 us
  waiting for transfers between devices  65.4 us (58%)
  starting transfers between devices  24.8 us (22%)
  Pallas kernels  21.2 us (19%)
    ppermute x28, waiting for transfers between devices, hop(): lax.ppermute(piece, 'ctx', [(i, i ^ distance) for i in range(devices)])  65.4 us
    ppermute x28, starting transfers between devices, hop(): lax.ppermute(piece, 'ctx', [(i, i ^ distance) for i in range(devices)])  24.8 us
    pallas_call x9, Pallas kernels, call(): pl.pallas_call(kernel, out_shape=out_shape, in_specs=[smem] * len(place)...  17.8 us
    pallas_call x2, Pallas kernels, own_columns(): pl.pallas_call(kernel, out_shape=jax.ShapeDtypeStruct((chips, count, rows...  3.35 us
  transfers between devices with their start and end apart: 28, of which 12 were waited for; matrix products, arithmetic and copies ran while one was open for 0% of the time, Pallas kernels for 16%

profile of v5, /device:TPU:9, one launch (start us, length us, event | category | flops | bytes accessed | tf_op | source)
XLA Modules:
  0.0 112.2 jit_solution(13353748474791125752)
XLA Ops:
  0.6 0.7 collective-permute-start.5
  1.4 0.1 collective-permute-start.6
  1.5 0.4 collective-permute-start.7
  1.9 0.1 collective-permute-start
  2.0 0.1 pad_add_fusion.where
  2.0 1.9 %shard_map.86.refs_0_ = bf16[8,3,128,128]{3,2,1,0:T(8,128)(2,1)S(1)} custom-call(s32[2]{0:T(128)S(1)} %pad_add_fusion.where, bf16[128,2048]{1,0:T(8,128)(2,1)} %refs_0_.3, bf16[128,2048]{1,0:T(8,128)(2,1)} %refs_1_.1, bf16[128,2048]{1,0:T(8,128)(2,1)} %refs_2_.1), custom_call_target="tpu_custom_call" | custom-call | tf_op jit(solution)/shard_map/pallas_call | solution.py:213
  3.9 0.0 collective-permute-done.5.refs_2_.refs_1_
  3.9 0.0 collective-permute-done.6.refs_3_.refs_2_
  3.9 0.7 collective-permute-done.7.refs_4_.refs_3_
  4.6 0.7 shard_map.88
  5.3 2.4 %collective-permute-start.9 = (bf16[3,256,128]{2,1,0:T(8,128)(2,1)S(1)}, bf16[3,256,128]{2,1,0:T(8,128)(2,1)S(1)}, u32[]{:S(2)}, u32[]{:S(2)}) collective-permute-start(bf16[3,256,128]{2,1,0:T(8,128)(2,1)S(1)} %get-tuple-element.51), channel_id=1, source_target_pairs={{0,8},{1,9},{2,10},{3,11},{4,12},{5,13},{6,14},{7,15},{8,0},{9,1},... | collective-permute-start | bytes 589832 | tf_op jit(solution)/shard_map/ppermute | solution.py:380
  7.7 1.0 collective-permute-start.10
  8.7 1.5 %shard_map.84.refs_0_.refs_1_ = bf16[8,1,128,128]{3,2,1,0:T(8,128)(2,1)S(1)} custom-call(s32[2]{0:T(128)S(1)} %pad_add_fusion.where, bf16[128,2048]{1,0:T(8,128)(2,1)} %refs_0_.2), custom_call_target="tpu_custom_call" | custom-call | tf_op jit(solution)/shard_map/pallas_call | solution.py:213
  10.2 0.0 collective-permute-done.refs_1_.refs_5_
  10.2 0.7 shard_map.87
  10.9 0.3 collective-permute-start.8
  11.2 0.2 collective-permute-start.11
  11.4 2.3 %collective-permute-start.13 = (bf16[4,256,128]{2,1,0:T(8,128)(2,1)S(1)}, bf16[4,256,128]{2,1,0:T(8,128)(2,1)S(1)}, u32[]{:S(2)}, u32[]{:S(2)}) collective-permute-start(bf16[4,256,128]{2,1,0:T(8,128)(2,1)S(1)} %get-tuple-element.55), channel_id=1, source_target_pairs={{0,6},{1,7},{2,4},{3,5},{4,2},{5,3},{6,0},{7,1},{8,14},{9,15},{10,... | collective-permute-start | bytes 786440 | tf_op jit(solution)/shard_map/ppermute | solution.py:380
  13.7 7.0 %collective-permute-done.9.refs_2_ = bf16[3,256,128]{2,1,0:T(8,128)(2,1)S(1)} collective-permute-done((bf16[3,256,128]{2,1,0:T(8,128)(2,1)S(1)}, bf16[3,256,128]{2,1,0:T(8,128)(2,1)S(1)}, u32[]{:S(2)}, u32[]{:S(2)}) %collective-permute-start.9) | collective-permute-done | bytes 196640 | tf_op jit(solution)/shard_map/ppermute | solution.py:380
  20.7 0.0 collective-permute-start.12
  20.7 4.2 %collective-permute-done.10.refs_3_ = bf16[3,256,128]{2,1,0:T(8,128)(2,1)S(1)} collective-permute-done((bf16[3,256,128]{2,1,0:T(8,128)(2,1)S(1)}, bf16[3,256,128]{2,1,0:T(8,128)(2,1)S(1)}, u32[]{:S(2)}, u32[]{:S(2)}) %collective-permute-start.10) | collective-permute-done | bytes 196640 | tf_op jit(solution)/shard_map/ppermute | solution.py:380
  24.9 0.0 collective-permute-start.14
  24.9 0.6 shard_map.85
  25.5 12.0 %collective-permute-done.12.refs_5_ = bf16[3,256,128]{2,1,0:T(8,128)(2,1)S(1)} collective-permute-done((bf16[3,256,128]{2,1,0:T(8,128)(2,1)S(1)}, bf16[3,256,128]{2,1,0:T(8,128)(2,1)S(1)}, u32[]{:S(2)}, u32[]{:S(2)}) %collective-permute-start.12) | collective-permute-done | bytes 196640 | tf_op jit(solution)/shard_map/ppermute | solution.py:380
  37.5 0.0 collective-permute-start.1
  37.5 4.8 %collective-permute-done.14.refs_7_ = bf16[3,256,128]{2,1,0:T(8,128)(2,1)S(1)} collective-permute-done((bf16[3,256,128]{2,1,0:T(8,128)(2,1)S(1)}, bf16[3,256,128]{2,1,0:T(8,128)(2,1)S(1)}, u32[]{:S(2)}, u32[]{:S(2)}) %collective-permute-start.14) | collective-permute-done | bytes 196640 | tf_op jit(solution)/shard_map/ppermute | solution.py:380
  42.3 0.0 collective-permute-start.2
  42.3 0.0 collective-permute-done.8.refs_1_
  42.3 4.0 %collective-permute-start.3 = (bf16[1,256,128]{2,1,0:T(8,128)(2,1)S(1)}, bf16[1,256,128]{2,1,0:T(8,128)(2,1)S(1)}, u32[]{:S(2)}, u32[]{:S(2)}) collective-permute-start(bf16[1,256,128]{2,1,0:T(8,128)(2,1)S(1)} %get-tuple-element.47), channel_id=1, source_target_pairs={{0,12},{1,13},{2,14},{3,15},{4,8},{5,9},{6,10},{7,11},{8,4},{9,5},... | collective-permute-start | bytes 196616 | tf_op jit(solution)/shard_map/ppermute | solution.py:380
  46.3 0.0 collective-permute-done.11.refs_4_
  46.3 0.0 collective-permute-start.4
  46.3 0.0 collective-permute-done.13.refs_6_
  46.3 5.3 %shard_map.89 = (bf16[1,256,128]{2,1,0:T(8,128)(2,1)S(1)}, bf16[1,256,128]{2,1,0:T(8,128)(2,1)S(1)}, bf16[1,256,128]{2,1,0:T(8,128)(2,1)S(1)}, bf16[1,256,128]{2...) custom-call(s32[2]{0:T(128)S(1)} %pad_add_fusion.where, s32[8]{0:T(128)S(1)} %copy-done, ...), custom_call_target="tpu_custom_call" | custom-call | flops 536870912 | bytes 8912896 | tf_op jit(solution)/shard_map/pallas_call | solution.py:183
  51.7 0.0 collective-permute-done.1.refs_0_
  51.7 0.0 collective-permute-done.2.refs_1_
  51.7 0.0 collective-permute-done.3.refs_2_
  51.7 3.2 %collective-permute-done.4.refs_3_ = bf16[1,256,128]{2,1,0:T(8,128)(2,1)S(1)} collective-permute-done((bf16[1,256,128]{2,1,0:T(8,128)(2,1)S(1)}, bf16[1,256,128]{2,1,0:T(8,128)(2,1)S(1)}, u32[]{:S(2)}, u32[]{:S(2)}) %collective-permute-start.4) | collective-permute-done | bytes 65568 | tf_op jit(solution)/shard_map/ppermute | solution.py:380
  54.9 0.0 collective-permute-start.18
  54.9 1.4 %collective-permute-start.17 = (bf16[1,256,128]{2,1,0:T(8,128)(2,1)S(1)}, bf16[1,256,128]{2,1,0:T(8,128)(2,1)S(1)}, u32[]{:S(2)}, u32[]{:S(2)}) collective-permute-start(bf16[1,256,128]{2,1,0:T(8,128)(2,1)S(1)} %get-tuple-element.66), channel_id=1, source_target_pairs={{0,12},{1,13},{2,14},{3,15},{4,8},{5,9},{6,10},{7,11},{8,4},{9,5},... | collective-permute-start | bytes 196616 | tf_op jit(solution)/shard_map/ppermute | solution.py:380
  56.3 3.9 %collective-permute-start.16 = (bf16[1,256,128]{2,1,0:T(8,128)(2,1)S(1)}, bf16[1,256,128]{2,1,0:T(8,128)(2,1)S(1)}, u32[]{:S(2)}, u32[]{:S(2)}) collective-permute-start(bf16[1,256,128]{2,1,0:T(8,128)(2,1)S(1)} %get-tuple-element.64), channel_id=1, source_target_pairs={{0,10},{1,11},{2,8},{3,9},{4,14},{5,15},{6,12},{7,13},{8,2},{9,3},... | collective-permute-start | bytes 196616 | tf_op jit(solution)/shard_map/ppermute | solution.py:380
  60.1 0.0 collective-permute-start.15
  60.1 5.8 %shard_map.90 = (bf16[4,256,128]{2,1,0:T(8,128)(2,1)S(1)}, bf16[4,256,128]{2,1,0:T(8,128)(2,1)S(1)}, bf16[4,256,128]{2,1,0:T(8,128)(2,1)S(1)}, bf16[4,256,128]{2...) custom-call(s32[2]{0:T(128)S(1)} %pad_add_fusion.where, ...), custom_call_target="tpu_custom_call" | custom-call | flops 1073741824 | bytes 8912896 | tf_op jit(solution)/shard_map/pallas_call | solution.py:183
  65.9 0.0 collective-permute-done.18.refs_7_
  66.0 0.0 collective-permute-done.16.refs_3_
  66.0 1.9 %collective-permute-done.15.refs_2_ = bf16[1,256,128]{2,1,0:T(8,128)(2,1)S(1)} collective-permute-done((bf16[1,256,128]{2,1,0:T(8,128)(2,1)S(1)}, bf16[1,256,128]{2,1,0:T(8,128)(2,1)S(1)}, u32[]{:S(2)}, u32[]{:S(2)}) %collective-permute-start.15) | collective-permute-done | bytes 65568 | tf_op jit(solution)/shard_map/ppermute | solution.py:380
  67.9 3.2 %collective-permute-start.19 = (bf16[3,256,128]{2,1,0:T(8,128)(2,1)S(1)}, bf16[3,256,128]{2,1,0:T(8,128)(2,1)S(1)}, u32[]{:S(2)}, u32[]{:S(2)}) collective-permute-start(bf16[3,256,128]{2,1,0:T(8,128)(2,1)S(1)} %get-tuple-element.69), channel_id=1, source_target_pairs={{0,8},{1,9},{2,10},{3,11},{4,12},{5,13},{6,14},{7,15},{8,0},{9,1},... | collective-permute-start | bytes 589832 | tf_op jit(solution)/shard_map/ppermute | solution.py:380
  71.1 0.0 collective-permute-start.20
  71.1 1.2 %collective-permute-start.22 = (bf16[4,256,128]{2,1,0:T(8,128)(2,1)S(1)}, bf16[4,256,128]{2,1,0:T(8,128)(2,1)S(1)}, u32[]{:S(2)}, u32[]{:S(2)}) collective-permute-start(bf16[4,256,128]{2,1,0:T(8,128)(2,1)S(1)} %get-tuple-element.76), channel_id=1, source_target_pairs={{0,2},{1,3},{2,0},{3,1},{4,6},{5,7},{6,4},{7,5},{8,10},{9,11},{10,... | collective-permute-start | bytes 786440 | tf_op jit(solution)/shard_map/ppermute | solution.py:380
  72.3 1.8 %collective-permute-start.23 = (bf16[4,256,128]{2,1,0:T(8,128)(2,1)S(1)}, bf16[4,256,128]{2,1,0:T(8,128)(2,1)S(1)}, u32[]{:S(2)}, u32[]{:S(2)}) collective-permute-start(bf16[4,256,128]{2,1,0:T(8,128)(2,1)S(1)} %get-tuple-element.78), channel_id=1, source_target_pairs={{0,4},{1,5},{2,6},{3,7},{4,0},{5,1},{6,2},{7,3},{8,12},{9,13},{10,... | collective-permute-start | bytes 786440 | tf_op jit(solution)/shard_map/ppermute | solution.py:380
  74.1 0.3 collective-permute-start.24
  74.4 9.0 %collective-permute-done.19.refs_2_ = bf16[3,256,128]{2,1,0:T(8,128)(2,1)S(1)} collective-permute-done((bf16[3,256,128]{2,1,0:T(8,128)(2,1)S(1)}, bf16[3,256,128]{2,1,0:T(8,128)(2,1)S(1)}, u32[]{:S(2)}, u32[]{:S(2)}) %collective-permute-start.19) | collective-permute-done | bytes 196640 | tf_op jit(solution)/shard_map/ppermute | solution.py:380
  83.4 0.8 collective-permute-start.21
  84.2 3.4 %collective-permute-done.20.refs_3_ = bf16[3,256,128]{2,1,0:T(8,128)(2,1)S(1)} collective-permute-done((bf16[3,256,128]{2,1,0:T(8,128)(2,1)S(1)}, bf16[3,256,128]{2,1,0:T(8,128)(2,1)S(1)}, u32[]{:S(2)}, u32[]{:S(2)}) %collective-permute-start.20) | collective-permute-done | bytes 196640 | tf_op jit(solution)/shard_map/ppermute | solution.py:380
  87.6 0.0 collective-permute-start.26
  87.6 14.2 %collective-permute-done.21.refs_5_ = bf16[3,256,128]{2,1,0:T(8,128)(2,1)S(1)} collective-permute-done((bf16[3,256,128]{2,1,0:T(8,128)(2,1)S(1)}, bf16[3,256,128]{2,1,0:T(8,128)(2,1)S(1)}, u32[]{:S(2)}, u32[]{:S(2)}) %collective-permute-start.21) | collective-permute-done | bytes 196640 | tf_op jit(solution)/shard_map/ppermute | solution.py:380
  101.8 3.4 %collective-permute-done.26.refs_7_ = bf16[3,256,128]{2,1,0:T(8,128)(2,1)S(1)} collective-permute-done((bf16[3,256,128]{2,1,0:T(8,128)(2,1)S(1)}, bf16[3,256,128]{2,1,0:T(8,128)(2,1)S(1)}, u32[]{:S(2)}, u32[]{:S(2)}) %collective-permute-start.26) | collective-permute-done | bytes 196640 | tf_op jit(solution)/shard_map/ppermute | solution.py:380
  105.2 0.0 collective-permute-done.22.refs_1_
  105.2 0.6 shard_map.93
  105.8 0.6 collective-permute-start.27
  106.4 0.6 shard_map.91
  106.9 0.1 collective-permute-start.25
  107.0 1.6 %collective-permute-done.25.refs_8_ = bf16[8,1,128,128]{3,2,1,0:T(8,128)(2,1)S(1)} collective-permute-done((bf16[8,1,128,128]{3,2,1,0:T(8,128)(2,1)S(1)}, bf16[8,1,128,128]{3,2,1,0:T(8,128)(2,1)S(1)}, u32[]{:S(2)}, u32[]{:S(2)}) %collective-permute-start.25) | collective-permute-done | bytes 262176 | tf_op jit(solution)/shard_map/ppermute | solution.py:380
  108.7 1.5 %shard_map.92 = bf16[128,2048]{1,0:T(8,128)(2,1)} custom-call(s32[2]{0:T(128)S(1)} %pad_add_fusion.where, bf16[4,256,128]{2,1,0:T(8,128)(2,1)S(1)} %get-tuple-element.74.refs_0_, bf16[4,256,128]{2,1,0:T(8,128)(2,1)S(1)} %collective-permute-done.22.refs_1_, bf16[1,256,128]{2,1,0:T(8,128)(2,1)S(1)} %collective-permute-done.15.refs_2_, ...), custom_call_target="tpu_custom_call" | custom-call | bytes 2097152 | tf_op jit(solution)/shard_map/pallas_call | solution.py:183
  110.1 2.1 %shard_map.94 = (bf16[128,2048]{1,0:T(8,128)(2,1)}, bf16[128,2048]{1,0:T(8,128)(2,1)}, bf16[128,2048]{1,0:T(8,128)(2,1)}) custom-call(s32[2]{0:T(128)S(1)} %pad_add_fusion.where, bf16[4,256,128]{2,1,0:T(8,128)(2,1)S(1)} %get-tuple-element.74.refs_0_, bf16[4,256,128]{2,1,0:T(8,128)(2,1)S(1)} %collective-permute-done.22.refs_1_, ...), custom_call_target="tpu_custom_call" | custom-call | bytes 4194304 | tf_op jit(solution)/shard_map/pallas_call | solution.py:183
  (6 shorter events, 0.0 us)
Async XLA Ops:
  0.6 3.3 %collective-permute-start.5 = (bf16[128,2048]{1,0:T(8,128)(2,1)}, bf16[128,2048]{1,0:T(8,128)(2,1)S(1)}, u32[]{:S(2)}, u32[]{:S(2)}) collective-permute-start(bf16[128,2048]{1,0:T(8,128)(2,1)} %refs_0_.3), channel_id=1, source_target_pairs={{0,1},{1,0},{2,3},{3,2},{4,5},{5,4},{6,7},{7,6},{8,9},{9,8},{10,11... | collective-permute-start | bytes 1572872 | tf_op jit(solution)/shard_map/ppermute | solution.py:380
  1.4 2.6 %collective-permute-start.6 = (bf16[128,2048]{1,0:T(8,128)(2,1)}, bf16[128,2048]{1,0:T(8,128)(2,1)S(1)}, u32[]{:S(2)}, u32[]{:S(2)}) collective-permute-start(bf16[128,2048]{1,0:T(8,128)(2,1)} %refs_1_.1), channel_id=1, source_target_pairs={{0,1},{1,0},{2,3},{3,2},{4,5},{5,4},{6,7},{7,6},{8,9},{9,8},{10,11... | collective-permute-start | bytes 1572872 | tf_op jit(solution)/shard_map/ppermute | solution.py:380
  1.5 3.2 %collective-permute-start.7 = (bf16[128,2048]{1,0:T(8,128)(2,1)}, bf16[128,2048]{1,0:T(8,128)(2,1)S(1)}, u32[]{:S(2)}, u32[]{:S(2)}) collective-permute-start(bf16[128,2048]{1,0:T(8,128)(2,1)} %refs_2_.1), channel_id=1, source_target_pairs={{0,1},{1,0},{2,3},{3,2},{4,5},{5,4},{6,7},{7,6},{8,9},{9,8},{10,11... | collective-permute-start | bytes 1572872 | tf_op jit(solution)/shard_map/ppermute | solution.py:380
  1.9 8.3 %collective-permute-start = (bf16[128,2048]{1,0:T(8,128)(2,1)}, bf16[128,2048]{1,0:T(8,128)(2,1)S(1)}, u32[]{:S(2)}, u32[]{:S(2)}) collective-permute-start(bf16[128,2048]{1,0:T(8,128)(2,1)} %refs_0_.2), channel_id=1, source_target_pairs={{0,1},{1,0},{2,3},{3,2},{4,5},{5,4},{6,7},{7,6},{8,9},{9,8},{10,11... | collective-permute-start | bytes 1572872 | tf_op jit(solution)/shard_map/ppermute | solution.py:380
  2.0 44.3 %copy-start = (s32[8]{0:T(128)S(1)}, s32[8]{0:T(128)}, u32[]{:S(2)}) copy-start(s32[8]{0:T(128)} %partner.3) | copy-start | bytes 100
  5.3 15.4 %collective-permute-start.9 = (bf16[3,256,128]{2,1,0:T(8,128)(2,1)S(1)}, bf16[3,256,128]{2,1,0:T(8,128)(2,1)S(1)}, u32[]{:S(2)}, u32[]{:S(2)}) collective-permute-start(bf16[3,256,128]{2,1,0:T(8,128)(2,1)S(1)} %get-tuple-element.51), channel_id=1, source_target_pairs={{0,8},{1,9},{2,10},{3,11},{4,12},{5,13},{6,14},{7,15},{8,0},{9,1},... | collective-permute-start | bytes 589832 | tf_op jit(solution)/shard_map/ppermute | solution.py:380
  7.7 17.2 %collective-permute-start.10 = (bf16[3,256,128]{2,1,0:T(8,128)(2,1)S(1)}, bf16[3,256,128]{2,1,0:T(8,128)(2,1)S(1)}, u32[]{:S(2)}, u32[]{:S(2)}) collective-permute-start(bf16[3,256,128]{2,1,0:T(8,128)(2,1)S(1)} %get-tuple-element.52), channel_id=1, source_target_pairs={{0,10},{1,11},{2,8},{3,9},{4,14},{5,15},{6,12},{7,13},{8,2},{9,3},... | collective-permute-start | bytes 589832 | tf_op jit(solution)/shard_map/ppermute | solution.py:380
  10.9 31.4 %collective-permute-start.8 = (bf16[4,256,128]{2,1,0:T(8,128)(2,1)S(1)}, bf16[4,256,128]{2,1,0:T(8,128)(2,1)S(1)}, u32[]{:S(2)}, u32[]{:S(2)}) collective-permute-start(bf16[4,256,128]{2,1,0:T(8,128)(2,1)S(1)} %get-tuple-element.50), channel_id=1, source_target_pairs={{0,2},{1,3},{2,0},{3,1},{4,6},{5,7},{6,4},{7,5},{8,10},{9,11},{10,... | collective-permute-start | bytes 786440 | tf_op jit(solution)/shard_map/ppermute | solution.py:380
  11.2 35.1 %collective-permute-start.11 = (bf16[4,256,128]{2,1,0:T(8,128)(2,1)S(1)}, bf16[4,256,128]{2,1,0:T(8,128)(2,1)S(1)}, u32[]{:S(2)}, u32[]{:S(2)}) collective-permute-start(bf16[4,256,128]{2,1,0:T(8,128)(2,1)S(1)} %get-tuple-element.53), channel_id=1, source_target_pairs={{0,4},{1,5},{2,6},{3,7},{4,0},{5,1},{6,2},{7,3},{8,12},{9,13},{10,... | collective-permute-start | bytes 786440 | tf_op jit(solution)/shard_map/ppermute | solution.py:380
  11.4 34.9 %collective-permute-start.13 = (bf16[4,256,128]{2,1,0:T(8,128)(2,1)S(1)}, bf16[4,256,128]{2,1,0:T(8,128)(2,1)S(1)}, u32[]{:S(2)}, u32[]{:S(2)}) collective-permute-start(bf16[4,256,128]{2,1,0:T(8,128)(2,1)S(1)} %get-tuple-element.55), channel_id=1, source_target_pairs={{0,6},{1,7},{2,4},{3,5},{4,2},{5,3},{6,0},{7,1},{8,14},{9,15},{10,... | collective-permute-start | bytes 786440 | tf_op jit(solution)/shard_map/ppermute | solution.py:380
  20.7 16.9 %collective-permute-start.12 = (bf16[3,256,128]{2,1,0:T(8,128)(2,1)S(1)}, bf16[3,256,128]{2,1,0:T(8,128)(2,1)S(1)}, u32[]{:S(2)}, u32[]{:S(2)}) collective-permute-start(bf16[3,256,128]{2,1,0:T(8,128)(2,1)S(1)} %get-tuple-element.54), channel_id=1, source_target_pairs={{0,12},{1,13},{2,14},{3,15},{4,8},{5,9},{6,10},{7,11},{8,4},{9,5},... | collective-permute-start | bytes 589832 | tf_op jit(solution)/shard_map/ppermute | solution.py:380
  24.9 17.4 %collective-permute-start.14 = (bf16[3,256,128]{2,1,0:T(8,128)(2,1)S(1)}, bf16[3,256,128]{2,1,0:T(8,128)(2,1)S(1)}, u32[]{:S(2)}, u32[]{:S(2)}) collective-permute-start(bf16[3,256,128]{2,1,0:T(8,128)(2,1)S(1)} %get-tuple-element.56), channel_id=1, source_target_pairs={{0,14},{1,15},{2,12},{3,13},{4,10},{5,11},{6,8},{7,9},{8,6},{9,7},... | collective-permute-start | bytes 589832 | tf_op jit(solution)/shard_map/ppermute | solution.py:380
  37.5 14.1 %collective-permute-start.1 = (bf16[1,256,128]{2,1,0:T(8,128)(2,1)S(1)}, bf16[1,256,128]{2,1,0:T(8,128)(2,1)S(1)}, u32[]{:S(2)}, u32[]{:S(2)}) collective-permute-start(bf16[1,256,128]{2,1,0:T(8,128)(2,1)S(1)} %get-tuple-element.45), channel_id=1, source_target_pairs={{0,8},{1,9},{2,10},{3,11},{4,12},{5,13},{6,14},{7,15},{8,0},{9,1},... | collective-permute-start | bytes 196616 | tf_op jit(solution)/shard_map/ppermute | solution.py:380
  42.3 9.4 %collective-permute-start.2 = (bf16[1,256,128]{2,1,0:T(8,128)(2,1)S(1)}, bf16[1,256,128]{2,1,0:T(8,128)(2,1)S(1)}, u32[]{:S(2)}, u32[]{:S(2)}) collective-permute-start(bf16[1,256,128]{2,1,0:T(8,128)(2,1)S(1)} %get-tuple-element.46), channel_id=1, source_target_pairs={{0,10},{1,11},{2,8},{3,9},{4,14},{5,15},{6,12},{7,13},{8,2},{9,3},... | collective-permute-start | bytes 196616 | tf_op jit(solution)/shard_map/ppermute | solution.py:380
  42.3 9.4 %collective-permute-start.3 = (bf16[1,256,128]{2,1,0:T(8,128)(2,1)S(1)}, bf16[1,256,128]{2,1,0:T(8,128)(2,1)S(1)}, u32[]{:S(2)}, u32[]{:S(2)}) collective-permute-start(bf16[1,256,128]{2,1,0:T(8,128)(2,1)S(1)} %get-tuple-element.47), channel_id=1, source_target_pairs={{0,12},{1,13},{2,14},{3,15},{4,8},{5,9},{6,10},{7,11},{8,4},{9,5},... | collective-permute-start | bytes 196616 | tf_op jit(solution)/shard_map/ppermute | solution.py:380
  46.3 8.6 %collective-permute-start.4 = (bf16[1,256,128]{2,1,0:T(8,128)(2,1)S(1)}, bf16[1,256,128]{2,1,0:T(8,128)(2,1)S(1)}, u32[]{:S(2)}, u32[]{:S(2)}) collective-permute-start(bf16[1,256,128]{2,1,0:T(8,128)(2,1)S(1)} %get-tuple-element.48), channel_id=1, source_target_pairs={{0,14},{1,15},{2,12},{3,13},{4,10},{5,11},{6,8},{7,9},{8,6},{9,7},... | collective-permute-start | bytes 196616 | tf_op jit(solution)/shard_map/ppermute | solution.py:380
  54.9 11.0 %collective-permute-start.18 = (bf16[1,256,128]{2,1,0:T(8,128)(2,1)S(1)}, bf16[1,256,128]{2,1,0:T(8,128)(2,1)S(1)}, u32[]{:S(2)}, u32[]{:S(2)}) collective-permute-start(bf16[1,256,128]{2,1,0:T(8,128)(2,1)S(1)} %get-tuple-element.68), channel_id=1, source_target_pairs={{0,14},{1,15},{2,12},{3,13},{4,10},{5,11},{6,8},{7,9},{8,6},{9,7},... | collective-permute-start | bytes 196616 | tf_op jit(solution)/shard_map/ppermute | solution.py:380
  54.9 11.1 %collective-permute-start.17 = (bf16[1,256,128]{2,1,0:T(8,128)(2,1)S(1)}, bf16[1,256,128]{2,1,0:T(8,128)(2,1)S(1)}, u32[]{:S(2)}, u32[]{:S(2)}) collective-permute-start(bf16[1,256,128]{2,1,0:T(8,128)(2,1)S(1)} %get-tuple-element.66), channel_id=1, source_target_pairs={{0,12},{1,13},{2,14},{3,15},{4,8},{5,9},{6,10},{7,11},{8,4},{9,5},... | collective-permute-start | bytes 196616 | tf_op jit(solution)/shard_map/ppermute | solution.py:380
  56.3 9.7 %collective-permute-start.16 = (bf16[1,256,128]{2,1,0:T(8,128)(2,1)S(1)}, bf16[1,256,128]{2,1,0:T(8,128)(2,1)S(1)}, u32[]{:S(2)}, u32[]{:S(2)}) collective-permute-start(bf16[1,256,128]{2,1,0:T(8,128)(2,1)S(1)} %get-tuple-element.64), channel_id=1, source_target_pairs={{0,10},{1,11},{2,8},{3,9},{4,14},{5,15},{6,12},{7,13},{8,2},{9,3},... | collective-permute-start | bytes 196616 | tf_op jit(solution)/shard_map/ppermute | solution.py:380
  60.1 7.7 %collective-permute-start.15 = (bf16[1,256,128]{2,1,0:T(8,128)(2,1)S(1)}, bf16[1,256,128]{2,1,0:T(8,128)(2,1)S(1)}, u32[]{:S(2)}, u32[]{:S(2)}) collective-permute-start(bf16[1,256,128]{2,1,0:T(8,128)(2,1)S(1)} %get-tuple-element.62), channel_id=1, source_target_pairs={{0,8},{1,9},{2,10},{3,11},{4,12},{5,13},{6,14},{7,15},{8,0},{9,1},... | collective-permute-start | bytes 196616 | tf_op jit(solution)/shard_map/ppermute | solution.py:380
  67.9 15.5 %collective-permute-start.19 = (bf16[3,256,128]{2,1,0:T(8,128)(2,1)S(1)}, bf16[3,256,128]{2,1,0:T(8,128)(2,1)S(1)}, u32[]{:S(2)}, u32[]{:S(2)}) collective-permute-start(bf16[3,256,128]{2,1,0:T(8,128)(2,1)S(1)} %get-tuple-element.69), channel_id=1, source_target_pairs={{0,8},{1,9},{2,10},{3,11},{4,12},{5,13},{6,14},{7,15},{8,0},{9,1},... | collective-permute-start | bytes 589832 | tf_op jit(solution)/shard_map/ppermute | solution.py:380
  71.1 16.5 %collective-permute-start.20 = (bf16[3,256,128]{2,1,0:T(8,128)(2,1)S(1)}, bf16[3,256,128]{2,1,0:T(8,128)(2,1)S(1)}, u32[]{:S(2)}, u32[]{:S(2)}) collective-permute-start(bf16[3,256,128]{2,1,0:T(8,128)(2,1)S(1)} %get-tuple-element.71), channel_id=1, source_target_pairs={{0,10},{1,11},{2,8},{3,9},{4,14},{5,15},{6,12},{7,13},{8,2},{9,3},... | collective-permute-start | bytes 589832 | tf_op jit(solution)/shard_map/ppermute | solution.py:380
  71.1 34.1 %collective-permute-start.22 = (bf16[4,256,128]{2,1,0:T(8,128)(2,1)S(1)}, bf16[4,256,128]{2,1,0:T(8,128)(2,1)S(1)}, u32[]{:S(2)}, u32[]{:S(2)}) collective-permute-start(bf16[4,256,128]{2,1,0:T(8,128)(2,1)S(1)} %get-tuple-element.76), channel_id=1, source_target_pairs={{0,2},{1,3},{2,0},{3,1},{4,6},{5,7},{6,4},{7,5},{8,10},{9,11},{10,... | collective-permute-start | bytes 786440 | tf_op jit(solution)/shard_map/ppermute | solution.py:380
  72.3 32.9 %collective-permute-start.23 = (bf16[4,256,128]{2,1,0:T(8,128)(2,1)S(1)}, bf16[4,256,128]{2,1,0:T(8,128)(2,1)S(1)}, u32[]{:S(2)}, u32[]{:S(2)}) collective-permute-start(bf16[4,256,128]{2,1,0:T(8,128)(2,1)S(1)} %get-tuple-element.78), channel_id=1, source_target_pairs={{0,4},{1,5},{2,6},{3,7},{4,0},{5,1},{6,2},{7,3},{8,12},{9,13},{10,... | collective-permute-start | bytes 786440 | tf_op jit(solution)/shard_map/ppermute | solution.py:380
  74.1 31.1 %collective-permute-start.24 = (bf16[4,256,128]{2,1,0:T(8,128)(2,1)S(1)}, bf16[4,256,128]{2,1,0:T(8,128)(2,1)S(1)}, u32[]{:S(2)}, u32[]{:S(2)}) collective-permute-start(bf16[4,256,128]{2,1,0:T(8,128)(2,1)S(1)} %get-tuple-element.80), channel_id=1, source_target_pairs={{0,6},{1,7},{2,4},{3,5},{4,2},{5,3},{6,0},{7,1},{8,14},{9,15},{10,... | collective-permute-start | bytes 786440 | tf_op jit(solution)/shard_map/ppermute | solution.py:380
  83.4 18.4 %collective-permute-start.21 = (bf16[3,256,128]{2,1,0:T(8,128)(2,1)S(1)}, bf16[3,256,128]{2,1,0:T(8,128)(2,1)S(1)}, u32[]{:S(2)}, u32[]{:S(2)}) collective-permute-start(bf16[3,256,128]{2,1,0:T(8,128)(2,1)S(1)} %get-tuple-element.73), channel_id=1, source_target_pairs={{0,12},{1,13},{2,14},{3,15},{4,8},{5,9},{6,10},{7,11},{8,4},{9,5},... | collective-permute-start | bytes 589832 | tf_op jit(solution)/shard_map/ppermute | solution.py:380
  87.6 17.6 %collective-permute-start.26 = (bf16[3,256,128]{2,1,0:T(8,128)(2,1)S(1)}, bf16[3,256,128]{2,1,0:T(8,128)(2,1)S(1)}, u32[]{:S(2)}, u32[]{:S(2)}) collective-permute-start(bf16[3,256,128]{2,1,0:T(8,128)(2,1)S(1)} %get-tuple-element.82), channel_id=1, source_target_pairs={{0,14},{1,15},{2,12},{3,13},{4,10},{5,11},{6,8},{7,9},{8,6},{9,7},... | collective-permute-start | bytes 589832 | tf_op jit(solution)/shard_map/ppermute | solution.py:380
  105.8 4.3 %collective-permute-start.27 = (bf16[8,3,128,128]{3,2,1,0:T(8,128)(2,1)S(1)}, bf16[8,3,128,128]{3,2,1,0:T(8,128)(2,1)S(1)}, u32[]{:S(2)}, u32[]{:S(2)}) collective-permute-start(bf16[8,3,128,128]{3,2,1,0:T(8,128)(2,1)S(1)} %shard_map.93), channel_id=1, source_target_pairs={{0,1},{1,0},{2,3},{3,2},{4,5},{5,4},{6,7},{7,6},{8,9},{9,8},{10,11... | collective-permute-start | bytes 2359304 | tf_op jit(solution)/shard_map/ppermute | solution.py:380
  106.9 1.7 %collective-permute-start.25 = (bf16[8,1,128,128]{3,2,1,0:T(8,128)(2,1)S(1)}, bf16[8,1,128,128]{3,2,1,0:T(8,128)(2,1)S(1)}, u32[]{:S(2)}, u32[]{:S(2)}) collective-permute-start(bf16[8,1,128,128]{3,2,1,0:T(8,128)(2,1)S(1)} %shard_map.91), channel_id=1, source_target_pairs={{0,1},{1,0},{2,3},{3,2},{4,5},{5,4},{6,7},{7,6},{8,9},{9,8},{10,11... | collective-permute-start | bytes 786440 | tf_op jit(solution)/shard_map/ppermute | solution.py:380

commit v6 on v5

--- a/solution.py
+++ b/solution.py
@@ -220,6 +220,44 @@
     )(place, *[pltpu.with_memory_space_constraint(a, pltpu.HBM) for a in arrays])
 
 
+def own_rows(place, k, arrays):
+    count = len(arrays)
+    rows = arrays[0].shape[0]
+    span = 2 * HEAD
+
+    def kernel(where, *refs):
+        out, sems = refs[count:]
+        column = pl.ds(pl.multiple_of((where[0] ^ k) * span, span), span)
+        copies = [
+            pltpu.make_async_copy(refs[i].at[:, column], out.at[i], sems.at[i])
+            for i in range(count)
+        ]
+        for copy in copies:
+            copy.start()
+        for copy in copies:
+            copy.wait()
+
+    return pl.pallas_call(
+        kernel,
+        out_shape=jax.ShapeDtypeStruct((count, rows, span), jnp.bfloat16),
+        in_specs=[pl.BlockSpec(memory_space=pltpu.SMEM)]
+        + [pl.BlockSpec(memory_space=pltpu.HBM)] * count,
+        out_specs=pl.BlockSpec(memory_space=pltpu.VMEM),
+        scratch_shapes=[pltpu.SemaphoreType.DMA((count,))],
+        compiler_params=pltpu.CompilerParams(vmem_limit_bytes=40 * 1024 * 1024),
+    )(place, *[pltpu.with_memory_space_constraint(a, pltpu.HBM) for a in arrays])
+
+
+def other_head(place, piece):
+    count, rows, _ = piece.shape
+
+    def kernel(where, piece, out):
+        out[...] = piece[:, :, pl.ds(pl.multiple_of((1 - where[1]) * HEAD, HEAD), HEAD)]
+
+    out = jax.ShapeDtypeStruct((count, rows, HEAD), jnp.bfloat16)
+    return call(kernel, [place], [piece], [out])[0]
+
+
 def pack(place, ks, keeps, theirs):
     rows = keeps[0].shape[2]
     count = len(theirs)
@@ -253,25 +291,71 @@
     return call(kernel, [place], pieces, [out])[0]
 
 
-def unpack(place, ks, pieces, bases, count, batches):
+def unpack_once(place, ks, pieces, bases, got):
     chips = len(pieces)
     size = pieces[0].shape[1]
 
     def kernel(where, *refs):
         core = where[1]
         half = halves(where, size // 2)[0]
-        outs = refs[chips + len(batches) :]
-        got = [ref.at[n] for ref in refs[chips : chips + len(batches)] for n in range(ref.shape[0])]
         for n, k in enumerate(ks):
             start = (where[0] ^ k) * 2
             here = pl.ds(pl.multiple_of((start + core) * HEAD, HEAD), HEAD)
             there = pl.ds(pl.multiple_of((start + 1 - core) * HEAD, HEAD), HEAD)
+            refs[chips + 1][:, here] = refs[n][bases[n], half]
+            refs[chips + 1][:, there] = refs[chips][n, 0]
+
+    out = jax.ShapeDtypeStruct((size // 2, chips * 2 * HEAD), jnp.bfloat16)
+    return call(kernel, [place], [*pieces, got], [out])
+
+
+def scatter(place, ks, arrays, picks, other, results, width):
+    count = len(picks)
+    rows = arrays[0].shape[-2] if other else arrays[0].shape[-2] // 2
+    total = len(ks) * count
+
+    def kernel(where, *refs):
+        core = where[1]
+        half = halves(where, rows)[0]
+        outs, sems = refs[-1 - count : -1], refs[-1]
+        copies = []
+        for n, k in enumerate(ks):
+            head = (where[0] ^ k) * 2 + (1 - core if other else core)
+            column = pl.ds(pl.multiple_of(head * HEAD, HEAD), HEAD)
             for i in range(count):
-                outs[i][:, here] = refs[n][bases[n] + i, half]
-                outs[i][:, there] = got[n][i]
-
-    out = jax.ShapeDtypeStruct((size // 2, chips * 2 * HEAD), jnp.bfloat16)
-    return call(kernel, [place], [*pieces, *batches], [out] * count)
+                array, index = picks[i][n]
+                source = refs[array].at[index] if other else refs[array].at[index, half]
+                copies.append(
+                    pltpu.make_async_copy(source, outs[i].at[:, column], sems.at[n * count + i])
+                )
+        for copy in copies:
+            copy.start()
+        for copy in copies:
+            copy.wait()
+
+    smem = pl.BlockSpec(memory_space=pltpu.SMEM)
+    vmem = pl.BlockSpec(memory_space=pltpu.VMEM)
+    hbm = pl.BlockSpec(memory_space=pltpu.HBM)
+    out = jax.ShapeDtypeStruct((rows, width), jnp.bfloat16)
+    moved = 2 * count * len(ks) * rows * HEAD * 2
+    return pl.pallas_call(
+        kernel,
+        out_shape=[out] * count,
+        in_specs=[smem] + [vmem] * len(arrays) + [hbm] * len(results),
+        out_specs=[hbm] * count,
+        scratch_shapes=[pltpu.SemaphoreType.DMA((total,))],
+        input_output_aliases={1 + len(arrays) + i: i for i in range(len(results))},
+        compiler_params=pltpu.CompilerParams(vmem_limit_bytes=40 * 1024 * 1024),
+        cost_estimate=pl.CostEstimate(flops=0, bytes_accessed=moved, transcendentals=0),
+    )(place, *arrays, *results)
+
+
+def unpack(place, ks, pieces, bases, count, got):
+    width = len(ks) * 2 * HEAD
+    picks = [[(n, bases[n] + i) for n in range(len(ks))] for i in range(count)]
+    outs = scatter(place, ks, pieces, picks, False, [], width)
+    picks = [[(0, (n, i)) for n in range(len(ks))] for i in range(count)]
+    return scatter(place, ks, [got], picks, True, outs, width)
 
 
 def halves(where, rows):
@@ -281,13 +365,18 @@
     return here, there
 
 
-def forward(place, partner, ks, far, pieces):
-    chips = len(pieces)
+def forward(place, partner, ks, far, early, pieces):
+    chips = len(pieces) + 1
     size = pieces[0].shape[1]
 
-    def kernel(where, partner, *refs):
-        outs = refs[chips:-2]
+    def kernel(where, partner, mine, theirs, *refs):
+        outs = refs[len(pieces) : -2]
         held, weights = refs[-2:]
+        here, there = halves(where, size // 2)
+        column = pl.ds(pl.multiple_of(where[1] * HEAD, HEAD), HEAD)
+        for i in range(3):
+            held[where[0] ^ far[0], i, here] = mine[i, :, column]
+            held[where[0] ^ far[0], i, there] = theirs[i]
         for n, k in enumerate(ks):
             b = where[0] ^ k
             held[b, :3] = refs[n][:3]
@@ -318,7 +407,8 @@
         jax.ShapeDtypeStruct((chips, 2, size, size), jnp.float32),
     ]
     flops = chips * 8 * size * size * HEAD
-    outs = call(kernel, [place, partner], pieces, out_shape, (), flops, chips * 2 * size * size)
+    exps = chips * 2 * size * size
+    outs = call(kernel, [place, partner], [*early, *pieces], out_shape, (), flops, exps)
     return dict(zip(far, outs)), outs[-2], outs[-1]
 
 
@@ -391,15 +481,20 @@
 
     ins = [queries, keys, values]
     theirs = [hop(a, 1) for a in ins]
-    keep = own_columns(place, ins, chips)
-    one = pack(place, far, [keep], theirs)
+    early = own_rows(place, far[0], ins)
+    keep = own_columns(after(place, early), ins, chips)
+    one = pack(place, far[1:], [keep], theirs)
     their_do = hop(cotangent, 1)
     keep_do = own_columns(place, [cotangent], chips)
     one |= pack(place, [0, *near], [keep, keep_do], [*theirs, their_do])
     two = pack(place, far, [keep_do], [their_do])
-    first = {0: one[0]} | to_chips(one, far + near)
+    first = {0: one[0]} | to_chips(one, far[1:] + near)
     second = to_chips(two, far)
-    three, held, weights = forward(place, partner, ks, far, in_order(first))
+    early = hop(early, 2 * far[0])
+    early = [early, hop(other_head(after(place, first[far[2]]), early), 1)]
+    later = [k for k in ks if k != far[0]]
+    first = [first[k] for k in later]
+    three, held, weights = forward(place, partner, later, far, early, first)
     third = {k: hop(after(three[k], second[k]), 2 * k) for k in far}
     four = backward(place, partner, far, [second[k] for k in far], held, weights)
     done = [third[k] for k in far]
@@ -408,11 +503,11 @@
     bases = [0 if k in far else 3 for k in ks]
     third = in_order(third)
     third[0] = after(third[0], *(fourth[k] for k in far[:3]))
-    outs = unpack(place, ks, third, bases, 1, [hop(cut(place, third, bases, 1), 1)])
+    outs = unpack_once(place, ks, third, bases, hop(cut(place, third, bases, 1), 1))
     fourth = in_order(fourth)
     bases = [0] * chips
-    batches = [hop(cut(place, fourth, bases, 3), 1)]
-    return tuple(outs) + tuple(unpack(place, ks, fourth, bases, 3, batches))
+    got = hop(cut(place, fourth, bases, 3), 1)
+    return tuple(outs) + tuple(unpack(place, ks, fourth, bases, 3, got))
 
 
 def body(queries, keys, values, cotangent, partner):

time: 113 us -> 112 us (level)
  waiting for transfers between devices: 65.4 us -> 50.6 us
  starting transfers between devices: 24.8 us -> 35.8 us
  Pallas kernels: 21.2 us -> 24.3 us
    ppermute x28 -> x29, waiting for transfers between devices: 65.4 us -> 50.6 us  [hop(): lax.ppermute(piece, 'ctx', [(i, i ^ distance) for i in range(devices)])]
    ppermute x28 -> x29, starting transfers between devices: 24.8 us -> 35.8 us  [hop(): lax.ppermute(piece, 'ctx', [(i, i ^ distance) for i in range(devices)])]
    pallas_call x0 -> x3, Pallas kernels: none -> 4.71 us  [the longest x2 3.23 us: scatter(): pl.pallas_call(kernel, out_shape=[out] * count, in_specs=[smem] + [vmem]...]
    pallas_call x9, Pallas kernels: 17.8 us -> 16.3 us  [call(): pl.pallas_call(kernel, out_shape=out_shape, in_specs=[smem] * len(place)...]
  transfers between devices with their start and end apart: 28 -> 29, of which waited for: 12 -> 11; matrix products, arithmetic and copies ran while one was open for 0% -> 0% of each run, Pallas kernels for 16% -> 20%
where the time goes in v6:
time: 112 us
  waiting for transfers between devices  50.6 us (45%)
  starting transfers between devices  35.8 us (32%)
  Pallas kernels  24.3 us (22%)
    ppermute x29, waiting for transfers between devices, hop(): lax.ppermute(piece, 'ctx', [(i, i ^ distance) for i in range(devices)])  50.6 us
    ppermute x29, starting transfers between devices, hop(): lax.ppermute(piece, 'ctx', [(i, i ^ distance) for i in range(devices)])  35.8 us
    pallas_call x9, Pallas kernels, call(): pl.pallas_call(kernel, out_shape=out_shape, in_specs=[smem] * len(place)...  16.3 us
    pallas_call x2, Pallas kernels, own_columns(): pl.pallas_call(kernel, out_shape=jax.ShapeDtypeStruct((chips, count, rows...  3.35 us
    pallas_call x2, Pallas kernels, scatter(): pl.pallas_call(kernel, out_shape=[out] * count, in_specs=[smem] + [vmem]...  3.23 us
  transfers between devices with their start and end apart: 29, of which 11 were waited for; matrix products, arithmetic and copies ran while one was open for 0% of the time, Pallas kernels for 20%

profile of v6, /device:TPU:9, one launch (start us, length us, event | category | flops | bytes accessed | tf_op | source)
XLA Modules:
  0.0 111.7 jit_solution(141017369508331237)
XLA Ops:
  0.6 0.7 collective-permute-start.6
  1.4 0.1 collective-permute-start.7
  1.5 0.4 collective-permute-start.8
  1.9 0.1 collective-permute-start
  2.0 0.1 pad_add_fusion.where
  2.0 1.5 %shard_map.86 = bf16[3,128,256]{2,1,0:T(8,128)(2,1)S(1)} custom-call(s32[2]{0:T(128)S(1)} %pad_add_fusion.where, bf16[128,2048]{1,0:T(8,128)(2,1)} %refs_0_.5, bf16[128,2048]{1,0:T(8,128)(2,1)} %refs_1_.3, bf16[128,2048]{1,0:T(8,128)(2,1)} %refs_2_.3), custom_call_target="tpu_custom_call" | custom-call | tf_op jit(solution)/shard_map/pallas_call | solution.py:240
  3.5 2.4 %collective-permute-start.5 = (bf16[3,128,256]{2,1,0:T(8,128)(2,1)S(1)}, bf16[3,128,256]{2,1,0:T(8,128)(2,1)S(1)}, u32[]{:S(2)}, u32[]{:S(2)}) collective-permute-start(bf16[3,128,256]{2,1,0:T(8,128)(2,1)S(1)} %shard_map.86), channel_id=1, source_target_pairs={{0,8},{1,9},{2,10},{3,11},{4,12},{5,13},{6,14},{7,15},{8,0},{9,1},... | collective-permute-start | bytes 589832 | tf_op jit(solution)/shard_map/ppermute | solution.py:470
  5.9 1.9 %shard_map.87.refs_0_ = bf16[8,3,128,128]{3,2,1,0:T(8,128)(2,1)S(1)} custom-call(s32[2]{0:T(128)S(1)} %pad_add_fusion.where, bf16[128,2048]{1,0:T(8,128)(2,1)} %refs_0_.5, bf16[128,2048]{1,0:T(8,128)(2,1)} %refs_1_.3, bf16[128,2048]{1,0:T(8,128)(2,1)} %refs_2_.3), custom_call_target="tpu_custom_call" | custom-call | tf_op jit(solution)/shard_map/pallas_call | solution.py:213
  7.8 0.0 copy-start
  7.8 0.0 collective-permute-done.6.refs_1_.refs_2_
  7.8 0.0 collective-permute-done.8.refs_3_.refs_4_
  7.8 0.6 shard_map.88
  8.5 0.1 collective-permute-start.9
  8.5 3.2 %collective-permute-start.12 = (bf16[3,256,128]{2,1,0:T(8,128)(2,1)S(1)}, bf16[3,256,128]{2,1,0:T(8,128)(2,1)S(1)}, u32[]{:S(2)}, u32[]{:S(2)}) collective-permute-start(bf16[3,256,128]{2,1,0:T(8,128)(2,1)S(1)} %get-tuple-element.58), channel_id=1, source_target_pairs={{0,10},{1,11},{2,8},{3,9},{4,14},{5,15},{6,12},{7,13},{8,2},{9,3},... | collective-permute-start | bytes 589832 | tf_op jit(solution)/shard_map/ppermute | solution.py:470
  11.7 1.5 %shard_map.84.refs_0_.refs_1_ = bf16[8,1,128,128]{3,2,1,0:T(8,128)(2,1)S(1)} custom-call(s32[2]{0:T(128)S(1)} %pad_add_fusion.where, bf16[128,2048]{1,0:T(8,128)(2,1)} %refs_0_.3), custom_call_target="tpu_custom_call" | custom-call | tf_op jit(solution)/shard_map/pallas_call | solution.py:213
  13.2 0.0 collective-permute-done.refs_1_.refs_5_
  13.2 0.7 shard_map.90
  14.0 0.3 collective-permute-start.11
  14.3 0.4 collective-permute-start.13
  14.7 8.4 %collective-permute-done.5.piece.mine = bf16[3,128,256]{2,1,0:T(8,128)(2,1)S(1)} collective-permute-done((bf16[3,128,256]{2,1,0:T(8,128)(2,1)S(1)}, bf16[3,128,256]{2,1,0:T(8,128)(2,1)S(1)}, u32[]{:S(2)}, u32[]{:S(2)}) %collective-permute-start.5) | collective-permute-done | bytes 196640 | tf_op jit(solution)/shard_map/ppermute | solution.py:470
  23.1 1.2 %collective-permute-start.14 = (bf16[4,256,128]{2,1,0:T(8,128)(2,1)S(1)}, bf16[4,256,128]{2,1,0:T(8,128)(2,1)S(1)}, u32[]{:S(2)}, u32[]{:S(2)}) collective-permute-start(bf16[4,256,128]{2,1,0:T(8,128)(2,1)S(1)} %get-tuple-element.60), channel_id=1, source_target_pairs={{0,6},{1,7},{2,4},{3,5},{4,2},{5,3},{6,0},{7,1},{8,14},{9,15},{10,... | collective-permute-start | bytes 786440 | tf_op jit(solution)/shard_map/ppermute | solution.py:470
  24.3 3.0 %collective-permute-done.9.refs_4_ = bf16[3,256,128]{2,1,0:T(8,128)(2,1)S(1)} collective-permute-done((bf16[3,256,128]{2,1,0:T(8,128)(2,1)S(1)}, bf16[3,256,128]{2,1,0:T(8,128)(2,1)S(1)}, u32[]{:S(2)}, u32[]{:S(2)}) %collective-permute-start.9) | collective-permute-done | bytes 196640 | tf_op jit(solution)/shard_map/ppermute | solution.py:470
  27.3 3.2 %collective-permute-start.15 = (bf16[3,256,128]{2,1,0:T(8,128)(2,1)S(1)}, bf16[3,256,128]{2,1,0:T(8,128)(2,1)S(1)}, u32[]{:S(2)}, u32[]{:S(2)}) collective-permute-start(bf16[3,256,128]{2,1,0:T(8,128)(2,1)S(1)} %get-tuple-element.61), channel_id=1, source_target_pairs={{0,14},{1,15},{2,12},{3,13},{4,10},{5,11},{6,8},{7,9},{8,6},{9,7},... | collective-permute-start | bytes 589832 | tf_op jit(solution)/shard_map/ppermute | solution.py:470
  30.5 0.6 shard_map.89
  31.0 1.3 %collective-permute-done.12.refs_2_ = bf16[3,256,128]{2,1,0:T(8,128)(2,1)S(1)} collective-permute-done((bf16[3,256,128]{2,1,0:T(8,128)(2,1)S(1)}, bf16[3,256,128]{2,1,0:T(8,128)(2,1)S(1)}, u32[]{:S(2)}, u32[]{:S(2)}) %collective-permute-start.12) | collective-permute-done | bytes 196640 | tf_op jit(solution)/shard_map/ppermute | solution.py:470
  32.3 4.0 %collective-permute-start.10 = (bf16[3,128,128]{2,1,0:T(8,128)(2,1)S(1)}, bf16[3,128,128]{2,1,0:T(8,128)(2,1)S(1)}, u32[]{:S(2)}, u32[]{:S(2)}) collective-permute-start(bf16[3,128,128]{2,1,0:T(8,128)(2,1)S(1)} %shard_map.89), channel_id=1, source_target_pairs={{0,1},{1,0},{2,3},{3,2},{4,5},{5,4},{6,7},{7,6},{8,9},{9,8},{10,11... | collective-permute-start | bytes 294920 | tf_op jit(solution)/shard_map/ppermute | solution.py:470
  36.3 0.6 shard_map.85
  36.9 3.3 %collective-permute-done.15.refs_6_ = bf16[3,256,128]{2,1,0:T(8,128)(2,1)S(1)} collective-permute-done((bf16[3,256,128]{2,1,0:T(8,128)(2,1)S(1)}, bf16[3,256,128]{2,1,0:T(8,128)(2,1)S(1)}, u32[]{:S(2)}, u32[]{:S(2)}) %collective-permute-start.15) | collective-permute-done | bytes 196640 | tf_op jit(solution)/shard_map/ppermute | solution.py:470
  40.2 0.9 collective-permute-start.1
  41.1 0.0 collective-permute-done.11.refs_1_
  41.1 2.2 %collective-permute-start.2 = (bf16[1,256,128]{2,1,0:T(8,128)(2,1)S(1)}, bf16[1,256,128]{2,1,0:T(8,128)(2,1)S(1)}, u32[]{:S(2)}, u32[]{:S(2)}) collective-permute-start(bf16[1,256,128]{2,1,0:T(8,128)(2,1)S(1)} %get-tuple-element.50), channel_id=1, source_target_pairs={{0,10},{1,11},{2,8},{3,9},{4,14},{5,15},{6,12},{7,13},{8,2},{9,3},... | collective-permute-start | bytes 196616 | tf_op jit(solution)/shard_map/ppermute | solution.py:470
  43.3 0.0 collective-permute-done.13.refs_3_
  43.3 2.1 %collective-permute-start.3 = (bf16[1,256,128]{2,1,0:T(8,128)(2,1)S(1)}, bf16[1,256,128]{2,1,0:T(8,128)(2,1)S(1)}, u32[]{:S(2)}, u32[]{:S(2)}) collective-permute-start(bf16[1,256,128]{2,1,0:T(8,128)(2,1)S(1)} %get-tuple-element.51), channel_id=1, source_target_pairs={{0,12},{1,13},{2,14},{3,15},{4,8},{5,9},{6,10},{7,11},{8,4},{9,5},... | collective-permute-start | bytes 196616 | tf_op jit(solution)/shard_map/ppermute | solution.py:470
  45.5 0.0 collective-permute-done.14.refs_5_
  45.5 1.0 collective-permute-start.4
  46.5 0.0 collective-permute-done.10.theirs
  46.5 5.3 %shard_map.91 = (bf16[1,256,128]{2,1,0:T(8,128)(2,1)S(1)}, bf16[1,256,128]{2,1,0:T(8,128)(2,1)S(1)}, bf16[1,256,128]{2,1,0:T(8,128)(2,1)S(1)}, bf16[1,256,128]{2...) custom-call(s32[2]{0:T(128)S(1)} %pad_add_fusion.where, s32[8]{0:T(128)S(1)} %copy-done, ...), custom_call_target="tpu_custom_call" | custom-call | flops 536870912 | bytes 9011200 | tf_op jit(solution)/shard_map/pallas_call | solution.py:183
  51.8 0.0 collective-permute-done.1.refs_0_
  51.9 1.7 %collective-permute-done.3.refs_2_ = bf16[1,256,128]{2,1,0:T(8,128)(2,1)S(1)} collective-permute-done((bf16[1,256,128]{2,1,0:T(8,128)(2,1)S(1)}, bf16[1,256,128]{2,1,0:T(8,128)(2,1)S(1)}, u32[]{:S(2)}, u32[]{:S(2)}) %collective-permute-start.3) | collective-permute-done | bytes 65568 | tf_op jit(solution)/shard_map/ppermute | solution.py:470
  53.5 1.7 %collective-permute-done.4.refs_3_ = bf16[1,256,128]{2,1,0:T(8,128)(2,1)S(1)} collective-permute-done((bf16[1,256,128]{2,1,0:T(8,128)(2,1)S(1)}, bf16[1,256,128]{2,1,0:T(8,128)(2,1)S(1)}, u32[]{:S(2)}, u32[]{:S(2)}) %collective-permute-start.4) | collective-permute-done | bytes 65568 | tf_op jit(solution)/shard_map/ppermute | solution.py:470
  55.3 0.9 collective-permute-start.19
  56.2 1.1 %collective-permute-start.18 = (bf16[1,256,128]{2,1,0:T(8,128)(2,1)S(1)}, bf16[1,256,128]{2,1,0:T(8,128)(2,1)S(1)}, u32[]{:S(2)}, u32[]{:S(2)}) collective-permute-start(bf16[1,256,128]{2,1,0:T(8,128)(2,1)S(1)} %get-tuple-element.71), channel_id=1, source_target_pairs={{0,12},{1,13},{2,14},{3,15},{4,8},{5,9},{6,10},{7,11},{8,4},{9,5},... | collective-permute-start | bytes 196616 | tf_op jit(solution)/shard_map/ppermute | solution.py:470
  57.3 2.7 %collective-permute-start.16 = (bf16[1,256,128]{2,1,0:T(8,128)(2,1)S(1)}, bf16[1,256,128]{2,1,0:T(8,128)(2,1)S(1)}, u32[]{:S(2)}, u32[]{:S(2)}) collective-permute-start(bf16[1,256,128]{2,1,0:T(8,128)(2,1)S(1)} %get-tuple-element.67), channel_id=1, source_target_pairs={{0,8},{1,9},{2,10},{3,11},{4,12},{5,13},{6,14},{7,15},{8,0},{9,1},... | collective-permute-start | bytes 196616 | tf_op jit(solution)/shard_map/ppermute | solution.py:470
  60.0 5.8 %shard_map.92 = (bf16[4,256,128]{2,1,0:T(8,128)(2,1)S(1)}, bf16[4,256,128]{2,1,0:T(8,128)(2,1)S(1)}, bf16[4,256,128]{2,1,0:T(8,128)(2,1)S(1)}, bf16[4,256,128]{2...) custom-call(s32[2]{0:T(128)S(1)} %pad_add_fusion.where, ...), custom_call_target="tpu_custom_call" | custom-call | flops 1073741824 | bytes 8912896 | tf_op jit(solution)/shard_map/pallas_call | solution.py:183
  65.8 1.0 collective-permute-done.16.refs_2_
  66.8 3.1 %collective-permute-start.20 = (bf16[3,256,128]{2,1,0:T(8,128)(2,1)S(1)}, bf16[3,256,128]{2,1,0:T(8,128)(2,1)S(1)}, u32[]{:S(2)}, u32[]{:S(2)}) collective-permute-start(bf16[3,256,128]{2,1,0:T(8,128)(2,1)S(1)} %get-tuple-element.74), channel_id=1, source_target_pairs={{0,8},{1,9},{2,10},{3,11},{4,12},{5,13},{6,14},{7,15},{8,0},{9,1},... | collective-permute-start | bytes 589832 | tf_op jit(solution)/shard_map/ppermute | solution.py:470
  69.9 0.3 collective-permute-start.21
  70.2 0.8 collective-permute-start.23
  71.1 2.2 %collective-permute-start.24 = (bf16[4,256,128]{2,1,0:T(8,128)(2,1)S(1)}, bf16[4,256,128]{2,1,0:T(8,128)(2,1)S(1)}, u32[]{:S(2)}, u32[]{:S(2)}) collective-permute-start(bf16[4,256,128]{2,1,0:T(8,128)(2,1)S(1)} %get-tuple-element.83), channel_id=1, source_target_pairs={{0,4},{1,5},{2,6},{3,7},{4,0},{5,1},{6,2},{7,3},{8,12},{9,13},{10,... | collective-permute-start | bytes 786440 | tf_op jit(solution)/shard_map/ppermute | solution.py:470
  73.3 0.5 collective-permute-start.25
  73.8 8.8 %collective-permute-done.20.refs_2_ = bf16[3,256,128]{2,1,0:T(8,128)(2,1)S(1)} collective-permute-done((bf16[3,256,128]{2,1,0:T(8,128)(2,1)S(1)}, bf16[3,256,128]{2,1,0:T(8,128)(2,1)S(1)}, u32[]{:S(2)}, u32[]{:S(2)}) %collective-permute-start.20) | collective-permute-done | bytes 196640 | tf_op jit(solution)/shard_map/ppermute | solution.py:470
  82.6 0.4 collective-permute-start.22
  83.0 3.8 %collective-permute-done.21.refs_3_ = bf16[3,256,128]{2,1,0:T(8,128)(2,1)S(1)} collective-permute-done((bf16[3,256,128]{2,1,0:T(8,128)(2,1)S(1)}, bf16[3,256,128]{2,1,0:T(8,128)(2,1)S(1)}, u32[]{:S(2)}, u32[]{:S(2)}) %collective-permute-start.21) | collective-permute-done | bytes 196640 | tf_op jit(solution)/shard_map/ppermute | solution.py:470
  86.8 0.8 collective-permute-start.27
  87.6 13.0 %collective-permute-done.22.refs_5_ = bf16[3,256,128]{2,1,0:T(8,128)(2,1)S(1)} collective-permute-done((bf16[3,256,128]{2,1,0:T(8,128)(2,1)S(1)}, bf16[3,256,128]{2,1,0:T(8,128)(2,1)S(1)}, u32[]{:S(2)}, u32[]{:S(2)}) %collective-permute-start.22) | collective-permute-done | bytes 196640 | tf_op jit(solution)/shard_map/ppermute | solution.py:470
  100.6 4.6 %collective-permute-done.27.refs_7_ = bf16[3,256,128]{2,1,0:T(8,128)(2,1)S(1)} collective-permute-done((bf16[3,256,128]{2,1,0:T(8,128)(2,1)S(1)}, bf16[3,256,128]{2,1,0:T(8,128)(2,1)S(1)}, u32[]{:S(2)}, u32[]{:S(2)}) %collective-permute-start.27) | collective-permute-done | bytes 196640 | tf_op jit(solution)/shard_map/ppermute | solution.py:470
  105.2 0.6 shard_map.95
  105.8 0.6 collective-permute-start.28
  106.3 0.6 shard_map.93
  106.9 0.1 collective-permute-start.26
  107.0 1.6 %shard_map.96 = (bf16[128,2048]{1,0:T(8,128)(2,1)}, bf16[128,2048]{1,0:T(8,128)(2,1)}, bf16[128,2048]{1,0:T(8,128)(2,1)}) custom-call(s32[2]{0:T(128)S(1)} %pad_add_fusion.where, bf16[4,256,128]{2,1,0:T(8,128)(2,1)S(1)} %get-tuple-element.79.refs_0_, bf16[4,256,128]{2,1,0:T(8,128)(2,1)S(1)} %collective-permute-done.23.refs_1_, ...), custom_call_target="tpu_custom_call" | custom-call | bytes 1572864 | tf_op jit(solution)/shard_map/pallas_call | solution.py:341
  108.6 0.0 collective-permute-done.26.refs_8_
  108.6 1.5 %shard_map.94 = bf16[128,2048]{1,0:T(8,128)(2,1)} custom-call(s32[2]{0:T(128)S(1)} %pad_add_fusion.where, bf16[4,256,128]{2,1,0:T(8,128)(2,1)S(1)} %get-tuple-element.79.refs_0_, bf16[4,256,128]{2,1,0:T(8,128)(2,1)S(1)} %collective-permute-done.23.refs_1_, bf16[1,256,128]{2,1,0:T(8,128)(2,1)S(1)} %collective-permute-done.16.refs_2_, ...), custom_call_target="tpu_custom_call" | custom-call | bytes 2097152 | tf_op jit(solution)/shard_map/pallas_call | solution.py:183
  110.1 1.6 %shard_map.97 = (bf16[128,2048]{1,0:T(8,128)(2,1)}, bf16[128,2048]{1,0:T(8,128)(2,1)}, bf16[128,2048]{1,0:T(8,128)(2,1)}) custom-call(s32[2]{0:T(128)S(1)} %pad_add_fusion.where, bf16[8,3,128,128]{3,2,1,0:T(8,128)(2,1)S(1)} %collective-permute-done.28.refs_0_, ...), custom_call_target="tpu_custom_call", output_to_operand_aliasing={{0}: (2, {}), {1}: (3, {}), {2}: (4, {})} | custom-call | bytes 1572864 | tf_op jit(solution)/shard_map/pallas_call | solution.py:341
  (11 shorter events, 0.0 us)
Async XLA Ops:
  0.6 7.1 %collective-permute-start.6 = (bf16[128,2048]{1,0:T(8,128)(2,1)}, bf16[128,2048]{1,0:T(8,128)(2,1)S(1)}, u32[]{:S(2)}, u32[]{:S(2)}) collective-permute-start(bf16[128,2048]{1,0:T(8,128)(2,1)} %refs_0_.5), channel_id=1, source_target_pairs={{0,1},{1,0},{2,3},{3,2},{4,5},{5,4},{6,7},{7,6},{8,9},{9,8},{10,11... | collective-permute-start | bytes 1572872 | tf_op jit(solution)/shard_map/ppermute | solution.py:470
  1.4 6.4 %collective-permute-start.7 = (bf16[128,2048]{1,0:T(8,128)(2,1)}, bf16[128,2048]{1,0:T(8,128)(2,1)S(1)}, u32[]{:S(2)}, u32[]{:S(2)}) collective-permute-start(bf16[128,2048]{1,0:T(8,128)(2,1)} %refs_1_.3), channel_id=1, source_target_pairs={{0,1},{1,0},{2,3},{3,2},{4,5},{5,4},{6,7},{7,6},{8,9},{9,8},{10,11... | collective-permute-start | bytes 1572872 | tf_op jit(solution)/shard_map/ppermute | solution.py:470
  1.5 6.3 %collective-permute-start.8 = (bf16[128,2048]{1,0:T(8,128)(2,1)}, bf16[128,2048]{1,0:T(8,128)(2,1)S(1)}, u32[]{:S(2)}, u32[]{:S(2)}) collective-permute-start(bf16[128,2048]{1,0:T(8,128)(2,1)} %refs_2_.3), channel_id=1, source_target_pairs={{0,1},{1,0},{2,3},{3,2},{4,5},{5,4},{6,7},{7,6},{8,9},{9,8},{10,11... | collective-permute-start | bytes 1572872 | tf_op jit(solution)/shard_map/ppermute | solution.py:470
  1.9 11.4 %collective-permute-start = (bf16[128,2048]{1,0:T(8,128)(2,1)}, bf16[128,2048]{1,0:T(8,128)(2,1)S(1)}, u32[]{:S(2)}, u32[]{:S(2)}) collective-permute-start(bf16[128,2048]{1,0:T(8,128)(2,1)} %refs_0_.3), channel_id=1, source_target_pairs={{0,1},{1,0},{2,3},{3,2},{4,5},{5,4},{6,7},{7,6},{8,9},{9,8},{10,11... | collective-permute-start | bytes 1572872 | tf_op jit(solution)/shard_map/ppermute | solution.py:470
  3.5 19.6 %collective-permute-start.5 = (bf16[3,128,256]{2,1,0:T(8,128)(2,1)S(1)}, bf16[3,128,256]{2,1,0:T(8,128)(2,1)S(1)}, u32[]{:S(2)}, u32[]{:S(2)}) collective-permute-start(bf16[3,128,256]{2,1,0:T(8,128)(2,1)S(1)} %shard_map.86), channel_id=1, source_target_pairs={{0,8},{1,9},{2,10},{3,11},{4,12},{5,13},{6,14},{7,15},{8,0},{9,1},... | collective-permute-start | bytes 589832 | tf_op jit(solution)/shard_map/ppermute | solution.py:470
  7.8 38.7 %copy-start = (s32[8]{0:T(128)S(1)}, s32[8]{0:T(128)}, u32[]{:S(2)}) copy-start(s32[8]{0:T(128)} %partner.3) | copy-start | bytes 100
  8.5 18.9 %collective-permute-start.9 = (bf16[3,256,128]{2,1,0:T(8,128)(2,1)S(1)}, bf16[3,256,128]{2,1,0:T(8,128)(2,1)S(1)}, u32[]{:S(2)}, u32[]{:S(2)}) collective-permute-start(bf16[3,256,128]{2,1,0:T(8,128)(2,1)S(1)} %get-tuple-element.54), channel_id=1, source_target_pairs={{0,12},{1,13},{2,14},{3,15},{4,8},{5,9},{6,10},{7,11},{8,4},{9,5},... | collective-permute-start | bytes 589832 | tf_op jit(solution)/shard_map/ppermute | solution.py:470
  8.5 23.8 %collective-permute-start.12 = (bf16[3,256,128]{2,1,0:T(8,128)(2,1)S(1)}, bf16[3,256,128]{2,1,0:T(8,128)(2,1)S(1)}, u32[]{:S(2)}, u32[]{:S(2)}) collective-permute-start(bf16[3,256,128]{2,1,0:T(8,128)(2,1)S(1)} %get-tuple-element.58), channel_id=1, source_target_pairs={{0,10},{1,11},{2,8},{3,9},{4,14},{5,15},{6,12},{7,13},{8,2},{9,3},... | collective-permute-start | bytes 589832 | tf_op jit(solution)/shard_map/ppermute | solution.py:470
  14.0 27.1 %collective-permute-start.11 = (bf16[4,256,128]{2,1,0:T(8,128)(2,1)S(1)}, bf16[4,256,128]{2,1,0:T(8,128)(2,1)S(1)}, u32[]{:S(2)}, u32[]{:S(2)}) collective-permute-start(bf16[4,256,128]{2,1,0:T(8,128)(2,1)S(1)} %get-tuple-element.57), channel_id=1, source_target_pairs={{0,2},{1,3},{2,0},{3,1},{4,6},{5,7},{6,4},{7,5},{8,10},{9,11},{10,... | collective-permute-start | bytes 786440 | tf_op jit(solution)/shard_map/ppermute | solution.py:470
  14.3 29.1 %collective-permute-start.13 = (bf16[4,256,128]{2,1,0:T(8,128)(2,1)S(1)}, bf16[4,256,128]{2,1,0:T(8,128)(2,1)S(1)}, u32[]{:S(2)}, u32[]{:S(2)}) collective-permute-start(bf16[4,256,128]{2,1,0:T(8,128)(2,1)S(1)} %get-tuple-element.59), channel_id=1, source_target_pairs={{0,4},{1,5},{2,6},{3,7},{4,0},{5,1},{6,2},{7,3},{8,12},{9,13},{10,... | collective-permute-start | bytes 786440 | tf_op jit(solution)/shard_map/ppermute | solution.py:470
  23.1 22.4 %collective-permute-start.14 = (bf16[4,256,128]{2,1,0:T(8,128)(2,1)S(1)}, bf16[4,256,128]{2,1,0:T(8,128)(2,1)S(1)}, u32[]{:S(2)}, u32[]{:S(2)}) collective-permute-start(bf16[4,256,128]{2,1,0:T(8,128)(2,1)S(1)} %get-tuple-element.60), channel_id=1, source_target_pairs={{0,6},{1,7},{2,4},{3,5},{4,2},{5,3},{6,0},{7,1},{8,14},{9,15},{10,... | collective-permute-start | bytes 786440 | tf_op jit(solution)/shard_map/ppermute | solution.py:470
  27.3 12.9 %collective-permute-start.15 = (bf16[3,256,128]{2,1,0:T(8,128)(2,1)S(1)}, bf16[3,256,128]{2,1,0:T(8,128)(2,1)S(1)}, u32[]{:S(2)}, u32[]{:S(2)}) collective-permute-start(bf16[3,256,128]{2,1,0:T(8,128)(2,1)S(1)} %get-tuple-element.61), channel_id=1, source_target_pairs={{0,14},{1,15},{2,12},{3,13},{4,10},{5,11},{6,8},{7,9},{8,6},{9,7},... | collective-permute-start | bytes 589832 | tf_op jit(solution)/shard_map/ppermute | solution.py:470
  32.3 14.2 %collective-permute-start.10 = (bf16[3,128,128]{2,1,0:T(8,128)(2,1)S(1)}, bf16[3,128,128]{2,1,0:T(8,128)(2,1)S(1)}, u32[]{:S(2)}, u32[]{:S(2)}) collective-permute-start(bf16[3,128,128]{2,1,0:T(8,128)(2,1)S(1)} %shard_map.89), channel_id=1, source_target_pairs={{0,1},{1,0},{2,3},{3,2},{4,5},{5,4},{6,7},{7,6},{8,9},{9,8},{10,11... | collective-permute-start | bytes 294920 | tf_op jit(solution)/shard_map/ppermute | solution.py:470
  40.2 11.6 %collective-permute-start.1 = (bf16[1,256,128]{2,1,0:T(8,128)(2,1)S(1)}, bf16[1,256,128]{2,1,0:T(8,128)(2,1)S(1)}, u32[]{:S(2)}, u32[]{:S(2)}) collective-permute-start(bf16[1,256,128]{2,1,0:T(8,128)(2,1)S(1)} %get-tuple-element.49), channel_id=1, source_target_pairs={{0,8},{1,9},{2,10},{3,11},{4,12},{5,13},{6,14},{7,15},{8,0},{9,1},... | collective-permute-start | bytes 196616 | tf_op jit(solution)/shard_map/ppermute | solution.py:470
  41.1 10.8 %collective-permute-start.2 = (bf16[1,256,128]{2,1,0:T(8,128)(2,1)S(1)}, bf16[1,256,128]{2,1,0:T(8,128)(2,1)S(1)}, u32[]{:S(2)}, u32[]{:S(2)}) collective-permute-start(bf16[1,256,128]{2,1,0:T(8,128)(2,1)S(1)} %get-tuple-element.50), channel_id=1, source_target_pairs={{0,10},{1,11},{2,8},{3,9},{4,14},{5,15},{6,12},{7,13},{8,2},{9,3},... | collective-permute-start | bytes 196616 | tf_op jit(solution)/shard_map/ppermute | solution.py:470
  43.3 10.2 %collective-permute-start.3 = (bf16[1,256,128]{2,1,0:T(8,128)(2,1)S(1)}, bf16[1,256,128]{2,1,0:T(8,128)(2,1)S(1)}, u32[]{:S(2)}, u32[]{:S(2)}) collective-permute-start(bf16[1,256,128]{2,1,0:T(8,128)(2,1)S(1)} %get-tuple-element.51), channel_id=1, source_target_pairs={{0,12},{1,13},{2,14},{3,15},{4,8},{5,9},{6,10},{7,11},{8,4},{9,5},... | collective-permute-start | bytes 196616 | tf_op jit(solution)/shard_map/ppermute | solution.py:470
  45.5 9.8 %collective-permute-start.4 = (bf16[1,256,128]{2,1,0:T(8,128)(2,1)S(1)}, bf16[1,256,128]{2,1,0:T(8,128)(2,1)S(1)}, u32[]{:S(2)}, u32[]{:S(2)}) collective-permute-start(bf16[1,256,128]{2,1,0:T(8,128)(2,1)S(1)} %get-tuple-element.52), channel_id=1, source_target_pairs={{0,14},{1,15},{2,12},{3,13},{4,10},{5,11},{6,8},{7,9},{8,6},{9,7},... | collective-permute-start | bytes 196616 | tf_op jit(solution)/shard_map/ppermute | solution.py:470
  55.3 10.5 %collective-permute-start.19 = (bf16[1,256,128]{2,1,0:T(8,128)(2,1)S(1)}, bf16[1,256,128]{2,1,0:T(8,128)(2,1)S(1)}, u32[]{:S(2)}, u32[]{:S(2)}) collective-permute-start(bf16[1,256,128]{2,1,0:T(8,128)(2,1)S(1)} %get-tuple-element.73), channel_id=1, source_target_pairs={{0,14},{1,15},{2,12},{3,13},{4,10},{5,11},{6,8},{7,9},{8,6},{9,7},... | collective-permute-start | bytes 196616 | tf_op jit(solution)/shard_map/ppermute | solution.py:470
  56.2 9.6 %collective-permute-start.18 = (bf16[1,256,128]{2,1,0:T(8,128)(2,1)S(1)}, bf16[1,256,128]{2,1,0:T(8,128)(2,1)S(1)}, u32[]{:S(2)}, u32[]{:S(2)}) collective-permute-start(bf16[1,256,128]{2,1,0:T(8,128)(2,1)S(1)} %get-tuple-element.71), channel_id=1, source_target_pairs={{0,12},{1,13},{2,14},{3,15},{4,8},{5,9},{6,10},{7,11},{8,4},{9,5},... | collective-permute-start | bytes 196616 | tf_op jit(solution)/shard_map/ppermute | solution.py:470
  57.3 8.5 %collective-permute-start.17 = (bf16[1,256,128]{2,1,0:T(8,128)(2,1)S(1)}, bf16[1,256,128]{2,1,0:T(8,128)(2,1)S(1)}, u32[]{:S(2)}, u32[]{:S(2)}) collective-permute-start(bf16[1,256,128]{2,1,0:T(8,128)(2,1)S(1)} %get-tuple-element.69), channel_id=1, source_target_pairs={{0,10},{1,11},{2,8},{3,9},{4,14},{5,15},{6,12},{7,13},{8,2},{9,3},... | collective-permute-start | bytes 196616 | tf_op jit(solution)/shard_map/ppermute | solution.py:470
  57.3 9.5 %collective-permute-start.16 = (bf16[1,256,128]{2,1,0:T(8,128)(2,1)S(1)}, bf16[1,256,128]{2,1,0:T(8,128)(2,1)S(1)}, u32[]{:S(2)}, u32[]{:S(2)}) collective-permute-start(bf16[1,256,128]{2,1,0:T(8,128)(2,1)S(1)} %get-tuple-element.67), channel_id=1, source_target_pairs={{0,8},{1,9},{2,10},{3,11},{4,12},{5,13},{6,14},{7,15},{8,0},{9,1},... | collective-permute-start | bytes 196616 | tf_op jit(solution)/shard_map/ppermute | solution.py:470
  66.8 15.8 %collective-permute-start.20 = (bf16[3,256,128]{2,1,0:T(8,128)(2,1)S(1)}, bf16[3,256,128]{2,1,0:T(8,128)(2,1)S(1)}, u32[]{:S(2)}, u32[]{:S(2)}) collective-permute-start(bf16[3,256,128]{2,1,0:T(8,128)(2,1)S(1)} %get-tuple-element.74), channel_id=1, source_target_pairs={{0,8},{1,9},{2,10},{3,11},{4,12},{5,13},{6,14},{7,15},{8,0},{9,1},... | collective-permute-start | bytes 589832 | tf_op jit(solution)/shard_map/ppermute | solution.py:470
  69.9 16.9 %collective-permute-start.21 = (bf16[3,256,128]{2,1,0:T(8,128)(2,1)S(1)}, bf16[3,256,128]{2,1,0:T(8,128)(2,1)S(1)}, u32[]{:S(2)}, u32[]{:S(2)}) collective-permute-start(bf16[3,256,128]{2,1,0:T(8,128)(2,1)S(1)} %get-tuple-element.76), channel_id=1, source_target_pairs={{0,10},{1,11},{2,8},{3,9},{4,14},{5,15},{6,12},{7,13},{8,2},{9,3},... | collective-permute-start | bytes 589832 | tf_op jit(solution)/shard_map/ppermute | solution.py:470
  70.2 34.9 %collective-permute-start.23 = (bf16[4,256,128]{2,1,0:T(8,128)(2,1)S(1)}, bf16[4,256,128]{2,1,0:T(8,128)(2,1)S(1)}, u32[]{:S(2)}, u32[]{:S(2)}) collective-permute-start(bf16[4,256,128]{2,1,0:T(8,128)(2,1)S(1)} %get-tuple-element.81), channel_id=1, source_target_pairs={{0,2},{1,3},{2,0},{3,1},{4,6},{5,7},{6,4},{7,5},{8,10},{9,11},{10,... | collective-permute-start | bytes 786440 | tf_op jit(solution)/shard_map/ppermute | solution.py:470
  71.1 34.1 %collective-permute-start.24 = (bf16[4,256,128]{2,1,0:T(8,128)(2,1)S(1)}, bf16[4,256,128]{2,1,0:T(8,128)(2,1)S(1)}, u32[]{:S(2)}, u32[]{:S(2)}) collective-permute-start(bf16[4,256,128]{2,1,0:T(8,128)(2,1)S(1)} %get-tuple-element.83), channel_id=1, source_target_pairs={{0,4},{1,5},{2,6},{3,7},{4,0},{5,1},{6,2},{7,3},{8,12},{9,13},{10,... | collective-permute-start | bytes 786440 | tf_op jit(solution)/shard_map/ppermute | solution.py:470
  73.3 31.8 %collective-permute-start.25 = (bf16[4,256,128]{2,1,0:T(8,128)(2,1)S(1)}, bf16[4,256,128]{2,1,0:T(8,128)(2,1)S(1)}, u32[]{:S(2)}, u32[]{:S(2)}) collective-permute-start(bf16[4,256,128]{2,1,0:T(8,128)(2,1)S(1)} %get-tuple-element.85), channel_id=1, source_target_pairs={{0,6},{1,7},{2,4},{3,5},{4,2},{5,3},{6,0},{7,1},{8,14},{9,15},{10,... | collective-permute-start | bytes 786440 | tf_op jit(solution)/shard_map/ppermute | solution.py:470
  82.6 18.0 %collective-permute-start.22 = (bf16[3,256,128]{2,1,0:T(8,128)(2,1)S(1)}, bf16[3,256,128]{2,1,0:T(8,128)(2,1)S(1)}, u32[]{:S(2)}, u32[]{:S(2)}) collective-permute-start(bf16[3,256,128]{2,1,0:T(8,128)(2,1)S(1)} %get-tuple-element.78), channel_id=1, source_target_pairs={{0,12},{1,13},{2,14},{3,15},{4,8},{5,9},{6,10},{7,11},{8,4},{9,5},... | collective-permute-start | bytes 589832 | tf_op jit(solution)/shard_map/ppermute | solution.py:470
  86.8 18.4 %collective-permute-start.27 = (bf16[3,256,128]{2,1,0:T(8,128)(2,1)S(1)}, bf16[3,256,128]{2,1,0:T(8,128)(2,1)S(1)}, u32[]{:S(2)}, u32[]{:S(2)}) collective-permute-start(bf16[3,256,128]{2,1,0:T(8,128)(2,1)S(1)} %get-tuple-element.87), channel_id=1, source_target_pairs={{0,14},{1,15},{2,12},{3,13},{4,10},{5,11},{6,8},{7,9},{8,6},{9,7},... | collective-permute-start | bytes 589832 | tf_op jit(solution)/shard_map/ppermute | solution.py:470
  105.8 4.3 %collective-permute-start.28 = (bf16[8,3,128,128]{3,2,1,0:T(8,128)(2,1)S(1)}, bf16[8,3,128,128]{3,2,1,0:T(8,128)(2,1)S(1)}, u32[]{:S(2)}, u32[]{:S(2)}) collective-permute-start(bf16[8,3,128,128]{3,2,1,0:T(8,128)(2,1)S(1)} %shard_map.95), channel_id=1, source_target_pairs={{0,1},{1,0},{2,3},{3,2},{4,5},{5,4},{6,7},{7,6},{8,9},{9,8},{10,11... | collective-permute-start | bytes 2359304 | tf_op jit(solution)/shard_map/ppermute | solution.py:470
  106.9 1.7 %collective-permute-start.26 = (bf16[8,1,128,128]{3,2,1,0:T(8,128)(2,1)S(1)}, bf16[8,1,128,128]{3,2,1,0:T(8,128)(2,1)S(1)}, u32[]{:S(2)}, u32[]{:S(2)}) collective-permute-start(bf16[8,1,128,128]{3,2,1,0:T(8,128)(2,1)S(1)} %shard_map.93), channel_id=1, source_target_pairs={{0,1},{1,0},{2,3},{3,2},{4,5},{5,4},{6,7},{7,6},{8,9},{9,8},{10,11... | collective-permute-start | bytes 786440 | tf_op jit(solution)/shard_map/ppermute | solution.py:470

commit v7 on v6

--- a/solution.py
+++ b/solution.py
@@ -291,24 +291,6 @@
     return call(kernel, [place], pieces, [out])[0]
 
 
-def unpack_once(place, ks, pieces, bases, got):
-    chips = len(pieces)
-    size = pieces[0].shape[1]
-
-    def kernel(where, *refs):
-        core = where[1]
-        half = halves(where, size // 2)[0]
-        for n, k in enumerate(ks):
-            start = (where[0] ^ k) * 2
-            here = pl.ds(pl.multiple_of((start + core) * HEAD, HEAD), HEAD)
-            there = pl.ds(pl.multiple_of((start + 1 - core) * HEAD, HEAD), HEAD)
-            refs[chips + 1][:, here] = refs[n][bases[n], half]
-            refs[chips + 1][:, there] = refs[chips][n, 0]
-
-    out = jax.ShapeDtypeStruct((size // 2, chips * 2 * HEAD), jnp.bfloat16)
-    return call(kernel, [place], [*pieces, got], [out])
-
-
 def scatter(place, ks, arrays, picks, other, results, width):
     count = len(picks)
     rows = arrays[0].shape[-2] if other else arrays[0].shape[-2] // 2
@@ -350,12 +332,15 @@
     )(place, *arrays, *results)
 
 
-def unpack(place, ks, pieces, bases, count, got):
+def unpack(place, ks, third, fourth, bases, got_attended, got_grads):
     width = len(ks) * 2 * HEAD
-    picks = [[(n, bases[n] + i) for n in range(len(ks))] for i in range(count)]
-    outs = scatter(place, ks, pieces, picks, False, [], width)
-    picks = [[(0, (n, i)) for n in range(len(ks))] for i in range(count)]
-    return scatter(place, ks, [got], picks, True, outs, width)
+    chips = range(len(ks))
+    picks = [[(n, bases[n]) for n in chips]]
+    picks += [[(len(ks) + n, i) for n in chips] for i in range(3)]
+    outs = scatter(place, ks, [*third, *fourth], picks, False, [], width)
+    picks = [[(0, (n, 0)) for n in chips]]
+    picks += [[(1, (n, i)) for n in chips] for i in range(3)]
+    return scatter(place, ks, [got_attended, got_grads], picks, True, outs, width)
 
 
 def halves(where, rows):
@@ -503,11 +488,10 @@
     bases = [0 if k in far else 3 for k in ks]
     third = in_order(third)
     third[0] = after(third[0], *(fourth[k] for k in far[:3]))
-    outs = unpack_once(place, ks, third, bases, hop(cut(place, third, bases, 1), 1))
+    got_attended = hop(cut(place, third, bases, 1), 1)
     fourth = in_order(fourth)
-    bases = [0] * chips
-    got = hop(cut(place, fourth, bases, 3), 1)
-    return tuple(outs) + tuple(unpack(place, ks, fourth, bases, 3, got))
+    got_grads = hop(cut(place, fourth, [0] * chips, 3), 1)
+    return tuple(unpack(place, ks, third, fourth, bases, got_attended, got_grads))
 
 
 def body(queries, keys, values, cotangent, partner):

time: 112 us -> 111 us (level)
    pallas_call x9 -> x8, Pallas kernels: 16.3 us -> 14.8 us  [call(): pl.pallas_call(kernel, out_shape=out_shape, in_specs=[smem] * len(place)...]
  transfers between devices with their start and end apart: 29 -> 29, of which waited for: 11 -> 11; matrix products, arithmetic and copies ran while one was open for 0% -> 0% of each run, Pallas kernels for 20% -> 19%
where the time goes in v7:
time: 111 us
  waiting for transfers between devices  50.6 us (46%)
  starting transfers between devices  35.8 us (32%)
  Pallas kernels  23.2 us (21%)
    ppermute x29, waiting for transfers between devices, hop(): lax.ppermute(piece, 'ctx', [(i, i ^ distance) for i in range(devices)])  50.6 us
    ppermute x29, starting transfers between devices, hop(): lax.ppermute(piece, 'ctx', [(i, i ^ distance) for i in range(devices)])  35.8 us
    pallas_call x8, Pallas kernels, call(): pl.pallas_call(kernel, out_shape=out_shape, in_specs=[smem] * len(place)...  14.8 us
    pallas_call x2, Pallas kernels, scatter(): pl.pallas_call(kernel, out_shape=[out] * count, in_specs=[smem] + [vmem]...  3.56 us
    pallas_call x2, Pallas kernels, own_columns(): pl.pallas_call(kernel, out_shape=jax.ShapeDtypeStruct((chips, count, rows...  3.35 us
  transfers between devices with their start and end apart: 29, of which 11 were waited for; matrix products, arithmetic and copies ran while one was open for 0% of the time, Pallas kernels for 19%

profile of v7, /device:TPU:9, one launch (start us, length us, event | category | flops | bytes accessed | tf_op | source)
XLA Modules:
  0.0 110.6 jit_solution(14061235545319435482)
XLA Ops:
  0.6 0.7 collective-permute-start.6
  1.4 0.1 collective-permute-start.7
  1.5 0.4 collective-permute-start.8
  1.9 0.1 collective-permute-start
  2.0 0.1 pad_add_fusion.where
  2.0 1.5 %shard_map.86 = bf16[3,128,256]{2,1,0:T(8,128)(2,1)S(1)} custom-call(s32[2]{0:T(128)S(1)} %pad_add_fusion.where, bf16[128,2048]{1,0:T(8,128)(2,1)} %refs_0_.5, bf16[128,2048]{1,0:T(8,128)(2,1)} %refs_1_.3, bf16[128,2048]{1,0:T(8,128)(2,1)} %refs_2_.3), custom_call_target="tpu_custom_call" | custom-call | tf_op jit(solution)/shard_map/pallas_call | solution.py:240
  3.5 2.4 %collective-permute-start.5 = (bf16[3,128,256]{2,1,0:T(8,128)(2,1)S(1)}, bf16[3,128,256]{2,1,0:T(8,128)(2,1)S(1)}, u32[]{:S(2)}, u32[]{:S(2)}) collective-permute-start(bf16[3,128,256]{2,1,0:T(8,128)(2,1)S(1)} %shard_map.86), channel_id=1, source_target_pairs={{0,8},{1,9},{2,10},{3,11},{4,12},{5,13},{6,14},{7,15},{8,0},{9,1},... | collective-permute-start | bytes 589832 | tf_op jit(solution)/shard_map/ppermute | solution.py:455
  5.9 1.9 %shard_map.87.refs_0_ = bf16[8,3,128,128]{3,2,1,0:T(8,128)(2,1)S(1)} custom-call(s32[2]{0:T(128)S(1)} %pad_add_fusion.where, bf16[128,2048]{1,0:T(8,128)(2,1)} %refs_0_.5, bf16[128,2048]{1,0:T(8,128)(2,1)} %refs_1_.3, bf16[128,2048]{1,0:T(8,128)(2,1)} %refs_2_.3), custom_call_target="tpu_custom_call" | custom-call | tf_op jit(solution)/shard_map/pallas_call | solution.py:213
  7.8 0.0 copy-start
  7.8 0.0 collective-permute-done.6.refs_1_.refs_2_
  7.8 0.0 collective-permute-done.8.refs_3_.refs_4_
  7.8 0.6 shard_map.88
  8.5 0.1 collective-permute-start.9
  8.5 3.2 %collective-permute-start.12 = (bf16[3,256,128]{2,1,0:T(8,128)(2,1)S(1)}, bf16[3,256,128]{2,1,0:T(8,128)(2,1)S(1)}, u32[]{:S(2)}, u32[]{:S(2)}) collective-permute-start(bf16[3,256,128]{2,1,0:T(8,128)(2,1)S(1)} %get-tuple-element.56), channel_id=1, source_target_pairs={{0,10},{1,11},{2,8},{3,9},{4,14},{5,15},{6,12},{7,13},{8,2},{9,3},... | collective-permute-start | bytes 589832 | tf_op jit(solution)/shard_map/ppermute | solution.py:455
  11.7 1.5 %shard_map.84.refs_0_.refs_1_ = bf16[8,1,128,128]{3,2,1,0:T(8,128)(2,1)S(1)} custom-call(s32[2]{0:T(128)S(1)} %pad_add_fusion.where, bf16[128,2048]{1,0:T(8,128)(2,1)} %refs_0_.3), custom_call_target="tpu_custom_call" | custom-call | tf_op jit(solution)/shard_map/pallas_call | solution.py:213
  13.2 0.0 collective-permute-done.refs_1_.refs_5_
  13.2 0.7 shard_map.90
  14.0 0.3 collective-permute-start.11
  14.3 0.4 collective-permute-start.13
  14.7 8.4 %collective-permute-done.5.piece.mine = bf16[3,128,256]{2,1,0:T(8,128)(2,1)S(1)} collective-permute-done((bf16[3,128,256]{2,1,0:T(8,128)(2,1)S(1)}, bf16[3,128,256]{2,1,0:T(8,128)(2,1)S(1)}, u32[]{:S(2)}, u32[]{:S(2)}) %collective-permute-start.5) | collective-permute-done | bytes 196640 | tf_op jit(solution)/shard_map/ppermute | solution.py:455
  23.1 1.2 %collective-permute-start.14 = (bf16[4,256,128]{2,1,0:T(8,128)(2,1)S(1)}, bf16[4,256,128]{2,1,0:T(8,128)(2,1)S(1)}, u32[]{:S(2)}, u32[]{:S(2)}) collective-permute-start(bf16[4,256,128]{2,1,0:T(8,128)(2,1)S(1)} %get-tuple-element.58), channel_id=1, source_target_pairs={{0,6},{1,7},{2,4},{3,5},{4,2},{5,3},{6,0},{7,1},{8,14},{9,15},{10,... | collective-permute-start | bytes 786440 | tf_op jit(solution)/shard_map/ppermute | solution.py:455
  24.3 3.0 %collective-permute-done.9.refs_4_ = bf16[3,256,128]{2,1,0:T(8,128)(2,1)S(1)} collective-permute-done((bf16[3,256,128]{2,1,0:T(8,128)(2,1)S(1)}, bf16[3,256,128]{2,1,0:T(8,128)(2,1)S(1)}, u32[]{:S(2)}, u32[]{:S(2)}) %collective-permute-start.9) | collective-permute-done | bytes 196640 | tf_op jit(solution)/shard_map/ppermute | solution.py:455
  27.3 3.2 %collective-permute-start.15 = (bf16[3,256,128]{2,1,0:T(8,128)(2,1)S(1)}, bf16[3,256,128]{2,1,0:T(8,128)(2,1)S(1)}, u32[]{:S(2)}, u32[]{:S(2)}) collective-permute-start(bf16[3,256,128]{2,1,0:T(8,128)(2,1)S(1)} %get-tuple-element.59), channel_id=1, source_target_pairs={{0,14},{1,15},{2,12},{3,13},{4,10},{5,11},{6,8},{7,9},{8,6},{9,7},... | collective-permute-start | bytes 589832 | tf_op jit(solution)/shard_map/ppermute | solution.py:455
  30.5 0.6 shard_map.89
  31.0 1.3 %collective-permute-done.12.refs_2_ = bf16[3,256,128]{2,1,0:T(8,128)(2,1)S(1)} collective-permute-done((bf16[3,256,128]{2,1,0:T(8,128)(2,1)S(1)}, bf16[3,256,128]{2,1,0:T(8,128)(2,1)S(1)}, u32[]{:S(2)}, u32[]{:S(2)}) %collective-permute-start.12) | collective-permute-done | bytes 196640 | tf_op jit(solution)/shard_map/ppermute | solution.py:455
  32.3 4.0 %collective-permute-start.10 = (bf16[3,128,128]{2,1,0:T(8,128)(2,1)S(1)}, bf16[3,128,128]{2,1,0:T(8,128)(2,1)S(1)}, u32[]{:S(2)}, u32[]{:S(2)}) collective-permute-start(bf16[3,128,128]{2,1,0:T(8,128)(2,1)S(1)} %shard_map.89), channel_id=1, source_target_pairs={{0,1},{1,0},{2,3},{3,2},{4,5},{5,4},{6,7},{7,6},{8,9},{9,8},{10,11... | collective-permute-start | bytes 294920 | tf_op jit(solution)/shard_map/ppermute | solution.py:455
  36.3 0.6 shard_map.85
  36.9 3.3 %collective-permute-done.15.refs_6_ = bf16[3,256,128]{2,1,0:T(8,128)(2,1)S(1)} collective-permute-done((bf16[3,256,128]{2,1,0:T(8,128)(2,1)S(1)}, bf16[3,256,128]{2,1,0:T(8,128)(2,1)S(1)}, u32[]{:S(2)}, u32[]{:S(2)}) %collective-permute-start.15) | collective-permute-done | bytes 196640 | tf_op jit(solution)/shard_map/ppermute | solution.py:455
  40.2 0.9 collective-permute-start.1
  41.1 0.0 collective-permute-done.11.refs_1_
  41.1 2.2 %collective-permute-start.2 = (bf16[1,256,128]{2,1,0:T(8,128)(2,1)S(1)}, bf16[1,256,128]{2,1,0:T(8,128)(2,1)S(1)}, u32[]{:S(2)}, u32[]{:S(2)}) collective-permute-start(bf16[1,256,128]{2,1,0:T(8,128)(2,1)S(1)} %get-tuple-element.48), channel_id=1, source_target_pairs={{0,10},{1,11},{2,8},{3,9},{4,14},{5,15},{6,12},{7,13},{8,2},{9,3},... | collective-permute-start | bytes 196616 | tf_op jit(solution)/shard_map/ppermute | solution.py:455
  43.3 0.0 collective-permute-done.13.refs_3_
  43.3 2.1 %collective-permute-start.3 = (bf16[1,256,128]{2,1,0:T(8,128)(2,1)S(1)}, bf16[1,256,128]{2,1,0:T(8,128)(2,1)S(1)}, u32[]{:S(2)}, u32[]{:S(2)}) collective-permute-start(bf16[1,256,128]{2,1,0:T(8,128)(2,1)S(1)} %get-tuple-element.49), channel_id=1, source_target_pairs={{0,12},{1,13},{2,14},{3,15},{4,8},{5,9},{6,10},{7,11},{8,4},{9,5},... | collective-permute-start | bytes 196616 | tf_op jit(solution)/shard_map/ppermute | solution.py:455
  45.5 0.0 collective-permute-done.14.refs_5_
  45.5 1.0 collective-permute-start.4
  46.5 0.0 collective-permute-done.10.theirs
  46.5 5.3 %shard_map.91 = (bf16[1,256,128]{2,1,0:T(8,128)(2,1)S(1)}, bf16[1,256,128]{2,1,0:T(8,128)(2,1)S(1)}, bf16[1,256,128]{2,1,0:T(8,128)(2,1)S(1)}, bf16[1,256,128]{2...) custom-call(s32[2]{0:T(128)S(1)} %pad_add_fusion.where, s32[8]{0:T(128)S(1)} %copy-done, ...), custom_call_target="tpu_custom_call" | custom-call | flops 536870912 | bytes 9011200 | tf_op jit(solution)/shard_map/pallas_call | solution.py:183
  51.8 0.0 collective-permute-done.1.refs_0_
  51.9 0.0 collective-permute-done.2.refs_1_
  51.9 1.7 %collective-permute-done.3.refs_2_ = bf16[1,256,128]{2,1,0:T(8,128)(2,1)S(1)} collective-permute-done((bf16[1,256,128]{2,1,0:T(8,128)(2,1)S(1)}, bf16[1,256,128]{2,1,0:T(8,128)(2,1)S(1)}, u32[]{:S(2)}, u32[]{:S(2)}) %collective-permute-start.3) | collective-permute-done | bytes 65568 | tf_op jit(solution)/shard_map/ppermute | solution.py:455
  53.5 1.7 %collective-permute-done.4.refs_3_ = bf16[1,256,128]{2,1,0:T(8,128)(2,1)S(1)} collective-permute-done((bf16[1,256,128]{2,1,0:T(8,128)(2,1)S(1)}, bf16[1,256,128]{2,1,0:T(8,128)(2,1)S(1)}, u32[]{:S(2)}, u32[]{:S(2)}) %collective-permute-start.4) | collective-permute-done | bytes 65568 | tf_op jit(solution)/shard_map/ppermute | solution.py:455
  55.3 0.9 collective-permute-start.19
  56.2 1.1 %collective-permute-start.18 = (bf16[1,256,128]{2,1,0:T(8,128)(2,1)S(1)}, bf16[1,256,128]{2,1,0:T(8,128)(2,1)S(1)}, u32[]{:S(2)}, u32[]{:S(2)}) collective-permute-start(bf16[1,256,128]{2,1,0:T(8,128)(2,1)S(1)} %get-tuple-element.69), channel_id=1, source_target_pairs={{0,12},{1,13},{2,14},{3,15},{4,8},{5,9},{6,10},{7,11},{8,4},{9,5},... | collective-permute-start | bytes 196616 | tf_op jit(solution)/shard_map/ppermute | solution.py:455
  57.3 0.0 collective-permute-start.17
  57.3 2.7 %collective-permute-start.16 = (bf16[1,256,128]{2,1,0:T(8,128)(2,1)S(1)}, bf16[1,256,128]{2,1,0:T(8,128)(2,1)S(1)}, u32[]{:S(2)}, u32[]{:S(2)}) collective-permute-start(bf16[1,256,128]{2,1,0:T(8,128)(2,1)S(1)} %get-tuple-element.65), channel_id=1, source_target_pairs={{0,8},{1,9},{2,10},{3,11},{4,12},{5,13},{6,14},{7,15},{8,0},{9,1},... | collective-permute-start | bytes 196616 | tf_op jit(solution)/shard_map/ppermute | solution.py:455
  60.0 5.8 %shard_map.92 = (bf16[4,256,128]{2,1,0:T(8,128)(2,1)S(1)}, bf16[4,256,128]{2,1,0:T(8,128)(2,1)S(1)}, bf16[4,256,128]{2,1,0:T(8,128)(2,1)S(1)}, bf16[4,256,128]{2...) custom-call(s32[2]{0:T(128)S(1)} %pad_add_fusion.where, ...), custom_call_target="tpu_custom_call" | custom-call | flops 1073741824 | bytes 8912896 | tf_op jit(solution)/shard_map/pallas_call | solution.py:183
  65.8 1.0 collective-permute-done.16.refs_2_
  66.8 3.1 %collective-permute-start.20 = (bf16[3,256,128]{2,1,0:T(8,128)(2,1)S(1)}, bf16[3,256,128]{2,1,0:T(8,128)(2,1)S(1)}, u32[]{:S(2)}, u32[]{:S(2)}) collective-permute-start(bf16[3,256,128]{2,1,0:T(8,128)(2,1)S(1)} %get-tuple-element.72), channel_id=1, source_target_pairs={{0,8},{1,9},{2,10},{3,11},{4,12},{5,13},{6,14},{7,15},{8,0},{9,1},... | collective-permute-start | bytes 589832 | tf_op jit(solution)/shard_map/ppermute | solution.py:455
  69.9 0.3 collective-permute-start.21
  70.2 0.8 collective-permute-start.23
  71.1 2.2 %collective-permute-start.24 = (bf16[4,256,128]{2,1,0:T(8,128)(2,1)S(1)}, bf16[4,256,128]{2,1,0:T(8,128)(2,1)S(1)}, u32[]{:S(2)}, u32[]{:S(2)}) collective-permute-start(bf16[4,256,128]{2,1,0:T(8,128)(2,1)S(1)} %get-tuple-element.81), channel_id=1, source_target_pairs={{0,4},{1,5},{2,6},{3,7},{4,0},{5,1},{6,2},{7,3},{8,12},{9,13},{10,... | collective-permute-start | bytes 786440 | tf_op jit(solution)/shard_map/ppermute | solution.py:455
  73.3 0.5 collective-permute-start.25
  73.8 8.8 %collective-permute-done.20.refs_2_.refs_10_ = bf16[3,256,128]{2,1,0:T(8,128)(2,1)S(1)} collective-permute-done((bf16[3,256,128]{2,1,0:T(8,128)(2,1)S(1)}, bf16[3,256,128]{2,1,0:T(8,128)(2,1)S(1)}, u32[]{:S(2)}, u32[]{:S(2)}) %collective-permute-start.20) | collective-permute-done | bytes 196640 | tf_op jit(solution)/shard_map/ppermute | solution.py:455
  82.6 0.4 collective-permute-start.22
  83.0 3.8 %collective-permute-done.21.refs_3_.refs_11_ = bf16[3,256,128]{2,1,0:T(8,128)(2,1)S(1)} collective-permute-done((bf16[3,256,128]{2,1,0:T(8,128)(2,1)S(1)}, bf16[3,256,128]{2,1,0:T(8,128)(2,1)S(1)}, u32[]{:S(2)}, u32[]{:S(2)}) %collective-permute-start.21) | collective-permute-done | bytes 196640 | tf_op jit(solution)/shard_map/ppermute | solution.py:455
  86.8 0.8 collective-permute-start.27
  87.6 13.0 %collective-permute-done.22.refs_5_.refs_13_ = bf16[3,256,128]{2,1,0:T(8,128)(2,1)S(1)} collective-permute-done((bf16[3,256,128]{2,1,0:T(8,128)(2,1)S(1)}, bf16[3,256,128]{2,1,0:T(8,128)(2,1)S(1)}, u32[]{:S(2)}, u32[]{:S(2)}) %collective-permute-start.22) | collective-permute-done | bytes 196640 | tf_op jit(solution)/shard_map/ppermute | solution.py:455
  100.6 4.6 %collective-permute-done.27.refs_7_.refs_15_ = bf16[3,256,128]{2,1,0:T(8,128)(2,1)S(1)} collective-permute-done((bf16[3,256,128]{2,1,0:T(8,128)(2,1)S(1)}, bf16[3,256,128]{2,1,0:T(8,128)(2,1)S(1)}, u32[]{:S(2)}, u32[]{:S(2)}) %collective-permute-start.27) | collective-permute-done | bytes 196640 | tf_op jit(solution)/shard_map/ppermute | solution.py:455
  105.2 0.6 shard_map.94
  105.8 0.6 collective-permute-start.28
  106.3 0.6 shard_map.93
  106.9 0.1 collective-permute-start.26
  107.0 1.8 %shard_map.95 = (bf16[128,2048]{1,0:T(8,128)(2,1)}, bf16[128,2048]{1,0:T(8,128)(2,1)}, bf16[128,2048]{1,0:T(8,128)(2,1)}, bf16[128,2048]{1,0:T(8,128)(2,1)}) custom-call(s32[2]{0:T(128)S(1)} %pad_add_fusion.where, bf16[4,256,128]{2,1,0:T(8,128)(2,1)S(1)} %get-tuple-element.77.refs_0_.refs_8_, ...), custom_call_target="tpu_custom_call" | custom-call | bytes 2097152 | tf_op jit(solution)/shard_map/pallas_call | solution.py:323
  108.8 1.8 %shard_map.96 = (bf16[128,2048]{1,0:T(8,128)(2,1)}, bf16[128,2048]{1,0:T(8,128)(2,1)}, bf16[128,2048]{1,0:T(8,128)(2,1)}, bf16[128,2048]{1,0:T(8,128)(2,1)}) custom-call(s32[2]{0:T(128)S(1)} %pad_add_fusion.where, ...), custom_call_target="tpu_custom_call", output_to_operand_aliasing={{0}: (3, {}), {1}: (4, {}), {2}: (5, {}), {3}: (6, {})} | custom-call | bytes 2097152 | tf_op jit(solution)/shard_map/pallas_call | solution.py:323
  (10 shorter events, 0.0 us)
Async XLA Ops:
  0.6 7.1 %collective-permute-start.6 = (bf16[128,2048]{1,0:T(8,128)(2,1)}, bf16[128,2048]{1,0:T(8,128)(2,1)S(1)}, u32[]{:S(2)}, u32[]{:S(2)}) collective-permute-start(bf16[128,2048]{1,0:T(8,128)(2,1)} %refs_0_.5), channel_id=1, source_target_pairs={{0,1},{1,0},{2,3},{3,2},{4,5},{5,4},{6,7},{7,6},{8,9},{9,8},{10,11... | collective-permute-start | bytes 1572872 | tf_op jit(solution)/shard_map/ppermute | solution.py:455
  1.4 6.4 %collective-permute-start.7 = (bf16[128,2048]{1,0:T(8,128)(2,1)}, bf16[128,2048]{1,0:T(8,128)(2,1)S(1)}, u32[]{:S(2)}, u32[]{:S(2)}) collective-permute-start(bf16[128,2048]{1,0:T(8,128)(2,1)} %refs_1_.3), channel_id=1, source_target_pairs={{0,1},{1,0},{2,3},{3,2},{4,5},{5,4},{6,7},{7,6},{8,9},{9,8},{10,11... | collective-permute-start | bytes 1572872 | tf_op jit(solution)/shard_map/ppermute | solution.py:455
  1.5 6.3 %collective-permute-start.8 = (bf16[128,2048]{1,0:T(8,128)(2,1)}, bf16[128,2048]{1,0:T(8,128)(2,1)S(1)}, u32[]{:S(2)}, u32[]{:S(2)}) collective-permute-start(bf16[128,2048]{1,0:T(8,128)(2,1)} %refs_2_.3), channel_id=1, source_target_pairs={{0,1},{1,0},{2,3},{3,2},{4,5},{5,4},{6,7},{7,6},{8,9},{9,8},{10,11... | collective-permute-start | bytes 1572872 | tf_op jit(solution)/shard_map/ppermute | solution.py:455
  1.9 11.4 %collective-permute-start = (bf16[128,2048]{1,0:T(8,128)(2,1)}, bf16[128,2048]{1,0:T(8,128)(2,1)S(1)}, u32[]{:S(2)}, u32[]{:S(2)}) collective-permute-start(bf16[128,2048]{1,0:T(8,128)(2,1)} %refs_0_.3), channel_id=1, source_target_pairs={{0,1},{1,0},{2,3},{3,2},{4,5},{5,4},{6,7},{7,6},{8,9},{9,8},{10,11... | collective-permute-start | bytes 1572872 | tf_op jit(solution)/shard_map/ppermute | solution.py:455
  3.5 19.6 %collective-permute-start.5 = (bf16[3,128,256]{2,1,0:T(8,128)(2,1)S(1)}, bf16[3,128,256]{2,1,0:T(8,128)(2,1)S(1)}, u32[]{:S(2)}, u32[]{:S(2)}) collective-permute-start(bf16[3,128,256]{2,1,0:T(8,128)(2,1)S(1)} %shard_map.86), channel_id=1, source_target_pairs={{0,8},{1,9},{2,10},{3,11},{4,12},{5,13},{6,14},{7,15},{8,0},{9,1},... | collective-permute-start | bytes 589832 | tf_op jit(solution)/shard_map/ppermute | solution.py:455
  7.8 38.7 %copy-start = (s32[8]{0:T(128)S(1)}, s32[8]{0:T(128)}, u32[]{:S(2)}) copy-start(s32[8]{0:T(128)} %partner.3) | copy-start | bytes 100
  8.5 18.9 %collective-permute-start.9 = (bf16[3,256,128]{2,1,0:T(8,128)(2,1)S(1)}, bf16[3,256,128]{2,1,0:T(8,128)(2,1)S(1)}, u32[]{:S(2)}, u32[]{:S(2)}) collective-permute-start(bf16[3,256,128]{2,1,0:T(8,128)(2,1)S(1)} %get-tuple-element.52), channel_id=1, source_target_pairs={{0,12},{1,13},{2,14},{3,15},{4,8},{5,9},{6,10},{7,11},{8,4},{9,5},... | collective-permute-start | bytes 589832 | tf_op jit(solution)/shard_map/ppermute | solution.py:455
  8.5 23.8 %collective-permute-start.12 = (bf16[3,256,128]{2,1,0:T(8,128)(2,1)S(1)}, bf16[3,256,128]{2,1,0:T(8,128)(2,1)S(1)}, u32[]{:S(2)}, u32[]{:S(2)}) collective-permute-start(bf16[3,256,128]{2,1,0:T(8,128)(2,1)S(1)} %get-tuple-element.56), channel_id=1, source_target_pairs={{0,10},{1,11},{2,8},{3,9},{4,14},{5,15},{6,12},{7,13},{8,2},{9,3},... | collective-permute-start | bytes 589832 | tf_op jit(solution)/shard_map/ppermute | solution.py:455
  14.0 27.1 %collective-permute-start.11 = (bf16[4,256,128]{2,1,0:T(8,128)(2,1)S(1)}, bf16[4,256,128]{2,1,0:T(8,128)(2,1)S(1)}, u32[]{:S(2)}, u32[]{:S(2)}) collective-permute-start(bf16[4,256,128]{2,1,0:T(8,128)(2,1)S(1)} %get-tuple-element.55), channel_id=1, source_target_pairs={{0,2},{1,3},{2,0},{3,1},{4,6},{5,7},{6,4},{7,5},{8,10},{9,11},{10,... | collective-permute-start | bytes 786440 | tf_op jit(solution)/shard_map/ppermute | solution.py:455
  14.3 29.1 %collective-permute-start.13 = (bf16[4,256,128]{2,1,0:T(8,128)(2,1)S(1)}, bf16[4,256,128]{2,1,0:T(8,128)(2,1)S(1)}, u32[]{:S(2)}, u32[]{:S(2)}) collective-permute-start(bf16[4,256,128]{2,1,0:T(8,128)(2,1)S(1)} %get-tuple-element.57), channel_id=1, source_target_pairs={{0,4},{1,5},{2,6},{3,7},{4,0},{5,1},{6,2},{7,3},{8,12},{9,13},{10,... | collective-permute-start | bytes 786440 | tf_op jit(solution)/shard_map/ppermute | solution.py:455
  23.1 22.4 %collective-permute-start.14 = (bf16[4,256,128]{2,1,0:T(8,128)(2,1)S(1)}, bf16[4,256,128]{2,1,0:T(8,128)(2,1)S(1)}, u32[]{:S(2)}, u32[]{:S(2)}) collective-permute-start(bf16[4,256,128]{2,1,0:T(8,128)(2,1)S(1)} %get-tuple-element.58), channel_id=1, source_target_pairs={{0,6},{1,7},{2,4},{3,5},{4,2},{5,3},{6,0},{7,1},{8,14},{9,15},{10,... | collective-permute-start | bytes 786440 | tf_op jit(solution)/shard_map/ppermute | solution.py:455
  27.3 12.9 %collective-permute-start.15 = (bf16[3,256,128]{2,1,0:T(8,128)(2,1)S(1)}, bf16[3,256,128]{2,1,0:T(8,128)(2,1)S(1)}, u32[]{:S(2)}, u32[]{:S(2)}) collective-permute-start(bf16[3,256,128]{2,1,0:T(8,128)(2,1)S(1)} %get-tuple-element.59), channel_id=1, source_target_pairs={{0,14},{1,15},{2,12},{3,13},{4,10},{5,11},{6,8},{7,9},{8,6},{9,7},... | collective-permute-start | bytes 589832 | tf_op jit(solution)/shard_map/ppermute | solution.py:455
  32.3 14.2 %collective-permute-start.10 = (bf16[3,128,128]{2,1,0:T(8,128)(2,1)S(1)}, bf16[3,128,128]{2,1,0:T(8,128)(2,1)S(1)}, u32[]{:S(2)}, u32[]{:S(2)}) collective-permute-start(bf16[3,128,128]{2,1,0:T(8,128)(2,1)S(1)} %shard_map.89), channel_id=1, source_target_pairs={{0,1},{1,0},{2,3},{3,2},{4,5},{5,4},{6,7},{7,6},{8,9},{9,8},{10,11... | collective-permute-start | bytes 294920 | tf_op jit(solution)/shard_map/ppermute | solution.py:455
  40.2 11.6 %collective-permute-start.1 = (bf16[1,256,128]{2,1,0:T(8,128)(2,1)S(1)}, bf16[1,256,128]{2,1,0:T(8,128)(2,1)S(1)}, u32[]{:S(2)}, u32[]{:S(2)}) collective-permute-start(bf16[1,256,128]{2,1,0:T(8,128)(2,1)S(1)} %get-tuple-element.47), channel_id=1, source_target_pairs={{0,8},{1,9},{2,10},{3,11},{4,12},{5,13},{6,14},{7,15},{8,0},{9,1},... | collective-permute-start | bytes 196616 | tf_op jit(solution)/shard_map/ppermute | solution.py:455
  41.1 10.8 %collective-permute-start.2 = (bf16[1,256,128]{2,1,0:T(8,128)(2,1)S(1)}, bf16[1,256,128]{2,1,0:T(8,128)(2,1)S(1)}, u32[]{:S(2)}, u32[]{:S(2)}) collective-permute-start(bf16[1,256,128]{2,1,0:T(8,128)(2,1)S(1)} %get-tuple-element.48), channel_id=1, source_target_pairs={{0,10},{1,11},{2,8},{3,9},{4,14},{5,15},{6,12},{7,13},{8,2},{9,3},... | collective-permute-start | bytes 196616 | tf_op jit(solution)/shard_map/ppermute | solution.py:455
  43.3 10.2 %collective-permute-start.3 = (bf16[1,256,128]{2,1,0:T(8,128)(2,1)S(1)}, bf16[1,256,128]{2,1,0:T(8,128)(2,1)S(1)}, u32[]{:S(2)}, u32[]{:S(2)}) collective-permute-start(bf16[1,256,128]{2,1,0:T(8,128)(2,1)S(1)} %get-tuple-element.49), channel_id=1, source_target_pairs={{0,12},{1,13},{2,14},{3,15},{4,8},{5,9},{6,10},{7,11},{8,4},{9,5},... | collective-permute-start | bytes 196616 | tf_op jit(solution)/shard_map/ppermute | solution.py:455
  45.5 9.8 %collective-permute-start.4 = (bf16[1,256,128]{2,1,0:T(8,128)(2,1)S(1)}, bf16[1,256,128]{2,1,0:T(8,128)(2,1)S(1)}, u32[]{:S(2)}, u32[]{:S(2)}) collective-permute-start(bf16[1,256,128]{2,1,0:T(8,128)(2,1)S(1)} %get-tuple-element.50), channel_id=1, source_target_pairs={{0,14},{1,15},{2,12},{3,13},{4,10},{5,11},{6,8},{7,9},{8,6},{9,7},... | collective-permute-start | bytes 196616 | tf_op jit(solution)/shard_map/ppermute | solution.py:455
  55.3 10.5 %collective-permute-start.19 = (bf16[1,256,128]{2,1,0:T(8,128)(2,1)S(1)}, bf16[1,256,128]{2,1,0:T(8,128)(2,1)S(1)}, u32[]{:S(2)}, u32[]{:S(2)}) collective-permute-start(bf16[1,256,128]{2,1,0:T(8,128)(2,1)S(1)} %get-tuple-element.71), channel_id=1, source_target_pairs={{0,14},{1,15},{2,12},{3,13},{4,10},{5,11},{6,8},{7,9},{8,6},{9,7},... | collective-permute-start | bytes 196616 | tf_op jit(solution)/shard_map/ppermute | solution.py:455
  56.2 9.6 %collective-permute-start.18 = (bf16[1,256,128]{2,1,0:T(8,128)(2,1)S(1)}, bf16[1,256,128]{2,1,0:T(8,128)(2,1)S(1)}, u32[]{:S(2)}, u32[]{:S(2)}) collective-permute-start(bf16[1,256,128]{2,1,0:T(8,128)(2,1)S(1)} %get-tuple-element.69), channel_id=1, source_target_pairs={{0,12},{1,13},{2,14},{3,15},{4,8},{5,9},{6,10},{7,11},{8,4},{9,5},... | collective-permute-start | bytes 196616 | tf_op jit(solution)/shard_map/ppermute | solution.py:455
  57.3 8.5 %collective-permute-start.17 = (bf16[1,256,128]{2,1,0:T(8,128)(2,1)S(1)}, bf16[1,256,128]{2,1,0:T(8,128)(2,1)S(1)}, u32[]{:S(2)}, u32[]{:S(2)}) collective-permute-start(bf16[1,256,128]{2,1,0:T(8,128)(2,1)S(1)} %get-tuple-element.67), channel_id=1, source_target_pairs={{0,10},{1,11},{2,8},{3,9},{4,14},{5,15},{6,12},{7,13},{8,2},{9,3},... | collective-permute-start | bytes 196616 | tf_op jit(solution)/shard_map/ppermute | solution.py:455
  57.3 9.5 %collective-permute-start.16 = (bf16[1,256,128]{2,1,0:T(8,128)(2,1)S(1)}, bf16[1,256,128]{2,1,0:T(8,128)(2,1)S(1)}, u32[]{:S(2)}, u32[]{:S(2)}) collective-permute-start(bf16[1,256,128]{2,1,0:T(8,128)(2,1)S(1)} %get-tuple-element.65), channel_id=1, source_target_pairs={{0,8},{1,9},{2,10},{3,11},{4,12},{5,13},{6,14},{7,15},{8,0},{9,1},... | collective-permute-start | bytes 196616 | tf_op jit(solution)/shard_map/ppermute | solution.py:455
  66.8 15.8 %collective-permute-start.20 = (bf16[3,256,128]{2,1,0:T(8,128)(2,1)S(1)}, bf16[3,256,128]{2,1,0:T(8,128)(2,1)S(1)}, u32[]{:S(2)}, u32[]{:S(2)}) collective-permute-start(bf16[3,256,128]{2,1,0:T(8,128)(2,1)S(1)} %get-tuple-element.72), channel_id=1, source_target_pairs={{0,8},{1,9},{2,10},{3,11},{4,12},{5,13},{6,14},{7,15},{8,0},{9,1},... | collective-permute-start | bytes 589832 | tf_op jit(solution)/shard_map/ppermute | solution.py:455
  69.9 16.9 %collective-permute-start.21 = (bf16[3,256,128]{2,1,0:T(8,128)(2,1)S(1)}, bf16[3,256,128]{2,1,0:T(8,128)(2,1)S(1)}, u32[]{:S(2)}, u32[]{:S(2)}) collective-permute-start(bf16[3,256,128]{2,1,0:T(8,128)(2,1)S(1)} %get-tuple-element.74), channel_id=1, source_target_pairs={{0,10},{1,11},{2,8},{3,9},{4,14},{5,15},{6,12},{7,13},{8,2},{9,3},... | collective-permute-start | bytes 589832 | tf_op jit(solution)/shard_map/ppermute | solution.py:455
  70.2 34.9 %collective-permute-start.23 = (bf16[4,256,128]{2,1,0:T(8,128)(2,1)S(1)}, bf16[4,256,128]{2,1,0:T(8,128)(2,1)S(1)}, u32[]{:S(2)}, u32[]{:S(2)}) collective-permute-start(bf16[4,256,128]{2,1,0:T(8,128)(2,1)S(1)} %get-tuple-element.79), channel_id=1, source_target_pairs={{0,2},{1,3},{2,0},{3,1},{4,6},{5,7},{6,4},{7,5},{8,10},{9,11},{10,... | collective-permute-start | bytes 786440 | tf_op jit(solution)/shard_map/ppermute | solution.py:455
  71.1 34.1 %collective-permute-start.24 = (bf16[4,256,128]{2,1,0:T(8,128)(2,1)S(1)}, bf16[4,256,128]{2,1,0:T(8,128)(2,1)S(1)}, u32[]{:S(2)}, u32[]{:S(2)}) collective-permute-start(bf16[4,256,128]{2,1,0:T(8,128)(2,1)S(1)} %get-tuple-element.81), channel_id=1, source_target_pairs={{0,4},{1,5},{2,6},{3,7},{4,0},{5,1},{6,2},{7,3},{8,12},{9,13},{10,... | collective-permute-start | bytes 786440 | tf_op jit(solution)/shard_map/ppermute | solution.py:455
  73.3 31.8 %collective-permute-start.25 = (bf16[4,256,128]{2,1,0:T(8,128)(2,1)S(1)}, bf16[4,256,128]{2,1,0:T(8,128)(2,1)S(1)}, u32[]{:S(2)}, u32[]{:S(2)}) collective-permute-start(bf16[4,256,128]{2,1,0:T(8,128)(2,1)S(1)} %get-tuple-element.83), channel_id=1, source_target_pairs={{0,6},{1,7},{2,4},{3,5},{4,2},{5,3},{6,0},{7,1},{8,14},{9,15},{10,... | collective-permute-start | bytes 786440 | tf_op jit(solution)/shard_map/ppermute | solution.py:455
  82.6 18.0 %collective-permute-start.22 = (bf16[3,256,128]{2,1,0:T(8,128)(2,1)S(1)}, bf16[3,256,128]{2,1,0:T(8,128)(2,1)S(1)}, u32[]{:S(2)}, u32[]{:S(2)}) collective-permute-start(bf16[3,256,128]{2,1,0:T(8,128)(2,1)S(1)} %get-tuple-element.76), channel_id=1, source_target_pairs={{0,12},{1,13},{2,14},{3,15},{4,8},{5,9},{6,10},{7,11},{8,4},{9,5},... | collective-permute-start | bytes 589832 | tf_op jit(solution)/shard_map/ppermute | solution.py:455
  86.8 18.4 %collective-permute-start.27 = (bf16[3,256,128]{2,1,0:T(8,128)(2,1)S(1)}, bf16[3,256,128]{2,1,0:T(8,128)(2,1)S(1)}, u32[]{:S(2)}, u32[]{:S(2)}) collective-permute-start(bf16[3,256,128]{2,1,0:T(8,128)(2,1)S(1)} %get-tuple-element.85), channel_id=1, source_target_pairs={{0,14},{1,15},{2,12},{3,13},{4,10},{5,11},{6,8},{7,9},{8,6},{9,7},... | collective-permute-start | bytes 589832 | tf_op jit(solution)/shard_map/ppermute | solution.py:455
  105.8 3.0 %collective-permute-start.28 = (bf16[8,3,128,128]{3,2,1,0:T(8,128)(2,1)S(1)}, bf16[8,3,128,128]{3,2,1,0:T(8,128)(2,1)S(1)}, u32[]{:S(2)}, u32[]{:S(2)}) collective-permute-start(bf16[8,3,128,128]{3,2,1,0:T(8,128)(2,1)S(1)} %shard_map.94), channel_id=1, source_target_pairs={{0,1},{1,0},{2,3},{3,2},{4,5},{5,4},{6,7},{7,6},{8,9},{9,8},{10,11... | collective-permute-start | bytes 2359304 | tf_op jit(solution)/shard_map/ppermute | solution.py:455
  106.9 1.9 %collective-permute-start.26 = (bf16[8,1,128,128]{3,2,1,0:T(8,128)(2,1)S(1)}, bf16[8,1,128,128]{3,2,1,0:T(8,128)(2,1)S(1)}, u32[]{:S(2)}, u32[]{:S(2)}) collective-permute-start(bf16[8,1,128,128]{3,2,1,0:T(8,128)(2,1)S(1)} %shard_map.93), channel_id=1, source_target_pairs={{0,1},{1,0},{2,3},{3,2},{4,5},{5,4},{6,7},{7,6},{8,9},{9,8},{10,11... | collective-permute-start | bytes 786440 | tf_op jit(solution)/shard_map/ppermute | solution.py:455

commit v8 on v7

--- a/solution.py
+++ b/solution.py
@@ -472,8 +472,8 @@
     their_do = hop(cotangent, 1)
     keep_do = own_columns(place, [cotangent], chips)
     one |= pack(place, [0, *near], [keep, keep_do], [*theirs, their_do])
-    two = pack(place, far, [keep_do], [their_do])
     first = {0: one[0]} | to_chips(one, far[1:] + near)
+    two = pack(after(place, *(first[k] for k in near[:2])), far, [keep_do], [their_do])
     second = to_chips(two, far)
     early = hop(early, 2 * far[0])
     early = [early, hop(other_head(after(place, first[far[2]]), early), 1)]

time: 111 us -> 106 us (0.955)
  waiting for transfers between devices: 50.6 us -> 43.2 us
  starting transfers between devices: 35.8 us -> 38 us
    ppermute x29, waiting for transfers between devices: 50.6 us -> 43.2 us  [hop(): lax.ppermute(piece, 'ctx', [(i, i ^ distance) for i in range(devices)])]
    ppermute x29, starting transfers between devices: 35.8 us -> 38 us  [hop(): lax.ppermute(piece, 'ctx', [(i, i ^ distance) for i in range(devices)])]
  transfers between devices with their start and end apart: 29 -> 29, of which waited for: 11 -> 8; matrix products, arithmetic and copies ran while one was open for 0% -> 0% of each run, Pallas kernels for 19% -> 20%
where the time goes in v8:
time: 106 us; the launch traced here: 105 us
  waiting for transfers between devices  43.2 us (41%)
  starting transfers between devices  38 us (36%)
  Pallas kernels  23.2 us (22%)
    ppermute x29, waiting for transfers between devices, hop(): lax.ppermute(piece, 'ctx', [(i, i ^ distance) for i in range(devices)])  43.2 us
    ppermute x29, starting transfers between devices, hop(): lax.ppermute(piece, 'ctx', [(i, i ^ distance) for i in range(devices)])  38 us
    pallas_call x8, Pallas kernels, call(): pl.pallas_call(kernel, out_shape=out_shape, in_specs=[smem] * len(place)...  14.8 us
    pallas_call x2, Pallas kernels, scatter(): pl.pallas_call(kernel, out_shape=[out] * count, in_specs=[smem] + [vmem]...  3.56 us
    pallas_call x2, Pallas kernels, own_columns(): pl.pallas_call(kernel, out_shape=jax.ShapeDtypeStruct((chips, count, rows...  3.36 us
  transfers between devices with their start and end apart: 29, of which 8 were waited for; matrix products, arithmetic and copies ran while one was open for 0% of the time, Pallas kernels for 20%

profile of v8, /device:TPU:9, one launch (start us, length us, event | category | flops | bytes accessed | tf_op | source)
XLA Modules:
  0.0 105.3 jit_solution(15223392963394513902)
XLA Ops:
  0.6 0.7 collective-permute-start
  1.4 0.1 collective-permute-start.1
  1.5 0.4 collective-permute-start.2
  1.9 0.1 collective-permute-start.3
  2.0 0.1 pad_add_fusion.where
  2.0 1.5 %shard_map.84 = bf16[3,128,256]{2,1,0:T(8,128)(2,1)S(1)} custom-call(s32[2]{0:T(128)S(1)} %pad_add_fusion.where, bf16[128,2048]{1,0:T(8,128)(2,1)} %refs_0_.4, bf16[128,2048]{1,0:T(8,128)(2,1)} %refs_1_.3, bf16[128,2048]{1,0:T(8,128)(2,1)} %refs_2_.3), custom_call_target="tpu_custom_call" | custom-call | tf_op jit(solution)/shard_map/pallas_call | solution.py:240
  3.5 2.4 %collective-permute-start.10 = (bf16[3,128,256]{2,1,0:T(8,128)(2,1)S(1)}, bf16[3,128,256]{2,1,0:T(8,128)(2,1)S(1)}, u32[]{:S(2)}, u32[]{:S(2)}) collective-permute-start(bf16[3,128,256]{2,1,0:T(8,128)(2,1)S(1)} %shard_map.84), channel_id=1, source_target_pairs={{0,8},{1,9},{2,10},{3,11},{4,12},{5,13},{6,14},{7,15},{8,0},{9,1},... | collective-permute-start | bytes 589832 | tf_op jit(solution)/shard_map/ppermute | solution.py:455
  5.9 1.9 %shard_map.85.refs_0_ = bf16[8,3,128,128]{3,2,1,0:T(8,128)(2,1)S(1)} custom-call(s32[2]{0:T(128)S(1)} %pad_add_fusion.where, bf16[128,2048]{1,0:T(8,128)(2,1)} %refs_0_.4, bf16[128,2048]{1,0:T(8,128)(2,1)} %refs_1_.3, bf16[128,2048]{1,0:T(8,128)(2,1)} %refs_2_.3), custom_call_target="tpu_custom_call" | custom-call | tf_op jit(solution)/shard_map/pallas_call | solution.py:213
  7.8 0.0 copy-start
  7.8 0.0 collective-permute-done.refs_2_.refs_1_
  7.8 0.0 collective-permute-done.1.refs_3_.refs_2_
  7.8 0.0 collective-permute-done.2.refs_4_.refs_3_
  7.8 0.6 shard_map.89
  8.5 0.1 collective-permute-start.11
  8.5 1.5 %shard_map.86.refs_1_.refs_0_ = bf16[8,1,128,128]{3,2,1,0:T(8,128)(2,1)S(1)} custom-call(s32[2]{0:T(128)S(1)} %pad_add_fusion.where, bf16[128,2048]{1,0:T(8,128)(2,1)} %refs_0_.5), custom_call_target="tpu_custom_call" | custom-call | tf_op jit(solution)/shard_map/pallas_call | solution.py:213
  10.0 0.0 collective-permute-done.3.refs_5_.refs_1_
  10.0 0.7 shard_map.87
  10.8 1.3 %collective-permute-start.4 = (bf16[4,256,128]{2,1,0:T(8,128)(2,1)S(1)}, bf16[4,256,128]{2,1,0:T(8,128)(2,1)S(1)}, u32[]{:S(2)}, u32[]{:S(2)}) collective-permute-start(bf16[4,256,128]{2,1,0:T(8,128)(2,1)S(1)} %get-tuple-element.49), channel_id=1, source_target_pairs={{0,2},{1,3},{2,0},{3,1},{4,6},{5,7},{6,4},{7,5},{8,10},{9,11},{10,... | collective-permute-start | bytes 786440 | tf_op jit(solution)/shard_map/ppermute | solution.py:455
  12.1 1.2 %collective-permute-start.5 = (bf16[4,256,128]{2,1,0:T(8,128)(2,1)S(1)}, bf16[4,256,128]{2,1,0:T(8,128)(2,1)S(1)}, u32[]{:S(2)}, u32[]{:S(2)}) collective-permute-start(bf16[4,256,128]{2,1,0:T(8,128)(2,1)S(1)} %get-tuple-element.50), channel_id=1, source_target_pairs={{0,4},{1,5},{2,6},{3,7},{4,0},{5,1},{6,2},{7,3},{8,12},{9,13},{10,... | collective-permute-start | bytes 786440 | tf_op jit(solution)/shard_map/ppermute | solution.py:455
  13.3 0.2 collective-permute-start.14
  13.5 5.4 %collective-permute-done.10.piece.mine = bf16[3,128,256]{2,1,0:T(8,128)(2,1)S(1)} collective-permute-done((bf16[3,128,256]{2,1,0:T(8,128)(2,1)S(1)}, bf16[3,128,256]{2,1,0:T(8,128)(2,1)S(1)}, u32[]{:S(2)}, u32[]{:S(2)}) %collective-permute-start.10) | collective-permute-done | bytes 196640 | tf_op jit(solution)/shard_map/ppermute | solution.py:455
  18.9 4.1 %collective-permute-start.13 = (bf16[3,256,128]{2,1,0:T(8,128)(2,1)S(1)}, bf16[3,256,128]{2,1,0:T(8,128)(2,1)S(1)}, u32[]{:S(2)}, u32[]{:S(2)}) collective-permute-start(bf16[3,256,128]{2,1,0:T(8,128)(2,1)S(1)} %get-tuple-element.59), channel_id=1, source_target_pairs={{0,10},{1,11},{2,8},{3,9},{4,14},{5,15},{6,12},{7,13},{8,2},{9,3},... | collective-permute-start | bytes 589832 | tf_op jit(solution)/shard_map/ppermute | solution.py:455
  22.9 0.2 collective-permute-done.11.refs_4_
  23.1 3.2 %collective-permute-start.15 = (bf16[3,256,128]{2,1,0:T(8,128)(2,1)S(1)}, bf16[3,256,128]{2,1,0:T(8,128)(2,1)S(1)}, u32[]{:S(2)}, u32[]{:S(2)}) collective-permute-start(bf16[3,256,128]{2,1,0:T(8,128)(2,1)S(1)} %get-tuple-element.61), channel_id=1, source_target_pairs={{0,14},{1,15},{2,12},{3,13},{4,10},{5,11},{6,8},{7,9},{8,6},{9,7},... | collective-permute-start | bytes 589832 | tf_op jit(solution)/shard_map/ppermute | solution.py:455
  26.3 0.6 shard_map.90
  26.8 0.0 collective-permute-done.4.refs_1_
  26.8 0.9 collective-permute-start.12
  27.7 0.6 shard_map.88
  28.3 2.5 %collective-permute-start.6 = (bf16[1,256,128]{2,1,0:T(8,128)(2,1)S(1)}, bf16[1,256,128]{2,1,0:T(8,128)(2,1)S(1)}, u32[]{:S(2)}, u32[]{:S(2)}) collective-permute-start(bf16[1,256,128]{2,1,0:T(8,128)(2,1)S(1)} %get-tuple-element.52), channel_id=1, source_target_pairs={{0,8},{1,9},{2,10},{3,11},{4,12},{5,13},{6,14},{7,15},{8,0},{9,1},... | collective-permute-start | bytes 196616 | tf_op jit(solution)/shard_map/ppermute | solution.py:455
  30.8 6.4 %collective-permute-done.13.refs_2_ = bf16[3,256,128]{2,1,0:T(8,128)(2,1)S(1)} collective-permute-done((bf16[3,256,128]{2,1,0:T(8,128)(2,1)S(1)}, bf16[3,256,128]{2,1,0:T(8,128)(2,1)S(1)}, u32[]{:S(2)}, u32[]{:S(2)}) %collective-permute-start.13) | collective-permute-done | bytes 196640 | tf_op jit(solution)/shard_map/ppermute | solution.py:455
  37.2 4.1 %collective-permute-start.7 = (bf16[1,256,128]{2,1,0:T(8,128)(2,1)S(1)}, bf16[1,256,128]{2,1,0:T(8,128)(2,1)S(1)}, u32[]{:S(2)}, u32[]{:S(2)}) collective-permute-start(bf16[1,256,128]{2,1,0:T(8,128)(2,1)S(1)} %get-tuple-element.53), channel_id=1, source_target_pairs={{0,10},{1,11},{2,8},{3,9},{4,14},{5,15},{6,12},{7,13},{8,2},{9,3},... | collective-permute-start | bytes 196616 | tf_op jit(solution)/shard_map/ppermute | solution.py:455
  41.3 0.8 collective-permute-done.15.refs_6_
  42.1 4.4 %collective-permute-start.8 = (bf16[1,256,128]{2,1,0:T(8,128)(2,1)S(1)}, bf16[1,256,128]{2,1,0:T(8,128)(2,1)S(1)}, u32[]{:S(2)}, u32[]{:S(2)}) collective-permute-start(bf16[1,256,128]{2,1,0:T(8,128)(2,1)S(1)} %get-tuple-element.54), channel_id=1, source_target_pairs={{0,12},{1,13},{2,14},{3,15},{4,8},{5,9},{6,10},{7,11},{8,4},{9,5},... | collective-permute-start | bytes 196616 | tf_op jit(solution)/shard_map/ppermute | solution.py:455
  46.5 0.0 collective-permute-start.9
  46.5 0.0 collective-permute-done.12.theirs
  46.5 5.3 %shard_map.91 = (bf16[1,256,128]{2,1,0:T(8,128)(2,1)S(1)}, bf16[1,256,128]{2,1,0:T(8,128)(2,1)S(1)}, bf16[1,256,128]{2,1,0:T(8,128)(2,1)S(1)}, bf16[1,256,128]{2...) custom-call(s32[2]{0:T(128)S(1)} %pad_add_fusion.where, s32[8]{0:T(128)S(1)} %copy-done, ...), custom_call_target="tpu_custom_call" | custom-call | flops 536870912 | bytes 9011200 | tf_op jit(solution)/shard_map/pallas_call | solution.py:183
  51.9 0.0 collective-permute-done.7.refs_1_
  51.9 0.0 collective-permute-done.9.refs_3_
  51.9 2.4 %collective-permute-start.19 = (bf16[1,256,128]{2,1,0:T(8,128)(2,1)S(1)}, bf16[1,256,128]{2,1,0:T(8,128)(2,1)S(1)}, u32[]{:S(2)}, u32[]{:S(2)}) collective-permute-start(bf16[1,256,128]{2,1,0:T(8,128)(2,1)S(1)} %get-tuple-element.73), channel_id=1, source_target_pairs={{0,14},{1,15},{2,12},{3,13},{4,10},{5,11},{6,8},{7,9},{8,6},{9,7},... | collective-permute-start | bytes 196616 | tf_op jit(solution)/shard_map/ppermute | solution.py:455
  54.3 0.0 collective-permute-start.18
  54.3 2.2 %collective-permute-start.17 = (bf16[1,256,128]{2,1,0:T(8,128)(2,1)S(1)}, bf16[1,256,128]{2,1,0:T(8,128)(2,1)S(1)}, u32[]{:S(2)}, u32[]{:S(2)}) collective-permute-start(bf16[1,256,128]{2,1,0:T(8,128)(2,1)S(1)} %get-tuple-element.69), channel_id=1, source_target_pairs={{0,10},{1,11},{2,8},{3,9},{4,14},{5,15},{6,12},{7,13},{8,2},{9,3},... | collective-permute-start | bytes 196616 | tf_op jit(solution)/shard_map/ppermute | solution.py:455
  56.5 0.3 collective-permute-start.16
  56.8 5.8 %shard_map.92 = (bf16[4,256,128]{2,1,0:T(8,128)(2,1)S(1)}, bf16[4,256,128]{2,1,0:T(8,128)(2,1)S(1)}, bf16[4,256,128]{2,1,0:T(8,128)(2,1)S(1)}, bf16[4,256,128]{2...) custom-call(s32[2]{0:T(128)S(1)} %pad_add_fusion.where, ...), custom_call_target="tpu_custom_call" | custom-call | flops 1073741824 | bytes 8912896 | tf_op jit(solution)/shard_map/pallas_call | solution.py:183
  62.5 0.0 collective-permute-done.19.refs_7_
  62.6 0.0 collective-permute-done.18.refs_5_
  62.6 2.2 %collective-permute-start.20 = (bf16[3,256,128]{2,1,0:T(8,128)(2,1)S(1)}, bf16[3,256,128]{2,1,0:T(8,128)(2,1)S(1)}, u32[]{:S(2)}, u32[]{:S(2)}) collective-permute-start(bf16[3,256,128]{2,1,0:T(8,128)(2,1)S(1)} %get-tuple-element.74), channel_id=1, source_target_pairs={{0,8},{1,9},{2,10},{3,11},{4,12},{5,13},{6,14},{7,15},{8,0},{9,1},... | collective-permute-start | bytes 589832 | tf_op jit(solution)/shard_map/ppermute | solution.py:455
  64.8 1.1 %collective-permute-start.21 = (bf16[3,256,128]{2,1,0:T(8,128)(2,1)S(1)}, bf16[3,256,128]{2,1,0:T(8,128)(2,1)S(1)}, u32[]{:S(2)}, u32[]{:S(2)}) collective-permute-start(bf16[3,256,128]{2,1,0:T(8,128)(2,1)S(1)} %get-tuple-element.76), channel_id=1, source_target_pairs={{0,10},{1,11},{2,8},{3,9},{4,14},{5,15},{6,12},{7,13},{8,2},{9,3},... | collective-permute-start | bytes 589832 | tf_op jit(solution)/shard_map/ppermute | solution.py:455
  65.8 0.3 collective-permute-start.23
  66.2 1.0 collective-permute-start.24
  67.2 1.3 %collective-permute-start.25 = (bf16[4,256,128]{2,1,0:T(8,128)(2,1)S(1)}, bf16[4,256,128]{2,1,0:T(8,128)(2,1)S(1)}, u32[]{:S(2)}, u32[]{:S(2)}) collective-permute-start(bf16[4,256,128]{2,1,0:T(8,128)(2,1)S(1)} %get-tuple-element.85), channel_id=1, source_target_pairs={{0,6},{1,7},{2,4},{3,5},{4,2},{5,3},{6,0},{7,1},{8,14},{9,15},{10,... | collective-permute-start | bytes 786440 | tf_op jit(solution)/shard_map/ppermute | solution.py:455
  68.5 5.7 %collective-permute-done.20.refs_2_.refs_10_ = bf16[3,256,128]{2,1,0:T(8,128)(2,1)S(1)} collective-permute-done((bf16[3,256,128]{2,1,0:T(8,128)(2,1)S(1)}, bf16[3,256,128]{2,1,0:T(8,128)(2,1)S(1)}, u32[]{:S(2)}, u32[]{:S(2)}) %collective-permute-start.20) | collective-permute-done | bytes 196640 | tf_op jit(solution)/shard_map/ppermute | solution.py:455
  74.2 9.3 %collective-permute-done.21.refs_3_.refs_11_ = bf16[3,256,128]{2,1,0:T(8,128)(2,1)S(1)} collective-permute-done((bf16[3,256,128]{2,1,0:T(8,128)(2,1)S(1)}, bf16[3,256,128]{2,1,0:T(8,128)(2,1)S(1)}, u32[]{:S(2)}, u32[]{:S(2)}) %collective-permute-start.21) | collective-permute-done | bytes 196640 | tf_op jit(solution)/shard_map/ppermute | solution.py:455
  83.5 10.8 %collective-permute-done.22.refs_5_.refs_13_ = bf16[3,256,128]{2,1,0:T(8,128)(2,1)S(1)} collective-permute-done((bf16[3,256,128]{2,1,0:T(8,128)(2,1)S(1)}, bf16[3,256,128]{2,1,0:T(8,128)(2,1)S(1)}, u32[]{:S(2)}, u32[]{:S(2)}) %collective-permute-start.22) | collective-permute-done | bytes 196640 | tf_op jit(solution)/shard_map/ppermute | solution.py:455
  94.3 4.7 %collective-permute-done.27.refs_7_.refs_15_ = bf16[3,256,128]{2,1,0:T(8,128)(2,1)S(1)} collective-permute-done((bf16[3,256,128]{2,1,0:T(8,128)(2,1)S(1)}, bf16[3,256,128]{2,1,0:T(8,128)(2,1)S(1)}, u32[]{:S(2)}, u32[]{:S(2)}) %collective-permute-start.27) | collective-permute-done | bytes 196640 | tf_op jit(solution)/shard_map/ppermute | solution.py:455
  99.0 0.0 collective-permute-done.24.refs_4_.refs_12_
  99.0 0.0 collective-permute-done.25.refs_6_.refs_14_
  99.0 0.6 shard_map.94
  99.6 1.5 %collective-permute-start.28 = (bf16[8,3,128,128]{3,2,1,0:T(8,128)(2,1)S(1)}, bf16[8,3,128,128]{3,2,1,0:T(8,128)(2,1)S(1)}, u32[]{:S(2)}, u32[]{:S(2)}) collective-permute-start(bf16[8,3,128,128]{3,2,1,0:T(8,128)(2,1)S(1)} %shard_map.94), channel_id=1, source_target_pairs={{0,1},{1,0},{2,3},{3,2},{4,5},{5,4},{6,7},{7,6},{8,9},{9,8},{10,11... | collective-permute-start | bytes 2359304 | tf_op jit(solution)/shard_map/ppermute | solution.py:455
  101.1 0.6 shard_map.93
  101.6 0.1 collective-permute-start.26
  101.7 1.8 %shard_map.95 = (bf16[128,2048]{1,0:T(8,128)(2,1)}, bf16[128,2048]{1,0:T(8,128)(2,1)}, bf16[128,2048]{1,0:T(8,128)(2,1)}, bf16[128,2048]{1,0:T(8,128)(2,1)}) custom-call(s32[2]{0:T(128)S(1)} %pad_add_fusion.where, bf16[4,256,128]{2,1,0:T(8,128)(2,1)S(1)} %get-tuple-element.79.refs_0_.refs_8_, ...), custom_call_target="tpu_custom_call" | custom-call | bytes 2097152 | tf_op jit(solution)/shard_map/pallas_call | solution.py:323
  103.5 0.0 collective-permute-done.26.refs_0_
  103.5 0.0 collective-permute-done.28.refs_1_
  103.5 1.8 %shard_map.96 = (bf16[128,2048]{1,0:T(8,128)(2,1)}, bf16[128,2048]{1,0:T(8,128)(2,1)}, bf16[128,2048]{1,0:T(8,128)(2,1)}, bf16[128,2048]{1,0:T(8,128)(2,1)}) custom-call(s32[2]{0:T(128)S(1)} %pad_add_fusion.where, ...), custom_call_target="tpu_custom_call", output_to_operand_aliasing={{0}: (3, {}), {1}: (4, {}), {2}: (5, {}), {3}: (6, {})} | custom-call | bytes 2097152 | tf_op jit(solution)/shard_map/pallas_call | solution.py:323
  (10 shorter events, 0.0 us)
Async XLA Ops:
  0.6 7.1 %collective-permute-start = (bf16[128,2048]{1,0:T(8,128)(2,1)}, bf16[128,2048]{1,0:T(8,128)(2,1)S(1)}, u32[]{:S(2)}, u32[]{:S(2)}) collective-permute-start(bf16[128,2048]{1,0:T(8,128)(2,1)} %refs_0_.4), channel_id=1, source_target_pairs={{0,1},{1,0},{2,3},{3,2},{4,5},{5,4},{6,7},{7,6},{8,9},{9,8},{10,11... | collective-permute-start | bytes 1572872 | tf_op jit(solution)/shard_map/ppermute | solution.py:455
  1.4 6.4 %collective-permute-start.1 = (bf16[128,2048]{1,0:T(8,128)(2,1)}, bf16[128,2048]{1,0:T(8,128)(2,1)S(1)}, u32[]{:S(2)}, u32[]{:S(2)}) collective-permute-start(bf16[128,2048]{1,0:T(8,128)(2,1)} %refs_1_.3), channel_id=1, source_target_pairs={{0,1},{1,0},{2,3},{3,2},{4,5},{5,4},{6,7},{7,6},{8,9},{9,8},{10,11... | collective-permute-start | bytes 1572872 | tf_op jit(solution)/shard_map/ppermute | solution.py:455
  1.5 6.3 %collective-permute-start.2 = (bf16[128,2048]{1,0:T(8,128)(2,1)}, bf16[128,2048]{1,0:T(8,128)(2,1)S(1)}, u32[]{:S(2)}, u32[]{:S(2)}) collective-permute-start(bf16[128,2048]{1,0:T(8,128)(2,1)} %refs_2_.3), channel_id=1, source_target_pairs={{0,1},{1,0},{2,3},{3,2},{4,5},{5,4},{6,7},{7,6},{8,9},{9,8},{10,11... | collective-permute-start | bytes 1572872 | tf_op jit(solution)/shard_map/ppermute | solution.py:455
  1.9 8.2 %collective-permute-start.3 = (bf16[128,2048]{1,0:T(8,128)(2,1)}, bf16[128,2048]{1,0:T(8,128)(2,1)S(1)}, u32[]{:S(2)}, u32[]{:S(2)}) collective-permute-start(bf16[128,2048]{1,0:T(8,128)(2,1)} %refs_0_.5), channel_id=1, source_target_pairs={{0,1},{1,0},{2,3},{3,2},{4,5},{5,4},{6,7},{7,6},{8,9},{9,8},{10,11... | collective-permute-start | bytes 1572872 | tf_op jit(solution)/shard_map/ppermute | solution.py:455
  3.5 15.4 %collective-permute-start.10 = (bf16[3,128,256]{2,1,0:T(8,128)(2,1)S(1)}, bf16[3,128,256]{2,1,0:T(8,128)(2,1)S(1)}, u32[]{:S(2)}, u32[]{:S(2)}) collective-permute-start(bf16[3,128,256]{2,1,0:T(8,128)(2,1)S(1)} %shard_map.84), channel_id=1, source_target_pairs={{0,8},{1,9},{2,10},{3,11},{4,12},{5,13},{6,14},{7,15},{8,0},{9,1},... | collective-permute-start | bytes 589832 | tf_op jit(solution)/shard_map/ppermute | solution.py:455
  7.8 38.7 %copy-start = (s32[8]{0:T(128)S(1)}, s32[8]{0:T(128)}, u32[]{:S(2)}) copy-start(s32[8]{0:T(128)} %partner.3) | copy-start | bytes 100
  8.5 14.6 %collective-permute-start.11 = (bf16[3,256,128]{2,1,0:T(8,128)(2,1)S(1)}, bf16[3,256,128]{2,1,0:T(8,128)(2,1)S(1)}, u32[]{:S(2)}, u32[]{:S(2)}) collective-permute-start(bf16[3,256,128]{2,1,0:T(8,128)(2,1)S(1)} %get-tuple-element.56), channel_id=1, source_target_pairs={{0,12},{1,13},{2,14},{3,15},{4,8},{5,9},{6,10},{7,11},{8,4},{9,5},... | collective-permute-start | bytes 589832 | tf_op jit(solution)/shard_map/ppermute | solution.py:455
  10.8 16.1 %collective-permute-start.4 = (bf16[4,256,128]{2,1,0:T(8,128)(2,1)S(1)}, bf16[4,256,128]{2,1,0:T(8,128)(2,1)S(1)}, u32[]{:S(2)}, u32[]{:S(2)}) collective-permute-start(bf16[4,256,128]{2,1,0:T(8,128)(2,1)S(1)} %get-tuple-element.49), channel_id=1, source_target_pairs={{0,2},{1,3},{2,0},{3,1},{4,6},{5,7},{6,4},{7,5},{8,10},{9,11},{10,... | collective-permute-start | bytes 786440 | tf_op jit(solution)/shard_map/ppermute | solution.py:455
  12.1 15.7 %collective-permute-start.5 = (bf16[4,256,128]{2,1,0:T(8,128)(2,1)S(1)}, bf16[4,256,128]{2,1,0:T(8,128)(2,1)S(1)}, u32[]{:S(2)}, u32[]{:S(2)}) collective-permute-start(bf16[4,256,128]{2,1,0:T(8,128)(2,1)S(1)} %get-tuple-element.50), channel_id=1, source_target_pairs={{0,4},{1,5},{2,6},{3,7},{4,0},{5,1},{6,2},{7,3},{8,12},{9,13},{10,... | collective-permute-start | bytes 786440 | tf_op jit(solution)/shard_map/ppermute | solution.py:455
  13.3 33.2 %collective-permute-start.14 = (bf16[4,256,128]{2,1,0:T(8,128)(2,1)S(1)}, bf16[4,256,128]{2,1,0:T(8,128)(2,1)S(1)}, u32[]{:S(2)}, u32[]{:S(2)}) collective-permute-start(bf16[4,256,128]{2,1,0:T(8,128)(2,1)S(1)} %get-tuple-element.60), channel_id=1, source_target_pairs={{0,6},{1,7},{2,4},{3,5},{4,2},{5,3},{6,0},{7,1},{8,14},{9,15},{10,... | collective-permute-start | bytes 786440 | tf_op jit(solution)/shard_map/ppermute | solution.py:455
  18.9 18.3 %collective-permute-start.13 = (bf16[3,256,128]{2,1,0:T(8,128)(2,1)S(1)}, bf16[3,256,128]{2,1,0:T(8,128)(2,1)S(1)}, u32[]{:S(2)}, u32[]{:S(2)}) collective-permute-start(bf16[3,256,128]{2,1,0:T(8,128)(2,1)S(1)} %get-tuple-element.59), channel_id=1, source_target_pairs={{0,10},{1,11},{2,8},{3,9},{4,14},{5,15},{6,12},{7,13},{8,2},{9,3},... | collective-permute-start | bytes 589832 | tf_op jit(solution)/shard_map/ppermute | solution.py:455
  23.1 19.0 %collective-permute-start.15 = (bf16[3,256,128]{2,1,0:T(8,128)(2,1)S(1)}, bf16[3,256,128]{2,1,0:T(8,128)(2,1)S(1)}, u32[]{:S(2)}, u32[]{:S(2)}) collective-permute-start(bf16[3,256,128]{2,1,0:T(8,128)(2,1)S(1)} %get-tuple-element.61), channel_id=1, source_target_pairs={{0,14},{1,15},{2,12},{3,13},{4,10},{5,11},{6,8},{7,9},{8,6},{9,7},... | collective-permute-start | bytes 589832 | tf_op jit(solution)/shard_map/ppermute | solution.py:455
  26.8 19.7 %collective-permute-start.12 = (bf16[3,128,128]{2,1,0:T(8,128)(2,1)S(1)}, bf16[3,128,128]{2,1,0:T(8,128)(2,1)S(1)}, u32[]{:S(2)}, u32[]{:S(2)}) collective-permute-start(bf16[3,128,128]{2,1,0:T(8,128)(2,1)S(1)} %shard_map.90), channel_id=1, source_target_pairs={{0,1},{1,0},{2,3},{3,2},{4,5},{5,4},{6,7},{7,6},{8,9},{9,8},{10,11... | collective-permute-start | bytes 294920 | tf_op jit(solution)/shard_map/ppermute | solution.py:455
  28.3 23.5 %collective-permute-start.6 = (bf16[1,256,128]{2,1,0:T(8,128)(2,1)S(1)}, bf16[1,256,128]{2,1,0:T(8,128)(2,1)S(1)}, u32[]{:S(2)}, u32[]{:S(2)}) collective-permute-start(bf16[1,256,128]{2,1,0:T(8,128)(2,1)S(1)} %get-tuple-element.52), channel_id=1, source_target_pairs={{0,8},{1,9},{2,10},{3,11},{4,12},{5,13},{6,14},{7,15},{8,0},{9,1},... | collective-permute-start | bytes 196616 | tf_op jit(solution)/shard_map/ppermute | solution.py:455
  37.2 14.7 %collective-permute-start.7 = (bf16[1,256,128]{2,1,0:T(8,128)(2,1)S(1)}, bf16[1,256,128]{2,1,0:T(8,128)(2,1)S(1)}, u32[]{:S(2)}, u32[]{:S(2)}) collective-permute-start(bf16[1,256,128]{2,1,0:T(8,128)(2,1)S(1)} %get-tuple-element.53), channel_id=1, source_target_pairs={{0,10},{1,11},{2,8},{3,9},{4,14},{5,15},{6,12},{7,13},{8,2},{9,3},... | collective-permute-start | bytes 196616 | tf_op jit(solution)/shard_map/ppermute | solution.py:455
  42.1 9.8 %collective-permute-start.8 = (bf16[1,256,128]{2,1,0:T(8,128)(2,1)S(1)}, bf16[1,256,128]{2,1,0:T(8,128)(2,1)S(1)}, u32[]{:S(2)}, u32[]{:S(2)}) collective-permute-start(bf16[1,256,128]{2,1,0:T(8,128)(2,1)S(1)} %get-tuple-element.54), channel_id=1, source_target_pairs={{0,12},{1,13},{2,14},{3,15},{4,8},{5,9},{6,10},{7,11},{8,4},{9,5},... | collective-permute-start | bytes 196616 | tf_op jit(solution)/shard_map/ppermute | solution.py:455
  46.5 5.4 %collective-permute-start.9 = (bf16[1,256,128]{2,1,0:T(8,128)(2,1)S(1)}, bf16[1,256,128]{2,1,0:T(8,128)(2,1)S(1)}, u32[]{:S(2)}, u32[]{:S(2)}) collective-permute-start(bf16[1,256,128]{2,1,0:T(8,128)(2,1)S(1)} %get-tuple-element.55), channel_id=1, source_target_pairs={{0,14},{1,15},{2,12},{3,13},{4,10},{5,11},{6,8},{7,9},{8,6},{9,7},... | collective-permute-start | bytes 196616 | tf_op jit(solution)/shard_map/ppermute | solution.py:455
  51.9 10.6 %collective-permute-start.19 = (bf16[1,256,128]{2,1,0:T(8,128)(2,1)S(1)}, bf16[1,256,128]{2,1,0:T(8,128)(2,1)S(1)}, u32[]{:S(2)}, u32[]{:S(2)}) collective-permute-start(bf16[1,256,128]{2,1,0:T(8,128)(2,1)S(1)} %get-tuple-element.73), channel_id=1, source_target_pairs={{0,14},{1,15},{2,12},{3,13},{4,10},{5,11},{6,8},{7,9},{8,6},{9,7},... | collective-permute-start | bytes 196616 | tf_op jit(solution)/shard_map/ppermute | solution.py:455
  54.3 8.2 %collective-permute-start.18 = (bf16[1,256,128]{2,1,0:T(8,128)(2,1)S(1)}, bf16[1,256,128]{2,1,0:T(8,128)(2,1)S(1)}, u32[]{:S(2)}, u32[]{:S(2)}) collective-permute-start(bf16[1,256,128]{2,1,0:T(8,128)(2,1)S(1)} %get-tuple-element.71), channel_id=1, source_target_pairs={{0,12},{1,13},{2,14},{3,15},{4,8},{5,9},{6,10},{7,11},{8,4},{9,5},... | collective-permute-start | bytes 196616 | tf_op jit(solution)/shard_map/ppermute | solution.py:455
  54.3 8.2 %collective-permute-start.17 = (bf16[1,256,128]{2,1,0:T(8,128)(2,1)S(1)}, bf16[1,256,128]{2,1,0:T(8,128)(2,1)S(1)}, u32[]{:S(2)}, u32[]{:S(2)}) collective-permute-start(bf16[1,256,128]{2,1,0:T(8,128)(2,1)S(1)} %get-tuple-element.69), channel_id=1, source_target_pairs={{0,10},{1,11},{2,8},{3,9},{4,14},{5,15},{6,12},{7,13},{8,2},{9,3},... | collective-permute-start | bytes 196616 | tf_op jit(solution)/shard_map/ppermute | solution.py:455
  56.5 6.1 %collective-permute-start.16 = (bf16[1,256,128]{2,1,0:T(8,128)(2,1)S(1)}, bf16[1,256,128]{2,1,0:T(8,128)(2,1)S(1)}, u32[]{:S(2)}, u32[]{:S(2)}) collective-permute-start(bf16[1,256,128]{2,1,0:T(8,128)(2,1)S(1)} %get-tuple-element.67), channel_id=1, source_target_pairs={{0,8},{1,9},{2,10},{3,11},{4,12},{5,13},{6,14},{7,15},{8,0},{9,1},... | collective-permute-start | bytes 196616 | tf_op jit(solution)/shard_map/ppermute | solution.py:455
  62.6 11.6 %collective-permute-start.20 = (bf16[3,256,128]{2,1,0:T(8,128)(2,1)S(1)}, bf16[3,256,128]{2,1,0:T(8,128)(2,1)S(1)}, u32[]{:S(2)}, u32[]{:S(2)}) collective-permute-start(bf16[3,256,128]{2,1,0:T(8,128)(2,1)S(1)} %get-tuple-element.74), channel_id=1, source_target_pairs={{0,8},{1,9},{2,10},{3,11},{4,12},{5,13},{6,14},{7,15},{8,0},{9,1},... | collective-permute-start | bytes 589832 | tf_op jit(solution)/shard_map/ppermute | solution.py:455
  64.8 18.8 %collective-permute-start.21 = (bf16[3,256,128]{2,1,0:T(8,128)(2,1)S(1)}, bf16[3,256,128]{2,1,0:T(8,128)(2,1)S(1)}, u32[]{:S(2)}, u32[]{:S(2)}) collective-permute-start(bf16[3,256,128]{2,1,0:T(8,128)(2,1)S(1)} %get-tuple-element.76), channel_id=1, source_target_pairs={{0,10},{1,11},{2,8},{3,9},{4,14},{5,15},{6,12},{7,13},{8,2},{9,3},... | collective-permute-start | bytes 589832 | tf_op jit(solution)/shard_map/ppermute | solution.py:455
  65.8 33.1 %collective-permute-start.23 = (bf16[4,256,128]{2,1,0:T(8,128)(2,1)S(1)}, bf16[4,256,128]{2,1,0:T(8,128)(2,1)S(1)}, u32[]{:S(2)}, u32[]{:S(2)}) collective-permute-start(bf16[4,256,128]{2,1,0:T(8,128)(2,1)S(1)} %get-tuple-element.81), channel_id=1, source_target_pairs={{0,2},{1,3},{2,0},{3,1},{4,6},{5,7},{6,4},{7,5},{8,10},{9,11},{10,... | collective-permute-start | bytes 786440 | tf_op jit(solution)/shard_map/ppermute | solution.py:455
  66.2 32.8 %collective-permute-start.24 = (bf16[4,256,128]{2,1,0:T(8,128)(2,1)S(1)}, bf16[4,256,128]{2,1,0:T(8,128)(2,1)S(1)}, u32[]{:S(2)}, u32[]{:S(2)}) collective-permute-start(bf16[4,256,128]{2,1,0:T(8,128)(2,1)S(1)} %get-tuple-element.83), channel_id=1, source_target_pairs={{0,4},{1,5},{2,6},{3,7},{4,0},{5,1},{6,2},{7,3},{8,12},{9,13},{10,... | collective-permute-start | bytes 786440 | tf_op jit(solution)/shard_map/ppermute | solution.py:455
  67.2 31.7 %collective-permute-start.25 = (bf16[4,256,128]{2,1,0:T(8,128)(2,1)S(1)}, bf16[4,256,128]{2,1,0:T(8,128)(2,1)S(1)}, u32[]{:S(2)}, u32[]{:S(2)}) collective-permute-start(bf16[4,256,128]{2,1,0:T(8,128)(2,1)S(1)} %get-tuple-element.85), channel_id=1, source_target_pairs={{0,6},{1,7},{2,4},{3,5},{4,2},{5,3},{6,0},{7,1},{8,14},{9,15},{10,... | collective-permute-start | bytes 786440 | tf_op jit(solution)/shard_map/ppermute | solution.py:455
  74.2 20.1 %collective-permute-start.22 = (bf16[3,256,128]{2,1,0:T(8,128)(2,1)S(1)}, bf16[3,256,128]{2,1,0:T(8,128)(2,1)S(1)}, u32[]{:S(2)}, u32[]{:S(2)}) collective-permute-start(bf16[3,256,128]{2,1,0:T(8,128)(2,1)S(1)} %get-tuple-element.78), channel_id=1, source_target_pairs={{0,12},{1,13},{2,14},{3,15},{4,8},{5,9},{6,10},{7,11},{8,4},{9,5},... | collective-permute-start | bytes 589832 | tf_op jit(solution)/shard_map/ppermute | solution.py:455
  83.5 15.4 %collective-permute-start.27 = (bf16[3,256,128]{2,1,0:T(8,128)(2,1)S(1)}, bf16[3,256,128]{2,1,0:T(8,128)(2,1)S(1)}, u32[]{:S(2)}, u32[]{:S(2)}) collective-permute-start(bf16[3,256,128]{2,1,0:T(8,128)(2,1)S(1)} %get-tuple-element.87), channel_id=1, source_target_pairs={{0,14},{1,15},{2,12},{3,13},{4,10},{5,11},{6,8},{7,9},{8,6},{9,7},... | collective-permute-start | bytes 589832 | tf_op jit(solution)/shard_map/ppermute | solution.py:455
  99.6 4.0 %collective-permute-start.28 = (bf16[8,3,128,128]{3,2,1,0:T(8,128)(2,1)S(1)}, bf16[8,3,128,128]{3,2,1,0:T(8,128)(2,1)S(1)}, u32[]{:S(2)}, u32[]{:S(2)}) collective-permute-start(bf16[8,3,128,128]{3,2,1,0:T(8,128)(2,1)S(1)} %shard_map.94), channel_id=1, source_target_pairs={{0,1},{1,0},{2,3},{3,2},{4,5},{5,4},{6,7},{7,6},{8,9},{9,8},{10,11... | collective-permute-start | bytes 2359304 | tf_op jit(solution)/shard_map/ppermute | solution.py:455
  101.6 1.9 %collective-permute-start.26 = (bf16[8,1,128,128]{3,2,1,0:T(8,128)(2,1)S(1)}, bf16[8,1,128,128]{3,2,1,0:T(8,128)(2,1)S(1)}, u32[]{:S(2)}, u32[]{:S(2)}) collective-permute-start(bf16[8,1,128,128]{3,2,1,0:T(8,128)(2,1)S(1)} %shard_map.93), channel_id=1, source_target_pairs={{0,1},{1,0},{2,3},{3,2},{4,5},{5,4},{6,7},{7,6},{8,9},{9,8},{10,11... | collective-permute-start | bytes 786440 | tf_op jit(solution)/shard_map/ppermute | solution.py:455
